TPU v7x, 32 devices: a whole 2x2x4 slice. The times are simulated.
32 devices in a mesh: wide: 2 (over x), narrow: 16 (over z, y, core).
Axes of the slice: x: 2, y: 2, z: 4, core: 2. Of those that a mesh axis runs over, the one named last changes fastest.
Arguments:
- target: bfloat16 [32, 1024, 768], P('narrow', 'wide'), may hold values from -6 to 6
- encoded: bfloat16 [32, 1024, 768], P('narrow', 'wide'), may hold values from -6 to 6
- segments: int32 [32, 1024], P('narrow', 'wide'), may hold values from 0 to 3, as said below
- out_grad: bfloat16 [32, 1024, 768], P('narrow', 'wide'), may hold values from -6 to 6
- self_qkv_w: bfloat16 [768, 2304], replicated, may hold values from -0.3125 to 0.3125
- self_q_b: float32 [768], replicated, may hold values from -2 to 2
- self_v_b: float32 [768], replicated, may hold values from -2 to 2
- self_out_w: bfloat16 [768, 768], replicated, may hold values from -0.625 to 0.625
- self_out_b: float32 [768], replicated, may hold values from -3 to 3
- norm1_gain: float32 [768], replicated, may hold values from 0.5 to 1.5
- norm1_bias: float32 [768], replicated, may hold values from -2 to 2
- cross_q_w: bfloat16 [768, 768], replicated, may hold values from -0.3125 to 0.3125
- cross_q_b: float32 [768], replicated, may hold values from -2 to 2
- cross_kv_w: bfloat16 [768, 1536], replicated, may hold values from -0.3125 to 0.3125
- cross_v_b: float32 [768], replicated, may hold values from -2 to 2
- cross_out_w: bfloat16 [768, 768], replicated, may hold values from -0.625 to 0.625
- cross_out_b: float32 [768], replicated, may hold values from -3 to 3
- norm2_gain: float32 [768], replicated, may hold values from 0.5 to 1.5
- norm2_bias: float32 [768], replicated, may hold values from -2 to 2
- ffn_in_w: bfloat16 [768, 3072], replicated, may hold values from -0.21875 to 0.21875
- ffn_in_b: float32 [3072], replicated, may hold values from -2 to 2
- ffn_out_w: bfloat16 [3072, 768], replicated, may hold values from -0.15625 to 0.15625
- ffn_out_b: float32 [768], replicated, may hold values from -2 to 2
- norm3_gain: float32 [768], replicated, may hold values from 0.5 to 1.5
- norm3_bias: float32 [768], replicated, may hold values from -2 to 2
Outputs:
- layer_out: bfloat16 [32, 1024, 768], P('narrow', 'wide')
- target_grad: float32 [32, 1024, 768], P('narrow', 'wide')
- encoded_grad: float32 [32, 1024, 768], P('narrow', 'wide')
- self_qkv_w_grad: float32 [768, 2304], P('wide')
- self_q_b_grad: float32 [768], P('wide')
- self_v_b_grad: float32 [768], P('wide')
- self_out_w_grad: float32 [768, 768], P('wide')
- self_out_b_grad: float32 [768], P('wide')
- norm1_gain_grad: float32 [768], P('wide')
- norm1_bias_grad: float32 [768], P('wide')
- cross_q_w_grad: float32 [768, 768], P('wide')
- cross_q_b_grad: float32 [768], P('wide')
- cross_kv_w_grad: float32 [768, 1536], P('wide')
- cross_v_b_grad: float32 [768], P('wide')
- cross_out_w_grad: float32 [768, 768], P('wide')
- cross_out_b_grad: float32 [768], P('wide')
- norm2_gain_grad: float32 [768], P('wide')
- norm2_bias_grad: float32 [768], P('wide')
- ffn_in_w_grad: float32 [768, 3072], P('wide')
- ffn_in_b_grad: float32 [3072], P('wide')
- ffn_out_w_grad: float32 [3072, 768], P('wide')
- ffn_out_b_grad: float32 [768], P('wide')
- norm3_gain_grad: float32 [768], P('wide')
- norm3_bias_grad: float32 [768], P('wide')
Inputs may be any that keep to these rules, and one draw needn't show every extreme that they name: `segments`: rows come in aligned pairs (rows 2 i and 2 i + 1). In each pair one row, which one drawn from the seed, is a single document (id 0 throughout); the other holds four documents with ids 0, 1, 2, 3 in order, each of 256 tokens give or take 1024 // 8.
All inputs are finite; a program needn't handle non-finite values.
Results may differ from a plain program's by a relative error of at most 0.03.
Values may be sent and summed in bfloat16 or wider, within the bound.
No kernel may reach another device: no remote copies, remote signals or barrier semaphores. Data moves between devices by JAX's collectives and lax.ppermute only.
A program may use at most 256 MiB of HBM per device.

v0:
```python
import jax
import jax.numpy as jnp
from jax import lax
from jax.sharding import PartitionSpec as P

HD = 64


masked_score = -1000000000.0
norm_epsilon = 1e-05


def layer_norm(resid, gain_vec, bias_vec):
    center = resid - jnp.mean(resid, -1, keepdims=True)
    spread = jnp.mean(center * center, -1, keepdims=True)
    return center * lax.rsqrt(spread + norm_epsilon) * gain_vec + bias_vec


def exact_gelu(pre_act):
    return jax.nn.gelu(pre_act, approximate=False)


def matmul(left_op, right_op):
    return jnp.dot(left_op, right_op, preferred_element_type=jnp.float32)


def left_transposed(left_op, right_op):
    return lax.dot_general(
        left_op, right_op, (((0,), (0,)), ((), ())), preferred_element_type=jnp.float32
    )


def right_transposed(left_op, right_op):
    return lax.dot_general(
        left_op, right_op, (((1,), (1,)), ((), ())), preferred_element_type=jnp.float32
    )


def split_heads(tensor, heads):
    return tensor.reshape(tensor.shape[0], tensor.shape[1], heads, -1)


def allowed_mask(query_seg, key_seg, query_pos, key_pos, causal):
    allowed = query_seg[:, None, :, None] == key_seg[:, None, None, :]
    if causal:
        allowed = allowed & (key_pos[None, None, None, :] <= query_pos[None, None, :, None])
    return allowed


def masked_scores(query_heads, query_seg, query_pos, causal, key_block, key_seg, key_start):
    heads = query_heads.shape[2]
    key_pos = key_start + jnp.arange(key_seg.shape[1], dtype=jnp.int32)
    scores = jnp.einsum(
        "bthd,bshd->bhts",
        query_heads,
        split_heads(key_block, heads),
        preferred_element_type=jnp.float32,
    )
    return jnp.where(
        allowed_mask(query_seg, key_seg, query_pos, key_pos, causal), scores, masked_score
    )


def stats_block(carry, context, pieces, key_start):
    query_heads, query_seg, query_pos, causal = context
    key_block, key_seg = pieces
    top_old, total_old = carry
    scores = masked_scores(query_heads, query_seg, query_pos, causal, key_block, key_seg, key_start)
    top_new = jnp.maximum(top_old, jnp.max(scores, -1))
    total_new = total_old * jnp.exp(top_old - top_new) + jnp.sum(
        jnp.exp(scores - top_new[..., None]), -1
    )
    return (top_new, total_new)


def output_block(carry, context, pieces, key_start):
    query_heads, query_seg, query_pos, causal, log_total = context
    key_block, value_block, key_seg = pieces
    heads = query_heads.shape[2]
    scores = masked_scores(query_heads, query_seg, query_pos, causal, key_block, key_seg, key_start)
    weights = jnp.exp(scores - log_total[..., None]).astype(jnp.bfloat16)
    return carry + jnp.einsum(
        "bhts,bshd->bhtd",
        weights,
        split_heads(value_block, heads),
        preferred_element_type=jnp.float32,
    )


def back_terms(query_heads, grad_heads, log_total, delta_rows, key_heads, value_heads, allowed):
    scores = jnp.einsum(
        "bthd,bshd->bhts", query_heads, key_heads, preferred_element_type=jnp.float32
    )
    scores = jnp.where(allowed, scores, masked_score)
    probs = jnp.exp(scores - log_total[..., None])
    grad_probs = jnp.einsum(
        "bthd,bshd->bhts", grad_heads, value_heads, preferred_element_type=jnp.float32
    )
    grad_scores = (probs * (grad_probs - delta_rows[..., None])).astype(jnp.bfloat16)
    return (probs, grad_scores)


def attend_back(carry, context, pieces, key_start):
    query_heads, grad_heads, log_total, delta_rows, query_seg, query_pos, causal = context
    key_block, value_block, key_seg = pieces
    heads = query_heads.shape[2]
    grad_query, grad_keys, grad_values = carry
    key_heads = split_heads(key_block, heads)
    key_pos = key_start + jnp.arange(key_seg.shape[1], dtype=jnp.int32)
    allowed = allowed_mask(query_seg, key_seg, query_pos, key_pos, causal)
    probs, grad_scores = back_terms(
        query_heads,
        grad_heads,
        log_total,
        delta_rows,
        key_heads,
        split_heads(value_block, heads),
        allowed,
    )
    grad_query = grad_query + jnp.einsum(
        "bhts,bshd->bthd", grad_scores, key_heads, preferred_element_type=jnp.float32
    )
    key_part = jnp.einsum(
        "bhts,bthd->bshd", grad_scores, query_heads, preferred_element_type=jnp.float32
    )
    value_part = jnp.einsum(
        "bhts,bthd->bshd",
        probs.astype(jnp.bfloat16),
        grad_heads,
        preferred_element_type=jnp.float32,
    )
    key_part = key_part.reshape(key_part.shape[0], key_part.shape[1], -1)
    value_part = value_part.reshape(value_part.shape[0], value_part.shape[1], -1)
    grad_keys = lax.dynamic_update_slice_in_dim(grad_keys, key_part, key_start, 1)
    grad_values = lax.dynamic_update_slice_in_dim(grad_values, value_part, key_start, 1)
    return (grad_query, grad_keys, grad_values)


def fold_blocks(step, context, carry, parts, block_rows, skip_test):
    count = parts[0].shape[1]

    def one_block(block_index, inner):
        pieces = tuple(
            (
                lax.dynamic_slice_in_dim(member, block_index * block_rows, block_rows, 1)
                for member in parts
            )
        )
        block_start = block_index * block_rows

        def compute(current):
            return step(current, context, pieces, block_start)

        if skip_test is None:
            return compute(inner)
        return lax.cond(skip_test(block_start, block_rows), lambda current: current, compute, inner)

    return lax.fori_loop(0, count // block_rows, one_block, carry)


def body(
    target,
    encoded,
    segments,
    out_grad,
    self_qkv_w,
    self_q_b,
    self_v_b,
    self_out_w,
    self_out_b,
    norm1_gain,
    norm1_bias,
    cross_q_w,
    cross_q_b,
    cross_kv_w,
    cross_v_b,
    cross_out_w,
    cross_out_b,
    norm2_gain,
    norm2_bias,
    ffn_in_w,
    ffn_in_b,
    ffn_out_w,
    ffn_out_b,
    norm3_gain,
    norm3_bias,
):
    row_count, tok_count, width = target.shape
    heads = width // HD
    scaling = HD ** (-0.5)
    cycle_size = lax.axis_size("wide")
    full_len = tok_count * cycle_size
    first_pos = lax.axis_index("wide") * tok_count
    query_pos = first_pos + jnp.arange(tok_count, dtype=jnp.int32)
    last_pos = first_pos + tok_count - 1
    seg_marks = segments.astype(jnp.bfloat16)
    flat_in = target.reshape(-1, width)
    enc_flat = encoded.reshape(-1, width)

    def query_skip(block_start, stride):
        return block_start > last_pos

    def shaped(tensor):
        return tensor.reshape(row_count, tok_count, -1)

    def empty_stats():
        return (
            jnp.full((row_count, heads, tok_count), masked_score, jnp.float32),
            jnp.zeros((row_count, heads, tok_count), jnp.float32),
        )

    def empty_output():
        return jnp.zeros((row_count, heads, tok_count, HD), jnp.float32)

    def empty_back():
        return (
            jnp.zeros((row_count, tok_count, heads, HD), jnp.float32),
            jnp.zeros((row_count, full_len, width), jnp.float32),
            jnp.zeros((row_count, full_len, width), jnp.float32),
        )

    def merge_heads(normed):
        return jnp.transpose(normed, (0, 2, 1, 3)).reshape(-1, width)

    qkv_all = matmul(flat_in, self_qkv_w)
    self_query = shaped(((qkv_all[:, :width] + self_q_b) * scaling).astype(jnp.bfloat16))
    self_keys = shaped(qkv_all[:, width : 2 * width].astype(jnp.bfloat16))
    self_values = shaped((qkv_all[:, 2 * width :] + self_v_b).astype(jnp.bfloat16))
    self_qh = split_heads(self_query, heads)
    self_stat_ctx = (self_qh, seg_marks, query_pos, True)
    self_top, self_total = fold_blocks(
        stats_block,
        self_stat_ctx,
        empty_stats(),
        (
            lax.all_gather(self_keys, "wide", axis=1, tiled=True),
            lax.all_gather(seg_marks, "wide", axis=1, tiled=True),
        ),
        tok_count,
        query_skip,
    )
    self_lse = self_top + jnp.log(self_total)
    self_out_ctx = (self_qh, seg_marks, query_pos, True, self_lse)
    self_normed = fold_blocks(
        output_block,
        self_out_ctx,
        empty_output(),
        (
            lax.all_gather(self_keys, "wide", axis=1, tiled=True),
            lax.all_gather(self_values, "wide", axis=1, tiled=True),
            lax.all_gather(seg_marks, "wide", axis=1, tiled=True),
        ),
        tok_count,
        query_skip,
    )
    self_ob = merge_heads(self_normed).astype(jnp.bfloat16)
    branch_a = matmul(self_ob, self_out_w) + self_out_b
    hidden_one, norm1_pull = jax.vjp(
        layer_norm, flat_in.astype(jnp.float32) + branch_a, norm1_gain, norm1_bias
    )
    hidden_oneb = hidden_one.astype(jnp.bfloat16)
    cross_query = shaped(
        ((matmul(hidden_oneb, cross_q_w) + cross_q_b) * scaling).astype(jnp.bfloat16)
    )
    cross_qh = split_heads(cross_query, heads)
    kv_both = matmul(enc_flat, cross_kv_w)
    cross_keys = shaped(kv_both[:, :width].astype(jnp.bfloat16))
    cross_values = shaped((kv_both[:, width:] + cross_v_b).astype(jnp.bfloat16))
    cross_stat_ctx = (cross_qh, seg_marks, query_pos, False)
    cross_top, cross_total = fold_blocks(
        stats_block,
        cross_stat_ctx,
        empty_stats(),
        (
            lax.all_gather(cross_keys, "wide", axis=1, tiled=True),
            lax.all_gather(seg_marks, "wide", axis=1, tiled=True),
        ),
        tok_count,
        None,
    )
    cross_lse = cross_top + jnp.log(cross_total)
    cross_out_ctx = (cross_qh, seg_marks, query_pos, False, cross_lse)
    cross_normed = fold_blocks(
        output_block,
        cross_out_ctx,
        empty_output(),
        (
            lax.all_gather(cross_keys, "wide", axis=1, tiled=True),
            lax.all_gather(cross_values, "wide", axis=1, tiled=True),
            lax.all_gather(seg_marks, "wide", axis=1, tiled=True),
        ),
        tok_count,
        None,
    )
    cross_ob = merge_heads(cross_normed).astype(jnp.bfloat16)
    branch_c = matmul(cross_ob, cross_out_w) + cross_out_b
    hidden_two, norm2_pull = jax.vjp(layer_norm, hidden_one + branch_c, norm2_gain, norm2_bias)
    hidden_twob = hidden_two.astype(jnp.bfloat16)
    pre_act = matmul(hidden_twob, ffn_in_w) + ffn_in_b
    gelu_value, gelu_pull = jax.vjp(exact_gelu, pre_act)
    act_low = gelu_value.astype(jnp.bfloat16)
    branch_f = matmul(act_low, ffn_out_w) + ffn_out_b
    final_norm, norm3_pull = jax.vjp(layer_norm, hidden_two + branch_f, norm3_gain, norm3_bias)
    layer_out = final_norm.astype(jnp.bfloat16).reshape(row_count, tok_count, width)
    upstream = out_grad.reshape(-1, width).astype(jnp.float32)
    grad_r3, norm3_gain_grad, norm3_bias_grad = norm3_pull(upstream)
    grad_fb = grad_r3.astype(jnp.bfloat16)
    ffn_out_w_grad = left_transposed(act_low, grad_fb)
    ffn_out_b_grad = jnp.sum(grad_fb.astype(jnp.float32), 0)
    grad_pre = gelu_pull(right_transposed(grad_fb, ffn_out_w))[0].astype(jnp.bfloat16)
    ffn_in_w_grad = left_transposed(hidden_twob, grad_pre)
    ffn_in_b_grad = jnp.sum(grad_pre.astype(jnp.float32), 0)
    grad_h2 = grad_r3 + right_transposed(grad_pre, ffn_in_w)
    grad_r2, norm2_gain_grad, norm2_bias_grad = norm2_pull(grad_h2)
    grad_cb = grad_r2.astype(jnp.bfloat16)
    cross_out_w_grad = left_transposed(cross_ob, grad_cb)
    cross_out_b_grad = jnp.sum(grad_cb.astype(jnp.float32), 0)
    grad_co = shaped(right_transposed(grad_cb, cross_out_w).astype(jnp.bfloat16))
    cross_gh = split_heads(grad_co, heads)
    cross_delta = jnp.sum(
        jnp.transpose(cross_gh, (0, 2, 1, 3)).astype(jnp.float32) * cross_normed, -1
    )
    cross_back_ctx = (cross_qh, cross_gh, cross_lse, cross_delta, seg_marks, query_pos, False)
    cross_back_init = empty_back()
    cross_back = fold_blocks(
        attend_back,
        cross_back_ctx,
        cross_back_init,
        (
            lax.all_gather(cross_keys, "wide", axis=1, tiled=True),
            lax.all_gather(cross_values, "wide", axis=1, tiled=True),
            lax.all_gather(seg_marks, "wide", axis=1, tiled=True),
        ),
        tok_count,
        None,
    )
    cross_dq, cross_dk_all, cross_dv_all = cross_back
    cross_dk, cross_dv = (
        lax.psum_scatter(
            cross_dk_all.astype(jnp.bfloat16), "wide", scatter_dimension=1, tiled=True
        ).astype(jnp.float32),
        lax.psum_scatter(
            cross_dv_all.astype(jnp.bfloat16), "wide", scatter_dimension=1, tiled=True
        ).astype(jnp.float32),
    )
    grad_cq = cross_dq.reshape(-1, width).astype(jnp.bfloat16) * scaling
    grad_ckv = jnp.concatenate(
        [
            cross_dk.reshape(-1, width).astype(jnp.bfloat16),
            cross_dv.reshape(-1, width).astype(jnp.bfloat16),
        ],
        1,
    )
    cross_q_w_grad = left_transposed(hidden_oneb, grad_cq)
    cross_q_b_grad = jnp.sum(grad_cq.astype(jnp.float32), 0)
    cross_kv_w_grad = left_transposed(enc_flat, grad_ckv)
    cross_v_b_grad = jnp.sum(grad_ckv[:, width:].astype(jnp.float32), 0)
    encoded_grad = right_transposed(grad_ckv, cross_kv_w).reshape(row_count, tok_count, width)
    grad_h1 = grad_r2 + right_transposed(grad_cq, cross_q_w)
    grad_r1, norm1_gain_grad, norm1_bias_grad = norm1_pull(grad_h1)
    grad_ab = grad_r1.astype(jnp.bfloat16)
    self_out_w_grad = left_transposed(self_ob, grad_ab)
    self_out_b_grad = jnp.sum(grad_ab.astype(jnp.float32), 0)
    grad_so = shaped(right_transposed(grad_ab, self_out_w).astype(jnp.bfloat16))
    self_gh = split_heads(grad_so, heads)
    self_delta = jnp.sum(jnp.transpose(self_gh, (0, 2, 1, 3)).astype(jnp.float32) * self_normed, -1)
    self_back_ctx = (self_qh, self_gh, self_lse, self_delta, seg_marks, query_pos, True)
    self_back_init = empty_back()
    self_back = fold_blocks(
        attend_back,
        self_back_ctx,
        self_back_init,
        (
            lax.all_gather(self_keys, "wide", axis=1, tiled=True),
            lax.all_gather(self_values, "wide", axis=1, tiled=True),
            lax.all_gather(seg_marks, "wide", axis=1, tiled=True),
        ),
        tok_count,
        query_skip,
    )
    self_dq, self_dk_all, self_dv_all = self_back
    self_dk, self_dv = (
        lax.psum_scatter(
            self_dk_all.astype(jnp.bfloat16), "wide", scatter_dimension=1, tiled=True
        ).astype(jnp.float32),
        lax.psum_scatter(
            self_dv_all.astype(jnp.bfloat16), "wide", scatter_dimension=1, tiled=True
        ).astype(jnp.float32),
    )
    grad_qkv = jnp.concatenate(
        [
            self_dq.reshape(-1, width).astype(jnp.bfloat16) * scaling,
            self_dk.reshape(-1, width).astype(jnp.bfloat16),
            self_dv.reshape(-1, width).astype(jnp.bfloat16),
        ],
        1,
    )
    self_qkv_w_grad = left_transposed(flat_in, grad_qkv)
    self_q_b_grad = jnp.sum(grad_qkv[:, :width].astype(jnp.float32), 0)
    self_v_b_grad = jnp.sum(grad_qkv[:, 2 * width :].astype(jnp.float32), 0)
    target_grad = (grad_r1 + right_transposed(grad_qkv, self_qkv_w)).reshape(
        row_count, tok_count, width
    )
    local_grads = (
        self_qkv_w_grad,
        self_q_b_grad,
        self_v_b_grad,
        self_out_w_grad,
        self_out_b_grad,
        norm1_gain_grad,
        norm1_bias_grad,
        cross_q_w_grad,
        cross_q_b_grad,
        cross_kv_w_grad,
        cross_v_b_grad,
        cross_out_w_grad,
        cross_out_b_grad,
        norm2_gain_grad,
        norm2_bias_grad,
        ffn_in_w_grad,
        ffn_in_b_grad,
        ffn_out_w_grad,
        ffn_out_b_grad,
        norm3_gain_grad,
        norm3_bias_grad,
    )
    row_sums = (
        lax.psum_scatter(
            local_grads[0].astype(jnp.bfloat16), "wide", scatter_dimension=0, tiled=True
        ).astype(jnp.float32),
        lax.psum_scatter(
            local_grads[1].astype(jnp.bfloat16), "wide", scatter_dimension=0, tiled=True
        ).astype(jnp.float32),
        lax.psum_scatter(
            local_grads[2].astype(jnp.bfloat16), "wide", scatter_dimension=0, tiled=True
        ).astype(jnp.float32),
        lax.psum_scatter(
            local_grads[3].astype(jnp.bfloat16), "wide", scatter_dimension=0, tiled=True
        ).astype(jnp.float32),
        lax.psum_scatter(
            local_grads[4].astype(jnp.bfloat16), "wide", scatter_dimension=0, tiled=True
        ).astype(jnp.float32),
        lax.psum_scatter(
            local_grads[5].astype(jnp.bfloat16), "wide", scatter_dimension=0, tiled=True
        ).astype(jnp.float32),
        lax.psum_scatter(
            local_grads[6].astype(jnp.bfloat16), "wide", scatter_dimension=0, tiled=True
        ).astype(jnp.float32),
        lax.psum_scatter(
            local_grads[7].astype(jnp.bfloat16), "wide", scatter_dimension=0, tiled=True
        ).astype(jnp.float32),
        lax.psum_scatter(
            local_grads[8].astype(jnp.bfloat16), "wide", scatter_dimension=0, tiled=True
        ).astype(jnp.float32),
        lax.psum_scatter(
            local_grads[9].astype(jnp.bfloat16), "wide", scatter_dimension=0, tiled=True
        ).astype(jnp.float32),
        lax.psum_scatter(
            local_grads[10].astype(jnp.bfloat16), "wide", scatter_dimension=0, tiled=True
        ).astype(jnp.float32),
        lax.psum_scatter(
            local_grads[11].astype(jnp.bfloat16), "wide", scatter_dimension=0, tiled=True
        ).astype(jnp.float32),
        lax.psum_scatter(
            local_grads[12].astype(jnp.bfloat16), "wide", scatter_dimension=0, tiled=True
        ).astype(jnp.float32),
        lax.psum_scatter(
            local_grads[13].astype(jnp.bfloat16), "wide", scatter_dimension=0, tiled=True
        ).astype(jnp.float32),
        lax.psum_scatter(
            local_grads[14].astype(jnp.bfloat16), "wide", scatter_dimension=0, tiled=True
        ).astype(jnp.float32),
        lax.psum_scatter(
            local_grads[15].astype(jnp.bfloat16), "wide", scatter_dimension=0, tiled=True
        ).astype(jnp.float32),
        lax.psum_scatter(
            local_grads[16].astype(jnp.bfloat16), "wide", scatter_dimension=0, tiled=True
        ).astype(jnp.float32),
        lax.psum_scatter(
            local_grads[17].astype(jnp.bfloat16), "wide", scatter_dimension=0, tiled=True
        ).astype(jnp.float32),
        lax.psum_scatter(
            local_grads[18].astype(jnp.bfloat16), "wide", scatter_dimension=0, tiled=True
        ).astype(jnp.float32),
        lax.psum_scatter(
            local_grads[19].astype(jnp.bfloat16), "wide", scatter_dimension=0, tiled=True
        ).astype(jnp.float32),
        lax.psum_scatter(
            local_grads[20].astype(jnp.bfloat16), "wide", scatter_dimension=0, tiled=True
        ).astype(jnp.float32),
    )
    summed = (
        lax.psum(row_sums[0].astype(jnp.bfloat16), "narrow").astype(jnp.float32),
        lax.psum(row_sums[1].astype(jnp.bfloat16), "narrow").astype(jnp.float32),
        lax.psum(row_sums[2].astype(jnp.bfloat16), "narrow").astype(jnp.float32),
        lax.psum(row_sums[3].astype(jnp.bfloat16), "narrow").astype(jnp.float32),
        lax.psum(row_sums[4].astype(jnp.bfloat16), "narrow").astype(jnp.float32),
        lax.psum(row_sums[5].astype(jnp.bfloat16), "narrow").astype(jnp.float32),
        lax.psum(row_sums[6].astype(jnp.bfloat16), "narrow").astype(jnp.float32),
        lax.psum(row_sums[7].astype(jnp.bfloat16), "narrow").astype(jnp.float32),
        lax.psum(row_sums[8].astype(jnp.bfloat16), "narrow").astype(jnp.float32),
        lax.psum(row_sums[9].astype(jnp.bfloat16), "narrow").astype(jnp.float32),
        lax.psum(row_sums[10].astype(jnp.bfloat16), "narrow").astype(jnp.float32),
        lax.psum(row_sums[11].astype(jnp.bfloat16), "narrow").astype(jnp.float32),
        lax.psum(row_sums[12].astype(jnp.bfloat16), "narrow").astype(jnp.float32),
        lax.psum(row_sums[13].astype(jnp.bfloat16), "narrow").astype(jnp.float32),
        lax.psum(row_sums[14].astype(jnp.bfloat16), "narrow").astype(jnp.float32),
        lax.psum(row_sums[15].astype(jnp.bfloat16), "narrow").astype(jnp.float32),
        lax.psum(row_sums[16].astype(jnp.bfloat16), "narrow").astype(jnp.float32),
        lax.psum(row_sums[17].astype(jnp.bfloat16), "narrow").astype(jnp.float32),
        lax.psum(row_sums[18].astype(jnp.bfloat16), "narrow").astype(jnp.float32),
        lax.psum(row_sums[19].astype(jnp.bfloat16), "narrow").astype(jnp.float32),
        lax.psum(row_sums[20].astype(jnp.bfloat16), "narrow").astype(jnp.float32),
    )
    return (layer_out, target_grad, encoded_grad) + tuple(summed)


def solution(mesh):
    in_specs = (
        P("narrow", "wide", None),
        P("narrow", "wide", None),
        P("narrow", "wide"),
        P("narrow", "wide", None),
        P(),
        P(),
        P(),
        P(),
        P(),
        P(),
        P(),
        P(),
        P(),
        P(),
        P(),
        P(),
        P(),
        P(),
        P(),
        P(),
        P(),
        P(),
        P(),
        P(),
        P(),
    )
    out_specs = (
        P("narrow", "wide", None),
        P("narrow", "wide", None),
        P("narrow", "wide", None),
        P("wide", None),
        P("wide"),
        P("wide"),
        P("wide", None),
        P("wide"),
        P("wide"),
        P("wide"),
        P("wide", None),
        P("wide"),
        P("wide", None),
        P("wide"),
        P("wide", None),
        P("wide"),
        P("wide"),
        P("wide"),
        P("wide", None),
        P("wide"),
        P("wide", None),
        P("wide"),
        P("wide"),
        P("wide"),
    )
    return jax.shard_map(body, mesh=mesh, in_specs=in_specs, out_specs=out_specs, check_vma=False)
```

profile of v0, /device:TPU:0, one launch (start us, length us, event | category | flops | bytes accessed | tf_op | source)
XLA Modules:
  0.0 1297.6 jit_solution(13135531592529027559)
XLA Ops:
  9.2 5.2 fusion.107
  29.8 5.2 fusion.108
  47.7 5.6 all_gather.10
  62.6 7.2 all-gather.5.cloned.1.call-done
  71.1 27.3 %while.99 = (s32[]{:T(128)}, f32[2,12,512]{2,1,0:T(8,128)}, f32[2,12,512]{2,1,0:T(8,128)}, s32[]{:T(128)}, bf16[2,512]{1,0:T(2,128)(2,1)S(1)}, /*index=5*/bf16[2...) while((s32[]{:T(128)}, f32[2,12,512]{2,1,0:T(8,128)}, ...), condition=%wide.region_5.6_spmd.clone, body=%wide.region_0.5_spmd.clone.sunk | while | flops 839148544 | bytes 66261392 | solution.py:158
  71.1 25.2 %conditional.9 = (f32[2,12,512]{2,1,0:T(8,128)S(1)}, f32[2,12,512]{2,1,0:T(8,128)}) conditional(s32[]{:T(128)} %convert_element_type.500, (bf16[2,512]{1,0:T(2,128)(2,1)S(1)}, s32[]{:T(128)}, bf16[2,1024]{1,0:T(2,128)(2,1)S(1)}, s32[]{:T(128)}, bf16[2,1024,768]{1,2,0:T(8,128)(2,1)}, /*index=5*/bf16[2,512,12,64]{1,3,2,0:T(8,128)(2,1)}, ...), branch_computations={%region_1.3_spmd, %region_4.4_spmd} | conditional | flops 839148544 | bytes 66160816 | solution.py:156
  73.4 11.5 fusion.6
  84.9 10.8 exponential_reduce_fusion
  100.0 17.0 %all-gather.7.cloned.1.call-done = bf16[2,1024,768]{1,2,0:T(8,128)(2,1)} async-done(((bf16[2,512,768]{1,2,0:T(8,128)(2,1)}), bf16[2,1024,768]{1,2,0:T(8,128)(2,1)}) %all-gather.7.cloned.1.call-update) | async-done | bytes 3145744 | tf_op jit(solution)/shard_map/all_gather | solution.py:250
  119.0 18.2 %while.100 = (s32[]{:T(128)}, f32[2,12,512,64]{2,3,1,0:T(8,128)}, s32[]{:T(128)}, bf16[2,512]{1,0:T(2,128)(2,1)S(1)}, bf16[2,1024]{1,0:T(2,128)(2,1)S(1)}, /*ind...) while((s32[]{:T(128)}, f32[2,12,512,64]{2,3,1,0:T(8,128)}, ...), condition=%wide.region_9.10_spmd.clone, body=%wide.region_6.9_spmd.clone.sunk | while | flops 1632633856 | bytes 18944280 | solution.py:158
  119.0 17.7 %conditional.10 = (f32[2,12,512,64]{2,3,1,0:T(8,128)}) conditional(s32[]{:T(128)} %convert_element_type.501, (bf16[2,512]{1,0:T(2,128)(2,1)S(1)}, s32[]{:T(128)}, bf16[2,1024]{1,0:T(2,128)(2,1)S(1)}, s32[]{:T(128)}, bf16[2,1024,768]{1,2,0:T(8,128)(2,1)}, /*index=5*/bf16[2,512,12,64]{1,3,2,0:T(8,128)(2,1)}, f32[2,12,512]{2,1,0:T(8,128)}, ...), branch_computations={%region_7.7_spmd, %region_8.8_spmd} | conditional | flops 1632633856 | bytes 18942010 | solution.py:156
  124.2 12.5 fusion.17
  157.5 6.5 all-gather.9.cloned.1.call-done
  164.0 53.4 %while.102 = (s32[]{:T(128)}, f32[2,12,512]{2,1,0:T(8,128)}, f32[2,12,512]{2,1,0:T(8,128)}, bf16[2,512]{1,0:T(2,128)(2,1)S(1)}, bf16[2,1024]{1,0:T(2,128)(2,1)S(...) while((s32[]{:T(128)}, f32[2,12,512]{2,1,0:T(8,128)}, ...), condition=%wide.region_15.16_spmd.clone, body=%wide.region_12.15_spmd.clone.sunk | while | flops 837349376 | bytes 67821880 | solution.py:158
  166.2 12.1 fusion.195
  179.2 10.8 exponential_reduce_fusion.3
  193.5 10.9 fusion.195
  205.3 10.8 exponential_reduce_fusion.3
  219.0 32.3 %while.103 = (s32[]{:T(128)}, f32[2,12,512,64]{2,3,1,0:T(8,128)}, bf16[2,512]{1,0:T(2,128)(2,1)S(1)}, bf16[2,1024]{1,0:T(2,128)(2,1)S(1)}, bf16[2,1024,768]{1,2,...) while((s32[]{:T(128)}, f32[2,12,512,64]{2,3,1,0:T(8,128)}, ...), condition=%wide.region_17.18_spmd.clone, body=%wide.region_16.17_spmd.clone.sunk | while | flops 1631584256 | bytes 18407604 | solution.py:158
  224.0 10.9 select_add_fusion.2
  239.9 11.4 select_add_fusion.2
  260.4 35.3 %multiply_convert_fusion = (bf16[1024,3072]{1,0:T(8,128)(2,1)S(1)}, f32[1024,3072]{1,0:T(8,128)}, f32[1024,3072]{1,0:T(8,128)}) fusion(f32[3072]{0:T(1024)S(1)} %copy-done.88, bf16[768,3072]{1,0:T(8,128)(2,1)S(1)} %bitcast.314, f32[1024,768]{1,0:T(8,128)S(1)} %get-tuple-element.2083, f32[768]{0:T(1024)S(1)} %copy-done.95, f32[768]{0:T(1024)S(1)} %copy-done.77, ...), kind=kOutput, calls=%fused_computation.97 | convolution fusion | flops 5043388416 | bytes 39348224 | tf_op jit(solution)/shard_map/dot_general | solution.py:24
  295.7 5.5 fusion.101
  310.9 19.2 %fusion.102 = (bf16[3072]{0:T(1024)(128)(2,1)}, bf16[1024,3072]{1,0:T(8,128)(2,1)}) fusion(f32[1024,3072]{1,0:T(8,128)} %get-tuple-element.2058, bf16[1024,768]{1,0:T(8,128)(2,1)} %get-tuple-element.2042, bf16[3072,768]{1,0:T(8,128)(2,1)} %param.64, f32[1024,3072]{1,0:T(8,128)} %get-tuple-element.2084, f32[3072]{0:T(1024)S(1)} %copy-done.88), kind=kOutput, calls=%fused_computation.207 | convolution fusion | flops 4882166784 | bytes 37767168 | tf_op jit(solution)/shard_map/dot_general | solution.py:34
  330.2 10.6 multiply_reduce_fusion
  355.2 6.1 fusion.72
  367.3 141.6 %while.104 = (s32[]{:T(128)}, f32[2,512,12,64]{1,3,2,0:T(8,128)}, bf16[2,1024,768]{2,1,0:T(8,128)(2,1)}, bf16[2,1024,768]{2,1,0:T(8,128)(2,1)}, bf16[2,1024,768]...) while((s32[]{:T(128)}, f32[2,512,12,64]{1,3,2,0:T(8,128)}, ...), condition=%wide.region_28.29_spmd.clone, body=%wide.region_27.28_spmd.clone.sunk | while | flops 4078960640 | bytes 179462448 | solution.py:158
  369.3 10.1 fusion.211
  382.0 15.4 %fusion.212 = bf16[2,12,512,512]{2,3,1,0:T(8,128)(2,1)} fusion(f32[2,12,512,512]{3,2,1,0:T(8,128)} %fusion.211, f32[2,12,512]{2,1,0:T(8,128)} %get-tuple-element.2670, f32[2,12,512]{2,1,0:T(8,128)} %get-tuple-element.2667, pred[2,512,512]{1,2,0:T(8,128)(4,1)} %broadcast_compare_fusion.11, bf16[2,512,12,64]{1,3,2,0:T(8,128)(2,1)} %bitcast.289, ...), kind=kOutput, calls=%fused_computation.77.clone.1 | convolution fusion | flops 836763648 | bytes 41517056 | tf_op jit(solution)/shard_map/while/body/eval_jaxpr/bthd,bshd->bhts/dot_general | solution.py:96
  397.4 10.0 fusion.214
  410.0 12.4 fusion.213
  428.7 8.8 bitcast_add_fusion.3
  439.4 10.1 fusion.211
  452.0 15.4 %fusion.212 = bf16[2,12,512,512]{2,3,1,0:T(8,128)(2,1)} fusion(f32[2,12,512,512]{3,2,1,0:T(8,128)} %fusion.211, f32[2,12,512]{2,1,0:T(8,128)} %get-tuple-element.2670, f32[2,12,512]{2,1,0:T(8,128)} %get-tuple-element.2667, pred[2,512,512]{1,2,0:T(8,128)(4,1)} %broadcast_compare_fusion.11, bf16[2,512,12,64]{1,3,2,0:T(8,128)(2,1)} %bitcast.289, ...), kind=kOutput, calls=%fused_computation.77.clone.1 | convolution fusion | flops 836763648 | bytes 41517056 | tf_op jit(solution)/shard_map/while/body/eval_jaxpr/bthd,bshd->bhts/dot_general | solution.py:96
  467.4 10.0 fusion.214
  480.0 12.4 fusion.213
  498.8 9.7 bitcast_add_fusion.3
  535.8 5.4 fusion.71
  548.0 66.9 %while.101 = (s32[]{:T(128)}, f32[2,512,12,64]{1,3,2,0:T(8,128)}, bf16[2,1024,768]{1,2,0:T(8,128)(2,1)}, bf16[2,1024,768]{1,2,0:T(8,128)(2,1)}, s32[]{:T(128)}, ...) while((s32[]{:T(128)}, f32[2,512,12,64]{1,3,2,0:T(8,128)}, ...), condition=%wide.region_35.36_spmd.clone, body=%wide.region_32.35_spmd.clone.sunk | while | flops 4080010240 | bytes 201167488 | solution.py:158
  548.2 66.6 %conditional.11 = ((f32[2,512,12,64]{1,3,2,0:T(8,128)}, bf16[2,1024,768]{1,2,0:T(8,128)(2,1)}, bf16[2,1024,768]{1,2,0:T(8,128)(2,1)})) conditional(s32[]{:T(128)} %convert_element_type.502, (bf16[2,512]{1,0:T(2,128)(2,1)S(1)}, s32[]{:T(128)}, bf16[2,1024]{1,0:T(2,128)(2,1)S(1)}, s32[]{:T(128)}, bf16[2,1024,768]{1,2,0:T(8,128)(2,1)}, ...), branch_computations={%region_33.33_spmd, %region_34.34_spmd} | conditional | flops 4080010240 | bytes 201165120 | solution.py:156
  553.2 10.3 fusion.103
  563.5 15.6 %fusion.21 = bf16[2,12,512,512]{2,3,1,0:T(8,128)(2,1)} fusion(f32[2,12,512,512]{3,2,1,0:T(8,128)} %fusion.103, f32[2,12,512]{2,1,0:T(8,128)} %get-tuple-element.1378, f32[2,12,512]{2,1,0:T(8,128)} %get-tuple-element.1375, pred[2,512,512]{1,2,0:T(8,128)(4,1)} %compare_and_fusion.2, bf16[2,512,12,64]{1,3,2,0:T(8,128)(2,1)} %bitcast.288, ...), kind=kOutput, calls=%fused_computation.32 | convolution fusion | flops 836763648 | bytes 41517056 | tf_op jit(solution)/shard_map/while/body/eval_jaxpr/cond/branch_0_fun/bthd,bshd->bhts/dot_general | solution.py:96
  579.0 10.0 fusion.104
  591.8 9.6 bitcast_add_fusion
  601.4 11.4 fusion.25
  624.5 6.4 fusion.73
  640.8 103.8 %reduce-scatter.16.cloned.1.call-done = bf16[2,512,768]{2,1,0:T(8,128)(2,1)} async-done(((bf16[2,1024,768]{2,1,0:T(8,128)(2,1)}), bf16[2,512,768]{2,1,0:T(8,128)(2,1)}) %reduce-scatter.16.cloned.1.call-update) | async-done | bytes 1572880 | tf_op jit(solution)/shard_map/reduce_scatter | solution.py:383
  747.2 43.7 %reduce-scatter.18.cloned.1.call-done = bf16[2,512,768]{2,1,0:T(8,128)(2,1)} async-done(((bf16[2,1024,768]{2,1,0:T(8,128)(2,1)}), bf16[2,512,768]{2,1,0:T(8,128)(2,1)}) %reduce-scatter.18.cloned.1.call-update) | async-done | bytes 1572880 | tf_op jit(solution)/shard_map/reduce_scatter | solution.py:386
  793.4 8.5 fusion.62
  801.9 5.8 copy.155
  808.4 5.3 convolution_convert_fusion.7
  822.6 10.4 convolution_convert_fusion.1
  833.0 9.1 convolution_convert_fusion
  844.6 33.7 %reduce-scatter.34.cloned.1.call-done = bf16[384,2304]{1,0:T(8,128)(2,1)} async-done(((bf16[768,2304]{1,0:T(8,128)(2,1)}), bf16[384,2304]{1,0:T(8,128)(2,1)}) %reduce-scatter.34.cloned.1.call-update) | async-done | bytes 1769488
  882.2 20.8 %reduce-scatter.26.cloned.1.call-done = bf16[384,768]{1,0:T(8,128)(2,1)} async-done(((bf16[768,768]{1,0:T(8,128)(2,1)}), bf16[384,768]{1,0:T(8,128)(2,1)}) %reduce-scatter.26.cloned.1.call-update) | async-done | bytes 589840 | tf_op jit(solution)/shard_map/reduce_scatter | solution.py:449
  902.9 24.5 %reduce-scatter.24.cloned.1.call-done = bf16[384,768]{1,0:T(8,128)(2,1)} async-done(((bf16[768,768]{1,0:T(8,128)(2,1)}), bf16[384,768]{1,0:T(8,128)(2,1)}) %reduce-scatter.24.cloned.1.call-update) | async-done | bytes 589840 | tf_op jit(solution)/shard_map/reduce_scatter | solution.py:437
  927.5 24.6 %reduce-scatter.28.cloned.1.call-done = bf16[384,768]{1,0:T(8,128)(2,1)} async-done(((bf16[768,768]{1,0:T(8,128)(2,1)}), bf16[384,768]{1,0:T(8,128)(2,1)}) %reduce-scatter.28.cloned.1.call-update) | async-done | bytes 589840 | tf_op jit(solution)/shard_map/reduce_scatter | solution.py:461
  952.1 62.9 %reduce-scatter.30.cloned.1.call-done = bf16[384,3072]{1,0:T(8,128)(2,1)} async-done(((bf16[768,3072]{1,0:T(8,128)(2,1)}), bf16[384,3072]{1,0:T(8,128)(2,1)}) %reduce-scatter.30.cloned.1.call-update) | async-done | bytes 2359312 | tf_op jit(solution)/shard_map/reduce_scatter | solution.py:473
  1015.0 62.8 %reduce-scatter.32.cloned.1.call-done = bf16[1536,768]{1,0:T(8,128)(2,1)} async-done(((bf16[3072,768]{1,0:T(8,128)(2,1)}), bf16[1536,768]{1,0:T(8,128)(2,1)}) %reduce-scatter.32.cloned.1.call-update) | async-done | bytes 2359312 | tf_op jit(solution)/shard_map/reduce_scatter | solution.py:479
  1087.9 8.6 all-reduce.16
  1113.2 63.2 %all-reduce.14 = (bf16[384]{0:T(512)(128)(2,1)}, bf16[384]{0:T(512)(128)(2,1)}, bf16[384]{0:T(512)(128)(2,1)}, bf16[384]{0:T(512)(128)(2,1)}, bf16[384]{0:T(512)...) all-reduce(bf16[384]{0:T(512)(128)(2,1)S(1)} %dynamic-slice.1, ...), channel_id=1, replica_groups=mesh['wide'=2,'narrow'=16] {'narrow'}, use_global_device_ids=true, to_apply=%region_44.45 | all-reduce | flops 6528 | bytes 26112 | tf_op jit(solution)/shard_map/psum | solution.py:494
  1193.4 7.1 fusion.76
  1200.5 5.6 add_add_fusion.6
  1206.1 65.5 %all-reduce.19.cloned.1.call-done = (bf16[384,2304]{0,1:T(8,128)(2,1)}, bf16[384,1536]{0,1:T(8,128)(2,1)}, bf16[384,768]{1,0:T(8,128)(2,1)}, bf16[384,768]{1,0:T...) async-done(((bf16[384,2304]{0,1:T(8,128)(2,1)}, bf16[384,1536]{0,1:T(8,128)(2,1)}, bf16[384,768]{1,0:T(8,128)(2,1)}, ...) | async-done | bytes 9437200 | tf_op jit(solution)/shard_map/psum | solution.py:493
  (446 shorter events, 306.1 us)
Async XLA Ops:
  7.2 62.6 %all-gather.5.cloned.1.call-start = ((), (), s32[]{:S(2)}) async-start(), calls=%async_computation.11 | async-start | bytes 4718592 | tf_op jit(solution)/shard_map/all_gather | solution.py:249
  22.0 94.9 %all-gather.7.cloned.1.call-start = ((), (), s32[]{:S(2)}) async-start(), calls=%async_computation.12 | async-start | bytes 4718592 | tf_op jit(solution)/shard_map/all_gather | solution.py:250
  29.7 134.3 %all-gather.9.cloned.1.call-start = ((), (), s32[]{:S(2)}) async-start(), calls=%async_computation.13 | async-start | bytes 4718592 | tf_op jit(solution)/shard_map/all_gather | solution.py:288
  41.6 177.4 %all-gather.11.cloned.1.call-start = ((), (), s32[]{:S(2)}) async-start(), calls=%async_computation.14 | async-start | bytes 4718592 | tf_op jit(solution)/shard_map/all_gather | solution.py:289
  47.6 576.9 %reduce-scatter.20.cloned.1.call-start = ((), (), s32[]{:S(2)}) async-start(), calls=%async_computation.17 | async-start | bytes 4718592 | tf_op jit(solution)/shard_map/reduce_scatter | solution.py:339
  73.4 11.5 copy-start.11
  84.9 10.8 copy-start.29
  143.2 112.3 %copy-start.49 = (f32[1024]{0:T(1024)}, f32[1024]{0:T(1024)S(1)}, u32[]{:S(2)}) copy-start(f32[1024]{0:T(1024)S(1)} %broadcast_multiply_fusion.2) | copy-start | bytes 12292
  145.4 110.1 %copy-start.56 = (f32[1024]{0:T(1024)}, f32[1024]{0:T(1024)S(1)}, u32[]{:S(2)}) copy-start(f32[1024]{0:T(1024)S(1)} %fusion.78) | copy-start | bytes 12292
  164.4 13.9 %copy-start.8 = (pred[2,512,512]{1,2,0:T(8,128)(4,1)}, pred[2,512,512]{1,2,0:T(8,128)(4,1)S(1)}, u32[]{:S(2)}) copy-start(pred[2,512,512]{1,2,0:T(8,128)(4,1)S(1)} %broadcast_compare_fusion.9) | copy-start | bytes 1572868 | tf_op jit(solution)/shard_map/while
  179.2 10.8 copy-start.26
  179.2 10.8 copy-start.32
  191.7 12.7 copy-start.8
  205.3 10.8 copy-start.26
  205.3 10.8 copy-start.32
  251.2 3.8 copy-start.45
  255.6 40.1 %slice-start = ((s8[4718592]{0:T(1024)(128)(4,1)}), s8[4194304]{0:T(1024)(128)(4,1)S(1)}, s32[]{:S(2)}) async-start(s8[4718592]{0:T(1024)(128)(4,1)} %bitcast.311), calls=%async_computation.27 | async-start | bytes 8388608
  257.7 83.0 %copy-start.22 = (f32[1024,768]{1,0:T(8,128)}, f32[1024,768]{1,0:T(8,128)S(1)}, u32[]{:S(2)}) copy-start(f32[1024,768]{1,0:T(8,128)S(1)} %get-tuple-element.2083) | copy-start | bytes 9437188
  257.8 83.0 %copy-start.52 = (f32[1024]{0:T(1024)}, f32[1024]{0:T(1024)S(1)}, u32[]{:S(2)}) copy-start(f32[1024]{0:T(1024)S(1)} %broadcast_multiply_fusion.1) | copy-start | bytes 12292
  260.3 80.4 %copy-start.61 = (f32[1024]{0:T(1024)}, f32[1024]{0:T(1024)S(1)}, u32[]{:S(2)}) copy-start(f32[1024]{0:T(1024)S(1)} %fusion.79) | copy-start | bytes 12292
  260.3 35.3 %slice-start.1 = ((s8[4718592]{0:T(1024)(128)(4,1)}), s8[524288]{0:T(1024)(128)(4,1)S(1)}, s32[]{:S(2)}) async-start(s8[4718592]{0:T(1024)(128)(4,1)} %bitcast.311), calls=%async_computation.28 | async-start | bytes 1048576
  260.3 35.3 %copy-start.92 = (f32[768]{0:T(1024)S(1)}, f32[768]{0:T(1024)}, u32[]{:S(2)}) copy-start(f32[768]{0:T(1024)} %param.65) | copy-start | bytes 9220
  295.7 5.5 copy-start.96
  342.3 3.8 copy-start.83
  355.2 6.1 copy-start.12
  369.1 10.4 copy-start.1
  369.3 11.3 copy-start.9
  439.1 10.4 copy-start.1
  439.4 11.3 copy-start.9
  508.9 115.6 %reduce-scatter.22.cloned.1.call-start = ((), (), s32[]{:S(2)}) async-start(), calls=%async_computation.18 | async-start | bytes 4718592 | tf_op jit(solution)/shard_map/reduce_scatter | solution.py:342
  509.5 235.1 %reduce-scatter.16.cloned.1.call-start = ((), (), s32[]{:S(2)}) async-start(), calls=%async_computation.15 | async-start | bytes 4718592 | tf_op jit(solution)/shard_map/reduce_scatter | solution.py:383
  509.5 5.0 copy-start.57
  509.5 5.0 copy-start.64
  509.5 5.0 copy-start.75
  509.5 5.0 copy-start.85
  514.5 3.9 copy-start.43
  553.2 10.3 copy-start.2
  591.8 9.6 copy-start.14
  591.8 9.6 copy-start.44
  591.8 9.6 copy-start.48
  601.4 11.4 copy-start.15
  619.7 171.2 %reduce-scatter.18.cloned.1.call-start = ((), (), s32[]{:S(2)}) async-start(), calls=%async_computation.16 | async-start | bytes 4718592 | tf_op jit(solution)/shard_map/reduce_scatter | solution.py:386
  624.4 217.8 %reduce-scatter.36.cloned.1.call-start = ((), (), s32[]{:S(2)}) async-start(), calls=%async_computation.25 | async-start | bytes 3538944
  635.3 243.1 %reduce-scatter.34.cloned.1.call-start = ((), (), s32[]{:S(2)}) async-start(), calls=%async_computation.24 | async-start | bytes 5308416
  807.7 95.2 %reduce-scatter.26.cloned.1.call-start = ((), (), s32[]{:S(2)}) async-start(), calls=%async_computation.20 | async-start | bytes 1769472 | tf_op jit(solution)/shard_map/reduce_scatter | solution.py:449
  813.7 113.7 %reduce-scatter.24.cloned.1.call-start = ((), (), s32[]{:S(2)}) async-start(), calls=%async_computation.19 | async-start | bytes 1769472 | tf_op jit(solution)/shard_map/reduce_scatter | solution.py:437
  818.1 4.4 copy-start.53
  818.1 4.4 copy-start.62
  818.1 4.4 copy-start.78
  818.1 134.0 %reduce-scatter.28.cloned.1.call-start = ((), (), s32[]{:S(2)}) async-start(), calls=%async_computation.21 | async-start | bytes 1769472 | tf_op jit(solution)/shard_map/reduce_scatter | solution.py:461
  822.5 192.5 %reduce-scatter.30.cloned.1.call-start = ((), (), s32[]{:S(2)}) async-start(), calls=%async_computation.22 | async-start | bytes 7077888 | tf_op jit(solution)/shard_map/reduce_scatter | solution.py:473
  833.0 244.7 %reduce-scatter.32.cloned.1.call-start = ((), (), s32[]{:S(2)}) async-start(), calls=%async_computation.23 | async-start | bytes 7077888 | tf_op jit(solution)/shard_map/reduce_scatter | solution.py:479
  842.2 429.4 %all-reduce.19.cloned.1.call-start = ((), (), s32[]{:S(2)}) async-start(), calls=%async_computation.26 | async-start | bytes 18874368 | tf_op jit(solution)/shard_map/psum | solution.py:493
  1077.7 5.5 copy-start.66
  1077.7 10.1 copy-start.67
  1077.8 10.1 copy-start.68
  1083.2 4.6 copy-start.69
  1193.3 7.1 copy-start.21
  1193.4 7.1 copy-start.40
  1193.4 7.1 copy-start.41
  1193.4 7.1 copy-start.42
  1193.4 7.1 copy-start.60
  1271.6 4.6 copy-start.31
  1285.4 4.4 copy-start.47
  (61 other events, 133.0 us)
Sparse Core Ops, SparseCore 0:
  22.2 47.6 all-gather.4
  72.0 44.9 all-gather.6
  119.1 44.9 all-gather.8
  165.4 44.9 all-gather.10
  509.0 58.5 reduce-scatter.19
  570.4 43.3 reduce-scatter.21
  619.8 124.7 reduce-scatter.15
  747.5 43.3 reduce-scatter.17
  793.7 34.7 reduce-scatter.35
  830.6 47.6 reduce-scatter.33
  881.1 21.7 reduce-scatter.25
  905.7 21.7 reduce-scatter.23
  930.3 21.7 reduce-scatter.27
  954.9 59.9 reduce-scatter.29
  1017.7 59.9 reduce-scatter.31
  1083.4 188.1 all-reduce.18
where the time goes:
time: 1310 us; the launch traced here: 1300 us
  waiting for transfers between devices  474 us (36%)
  matrix products  397 us (30%)
  local copies, waits for them, and re-layouts  205 us (16%)
  other arithmetic  124 us (9%)
  blocking collectives  77.4 us (6%)
  between operations  16.5 us (1%)
    reduce_scatter x1, waiting for transfers between devices, body(): lax.psum_scatter(self_dk_all.astype(jnp.bfloat16), 'wide', scatter_dimens...  104 us
    unnamed x193, local copies, waits for them, and re-layouts  76.9 us
    psum x1, waiting for transfers between devices, body(): lax.psum(row_sums[0].astype(jnp.bfloat16), 'narrow').astype(jnp.float32)  65.5 us
    psum x1, blocking collectives, body(): lax.psum(row_sums[1].astype(jnp.bfloat16), 'narrow').astype(jnp.float32)  63.2 us
    reduce_scatter x1, waiting for transfers between devices, body(): lax.psum_scatter(local_grads[15].astype(jnp.bfloat16), 'wide', scatter_di...  62.9 us
    reduce_scatter x1, waiting for transfers between devices, body(): lax.psum_scatter(local_grads[17].astype(jnp.bfloat16), 'wide', scatter_di...  62.8 us
    dot_general x7, matrix products, matmul(): return jnp.dot(left_op, right_op, preferred_element_type=jnp.float32)  57.8 us
    dot_general x7, matrix products, right_transposed(): lax.dot_general(left_op, right_op, (((1,), (1,)), ((), ())), preferred_el...  50.8 us
  transfers between devices with their start and end apart: 16, of which 12 were waited for; matrix products, arithmetic and copies ran while one was open for 30% of the time, Pallas kernels for 0%

commit v1 on v0

v1 whole, which is shorter than its diff:
```python
import functools

import jax
import jax.numpy as jnp
from jax import lax
from jax.experimental import pallas as pl
from jax.experimental.pallas import tpu as pltpu
from jax.sharding import Mesh, PartitionSpec as P

HD = 64
LANES = 128
norm_epsilon = 1e-05
masked_score = -1e9
BF = jnp.bfloat16
F32 = jnp.float32

NN = (((1,), (0,)), ((), ()))
NT = (((1,), (1,)), ((), ()))
TN = (((0,), (0,)), ((), ()))


def dot(a, b, dims=NN):
    return lax.dot_general(a, b, dims, preferred_element_type=F32)


def segment_terms(seg):
    lane = jnp.arange(LANES) % HD
    same = seg[..., None] == lane
    query_terms = jnp.where((lane < 4) & ~same, masked_score, 0.0).astype(BF)
    key_terms = jnp.where(((lane < 4) & same) | ((lane >= 4) & (lane < 7)), 1.0, 0.0).astype(BF)
    return query_terms, key_terms


def head_lanes(shape, head):
    lane = lax.broadcasted_iota(jnp.int32, shape, 1)
    return (lane < HD) if head == 0 else (lane >= HD)


def causal_scores(scores, causal, first_query, block, query_axis):
    if causal == "block":
        queries = lax.broadcasted_iota(jnp.int32, (block, block), query_axis)
        keys = lax.broadcasted_iota(jnp.int32, (block, block), 1 - query_axis)
        count = scores.shape[1 - query_axis]
        before = lax.slice_in_dim(scores, 0, count - block, axis=1 - query_axis)
        corner = lax.slice_in_dim(scores, count - block, count, axis=1 - query_axis)
        corner = jnp.where(keys <= queries, corner, masked_score)
        if count == block:
            return corner
        return jnp.concatenate([before, corner], 1 - query_axis)
    if causal == "mask":
        queries = first_query + lax.broadcasted_iota(jnp.int32, scores.shape, query_axis)
        keys = lax.broadcasted_iota(jnp.int32, scores.shape, 1 - query_axis)
        return jnp.where(keys <= queries, scores, masked_score)
    return scores


def half_slices(count, shift, swapped):
    if not swapped:
        return [(slice(0, count), slice(0, count))]
    half = count // 2
    return [
        (
            slice(part * half, (part + 1) * half),
            pl.ds(pl.multiple_of(lax.rem(part * half + shift, count), half), half),
        )
        for part in (0, 1)
    ]


def row_block(index, block, count, shift, swapped):
    if not swapped:
        return pl.ds(index * block, block)
    return pl.ds(pl.multiple_of(lax.rem(index * block + shift, count), block), block)


def forward_kernel(
    shift_ref, q_ref, k_ref, v_ref, qt_ref, kt_ref, o_ref, lse_ref, ka, va, qa,
    *, causal, block, swapped,
):
    tq, ts = q_ref.shape[0], k_ref.shape[0]
    pair = pl.program_id(1)
    shift = shift_ref[0]
    for here, there in half_slices(ts, shift, swapped):
        k, v, extra = k_ref[there, :], v_ref[there, :], kt_ref[there, :]
        for head in (0, 1):
            own = head_lanes(k.shape, head)
            ka[head, here, :] = jnp.where(own, k, extra)
            va[head, here, :] = jnp.where(own, v, extra)
    for here, there in half_slices(tq, shift, swapped):
        q, extra = q_ref[there, :], qt_ref[there, :]
        for head in (0, 1):
            qa[head, here, :] = jnp.where(head_lanes(q.shape, head), q, extra)
    lane = lax.broadcasted_iota(jnp.int32, (block, LANES), 1)
    for index in range(tq // block):
        count = (index + 1) * block if causal == "block" else ts
        outs, lses = [], []
        for head in (0, 1):
            scores = dot(qa[head, index * block : (index + 1) * block, :], ka[head, :count, :], NT)
            scores = causal_scores(scores, causal, shift + index * block, block, 0)
            top = jnp.max(scores, 1, keepdims=True)
            weights = jnp.exp(scores - top).astype(BF)
            sums = dot(weights, va[head, :count, :])
            ones_lane = HD + 6 if head == 0 else 6
            total = sums[:, ones_lane : ones_lane + 1]
            outs.append(sums / total)
            lses.append(top + jnp.log(total))
        there = row_block(index, block, tq, shift, swapped)
        o_ref[there, :] = jnp.where(lane < HD, outs[0], outs[1]).astype(BF)
        lse_ref[there, :] = jnp.where(
            lane == 2 * pair, lses[0], jnp.where(lane == 2 * pair + 1, lses[1], lse_ref[there, :])
        )


def three_parts(x):
    parts = []
    for _ in range(3):
        part = x.astype(BF).astype(F32)
        parts.append(part)
        x = x - part
    return parts


def backward_kernel(
    shift_ref, q_ref, k_ref, v_ref, g_ref, o_ref, qt_ref, kt_ref, lse_ref,
    dq_ref, dk_ref, dv_ref, ka, va, qa, ga, k_turned, dk_sum, dv_sum, dq_turned,
    *, causal, block, swapped, scaling,
):
    tq, ts = q_ref.shape[0], k_ref.shape[0]
    pair = pl.program_id(1)
    shift = shift_ref[0]
    for here, there in half_slices(ts, shift, swapped):
        k, v, extra = k_ref[there, :], v_ref[there, :], kt_ref[there, :]
        for head in (0, 1):
            own = head_lanes(k.shape, head)
            ka[head, here, :] = jnp.where(own, k, extra)
            va[head, here, :] = jnp.where(own, v, extra)
        k_turned[:, here] = k.astype(F32).T.astype(BF)
    for here, there in half_slices(tq, shift, swapped):
        q, g, extra = q_ref[there, :], g_ref[there, :], qt_ref[there, :]
        products = g.astype(F32) * o_ref[there, :].astype(F32)
        lse = lse_ref[there, :]
        lane = lax.broadcasted_iota(jnp.int32, q.shape, 1)
        for head in (0, 1):
            own = head_lanes(q.shape, head)
            first = HD + 4 if head == 0 else 4
            delta = three_parts(-jnp.sum(jnp.where(own, products, 0.0), 1, keepdims=True))
            lse_col = three_parts(
                -jnp.sum(jnp.where(lane == 2 * pair + head, lse, 0.0), 1, keepdims=True)
            )
            q_extra, g_extra = extra.astype(F32), jnp.zeros(q.shape, F32)
            for part in range(3):
                q_extra = jnp.where(lane == first + part, lse_col[part], q_extra)
                g_extra = jnp.where(lane == first + part, delta[part], g_extra)
            qa[head, here, :] = jnp.where(own, q, q_extra.astype(BF))
            ga[head, here, :] = jnp.where(own, g, g_extra.astype(BF))
    blocks = tq // block
    for index in reversed(range(blocks)):
        count = (index + 1) * block if causal == "block" else ts
        rows = slice(index * block, (index + 1) * block)
        for head in (0, 1):
            q, g = qa[head, rows, :], ga[head, rows, :]
            scores = dot(ka[head, :count, :], q, NT)
            scores = causal_scores(scores, causal, shift + index * block, block, 1)
            probs = jnp.exp(scores)
            grads = (probs * dot(va[head, :count, :], g, NT)).astype(BF)
            dv, dk = dot(probs.astype(BF), g), dot(grads, q)
            if index == blocks - 1:
                dv_sum[head, :count, :] = dv
                dk_sum[head, :count, :] = dk
            else:
                dv_sum[head, :count, :] += dv
                dk_sum[head, :count, :] += dk
            own_rows = slice(HD * head, HD * (head + 1))
            dq_turned[own_rows, rows] = dot(k_turned[own_rows, :count], grads)
        there = row_block(index, block, tq, shift, swapped)
        dq_ref[there, :] = dq_turned[:, rows].T.astype(BF) * jnp.asarray(scaling, BF)
    for here, there in half_slices(ts, shift, swapped):
        own = head_lanes((ts // (2 if swapped else 1), LANES), 0)
        dk_ref[there, :] = jnp.where(own, dk_sum[0, here, :], dk_sum[1, here, :]).astype(BF)
        dv_ref[there, :] = jnp.where(own, dv_sum[0, here, :], dv_sum[1, here, :]).astype(BF)


def attention_specs(tq, ts, columns):
    none = pl.Squeezed()

    def of(count, start):
        return pl.BlockSpec((none, count, LANES), lambda row, pair, _: (row, 0, start + pair))

    def shared(count):
        return pl.BlockSpec((none, count, LANES), lambda row, pair, _: (row, 0, 0))

    q, k, v = (c // LANES for c in columns)
    return of(tq, q), of(ts, k), of(ts, v), of(tq, 0), of(ts, 0), shared(tq), shared(ts)


def attend(q, k, v, columns, terms, shift, width, causal, block, swapped):
    rows, tq, ts = q.shape[0], q.shape[1], k.shape[1]
    pairs = width // LANES
    sq, sk, sv, so, _, tq_spec, ts_spec = attention_specs(tq, ts, columns)
    elements = rows * pairs * 2 * tq * ts
    return pl.pallas_call(
        functools.partial(forward_kernel, causal=causal, block=block, swapped=swapped),
        grid_spec=pltpu.PrefetchScalarGridSpec(
            num_scalar_prefetch=1,
            grid=(rows, pairs),
            in_specs=[sq, sk, sv, tq_spec, ts_spec],
            out_specs=[so, tq_spec],
            scratch_shapes=[pltpu.VMEM((2, n, LANES), BF) for n in (ts, ts, tq)],
        ),
        out_shape=[
            jax.ShapeDtypeStruct((rows, tq, width), BF),
            jax.ShapeDtypeStruct((rows, tq, LANES), F32),
        ],
        compiler_params=pltpu.CompilerParams(vmem_limit_bytes=48 * 2**20),
        cost_estimate=pl.CostEstimate(
            flops=elements * 1200, bytes_accessed=rows * (tq + ts) * width * 4, transcendentals=elements
        ),
    )(shift, q, k, v, *terms)


def attend_back(q, k, v, columns, g, o, lse, terms, shift, width, causal, block, swapped):
    rows, tq, ts = q.shape[0], q.shape[1], k.shape[1]
    pairs = width // LANES
    sq, sk, sv, so, ss, tq_spec, ts_spec = attention_specs(tq, ts, columns)
    elements = rows * pairs * 2 * tq * ts
    return pl.pallas_call(
        functools.partial(
            backward_kernel, causal=causal, block=block, swapped=swapped, scaling=HD**-0.5
        ),
        grid_spec=pltpu.PrefetchScalarGridSpec(
            num_scalar_prefetch=1,
            grid=(rows, pairs),
            in_specs=[sq, sk, sv, so, so, tq_spec, ts_spec, tq_spec],
            out_specs=[so, ss, ss],
            scratch_shapes=[pltpu.VMEM((2, n, LANES), BF) for n in (ts, ts, tq, tq)]
            + [
                pltpu.VMEM((LANES, ts), BF),
                pltpu.VMEM((2, ts, LANES), F32),
                pltpu.VMEM((2, ts, LANES), F32),
                pltpu.VMEM((LANES, tq), F32),
            ],
        ),
        out_shape=[
            jax.ShapeDtypeStruct((rows, tq, width), BF),
            jax.ShapeDtypeStruct((rows, ts, width), BF),
            jax.ShapeDtypeStruct((rows, ts, width), BF),
        ],
        compiler_params=pltpu.CompilerParams(vmem_limit_bytes=48 * 2**20),
        cost_estimate=pl.CostEstimate(
            flops=elements * 2000, bytes_accessed=rows * (tq + ts) * width * 8, transcendentals=elements
        ),
    )(shift, q, k, v, g, o, *terms, lse)


def norm(resid, gain_vec, bias_vec):
    center = resid - jnp.mean(resid, -1, keepdims=True)
    inverse = lax.rsqrt(jnp.mean(center * center, -1, keepdims=True) + norm_epsilon)
    normed = center * inverse
    return normed * gain_vec + bias_vec, normed, inverse


def norm_back(upstream, normed, inverse, gain_vec):
    w = upstream * gain_vec
    grad = (
        w - jnp.mean(w, -1, keepdims=True) - normed * jnp.mean(w * normed, -1, keepdims=True)
    ) * inverse
    return grad, jnp.sum(upstream * normed, 0), jnp.sum(upstream, 0)


def column_sum(x):
    return jnp.sum(x.astype(F32), 0)


def partner(x, axis, bit=1):
    count = lax.axis_size(axis)
    return lax.ppermute(x, axis, [(i, i ^ bit) for i in range(count)])


def halve(x, axis):
    index = lax.axis_index(axis)
    half = x.shape[0] // 2
    sent = lax.dynamic_slice_in_dim(x, (1 - index) * half, half, 0)
    got = partner(sent, axis)
    return lax.dynamic_slice_in_dim(x, index * half, half, 0) + got


def join(x, axis):
    got = partner(x, axis)
    first = lax.axis_index(axis) == 0
    return jnp.concatenate([jnp.where(first, x, got), jnp.where(first, got, x)], 0)


def reduce_matrix(x):
    wide, rest, side, core = (lax.axis_size(a) for a in ("wide", "rest", "side", "core"))
    if not (wide == side == core == 2):
        x = lax.psum_scatter(x, "wide", scatter_dimension=0, tiled=True)
        return lax.psum(x, ("rest", "side", "core")).astype(F32)
    cols = x.shape[1]
    x = x.reshape(2, 2, -1, cols).transpose(1, 0, 2, 3).reshape(-1, cols)
    x = halve(x, "core")
    x = halve(x, "wide")
    x = halve(x, "side")
    bit = 1
    while bit < rest:
        x = x + partner(x, "rest", bit)
        bit *= 2
    x = join(x, "side")
    x = join(x, "core")
    return x.astype(F32)


def reduce_vectors(vectors):
    wide, rest, side, core = (lax.axis_size(a) for a in ("wide", "rest", "side", "core"))
    sizes = [v.shape[0] // wide for v in vectors]
    x = jnp.concatenate([v.reshape(wide, -1) for v in vectors], 1)
    if wide == side == core == 2:
        for axis in ("core", "side"):
            x = x + partner(x, axis)
        bit = 1
        while bit < rest:
            x = x + partner(x, "rest", bit)
            bit *= 2
        index = lax.axis_index("wide")
        got = partner(lax.dynamic_index_in_dim(x, 1 - index, 0, keepdims=False), "wide")
        x = lax.dynamic_index_in_dim(x, index, 0, keepdims=False) + got
    else:
        x = lax.psum_scatter(x, "wide", scatter_dimension=0, tiled=True)
        x = lax.psum(x, ("rest", "side", "core"))[0]
    outs, start = [], 0
    for size in sizes:
        outs.append(lax.slice_in_dim(x, start, start + size, axis=0))
        start += size
    return outs


def body(
    target, encoded, segments, out_grad,
    self_qkv_w, self_q_b, self_v_b, self_out_w, self_out_b, norm1_gain, norm1_bias,
    cross_q_w, cross_q_b, cross_kv_w, cross_v_b, cross_out_w, cross_out_b, norm2_gain, norm2_bias,
    ffn_in_w, ffn_in_b, ffn_out_w, ffn_out_b, norm3_gain, norm3_bias,
):
    row_count, tok_count, width = target.shape
    wide = lax.axis_size("wide")
    place = lax.axis_index("wide")
    scaling = HD**-0.5
    full_len = tok_count * wide
    swapped = wide == 2 and row_count == 2

    if swapped:
        def bring(x):
            kept = lax.dynamic_index_in_dim(x, place, 0, keepdims=False)
            sent = lax.dynamic_index_in_dim(x, 1 - place, 0, keepdims=False)
            return jnp.concatenate([kept, partner(sent, "wide")], 0)

        def give(x, dtype):
            kept = x[:tok_count]
            got = partner(x[tok_count:].astype(BF), "wide").astype(dtype)
            kept = kept.astype(dtype)
            first = place == 0
            return jnp.stack([jnp.where(first, kept, got), jnp.where(first, got, kept)])

        tokens, causal, block_f, block_b = full_len, "block", 512, 256
        shift = (place * tok_count).astype(jnp.int32).reshape(1)
        seg = bring(segments)[None]
        key_seg = seg
    else:
        def bring(x):
            return x.reshape((-1,) + x.shape[2:])

        def give(x, dtype):
            return x.astype(dtype).reshape(row_count, tok_count, width)

        tokens, causal = tok_count, "mask"
        block_f = block_b = min(tok_count, 256)
        shift = (place * tok_count).astype(jnp.int32).reshape(1)
        seg = segments
        key_seg = lax.all_gather(segments, "wide", axis=1, tiled=True)

    def by_row(x):
        return x.reshape(-1, tokens, x.shape[-1])

    def flat(x):
        return x.reshape(-1, x.shape[-1])

    def keys_of(x):
        return x if swapped else lax.all_gather(x, "wide", axis=1, tiled=True)

    def key_grads(x):
        return x if swapped else lax.psum_scatter(x, "wide", scatter_dimension=1, tiled=True)

    terms = (segment_terms(seg)[0], segment_terms(key_seg)[1])

    def attention(q, kv, columns, is_causal):
        return attend(
            q, kv, kv, columns, terms, shift, width, causal if is_causal else "no", block_f, swapped
        )

    def attention_back(q, kv, columns, g, o, lse, is_causal):
        dq, dk, dv = attend_back(
            q, kv, kv, columns, by_row(g), o, lse, terms, shift, width,
            causal if is_causal else "no", block_b, swapped,
        )
        return flat(dq), flat(key_grads(dk)), flat(key_grads(dv))

    flat_in = bring(target)
    flat_enc = bring(encoded)
    upstream = bring(out_grad)

    zeros = jnp.zeros_like(self_q_b)
    ones = jnp.ones_like(self_q_b)
    qkv_bias = jnp.concatenate([self_q_b, zeros, self_v_b])
    qkv_scale = jnp.concatenate([ones * scaling, ones, ones])
    qkv = by_row(((dot(flat_in, self_qkv_w) + qkv_bias) * qkv_scale).astype(BF))
    if swapped:
        self_kv, self_cols = qkv, (0, width, 2 * width)
    else:
        self_kv, self_cols = keys_of(qkv[..., width:]), (0, 0, width)
    self_o, self_lse = attention(qkv, self_kv, self_cols, True)
    self_ob = flat(self_o)
    h1, n1, i1 = norm(
        flat_in.astype(F32) + (dot(self_ob, self_out_w) + self_out_b), norm1_gain, norm1_bias
    )
    h1b = h1.astype(BF)
    cq = by_row(((dot(h1b, cross_q_w) + cross_q_b) * scaling).astype(BF))
    ckv = by_row((dot(flat_enc, cross_kv_w) + jnp.concatenate([zeros, cross_v_b])).astype(BF))
    ckv = keys_of(ckv)
    cross_cols = (0, 0, width)
    cross_o, cross_lse = attention(cq, ckv, cross_cols, False)
    cross_ob = flat(cross_o)
    h2, n2, i2 = norm(h1 + (dot(cross_ob, cross_out_w) + cross_out_b), norm2_gain, norm2_bias)
    h2b = h2.astype(BF)
    pre = dot(h2b, ffn_in_w) + ffn_in_b
    phi_sum = 0.5 * lax.erfc(-pre * (0.5**0.5))
    act = (pre * phi_sum).astype(BF)
    slope = phi_sum + pre * (jnp.exp(-0.5 * pre * pre) * 0.3989422804014327)
    h3, n3, i3 = norm(h2 + (dot(act, ffn_out_w) + ffn_out_b), norm3_gain, norm3_bias)
    layer_out = give(h3.astype(BF), BF)

    dr3, norm3_gain_grad, norm3_bias_grad = norm_back(upstream.astype(F32), n3, i3, norm3_gain)
    dbf = dr3.astype(BF)
    ffn_out_w_grad = reduce_matrix(dot(act, dbf, TN).astype(BF))
    dpre = (dot(dbf, ffn_out_w, NT) * slope).astype(BF)
    ffn_in_w_grad = reduce_matrix(dot(h2b, dpre, TN).astype(BF))
    dh2 = dr3 + dot(dpre, ffn_in_w, NT)
    dr2, norm2_gain_grad, norm2_bias_grad = norm_back(dh2, n2, i2, norm2_gain)
    dbc = dr2.astype(BF)
    dco = dot(dbc, cross_out_w, NT).astype(BF)
    dcq, dck, dcv = attention_back(cq, ckv, cross_cols, dco, cross_o, cross_lse, False)
    dckv = jnp.concatenate([dck, dcv], 1)
    cross_grads = reduce_matrix(
        jnp.concatenate(
            [
                dot(cross_ob, dbc, TN).astype(BF),
                dot(h1b, dcq, TN).astype(BF),
                dot(flat_enc, dckv, TN).astype(BF),
            ],
            1,
        )
    )
    encoded_grad = give(dot(dckv, cross_kv_w, NT), F32)
    dh1 = dr2 + dot(dcq, cross_q_w, NT)
    dr1, norm1_gain_grad, norm1_bias_grad = norm_back(dh1, n1, i1, norm1_gain)
    dba = dr1.astype(BF)
    dso = dot(dba, self_out_w, NT).astype(BF)
    dsq, dsk, dsv = attention_back(qkv, self_kv, self_cols, dso, self_o, self_lse, True)
    dqkv = jnp.concatenate([dsq, dsk, dsv], 1)
    self_grads = reduce_matrix(
        jnp.concatenate(
            [dot(self_ob, dba, TN).astype(BF), dot(flat_in, dqkv, TN).astype(BF)], 1
        )
    )
    target_grad = give(dr1 + dot(dqkv, self_qkv_w, NT), F32)

    (
        self_q_b_grad, self_v_b_grad, self_out_b_grad, norm1_gain_grad, norm1_bias_grad,
        cross_q_b_grad, cross_v_b_grad, cross_out_b_grad, norm2_gain_grad, norm2_bias_grad,
        ffn_in_b_grad, ffn_out_b_grad, norm3_gain_grad, norm3_bias_grad,
    ) = reduce_vectors(
        [
            column_sum(dsq), column_sum(dsv), column_sum(dba), norm1_gain_grad, norm1_bias_grad,
            column_sum(dcq), column_sum(dcv), column_sum(dbc), norm2_gain_grad, norm2_bias_grad,
            column_sum(dpre), column_sum(dbf), norm3_gain_grad, norm3_bias_grad,
        ]
    )
    return (
        layer_out, target_grad, encoded_grad,
        self_grads[:, width:], self_q_b_grad, self_v_b_grad,
        self_grads[:, :width], self_out_b_grad, norm1_gain_grad, norm1_bias_grad,
        cross_grads[:, width : 2 * width], cross_q_b_grad,
        cross_grads[:, 2 * width :], cross_v_b_grad,
        cross_grads[:, :width], cross_out_b_grad, norm2_gain_grad, norm2_bias_grad,
        ffn_in_w_grad, ffn_in_b_grad, ffn_out_w_grad, ffn_out_b_grad,
        norm3_gain_grad, norm3_bias_grad,
    )


def solution(mesh):
    wide, narrow = mesh.shape["wide"], mesh.shape["narrow"]
    core = 2 if narrow % 2 == 0 else 1
    side = 2 if narrow % (2 * core) == 0 else 1
    devices = mesh.devices.reshape(wide, narrow // (side * core), side, core)
    split = Mesh(devices, ("wide", "rest", "side", "core"))
    rows = ("rest", "side", "core")
    token_spec = P(rows, "wide", None)
    in_specs = (token_spec, token_spec, P(rows, "wide"), token_spec) + (P(),) * 21
    matrix, vector = P("wide", None), P("wide")
    out_specs = (token_spec,) * 3 + (
        matrix, vector, vector, matrix, vector, vector, vector,
        matrix, vector, matrix, vector, matrix, vector, vector, vector,
        matrix, vector, matrix, vector, vector, vector,
    )
    return jax.shard_map(body, mesh=split, in_specs=in_specs, out_specs=out_specs, check_vma=False)
```

time: 1310 us -> 744 us (0.57)
  matrix products: 397 us -> 149 us
  waiting for transfers between devices: 474 us -> 272 us
  local copies, waits for them, and re-layouts: 205 us -> 96.3 us
  Pallas kernels: 0 us -> 107 us
  blocking collectives: 77.4 us -> 0 us
  other arithmetic: 124 us -> 70.7 us
  starting transfers between devices: 1.07 us -> 36.9 us
  between operations: 16.5 us -> 2.35 us
    reduce_scatter x9 -> x0, waiting for transfers between devices: 343 us -> none  [the longest x1 104 us: body(): lax.psum_scatter(self_dk_all.astype(jnp.bfloat16), 'wide', scatter_dimens...]
    ppermute x0 -> x40, waiting for transfers between devices: none -> 272 us  [partner(): return lax.ppermute(x, axis, [(i, i ^ bit) for i in range(count)])]
    dot_general x42 -> x21, matrix products: 397 us -> 149 us  [dot(): return lax.dot_general(a, b, dims, preferred_element_type=F32)]
    pallas_call x0 -> x4, Pallas kernels: none -> 107 us  [the longest x2 64.1 us: attend_back(): pl.pallas_call(functools.partial(backward_kernel, causal=causal, block=bl...]
    psum x1 -> x0, waiting for transfers between devices: 65.5 us -> none  [body(): lax.psum(row_sums[0].astype(jnp.bfloat16), 'narrow').astype(jnp.float32)]
    psum x1 -> x0, blocking collectives: 63.2 us -> none  [body(): lax.psum(row_sums[1].astype(jnp.bfloat16), 'narrow').astype(jnp.float32)]
    reduce_sum x20 -> x11, other arithmetic: 68.2 us -> 17.1 us  [the longest x7 12.3 us: column_sum(): return jnp.sum(x.astype(F32), 0)]
    ppermute x0 -> x40, starting transfers between devices: none -> 36.9 us  [partner(): return lax.ppermute(x, axis, [(i, i ^ bit) for i in range(count)])]
  transfers between devices with their start and end apart: 16 -> 40, of which waited for: 12 -> 16; matrix products, arithmetic and copies ran while one was open for 30% -> 31% of each run, Pallas kernels for 0% -> 9%
where the time goes in v1:
time: 744 us; the launch traced here: 734 us
  waiting for transfers between devices  272 us (37%)
  matrix products  149 us (20%)
  Pallas kernels  107 us (14%)
  local copies, waits for them, and re-layouts  96.3 us (13%)
  other arithmetic  70.7 us (10%)
  starting transfers between devices  36.9 us (5%)
    ppermute x40, waiting for transfers between devices, partner(): return lax.ppermute(x, axis, [(i, i ^ bit) for i in range(count)])  272 us
    dot_general x21, matrix products, dot(): return lax.dot_general(a, b, dims, preferred_element_type=F32)  149 us
    pallas_call x2, Pallas kernels, attend_back(): pl.pallas_call(functools.partial(backward_kernel, causal=causal, block=bl...  64.1 us
    pallas_call x2, Pallas kernels, attend(): pl.pallas_call(functools.partial(forward_kernel, causal=causal, block=blo...  42.7 us
    unnamed x212, local copies, waits for them, and re-layouts  41.4 us
    ppermute x40, starting transfers between devices, partner(): return lax.ppermute(x, axis, [(i, i ^ bit) for i in range(count)])  36.9 us
  transfers between devices with their start and end apart: 40, of which 16 were waited for; matrix products, arithmetic and copies ran while one was open for 31% of the time, Pallas kernels for 9%

profile of v1, /device:TPU:0, one launch (start us, length us, event | category | flops | bytes accessed | tf_op | source)
XLA Modules:
  0.0 733.8 jit_solution(14542450002130210505)
XLA Ops:
  0.7 3.7 constant_dynamic-slice_fusion.13
  4.4 2.3 copy.50
  6.7 2.9 collective-permute-start
  10.2 2.6 dynamic-slice_bitcast_fusion.1
  14.9 2.3 copy.53
  18.9 2.3 copy.49
  22.5 2.3 copy.52
  24.8 3.6 collective-permute-done.1
  30.0 7.5 %fusion.14.q_ref.k_ref.v_ref = bf16[1,1024,2304]{2,1,0:T(8,128)(2,1)} fusion(bf16[768,2304]{1,0:T(8,128)(2,1)S(1)} %copy-done, f32[2304]{0:T(1024)} %constant.53.clone.1, f32[2304]{0:T(1024)S(1)} %pad_maximum_fusion.24, bf16[512,768]{0,1:T(8,128)(2,1)} %collective-permute-done, bf16[512,768]{0,1:T(8,128)(2,1)} %bitcast.140), kind=kOutput, calls=%fused_computation.31 | convolution fusion | flops 3634102272 | bytes 9848832 | tf_op jit(solution)/shard_map/dot_general | solution.py:23
  37.6 19.9 %shard_map.424 = (bf16[1,1024,768]{2,1,0:T(8,128)(2,1)S(1)}, f32[1,1024,128]{2,1,0:T(8,128)S(1)}) custom-call(s32[1]{0:T(128)} %bitcast.2.shift_ref, bf16[1,1024,2304]{2,1,0:T(8,128)(2,1)} %fusion.14.q_ref.k_ref.v_ref, bf16[1,1024,2304]{2,1,0:T(8,128)(2,1)} %fusion.14.q_ref.k_ref.v_ref, bf16[1,1024,2304]{2,1,0:T(8,128)(2,1)} %fusion.14.q_ref.k_ref.v_ref, ...), custom_call_target="tpu_custom_call" | custom-call | flops 15099494400 | bytes 6291456 | tf_op jit(solution)/shard_map/pallas_call | solution.py:201
  57.5 3.4 fusion.74
  65.1 5.6 fusion.18.k_ref.v_ref
  70.7 22.9 %shard_map.425 = (bf16[1,1024,768]{2,1,0:T(8,128)(2,1)S(1)}, f32[1,1024,128]{2,1,0:T(8,128)S(1)}) custom-call(s32[1]{0:T(128)} %bitcast.2.shift_ref, bf16[1,1024,768]{2,1,0:T(8,128)(2,1)S(1)} %fusion.52.q_ref, bf16[1,1024,1536]{2,1,0:T(8,128)(2,1)} %fusion.18.k_ref.v_ref, bf16[1,1024,1536]{2,1,0:T(8,128)(2,1)} %fusion.18.k_ref.v_ref, ...), custom_call_target="tpu_custom_call" | custom-call | flops 15099494400 | bytes 6291456 | tf_op jit(solution)/shard_map/pallas_call | solution.py:201
  96.6 35.8 %multiply_convert_fusion = (bf16[1024,3072]{1,0:T(8,128)(2,1)}, f32[1024,3072]{1,0:T(8,128)}, f32[1024,3072]{1,0:T(8,128)}) fusion(f32[3072]{0:T(1024)S(1)} %copy-done.73, bf16[768,3072]{1,0:T(8,128)(2,1)S(1)} %bitcast.149, f32[1024,768]{0,1:T(8,128)S(1)} %get-tuple-element.141, f32[768]{0:T(1024)S(1)} %copy-done.78, f32[768]{0:T(1024)S(1)} %copy-done.58, ...), kind=kOutput, calls=%fused_computation.11 | convolution fusion | flops 5043388416 | bytes 39348224 | tf_op jit(solution)/shard_map/dot_general | solution.py:23
  132.5 7.7 %fusion.76 = (f32[1024]{0:T(1024)S(1)}, f32[1024,768]{0,1:T(8,128)S(1)}) fusion(f32[768]{0:T(1024)S(1)} %copy-done.77, bf16[1024,3072]{1,0:T(8,128)(2,1)} %get-tuple-element.88, bf16[3072,768]{1,0:T(8,128)(2,1)S(1)} %bitcast.147, f32[768]{0:T(1024)S(1)} %copy-done.78, f32[768]{0:T(1024)S(1)} %copy-done.58, f32[1024]{0:T(1024)S(1)} %add_rsqrt_fusion.1, ...), kind=kOutput, calls=%fused_computation.231 | convolution fusion | flops 4837342208 | bytes 17323008 | tf_op jit(solution)/shard_map/dot_general | solution.py:23
  141.9 3.6 fusion.22
  145.5 3.7 convert_reduce_fusion.2
  149.3 7.0 convolution_convert_fusion
  156.2 15.5 %convert_reduce_fusion = (f32[3072]{0:T(1024)}, bf16[1024,3072]{1,0:T(8,128)(2,1)}) fusion(f32[1024,3072]{1,0:T(8,128)} %get-tuple-element.89, f32[1024,3072]{1,0:T(8,128)} %get-tuple-element.142, f32[3072]{0:T(1024)S(1)} %copy-done.73, bf16[1024,768]{0,1:T(8,128)(2,1)S(1)} %get-tuple-element.83, bf16[3072,768]{1,0:T(8,128)(2,1)} %param.46), kind=kOutput, calls=%fused_computation.10 | convolution fusion | flops 4863292416 | bytes 37773312 | tf_op jit(solution)/shard_map/dot_general | solution.py:23
  171.8 9.9 %convolution_convert_fusion.1 = bf16[768,3072]{1,0:T(8,128)(2,1)} fusion(bf16[1024,3072]{1,0:T(8,128)(2,1)} %get-tuple-element.148, f32[1024,768]{0,1:T(8,128)} %copy-done.32, f32[768]{0:T(1024)S(1)} %copy-done.78, f32[768]{0:T(1024)S(1)} %copy-done.58, f32[1024]{0:T(1024)S(1)} %add_rsqrt_fusion.1, f32[1024]{0:T(1024)S(1)} %broadcast_multiply_fusion.7), kind=kOutput, calls=%fused_computation.29 | convolution fusion | flops 4838129664 | bytes 14170112 | tf_op jit(solution)/shard_map/dot_general | solution.py:23
  181.6 9.8 %multiply_reduce_fusion = (f32[768]{0:T(1024)}, f32[1024]{0:T(1024)S(1)}, f32[1024]{0:T(1024)S(1)}, f32[768]{0:T(1024)}, f32[1024,768]{0,1:T(8,128)S(1)}) fusion(f32[1024,768]{0,1:T(8,128)S(1)} %copy-done.33, f32[1024]{0:T(1024)S(1)} %add_rsqrt_fusion.1, f32[1024]{0:T(1024)S(1)} %broadcast_multiply_fusion.7, f32[768]{0:T(1024)S(1)} %copy-done.58, ...), kind=kOutput, calls=%fused_computation.51 | convolution fusion | flops 4848349184 | bytes 22065152 | tf_op jit(solution)/shard_map/dot_general | solution.py:23
  192.7 2.6 fusion.50.g_ref
  195.4 2.4 fusion.44
  197.8 37.2 %shard_map.426 = (bf16[1,1024,768]{2,1,0:T(8,128)(2,1)S(1)}, bf16[1,1024,768]{2,1,0:T(8,128)(2,1)S(1)}, bf16[1,1024,768]{2,1,0:T(8,128)(2,1)S(1)}) custom-call(s32[1]{0:T(128)} %bitcast.2.shift_ref, bf16[1,1024,768]{2,1,0:T(8,128)(2,1)} %copy-done.21, bf16[1,1024,1536]{2,1,0:T(8,128)(2,1)} %fusion.18.k_ref.v_ref, bf16[1,1024,1536]{2,1,0:T(8,128)(2,1)} %fusion.18.k_ref.v_ref, ...), custom_call_target="tpu_custom_call" | custom-call | flops 25165824000 | bytes 12582912 | tf_op jit(solution)/shard_map/pallas_call | solution.py:226
  235.2 2.9 fusion.47
  238.9 4.4 multiply_reduce_fusion.1
  248.6 2.2 copy-done.26
  252.4 2.4 copy.62
  254.7 2.5 copy.61
  257.3 2.3 convert_reduce_fusion.4
  259.6 5.1 convolution_convert_fusion.3
  272.5 2.6 fusion.51.g_ref
  275.1 26.9 %shard_map.427 = (bf16[1,1024,768]{2,1,0:T(8,128)(2,1)S(1)}, bf16[1,1024,768]{2,1,0:T(8,128)(2,1)S(1)}, bf16[1,1024,768]{2,1,0:T(8,128)(2,1)S(1)}) custom-call(s32[1]{0:T(128)} %bitcast.2.shift_ref, bf16[1,1024,2304]{2,1,0:T(8,128)(2,1)} %fusion.14.q_ref.k_ref.v_ref, bf16[1,1024,2304]{2,1,0:T(8,128)(2,1)} %fusion.14.q_ref.k_ref.v_ref, ...), custom_call_target="tpu_custom_call" | custom-call | flops 25165824000 | bytes 12582912 | tf_op jit(solution)/shard_map/pallas_call | solution.py:226
  308.9 2.3 convert_reduce_fusion.7
  339.4 9.0 %fusion.27 = f32[1024,768]{0,1:T(8,128)} fusion(f32[1024,768]{0,1:T(8,128)} %copy-done.38, bf16[768,2304]{1,0:T(8,128)(2,1)S(1)} %copy-done, bf16[1024,768]{1,0:T(8,128)(2,1)} %bitcast.109, bf16[1024,768]{1,0:T(8,128)(2,1)} %bitcast.113, bf16[1024,768]{1,0:T(8,128)(2,1)} %bitcast.107), kind=kOutput, calls=%fused_computation.96 | convolution fusion | flops 3638820864 | bytes 14548992 | tf_op jit(solution)/shard_map/dot_general | solution.py:23
  348.4 4.3 fusion.25
  354.9 7.1 convolution_convert_fusion.2
  364.2 2.4 fusion.41
  366.6 2.8 copy.59
  370.3 2.7 collective-permute-start.17
  372.9 2.7 pad_maximum_fusion.1
  384.9 2.4 dynamic-slice_add_fusion
  388.7 2.5 dynamic-slice_add_fusion.1
  392.6 2.6 dynamic-slice_add_fusion.2
  397.1 64.1 %collective-permute-done.34 = bf16[768,768]{1,0:T(8,128)(2,1)} collective-permute-done((bf16[768,768]{1,0:T(8,128)(2,1)S(1)}, bf16[768,768]{1,0:T(8,128)(2,1)}, u32[]{:S(2)}, u32[]{:S(2)}) %collective-permute-start.34) | collective-permute-done | bytes 1179680 | tf_op jit(solution)/shard_map/ppermute | solution.py:276
  464.1 22.3 %collective-permute-done.27 = bf16[192,3072]{1,0:T(8,128)(2,1)S(1)} collective-permute-done((bf16[192,3072]{1,0:T(8,128)(2,1)S(1)}, bf16[192,3072]{1,0:T(8,128)(2,1)S(1)}, u32[]{:S(2)}, u32[]{:S(2)}) %collective-permute-start.27) | collective-permute-done | bytes 1179680 | tf_op jit(solution)/shard_map/ppermute | solution.py:276
  488.2 23.4 %collective-permute-done.20 = bf16[192,3072]{1,0:T(8,128)(2,1)S(1)} collective-permute-done((bf16[192,3072]{1,0:T(8,128)(2,1)S(1)}, bf16[192,3072]{1,0:T(8,128)(2,1)S(1)}, u32[]{:S(2)}, u32[]{:S(2)}) %collective-permute-start.20) | collective-permute-done | bytes 1179680 | tf_op jit(solution)/shard_map/ppermute | solution.py:276
  512.9 23.1 %collective-permute-done.8 = bf16[192,3072]{1,0:T(8,128)(2,1)S(1)} collective-permute-done((bf16[192,3072]{1,0:T(8,128)(2,1)S(1)}, bf16[192,3072]{1,0:T(8,128)(2,1)S(1)}, u32[]{:S(2)}, u32[]{:S(2)}) %collective-permute-start.8) | collective-permute-done | bytes 1179680 | tf_op jit(solution)/shard_map/ppermute | solution.py:276
  538.8 13.5 %collective-permute-done.28 = bf16[96,3072]{1,0:T(8,128)(2,1)S(1)} collective-permute-done((bf16[96,3072]{1,0:T(8,128)(2,1)S(1)}, bf16[96,3072]{1,0:T(8,128)(2,1)S(1)}, u32[]{:S(2)}, u32[]{:S(2)}) %collective-permute-start.28) | collective-permute-done | bytes 589856 | tf_op jit(solution)/shard_map/ppermute | solution.py:276
  553.2 11.7 %collective-permute-done.21 = bf16[96,3072]{1,0:T(8,128)(2,1)S(1)} collective-permute-done((bf16[96,3072]{1,0:T(8,128)(2,1)S(1)}, bf16[96,3072]{1,0:T(8,128)(2,1)S(1)}, u32[]{:S(2)}, u32[]{:S(2)}) %collective-permute-start.21) | collective-permute-done | bytes 589856 | tf_op jit(solution)/shard_map/ppermute | solution.py:276
  565.5 10.2 %collective-permute-done.9 = bf16[96,3072]{1,0:T(8,128)(2,1)S(1)} collective-permute-done((bf16[96,3072]{1,0:T(8,128)(2,1)S(1)}, bf16[96,3072]{1,0:T(8,128)(2,1)S(1)}, u32[]{:S(2)}, u32[]{:S(2)}) %collective-permute-start.9) | collective-permute-done | bytes 589856 | tf_op jit(solution)/shard_map/ppermute | solution.py:276
  578.8 25.8 %collective-permute-done.22 = bf16[96,3072]{1,0:T(8,128)(2,1)S(1)} collective-permute-done((bf16[96,3072]{1,0:T(8,128)(2,1)S(1)}, bf16[96,3072]{1,0:T(8,128)(2,1)S(1)}, u32[]{:S(2)}, u32[]{:S(2)}) %collective-permute-start.22) | collective-permute-done | bytes 589856 | tf_op jit(solution)/shard_map/ppermute | solution.py:276
  606.7 2.6 collective-permute-start.23
  610.9 14.2 %collective-permute-done.29 = bf16[96,3072]{1,0:T(8,128)(2,1)S(1)} collective-permute-done((bf16[96,3072]{1,0:T(8,128)(2,1)S(1)}, bf16[96,3072]{1,0:T(8,128)(2,1)S(1)}, u32[]{:S(2)}, u32[]{:S(2)}) %collective-permute-start.29) | collective-permute-done | bytes 589856 | tf_op jit(solution)/shard_map/ppermute | solution.py:276
  626.1 8.9 %collective-permute-done.10 = bf16[96,3072]{1,0:T(8,128)(2,1)S(1)} collective-permute-done((bf16[96,3072]{1,0:T(8,128)(2,1)S(1)}, bf16[96,3072]{1,0:T(8,128)(2,1)S(1)}, u32[]{:S(2)}, u32[]{:S(2)}) %collective-permute-start.10) | collective-permute-done | bytes 589856 | tf_op jit(solution)/shard_map/ppermute | solution.py:276
  637.7 2.4 select_bitcast_fusion.1
  642.1 34.9 %collective-permute-done.23 = bf16[96,3072]{1,0:T(8,128)(2,1)S(1)} collective-permute-done((bf16[96,3072]{1,0:T(8,128)(2,1)S(1)}, bf16[96,3072]{1,0:T(8,128)(2,1)S(1)}, u32[]{:S(2)}, u32[]{:S(2)}) %collective-permute-start.23) | collective-permute-done | bytes 589856 | tf_op jit(solution)/shard_map/ppermute | solution.py:276
  680.7 3.5 copy.68
  684.3 3.7 copy.67
  688.0 2.7 pad_maximum_fusion.14
  690.6 2.6 copy.66
  703.4 12.7 %collective-permute-done.12 = bf16[96,3072]{1,0:T(8,128)(2,1)S(1)} collective-permute-done((bf16[96,3072]{1,0:T(8,128)(2,1)S(1)}, bf16[96,3072]{1,0:T(8,128)(2,1)S(1)}, u32[]{:S(2)}, u32[]{:S(2)}) %collective-permute-start.12) | collective-permute-done | bytes 589856 | tf_op jit(solution)/shard_map/ppermute | solution.py:276
  727.7 2.5 maximum_convert_fusion.3
  730.8 2.8 maximum_convert_fusion.2
  (391 shorter events, 135.5 us)
Async XLA Ops:
  0.7 29.4 %copy-start = (bf16[768,2304]{1,0:T(8,128)(2,1)S(1)}, bf16[768,2304]{1,0:T(8,128)(2,1)}, u32[]{:S(2)}) copy-start(bf16[768,2304]{1,0:T(8,128)(2,1)} %param.29) | copy-start | bytes 10616836
  6.7 23.3 %collective-permute-start = (bf16[512,768]{0,1:T(8,128)(2,1)}, bf16[512,768]{0,1:T(8,128)(2,1)}, u32[]{:S(2)}, u32[]{:S(2)}) collective-permute-start(bf16[512,768]{0,1:T(8,128)(2,1)} %bitcast.144), channel_id=1, source_target_pairs={{0,16},{16,0},{1,17},{17,1},{2,18},{18,2},{3,19},{19,3},{4,20},{20... | collective-permute-start | bytes 2359304 | tf_op jit(solution)/shard_map/ppermute | solution.py:276
  10.2 18.1 %collective-permute-start.1 = (s32[512]{0:T(512)}, s32[512]{0:T(512)}, u32[]{:S(2)}, u32[]{:S(2)}) collective-permute-start(s32[512]{0:T(512)} %bitcast.5), channel_id=1, source_target_pairs={{0,16},{16,0},{1,17},{17,1},{2,18},{18,2},{3,19},{19,3},{4,20},{20... | collective-permute-start | bytes 6152 | tf_op jit(solution)/shard_map/ppermute | solution.py:276
  12.8 52.2 %collective-permute-start.2 = (bf16[512,768]{1,0:T(8,128)(2,1)}, bf16[512,768]{1,0:T(8,128)(2,1)}, u32[]{:S(2)}, u32[]{:S(2)}) collective-permute-start(bf16[512,768]{1,0:T(8,128)(2,1)} %get-tuple-element.110), channel_id=1, source_target_pairs={{0,16},{16,0},{1,17},{17,1},{2,18},{18,2},{3,19},{19,3},{4,20},{20... | collective-permute-start | bytes 2359304 | tf_op jit(solution)/shard_map/ppermute | solution.py:276
  17.1 123.5 %collective-permute-start.4 = (bf16[512,768]{0,1:T(8,128)(2,1)}, bf16[512,768]{0,1:T(8,128)(2,1)}, u32[]{:S(2)}, u32[]{:S(2)}) collective-permute-start(bf16[512,768]{0,1:T(8,128)(2,1)} %bitcast.143), channel_id=1, source_target_pairs={{0,16},{16,0},{1,17},{17,1},{2,18},{18,2},{3,19},{19,3},{4,20},{20... | collective-permute-start | bytes 2359304 | tf_op jit(solution)/shard_map/ppermute | solution.py:276
  30.0 40.7 %copy-start.7 = (bf16[1,1024,128]{2,1,0:T(8,128)(2,1)}, bf16[1,1024,128]{2,1,0:T(8,128)(2,1)S(1)}, u32[]{:S(2)}) copy-start(bf16[1,1024,128]{2,1,0:T(8,128)(2,1)S(1)} %get-tuple-element.134.kt_ref) | copy-start | bytes 786436
  30.0 40.7 %copy-start.10 = (bf16[1,1024,128]{2,1,0:T(8,128)(2,1)}, bf16[1,1024,128]{2,1,0:T(8,128)(2,1)S(1)}, u32[]{:S(2)}) copy-start(bf16[1,1024,128]{2,1,0:T(8,128)(2,1)S(1)} %get-tuple-element.135.qt_ref) | copy-start | bytes 786436
  37.6 19.9 %copy-start.45 = (bf16[1,512,768]{1,2,0:T(8,128)(2,1)S(1)}, bf16[1,512,768]{1,2,0:T(8,128)(2,1)}, u32[]{:S(2)}) copy-start(bf16[1,512,768]{1,2,0:T(8,128)(2,1)} %copy.49) | copy-start | bytes 2359300
  37.6 19.9 %copy-start.71 = (bf16[768,768]{1,0:T(8,128)(2,1)S(1)}, bf16[768,768]{1,0:T(8,128)(2,1)}, u32[]{:S(2)}) copy-start(bf16[768,768]{1,0:T(8,128)(2,1)} %param.32) | copy-start | bytes 3538948
  37.6 19.9 %copy-start.74 = (f32[768]{0:T(1024)S(1)}, f32[768]{0:T(1024)}, u32[]{:S(2)}) copy-start(f32[768]{0:T(1024)} %param.33) | copy-start | bytes 9220
  60.9 32.7 %copy-start.29 = (f32[1024,768]{0,1:T(8,128)}, f32[1024,768]{0,1:T(8,128)S(1)}, u32[]{:S(2)}) copy-start(f32[1024,768]{0,1:T(8,128)S(1)} %get-tuple-element.139) | copy-start | bytes 9437188
  61.0 32.7 %copy-start.49 = (f32[1024]{0:T(1024)}, f32[1024]{0:T(1024)S(1)}, u32[]{:S(2)}) copy-start(f32[1024]{0:T(1024)S(1)} %broadcast_multiply_fusion.8) | copy-start | bytes 12292
  63.1 30.5 %copy-start.52 = (f32[1024]{0:T(1024)}, f32[1024]{0:T(1024)S(1)}, u32[]{:S(2)}) copy-start(f32[1024]{0:T(1024)S(1)} %add_rsqrt_fusion.2) | copy-start | bytes 12292
  70.7 23.0 %copy-start.67 = (bf16[768,768]{1,0:T(8,128)(2,1)S(1)}, bf16[768,768]{1,0:T(8,128)(2,1)}, u32[]{:S(2)}) copy-start(bf16[768,768]{1,0:T(8,128)(2,1)} %param.40) | copy-start | bytes 3538948
  70.7 23.0 %copy-start.76 = (f32[768]{0:T(1024)S(1)}, f32[768]{0:T(1024)}, u32[]{:S(2)}) copy-start(f32[768]{0:T(1024)} %param.41) | copy-start | bytes 9220
  93.7 38.8 %slice-start.10 = ((s8[4718592]{0:T(1024)(128)(4,1)}), s8[524288]{0:T(1024)(128)(4,1)S(1)}, s32[]{:S(2)}) async-start(s8[4718592]{0:T(1024)(128)(4,1)} %bitcast.146), calls=%async_computation.10 | async-start | bytes 1048576
  95.8 36.7 %copy-start.32 = (f32[1024,768]{0,1:T(8,128)}, f32[1024,768]{0,1:T(8,128)S(1)}, u32[]{:S(2)}) copy-start(f32[1024,768]{0,1:T(8,128)S(1)} %get-tuple-element.141) | copy-start | bytes 9437188
  96.6 35.9 %slice-start.11 = ((s8[4718592]{0:T(1024)(128)(4,1)}), s8[4194304]{0:T(1024)(128)(4,1)S(1)}, s32[]{:S(2)}) async-start(s8[4718592]{0:T(1024)(128)(4,1)} %bitcast.146), calls=%async_computation.11 | async-start | bytes 8388608
  96.6 35.9 %copy-start.77 = (f32[768]{0:T(1024)S(1)}, f32[768]{0:T(1024)}, u32[]{:S(2)}) copy-start(f32[768]{0:T(1024)} %param.47) | copy-start | bytes 9220
  171.8 9.9 %copy-start.81 = (bf16[1024,3072]{1,0:T(8,128)(2,1)S(1)}, bf16[1024,3072]{1,0:T(8,128)(2,1)}, u32[]{:S(2)}) copy-start(bf16[1024,3072]{1,0:T(8,128)(2,1)} %get-tuple-element.148) | copy-start | bytes 18874372
  197.8 37.3 %copy-start.30 = (f32[1024,768]{0,1:T(8,128)S(1)}, f32[1024,768]{0,1:T(8,128)}, u32[]{:S(2)}) copy-start(f32[1024,768]{0,1:T(8,128)} %copy-done.29) | copy-start | bytes 9437188
  197.8 37.3 %copy-start.50 = (f32[1024]{0:T(1024)S(1)}, f32[1024]{0:T(1024)}, u32[]{:S(2)}) copy-start(f32[1024]{0:T(1024)} %copy-done.49) | copy-start | bytes 12292
  197.8 37.3 %copy-start.53 = (f32[1024]{0:T(1024)S(1)}, f32[1024]{0:T(1024)}, u32[]{:S(2)}) copy-start(f32[1024]{0:T(1024)} %copy-done.52) | copy-start | bytes 12292
  197.8 37.3 %copy-start.60 = (f32[768]{0:T(1024)S(1)}, f32[768]{0:T(1024)}, u32[]{:S(2)}) copy-start(f32[768]{0:T(1024)} %param.34) | copy-start | bytes 9220
  197.8 37.3 %copy-start.80 = (f32[768]{0:T(1024)S(1)}, f32[768]{0:T(1024)}, u32[]{:S(2)}) copy-start(f32[768]{0:T(1024)} %param.35) | copy-start | bytes 9220
  245.5 138.5 %collective-permute-start.33 = (bf16[1536,768]{1,0:T(8,128)(2,1)}, bf16[1536,768]{1,0:T(8,128)(2,1)}, u32[]{:S(2)}, u32[]{:S(2)}) collective-permute-start(bf16[1536,768]{1,0:T(8,128)(2,1)} %constant_dynamic-slice_fusion.2), channel_id=1, source_target_pairs={{0,1},{1,0},{2,3},{3,2},{4,5},{5,4},{6,7},{7,6},{8,9},{9,8},{10,11... | collective-permute-start | bytes 7077896 | tf_op jit(solution)/shard_map/ppermute | solution.py:276
  252.4 135.0 %collective-permute-start.26 = (bf16[384,3072]{1,0:T(8,128)(2,1)}, bf16[384,3072]{1,0:T(8,128)(2,1)}, u32[]{:S(2)}, u32[]{:S(2)}) collective-permute-start(bf16[384,3072]{1,0:T(8,128)(2,1)} %constant_dynamic-slice_fusion.5), channel_id=1, source_target_pairs={{0,1},{1,0},{2,3},{3,2},{4,5},{5,4},{6,7},{7,6},{8,9},{9,8},{10,11... | collective-permute-start | bytes 7077896 | tf_op jit(solution)/shard_map/ppermute | solution.py:276
  267.3 124.0 %collective-permute-start.19 = (bf16[384,3072]{1,0:T(8,128)(2,1)}, bf16[384,3072]{1,0:T(8,128)(2,1)}, u32[]{:S(2)}, u32[]{:S(2)}) collective-permute-start(bf16[384,3072]{1,0:T(8,128)(2,1)} %constant_dynamic-slice_fusion.8), channel_id=1, source_target_pairs={{0,1},{1,0},{2,3},{3,2},{4,5},{5,4},{6,7},{7,6},{8,9},{9,8},{10,11... | collective-permute-start | bytes 7077896 | tf_op jit(solution)/shard_map/ppermute | solution.py:276
  304.3 12.6 %copy-start.51 = (f32[768]{0:T(1024)S(1)}, f32[768]{0:T(1024)}, u32[]{:S(2)}) copy-start(f32[768]{0:T(1024)} %convert_reduce_fusion.4) | copy-start | bytes 9220
  338.8 13.9 %collective-permute-start.14 = (f32[2,6528]{1,0:T(2,128)}, f32[2,6528]{1,0:T(2,128)S(1)}, u32[]{:S(2)}, u32[]{:S(2)}) collective-permute-start(f32[2,6528]{1,0:T(2,128)} %constant_dynamic-update-slice_fusion), channel_id=1, source_target_pairs={{0,1},{1,0},{2,3},{3,2},{4,5},{5,4},{6,7},{7,6},{8,9},{9,8},{10,11... | collective-permute-start | bytes 156680 | tf_op jit(solution)/shard_map/ppermute | solution.py:276
  352.7 11.5 %copy-start.18 = (bf16[1,1024,768]{2,1,0:T(8,128)(2,1)S(1)}, bf16[1,1024,768]{2,1,0:T(8,128)(2,1)}, u32[]{:S(2)}) copy-start(bf16[1,1024,768]{2,1,0:T(8,128)(2,1)} %copy-done.17) | copy-start | bytes 4718596
  352.7 11.5 %copy-start.39 = (f32[1024,768]{0,1:T(8,128)S(1)}, f32[1024,768]{0,1:T(8,128)}, u32[]{:S(2)}) copy-start(f32[1024,768]{0,1:T(8,128)} %copy-done.38) | copy-start | bytes 9437188
  352.8 9.3 %collective-permute-start.15 = (f32[2,6528]{1,0:T(2,128)S(1)}, f32[2,6528]{1,0:T(2,128)S(1)}, u32[]{:S(2)}, u32[]{:S(2)}) collective-permute-start(f32[2,6528]{1,0:T(2,128)S(1)} %add.336), channel_id=1, source_target_pairs={{0,2},{2,0},{1,3},{3,1},{4,6},{6,4},{5,7},{7,5},{8,10},{10,8},{9,1... | collective-permute-start | bytes 156680 | tf_op jit(solution)/shard_map/ppermute | solution.py:276
  362.7 6.7 collective-permute-start.16
  370.3 5.8 collective-permute-start.17
  376.3 5.2 collective-permute-start.18
  378.0 17.2 %collective-permute-start.7 = (bf16[384,3072]{1,0:T(8,128)(2,1)S(1)}, bf16[384,3072]{1,0:T(8,128)(2,1)S(1)}, u32[]{:S(2)}, u32[]{:S(2)}) collective-permute-start(bf16[384,3072]{1,0:T(8,128)(2,1)S(1)} %constant_dynamic-slice_fusion.11), channel_id=1, source_target_pairs={{0,1},{1,0},{2,3},{3,2},{4,5},{5,4},{6,7},{7,6},{8,9},{9,8},{10,11... | collective-permute-start | bytes 7077896 | tf_op jit(solution)/shard_map/ppermute | solution.py:276
  381.5 196.6 %collective-permute-start.6 = (bf16[512,768]{0,1:T(8,128)(2,1)}, bf16[512,768]{0,1:T(8,128)(2,1)}, u32[]{:S(2)}, u32[]{:S(2)}) collective-permute-start(bf16[512,768]{0,1:T(8,128)(2,1)} %slice.132), channel_id=1, source_target_pairs={{0,16},{16,0},{1,17},{17,1},{2,18},{18,2},{3,19},{19,3},{4,20},{20... | collective-permute-start | bytes 2359304 | tf_op jit(solution)/shard_map/ppermute | solution.py:276
  384.0 222.7 %collective-permute-start.5 = (bf16[512,768]{0,1:T(8,128)(2,1)}, bf16[512,768]{0,1:T(8,128)(2,1)}, u32[]{:S(2)}, u32[]{:S(2)}) collective-permute-start(bf16[512,768]{0,1:T(8,128)(2,1)} %slice.133), channel_id=1, source_target_pairs={{0,16},{16,0},{1,17},{17,1},{2,18},{18,2},{3,19},{19,3},{4,20},{20... | collective-permute-start | bytes 2359304 | tf_op jit(solution)/shard_map/ppermute | solution.py:276
  387.4 250.4 %collective-permute-start.3 = (bf16[512,768]{0,1:T(8,128)(2,1)}, bf16[512,768]{0,1:T(8,128)(2,1)}, u32[]{:S(2)}, u32[]{:S(2)}) collective-permute-start(bf16[512,768]{0,1:T(8,128)(2,1)} %slice.103), channel_id=1, source_target_pairs={{0,16},{16,0},{1,17},{17,1},{2,18},{18,2},{3,19},{19,3},{4,20},{20... | collective-permute-start | bytes 2359304 | tf_op jit(solution)/shard_map/ppermute | solution.py:276
  391.3 69.9 %collective-permute-start.34 = (bf16[768,768]{1,0:T(8,128)(2,1)S(1)}, bf16[768,768]{1,0:T(8,128)(2,1)}, u32[]{:S(2)}, u32[]{:S(2)}) collective-permute-start(bf16[768,768]{1,0:T(8,128)(2,1)S(1)} %constant_dynamic-slice_fusion.1), channel_id=1, source_target_pairs={{0,16},{16,0},{1,17},{17,1},{2,18},{18,2},{3,19},{19,3},{4,20},{20... | collective-permute-start | bytes 3538952 | tf_op jit(solution)/shard_map/ppermute | solution.py:276
  395.2 91.2 %collective-permute-start.27 = (bf16[192,3072]{1,0:T(8,128)(2,1)S(1)}, bf16[192,3072]{1,0:T(8,128)(2,1)S(1)}, u32[]{:S(2)}, u32[]{:S(2)}) collective-permute-start(bf16[192,3072]{1,0:T(8,128)(2,1)S(1)} %constant_dynamic-slice_fusion.4), channel_id=1, source_target_pairs={{0,16},{16,0},{1,17},{17,1},{2,18},{18,2},{3,19},{19,3},{4,20},{20... | collective-permute-start | bytes 3538952 | tf_op jit(solution)/shard_map/ppermute | solution.py:276
  461.2 50.5 %collective-permute-start.20 = (bf16[192,3072]{1,0:T(8,128)(2,1)S(1)}, bf16[192,3072]{1,0:T(8,128)(2,1)S(1)}, u32[]{:S(2)}, u32[]{:S(2)}) collective-permute-start(bf16[192,3072]{1,0:T(8,128)(2,1)S(1)} %constant_dynamic-slice_fusion.7), channel_id=1, source_target_pairs={{0,16},{16,0},{1,17},{17,1},{2,18},{18,2},{3,19},{19,3},{4,20},{20... | collective-permute-start | bytes 3538952 | tf_op jit(solution)/shard_map/ppermute | solution.py:276
  486.4 49.6 %collective-permute-start.8 = (bf16[192,3072]{1,0:T(8,128)(2,1)S(1)}, bf16[192,3072]{1,0:T(8,128)(2,1)S(1)}, u32[]{:S(2)}, u32[]{:S(2)}) collective-permute-start(bf16[192,3072]{1,0:T(8,128)(2,1)S(1)} %constant_dynamic-slice_fusion.10), channel_id=1, source_target_pairs={{0,16},{16,0},{1,17},{17,1},{2,18},{18,2},{3,19},{19,3},{4,20},{20... | collective-permute-start | bytes 3538952 | tf_op jit(solution)/shard_map/ppermute | solution.py:276
  511.7 25.7 %collective-permute-start.35 = (bf16[384,768]{1,0:T(8,128)(2,1)S(1)}, bf16[384,768]{1,0:T(8,128)(2,1)S(1)}, u32[]{:S(2)}, u32[]{:S(2)}) collective-permute-start(bf16[384,768]{1,0:T(8,128)(2,1)S(1)} %constant_dynamic-slice_fusion), channel_id=1, source_target_pairs={{0,2},{2,0},{1,3},{3,1},{4,6},{6,4},{5,7},{7,5},{8,10},{10,8},{9,1... | collective-permute-start | bytes 1769480 | tf_op jit(solution)/shard_map/ppermute | solution.py:276
  536.0 16.3 %collective-permute-start.28 = (bf16[96,3072]{1,0:T(8,128)(2,1)S(1)}, bf16[96,3072]{1,0:T(8,128)(2,1)S(1)}, u32[]{:S(2)}, u32[]{:S(2)}) collective-permute-start(bf16[96,3072]{1,0:T(8,128)(2,1)S(1)} %constant_dynamic-slice_fusion.3), channel_id=1, source_target_pairs={{0,2},{2,0},{1,3},{3,1},{4,6},{6,4},{5,7},{7,5},{8,10},{10,8},{9,1... | collective-permute-start | bytes 1769480 | tf_op jit(solution)/shard_map/ppermute | solution.py:276
  537.4 27.6 %collective-permute-start.21 = (bf16[96,3072]{1,0:T(8,128)(2,1)S(1)}, bf16[96,3072]{1,0:T(8,128)(2,1)S(1)}, u32[]{:S(2)}, u32[]{:S(2)}) collective-permute-start(bf16[96,3072]{1,0:T(8,128)(2,1)S(1)} %constant_dynamic-slice_fusion.6), channel_id=1, source_target_pairs={{0,2},{2,0},{1,3},{3,1},{4,6},{6,4},{5,7},{7,5},{8,10},{10,8},{9,1... | collective-permute-start | bytes 1769480 | tf_op jit(solution)/shard_map/ppermute | solution.py:276
  552.3 23.4 %collective-permute-start.9 = (bf16[96,3072]{1,0:T(8,128)(2,1)S(1)}, bf16[96,3072]{1,0:T(8,128)(2,1)S(1)}, u32[]{:S(2)}, u32[]{:S(2)}) collective-permute-start(bf16[96,3072]{1,0:T(8,128)(2,1)S(1)} %constant_dynamic-slice_fusion.9), channel_id=1, source_target_pairs={{0,2},{2,0},{1,3},{3,1},{4,6},{6,4},{5,7},{7,5},{8,10},{10,8},{9,1... | collective-permute-start | bytes 1769480 | tf_op jit(solution)/shard_map/ppermute | solution.py:276
  564.9 11.6 %collective-permute-start.36 = (bf16[384,768]{1,0:T(8,128)(2,1)S(1)}, bf16[384,768]{1,0:T(8,128)(2,1)S(1)}, u32[]{:S(2)}, u32[]{:S(2)}) collective-permute-start(bf16[384,768]{1,0:T(8,128)(2,1)S(1)} %dynamic-slice_add_fusion.8), channel_id=1, source_target_pairs={{0,4},{4,0},{8,12},{12,8},{1,5},{5,1},{9,13},{13,9},{2,6},{6,2},{1... | collective-permute-start | bytes 1769480 | tf_op jit(solution)/shard_map/ppermute | solution.py:276
  575.7 28.9 %collective-permute-start.22 = (bf16[96,3072]{1,0:T(8,128)(2,1)S(1)}, bf16[96,3072]{1,0:T(8,128)(2,1)S(1)}, u32[]{:S(2)}, u32[]{:S(2)}) collective-permute-start(bf16[96,3072]{1,0:T(8,128)(2,1)S(1)} %dynamic-slice_add_fusion.10), channel_id=1, source_target_pairs={{0,4},{4,0},{8,12},{12,8},{1,5},{5,1},{9,13},{13,9},{2,6},{6,2},{1... | collective-permute-start | bytes 1769480 | tf_op jit(solution)/shard_map/ppermute | solution.py:276
  576.5 48.6 %collective-permute-start.29 = (bf16[96,3072]{1,0:T(8,128)(2,1)S(1)}, bf16[96,3072]{1,0:T(8,128)(2,1)S(1)}, u32[]{:S(2)}, u32[]{:S(2)}) collective-permute-start(bf16[96,3072]{1,0:T(8,128)(2,1)S(1)} %dynamic-slice_add_fusion.9), channel_id=1, source_target_pairs={{0,4},{4,0},{8,12},{12,8},{1,5},{5,1},{9,13},{13,9},{2,6},{6,2},{1... | collective-permute-start | bytes 1769480 | tf_op jit(solution)/shard_map/ppermute | solution.py:276
  578.1 56.9 %collective-permute-start.10 = (bf16[96,3072]{1,0:T(8,128)(2,1)S(1)}, bf16[96,3072]{1,0:T(8,128)(2,1)S(1)}, u32[]{:S(2)}, u32[]{:S(2)}) collective-permute-start(bf16[96,3072]{1,0:T(8,128)(2,1)S(1)} %dynamic-slice_add_fusion.11), channel_id=1, source_target_pairs={{0,4},{4,0},{8,12},{12,8},{1,5},{5,1},{9,13},{13,9},{2,6},{6,2},{1... | collective-permute-start | bytes 1769480 | tf_op jit(solution)/shard_map/ppermute | solution.py:276
  604.6 31.4 %collective-permute-start.37 = (bf16[384,768]{1,0:T(8,128)(2,1)S(1)}, bf16[384,768]{1,0:T(8,128)(2,1)S(1)}, u32[]{:S(2)}, u32[]{:S(2)}) collective-permute-start(bf16[384,768]{1,0:T(8,128)(2,1)S(1)} %add.360), channel_id=1, source_target_pairs={{0,8},{4,12},{8,0},{12,4},{1,9},{5,13},{9,1},{13,5},{2,10},{6,14},... | collective-permute-start | bytes 1769480 | tf_op jit(solution)/shard_map/ppermute | solution.py:276
  606.7 70.3 %collective-permute-start.23 = (bf16[96,3072]{1,0:T(8,128)(2,1)S(1)}, bf16[96,3072]{1,0:T(8,128)(2,1)S(1)}, u32[]{:S(2)}, u32[]{:S(2)}) collective-permute-start(bf16[96,3072]{1,0:T(8,128)(2,1)S(1)} %add.344), channel_id=1, source_target_pairs={{0,8},{4,12},{8,0},{12,4},{1,9},{5,13},{9,1},{13,5},{2,10},{6,14},... | collective-permute-start | bytes 1769480 | tf_op jit(solution)/shard_map/ppermute | solution.py:276
  626.1 67.1 %collective-permute-start.30 = (bf16[96,3072]{1,0:T(8,128)(2,1)}, bf16[96,3072]{1,0:T(8,128)(2,1)}, u32[]{:S(2)}, u32[]{:S(2)}) collective-permute-start(bf16[96,3072]{1,0:T(8,128)(2,1)} %add.349), channel_id=1, source_target_pairs={{0,8},{4,12},{8,0},{12,4},{1,9},{5,13},{9,1},{13,5},{2,10},{6,14},... | collective-permute-start | bytes 1769480 | tf_op jit(solution)/shard_map/ppermute | solution.py:276
  635.9 61.7 %collective-permute-start.11 = (bf16[96,3072]{1,0:T(8,128)(2,1)}, bf16[96,3072]{1,0:T(8,128)(2,1)}, u32[]{:S(2)}, u32[]{:S(2)}) collective-permute-start(bf16[96,3072]{1,0:T(8,128)(2,1)} %add.334), channel_id=1, source_target_pairs={{0,8},{4,12},{8,0},{12,4},{1,9},{5,13},{9,1},{13,5},{2,10},{6,14},... | collective-permute-start | bytes 1769480 | tf_op jit(solution)/shard_map/ppermute | solution.py:276
  636.9 63.1 %collective-permute-start.38 = (bf16[384,768]{1,0:T(8,128)(2,1)}, bf16[384,768]{1,0:T(8,128)(2,1)}, u32[]{:S(2)}, u32[]{:S(2)}) collective-permute-start(bf16[384,768]{1,0:T(8,128)(2,1)} %add.361), channel_id=1, source_target_pairs={{0,2},{2,0},{1,3},{3,1},{4,6},{6,4},{5,7},{7,5},{8,10},{10,8},{9,1... | collective-permute-start | bytes 1769480 | tf_op jit(solution)/shard_map/ppermute | solution.py:276
  678.0 23.5 %collective-permute-start.24 = (bf16[96,3072]{1,0:T(8,128)(2,1)}, bf16[96,3072]{1,0:T(8,128)(2,1)}, u32[]{:S(2)}, u32[]{:S(2)}) collective-permute-start(bf16[96,3072]{1,0:T(8,128)(2,1)} %add.345), channel_id=1, source_target_pairs={{0,2},{2,0},{1,3},{3,1},{4,6},{6,4},{5,7},{7,5},{8,10},{10,8},{9,1... | collective-permute-start | bytes 1769480 | tf_op jit(solution)/shard_map/ppermute | solution.py:276
  694.6 21.8 %collective-permute-start.31 = (bf16[96,3072]{1,0:T(8,128)(2,1)S(1)}, bf16[96,3072]{1,0:T(8,128)(2,1)S(1)}, u32[]{:S(2)}, u32[]{:S(2)}) collective-permute-start(bf16[96,3072]{1,0:T(8,128)(2,1)S(1)} %add.350), channel_id=1, source_target_pairs={{0,2},{2,0},{1,3},{3,1},{4,6},{6,4},{5,7},{7,5},{8,10},{10,8},{9,1... | collective-permute-start | bytes 1769480 | tf_op jit(solution)/shard_map/ppermute | solution.py:276
  699.1 17.0 %collective-permute-start.12 = (bf16[96,3072]{1,0:T(8,128)(2,1)S(1)}, bf16[96,3072]{1,0:T(8,128)(2,1)S(1)}, u32[]{:S(2)}, u32[]{:S(2)}) collective-permute-start(bf16[96,3072]{1,0:T(8,128)(2,1)S(1)} %add.335), channel_id=1, source_target_pairs={{0,2},{2,0},{1,3},{3,1},{4,6},{6,4},{5,7},{7,5},{8,10},{10,8},{9,1... | collective-permute-start | bytes 1769480 | tf_op jit(solution)/shard_map/ppermute | solution.py:276
  701.4 25.9 %collective-permute-start.39 = (bf16[768,768]{1,0:T(8,128)(2,1)S(1)}, bf16[768,768]{1,0:T(8,128)(2,1)S(1)}, u32[]{:S(2)}, u32[]{:S(2)}) collective-permute-start(bf16[768,768]{1,0:T(8,128)(2,1)S(1)} %pad_maximum_fusion.19), channel_id=1, source_target_pairs={{0,1},{1,0},{2,3},{3,2},{4,5},{5,4},{6,7},{7,6},{8,9},{9,8},{10,11... | collective-permute-start | bytes 3538952 | tf_op jit(solution)/shard_map/ppermute | solution.py:276
  702.9 14.2 %collective-permute-start.25 = (bf16[192,3072]{1,0:T(8,128)(2,1)S(1)}, bf16[192,3072]{1,0:T(8,128)(2,1)S(1)}, u32[]{:S(2)}, u32[]{:S(2)}) collective-permute-start(bf16[192,3072]{1,0:T(8,128)(2,1)S(1)} %pad_maximum_fusion.17), channel_id=1, source_target_pairs={{0,1},{1,0},{2,3},{3,2},{4,5},{5,4},{6,7},{7,6},{8,9},{9,8},{10,11... | collective-permute-start | bytes 3538952 | tf_op jit(solution)/shard_map/ppermute | solution.py:276
  716.3 2.9 collective-permute-start.13
  716.5 13.7 %collective-permute-start.32 = (bf16[192,3072]{1,0:T(8,128)(2,1)S(1)}, bf16[192,3072]{1,0:T(8,128)(2,1)S(1)}, u32[]{:S(2)}, u32[]{:S(2)}) collective-permute-start(bf16[192,3072]{1,0:T(8,128)(2,1)S(1)} %pad_maximum_fusion.18), channel_id=1, source_target_pairs={{0,1},{1,0},{2,3},{3,2},{4,5},{5,4},{6,7},{7,6},{8,9},{9,8},{10,11... | collective-permute-start | bytes 3538952 | tf_op jit(solution)/shard_map/ppermute | solution.py:276
  (74 other events, 301.2 us)

commit v2 on v1

--- a/solution.py
+++ b/solution.py
@@ -122,11 +122,11 @@
 
 def backward_kernel(
     shift_ref, q_ref, k_ref, v_ref, g_ref, o_ref, qt_ref, kt_ref, lse_ref,
-    dq_ref, dk_ref, dv_ref, ka, va, qa, ga, k_turned, dk_sum, dv_sum, dq_turned,
-    *, causal, block, swapped, scaling,
+    dq_ref, dk_ref, dv_ref, sums_ref, ka, va, qa, ga, k_turned, dk_sum, dv_sum, dq_turned,
+    *, causal, block, swapped, scaling, first,
 ):
     tq, ts = q_ref.shape[0], k_ref.shape[0]
-    pair = pl.program_id(1)
+    pair = pl.program_id(1) + first
     shift = shift_ref[0]
     for here, there in half_slices(ts, shift, swapped):
         k, v, extra = k_ref[there, :], v_ref[there, :], kt_ref[there, :]
@@ -154,6 +154,7 @@
             qa[head, here, :] = jnp.where(own, q, q_extra.astype(BF))
             ga[head, here, :] = jnp.where(own, g, g_extra.astype(BF))
     blocks = tq // block
+    dq_total = jnp.zeros((1, LANES), F32)
     for index in reversed(range(blocks)):
         count = (index + 1) * block if causal == "block" else ts
         rows = slice(index * block, (index + 1) * block)
@@ -173,14 +174,21 @@
             own_rows = slice(HD * head, HD * (head + 1))
             dq_turned[own_rows, rows] = dot(k_turned[own_rows, :count], grads)
         there = row_block(index, block, tq, shift, swapped)
-        dq_ref[there, :] = dq_turned[:, rows].T.astype(BF) * jnp.asarray(scaling, BF)
+        dq = dq_turned[:, rows].T.astype(BF) * jnp.asarray(scaling, BF)
+        dq_ref[there, :] = dq
+        dq_total += jnp.sum(dq.astype(F32), 0, keepdims=True)
+    dv_total = jnp.zeros((1, LANES), F32)
     for here, there in half_slices(ts, shift, swapped):
         own = head_lanes((ts // (2 if swapped else 1), LANES), 0)
         dk_ref[there, :] = jnp.where(own, dk_sum[0, here, :], dk_sum[1, here, :]).astype(BF)
-        dv_ref[there, :] = jnp.where(own, dv_sum[0, here, :], dv_sum[1, here, :]).astype(BF)
-
-
-def attention_specs(tq, ts, columns):
+        dv = jnp.where(own, dv_sum[0, here, :], dv_sum[1, here, :]).astype(BF)
+        dv_ref[there, :] = dv
+        dv_total += jnp.sum(dv.astype(F32), 0, keepdims=True)
+    row = lax.broadcasted_iota(jnp.int32, sums_ref.shape, 0)
+    sums_ref[...] = jnp.where(row == 0, dq_total, jnp.where(row == 1, dv_total, 0.0))
+
+
+def attention_specs(tq, ts, columns, first=0):
     none = pl.Squeezed()
 
     def of(count, start):
@@ -189,21 +197,30 @@
     def shared(count):
         return pl.BlockSpec((none, count, LANES), lambda row, pair, _: (row, 0, 0))
 
-    q, k, v = (c // LANES for c in columns)
-    return of(tq, q), of(ts, k), of(ts, v), of(tq, 0), of(ts, 0), shared(tq), shared(ts)
-
-
-def attend(q, k, v, columns, terms, shift, width, causal, block, swapped):
+    q, k, v = (c // LANES + first for c in columns)
+    return of(tq, q), of(ts, k), of(ts, v), of(tq, first), of(tq, 0), of(ts, 0), shared(tq), shared(ts)
+
+
+def skip_refs(kernel, start, count):
+    def run(*refs):
+        kernel(*refs[:start], *refs[start + count :])
+
+    return run
+
+
+def attend(q, k, v, columns, terms, shift, width, causal, block, swapped, after=()):
     rows, tq, ts = q.shape[0], q.shape[1], k.shape[1]
     pairs = width // LANES
-    sq, sk, sv, so, _, tq_spec, ts_spec = attention_specs(tq, ts, columns)
+    sq, sk, sv, _, so, _, tq_spec, ts_spec = attention_specs(tq, ts, columns)
     elements = rows * pairs * 2 * tq * ts
+    kernel = functools.partial(forward_kernel, causal=causal, block=block, swapped=swapped)
     return pl.pallas_call(
-        functools.partial(forward_kernel, causal=causal, block=block, swapped=swapped),
+        skip_refs(kernel, 6, len(after)),
         grid_spec=pltpu.PrefetchScalarGridSpec(
             num_scalar_prefetch=1,
             grid=(rows, pairs),
-            in_specs=[sq, sk, sv, tq_spec, ts_spec],
+            in_specs=[sq, sk, sv, tq_spec, ts_spec]
+            + [pl.BlockSpec(memory_space=pl.ANY)] * len(after),
             out_specs=[so, tq_spec],
             scratch_shapes=[pltpu.VMEM((2, n, LANES), BF) for n in (ts, ts, tq)],
         ),
@@ -213,25 +230,31 @@
         ],
         compiler_params=pltpu.CompilerParams(vmem_limit_bytes=48 * 2**20),
         cost_estimate=pl.CostEstimate(
-            flops=elements * 1200, bytes_accessed=rows * (tq + ts) * width * 4, transcendentals=elements
+            flops=elements * 1600, bytes_accessed=rows * (tq + ts) * width * 4, transcendentals=0
         ),
-    )(shift, q, k, v, *terms)
-
-
-def attend_back(q, k, v, columns, g, o, lse, terms, shift, width, causal, block, swapped):
+    )(shift, q, k, v, *terms, *after)
+
+
+def attend_back(
+    q, k, v, columns, g, o, lse, terms, shift, first, pairs, causal, block, swapped, after=()
+):
     rows, tq, ts = q.shape[0], q.shape[1], k.shape[1]
-    pairs = width // LANES
-    sq, sk, sv, so, ss, tq_spec, ts_spec = attention_specs(tq, ts, columns)
+    sq, sk, sv, sg, so, ss, tq_spec, ts_spec = attention_specs(tq, ts, columns, first)
     elements = rows * pairs * 2 * tq * ts
+    kernel = functools.partial(
+        backward_kernel, causal=causal, block=block, swapped=swapped, scaling=HD**-0.5, first=first
+    )
     return pl.pallas_call(
-        functools.partial(
-            backward_kernel, causal=causal, block=block, swapped=swapped, scaling=HD**-0.5
-        ),
+        skip_refs(kernel, 9, len(after)),
         grid_spec=pltpu.PrefetchScalarGridSpec(
             num_scalar_prefetch=1,
             grid=(rows, pairs),
-            in_specs=[sq, sk, sv, so, so, tq_spec, ts_spec, tq_spec],
-            out_specs=[so, ss, ss],
+            in_specs=[sq, sk, sv, sg, sg, tq_spec, ts_spec, tq_spec]
+            + [pl.BlockSpec(memory_space=pl.ANY)] * len(after),
+            out_specs=[
+                so, ss, ss,
+                pl.BlockSpec((pl.Squeezed(), 8, LANES), lambda row, pair, _: (row, 0, pair)),
+            ],
             scratch_shapes=[pltpu.VMEM((2, n, LANES), BF) for n in (ts, ts, tq, tq)]
             + [
                 pltpu.VMEM((LANES, ts), BF),
@@ -241,34 +264,154 @@
             ],
         ),
         out_shape=[
-            jax.ShapeDtypeStruct((rows, tq, width), BF),
-            jax.ShapeDtypeStruct((rows, ts, width), BF),
-            jax.ShapeDtypeStruct((rows, ts, width), BF),
+            jax.ShapeDtypeStruct((rows, tq, pairs * LANES), BF),
+            jax.ShapeDtypeStruct((rows, ts, pairs * LANES), BF),
+            jax.ShapeDtypeStruct((rows, ts, pairs * LANES), BF),
+            jax.ShapeDtypeStruct((rows, 8, pairs * LANES), F32),
         ],
         compiler_params=pltpu.CompilerParams(vmem_limit_bytes=48 * 2**20),
         cost_estimate=pl.CostEstimate(
-            flops=elements * 2000, bytes_accessed=rows * (tq + ts) * width * 8, transcendentals=elements
+            flops=elements * 2600, bytes_accessed=rows * (tq + ts) * pairs * 1024, transcendentals=0
         ),
-    )(shift, q, k, v, g, o, *terms, lse)
-
-
-def norm(resid, gain_vec, bias_vec):
+    )(shift, q, k, v, g, o, *terms, lse, *after)
+
+
+def norm(resid):
     center = resid - jnp.mean(resid, -1, keepdims=True)
     inverse = lax.rsqrt(jnp.mean(center * center, -1, keepdims=True) + norm_epsilon)
-    normed = center * inverse
-    return normed * gain_vec + bias_vec, normed, inverse
+    return center * inverse, inverse
 
 
 def norm_back(upstream, normed, inverse, gain_vec):
     w = upstream * gain_vec
-    grad = (
+    return (
         w - jnp.mean(w, -1, keepdims=True) - normed * jnp.mean(w * normed, -1, keepdims=True)
     ) * inverse
-    return grad, jnp.sum(upstream * normed, 0), jnp.sum(upstream, 0)
-
-
-def column_sum(x):
-    return jnp.sum(x.astype(F32), 0)
+
+
+def gelu_parts(pre):
+    bell = jnp.exp(pre * pre * -0.5)
+    t = 1.0 / (1.0 + jnp.abs(pre) * (0.3275911 * 0.5**0.5))
+    poly = 0.5 * 1.061405429
+    for c in (-1.453152027, 1.421413741, -0.284496736, 0.254829592):
+        poly = poly * t + 0.5 * c
+    tail = poly * t * bell
+    phi_sum = jnp.where(pre >= 0, 1.0 - tail, tail)
+    return pre * phi_sum, phi_sum + pre * (bell * 0.3989422804014327)
+
+
+def add_rows(sums_ref, rows):
+    for index, value in enumerate(rows):
+        total = jnp.sum(value.astype(F32), 0, keepdims=True)
+        here = slice(index, index + 1)
+        sums_ref[here, :] = jnp.where(pl.program_id(0) == 0, total, sums_ref[here, :] + total)
+
+
+def after_self_kernel(
+    o_ref, x_ref, w_ref, b_ref, gain_ref, bias_ref, qw_ref, qb_ref,
+    n1_ref, i1_ref, h1b_ref, cq_ref, *, scaling,
+):
+    resid = x_ref[...].astype(F32) + (dot(o_ref[...], w_ref[...]) + b_ref[...])
+    n1, i1 = norm(resid)
+    h1b = (n1 * gain_ref[...] + bias_ref[...]).astype(BF)
+    n1_ref[...] = n1
+    i1_ref[...] = jnp.broadcast_to(i1, i1_ref.shape)
+    h1b_ref[...] = h1b
+    cq_ref[...] = ((dot(h1b, qw_ref[...]) + qb_ref[...]) * scaling).astype(BF)
+
+
+def middle_kernel(
+    o_ref, n1_ref, up_ref, g1_ref, s1_ref, ow_ref, ob_ref, g2_ref, s2_ref,
+    w1_ref, b1_ref, w2_ref, b2_ref, g3_ref, s3_ref,
+    out_ref, act_ref, dbf_ref, h2b_ref, dpre_ref, dr2_ref, dbc_ref, dco_ref, sums_ref, wide_ref,
+    slope, *, chunk,
+):
+    h1 = n1_ref[...] * g1_ref[...] + s1_ref[...]
+    n2, i2 = norm(h1 + (dot(o_ref[...], ow_ref[...]) + ob_ref[...]))
+    h2 = n2 * g2_ref[...] + s2_ref[...]
+    h2b = h2.astype(BF)
+    h2b_ref[...] = h2b
+    hidden = w1_ref.shape[1]
+    cols = [slice(c, c + chunk) for c in range(0, hidden, chunk)]
+    branch = b2_ref[...]
+    for c in cols:
+        pre = dot(h2b, w1_ref[:, c]) + b1_ref[:, c]
+        value, slope_c = gelu_parts(pre)
+        slope[:, c] = slope_c
+        act_c = value.astype(BF)
+        act_ref[:, c] = act_c
+        branch = branch + dot(act_c, w2_ref[c, :])
+    n3, i3 = norm(h2 + branch)
+    out_ref[...] = (n3 * g3_ref[...] + s3_ref[...]).astype(BF)
+    up = up_ref[...].astype(F32)
+    dr3 = norm_back(up, n3, i3, g3_ref[...])
+    dbf = dr3.astype(BF)
+    dbf_ref[...] = dbf
+    dh2 = dr3
+    first = pl.program_id(0) == 0
+    for c in cols:
+        dpre_c = (dot(dbf, w2_ref[c, :], NT) * slope[:, c]).astype(BF)
+        dpre_ref[:, c] = dpre_c
+        total = jnp.sum(dpre_c.astype(F32), 0, keepdims=True)
+        wide_ref[0:1, c] = jnp.where(first, total, wide_ref[0:1, c] + total)
+        dh2 = dh2 + dot(dpre_c, w1_ref[:, c], NT)
+    dr2 = norm_back(dh2, n2, i2, g2_ref[...])
+    dbc = dr2.astype(BF)
+    dr2_ref[...] = dr2
+    dbc_ref[...] = dbc
+    dco_ref[...] = dot(dbc, ow_ref[...], NT).astype(BF)
+    add_rows(sums_ref, (up * n3, up, dbf, dh2 * n2, dh2, dbc))
+
+
+def before_self_kernel(
+    *refs, parts,
+):
+    dcq = jnp.concatenate([ref[...] for ref in refs[:parts]], 1)
+    dr2_ref, n1_ref, i1_ref, qw_ref, g1_ref, ow_ref = refs[parts : parts + 6]
+    dr1_ref, dba_ref, dso_ref, sums_ref = refs[parts + 6 :]
+    n1 = n1_ref[...]
+    dh1 = dr2_ref[...] + dot(dcq, qw_ref[...], NT)
+    dr1 = norm_back(dh1, n1, i1_ref[:, 0:1], g1_ref[...])
+    dba = dr1.astype(BF)
+    dr1_ref[...] = dr1
+    dba_ref[...] = dba
+    dso_ref[...] = dot(dba, ow_ref[...], NT).astype(BF)
+    add_rows(sums_ref, (dh1 * n1, dh1, dba))
+
+
+def token_call(kernel, block, blocked, whole, outs, scratch=(), flops=0, after=()):
+    tokens = blocked[0].shape[0]
+    whole = [w.reshape(1, -1) if w.ndim == 1 else w for w in whole]
+    in_specs = [pl.BlockSpec((block, a.shape[1]), lambda i: (i, 0)) for a in blocked]
+    in_specs += [
+        pl.BlockSpec(a.shape, lambda i: (0, 0), pipeline_mode=pl.Buffered(1)) for a in whole
+    ]
+    in_specs += [pl.BlockSpec(memory_space=pl.ANY)] * len(after)
+    out_specs, out_shape = [], []
+    for out in outs:
+        if len(out) == 2:
+            shape = (tokens, out[0])
+            out_specs.append(pl.BlockSpec((block, out[0]), lambda i: (i, 0)))
+        else:
+            shape = out[:2]
+            out_specs.append(pl.BlockSpec(shape, lambda i: (0, 0)))
+        out_shape.append(jax.ShapeDtypeStruct(shape, out[-1]))
+    used = len(blocked) + len(whole)
+
+    def run(*refs):
+        kernel(*refs[:used], *refs[used + len(after) :])
+
+    moved = sum(a.size * a.dtype.itemsize for a in (*blocked, *whole, *out_shape))
+    return pl.pallas_call(
+        run,
+        grid=(tokens // block,),
+        in_specs=in_specs,
+        out_specs=out_specs,
+        out_shape=out_shape,
+        scratch_shapes=list(scratch),
+        compiler_params=pltpu.CompilerParams(vmem_limit_bytes=56 * 2**20),
+        cost_estimate=pl.CostEstimate(flops=flops, bytes_accessed=moved, transcendentals=0),
+    )(*blocked, *whole, *after)
 
 
 def partner(x, axis, bit=1):
@@ -276,37 +419,79 @@
     return lax.ppermute(x, axis, [(i, i ^ bit) for i in range(count)])
 
 
-def halve(x, axis):
-    index = lax.axis_index(axis)
-    half = x.shape[0] // 2
-    sent = lax.dynamic_slice_in_dim(x, (1 - index) * half, half, 0)
-    got = partner(sent, axis)
-    return lax.dynamic_slice_in_dim(x, index * half, half, 0) + got
-
-
-def join(x, axis):
-    got = partner(x, axis)
-    first = lax.axis_index(axis) == 0
-    return jnp.concatenate([jnp.where(first, x, got), jnp.where(first, got, x)], 0)
-
-
-def reduce_matrix(x):
-    wide, rest, side, core = (lax.axis_size(a) for a in ("wide", "rest", "side", "core"))
-    if not (wide == side == core == 2):
-        x = lax.psum_scatter(x, "wide", scatter_dimension=0, tiled=True)
-        return lax.psum(x, ("rest", "side", "core")).astype(F32)
-    cols = x.shape[1]
-    x = x.reshape(2, 2, -1, cols).transpose(1, 0, 2, 3).reshape(-1, cols)
-    x = halve(x, "core")
-    x = halve(x, "wide")
-    x = halve(x, "side")
-    bit = 1
-    while bit < rest:
-        x = x + partner(x, "rest", bit)
-        bit *= 2
-    x = join(x, "side")
-    x = join(x, "core")
-    return x.astype(F32)
+def pick(x, axis, index):
+    return lax.dynamic_index_in_dim(x, index, axis, keepdims=False)
+
+
+class Reduction:
+    def __init__(self, parts, order):
+        self.split = all(lax.axis_size(a) == 2 for a in ("wide", "side", "core"))
+        self.parts = parts
+        self.rows = parts[0].shape[0] // lax.axis_size("wide")
+        self.got = None
+        if self.split:
+            eighth = parts[0].shape[0] // 8
+            self.acc = [x.reshape(2, 2, 2, 2, eighth // 2, x.shape[1]) for x in parts]
+            self.left = ["wide", "core", "side", "rest"]
+            self.steps = list(order)
+            self.joins = []
+
+    def place(self, axis):
+        index = lax.axis_index(axis)
+        return index % 2 if axis == "rest" else index
+
+    def send(self):
+        if not self.split:
+            return ()
+        step = self.steps[0]
+        if step in ("core", "wide", "side", "rest"):
+            at = self.left.index(step)
+            sent = [pick(x, at, 1 - self.place(step)) for x in self.acc]
+            sent = sent[0] if len(sent) == 1 else jnp.concatenate(sent, -1)
+            self.got = partner(sent, step)
+        elif step == "far":
+            sent = self.acc[0]
+            bit, total = 2, self.acc[0]
+            assert lax.axis_size("rest") in (2, 4)
+            self.got = partner(sent, "rest", 2) if lax.axis_size("rest") == 4 else None
+        else:
+            sent = self.acc[0]
+            self.got = partner(sent, step[5:])
+        return (sent,)
+
+    def take(self):
+        if not self.split:
+            return
+        step = self.steps.pop(0)
+        if step in ("core", "wide", "side", "rest"):
+            at = self.left.index(step)
+            kept = [pick(x, at, self.place(step)) for x in self.acc]
+            kept = kept[0] if len(kept) == 1 else jnp.concatenate(kept, -1)
+            self.acc = [kept + self.got]
+            self.left.pop(at)
+        elif step == "far":
+            if self.got is not None:
+                self.acc = [self.acc[0] + self.got]
+        else:
+            axis = step[5:]
+            x = self.acc[0]
+            first = self.place(axis) == 0
+            both = jnp.stack([jnp.where(first, x, self.got), jnp.where(first, self.got, x)])
+            self.acc = [both.reshape((-1,) + x.shape[1:]) if axis != "rest" else both.reshape(-1, x.shape[-1])]
+
+    def result(self):
+        if self.split:
+            assert not self.steps
+            return self.acc[0].reshape(self.rows, -1).astype(F32)
+        outs = []
+        for x in self.parts:
+            x = lax.psum_scatter(x, "wide", scatter_dimension=0, tiled=True)
+            outs.append(lax.psum(x, ("rest", "side", "core")).astype(F32))
+        return jnp.concatenate(outs, 1)
+
+
+X_FIRST = ("core", "wide", "side", "rest", "far", "join_rest", "join_side", "join_core")
+Y_FIRST = ("core", "side", "wide", "rest", "far", "join_rest", "join_side", "join_core")
 
 
 def reduce_vectors(vectors):
@@ -352,10 +537,12 @@
             sent = lax.dynamic_index_in_dim(x, 1 - place, 0, keepdims=False)
             return jnp.concatenate([kept, partner(sent, "wide")], 0)
 
-        def give(x, dtype):
-            kept = x[:tok_count]
-            got = partner(x[tok_count:].astype(BF), "wide").astype(dtype)
-            kept = kept.astype(dtype)
+        def send_back(x):
+            return (partner(x[tok_count:].astype(BF), "wide"),)
+
+        def give(x, got, dtype):
+            kept = x[:tok_count].astype(dtype)
+            got = got[0].astype(dtype)
             first = place == 0
             return jnp.stack([jnp.where(first, kept, got), jnp.where(first, got, kept)])
 
@@ -367,7 +554,10 @@
         def bring(x):
             return x.reshape((-1,) + x.shape[2:])
 
-        def give(x, dtype):
+        def send_back(x):
+            return ()
+
+        def give(x, got, dtype):
             return x.astype(dtype).reshape(row_count, tok_count, width)
 
         tokens, causal = tok_count, "mask"
@@ -389,23 +579,23 @@
         return x if swapped else lax.psum_scatter(x, "wide", scatter_dimension=1, tiled=True)
 
     terms = (segment_terms(seg)[0], segment_terms(key_seg)[1])
-
-    def attention(q, kv, columns, is_causal):
+    block = min(256, row_count * tok_count)
+
+    def attention(q, kv, columns, is_causal, after=()):
         return attend(
-            q, kv, kv, columns, terms, shift, width, causal if is_causal else "no", block_f, swapped
+            q, kv, kv, columns, terms, shift, width, causal if is_causal else "no", block_f,
+            swapped, after,
         )
 
-    def attention_back(q, kv, columns, g, o, lse, is_causal):
-        dq, dk, dv = attend_back(
-            q, kv, kv, columns, by_row(g), o, lse, terms, shift, width,
-            causal if is_causal else "no", block_b, swapped,
+    def attention_back(q, kv, columns, g, o, lse, is_causal, first, pairs, after):
+        dq, dk, dv, sums = attend_back(
+            q, kv, kv, columns, by_row(g), o, lse, terms, shift, first, pairs,
+            causal if is_causal else "no", block_b, swapped, after,
         )
-        return flat(dq), flat(key_grads(dk)), flat(key_grads(dv))
+        return flat(dq), flat(key_grads(dk)), flat(key_grads(dv)), jnp.sum(sums, 0)
 
     flat_in = bring(target)
     flat_enc = bring(encoded)
-    upstream = bring(out_grad)
-
     zeros = jnp.zeros_like(self_q_b)
     ones = jnp.ones_like(self_q_b)
     qkv_bias = jnp.concatenate([self_q_b, zeros, self_v_b])
@@ -417,79 +607,139 @@
         self_kv, self_cols = keys_of(qkv[..., width:]), (0, 0, width)
     self_o, self_lse = attention(qkv, self_kv, self_cols, True)
     self_ob = flat(self_o)
-    h1, n1, i1 = norm(
-        flat_in.astype(F32) + (dot(self_ob, self_out_w) + self_out_b), norm1_gain, norm1_bias
-    )
-    h1b = h1.astype(BF)
-    cq = by_row(((dot(h1b, cross_q_w) + cross_q_b) * scaling).astype(BF))
+    n1, i1, h1b, cq = token_call(
+        functools.partial(after_self_kernel, scaling=scaling), block,
+        (self_ob, flat_in),
+        (self_out_w, self_out_b, norm1_gain, norm1_bias, cross_q_w, cross_q_b),
+        [(width, F32), (LANES, F32), (width, BF), (width, BF)],
+        flops=4 * tokens * width * width, after=(flat_enc,),
+    )
+    upstream = bring(out_grad)
+    cq = by_row(cq)
     ckv = by_row((dot(flat_enc, cross_kv_w) + jnp.concatenate([zeros, cross_v_b])).astype(BF))
     ckv = keys_of(ckv)
     cross_cols = (0, 0, width)
     cross_o, cross_lse = attention(cq, ckv, cross_cols, False)
     cross_ob = flat(cross_o)
-    h2, n2, i2 = norm(h1 + (dot(cross_ob, cross_out_w) + cross_out_b), norm2_gain, norm2_bias)
-    h2b = h2.astype(BF)
-    pre = dot(h2b, ffn_in_w) + ffn_in_b
-    phi_sum = 0.5 * lax.erfc(-pre * (0.5**0.5))
-    act = (pre * phi_sum).astype(BF)
-    slope = phi_sum + pre * (jnp.exp(-0.5 * pre * pre) * 0.3989422804014327)
-    h3, n3, i3 = norm(h2 + (dot(act, ffn_out_w) + ffn_out_b), norm3_gain, norm3_bias)
-    layer_out = give(h3.astype(BF), BF)
-
-    dr3, norm3_gain_grad, norm3_bias_grad = norm_back(upstream.astype(F32), n3, i3, norm3_gain)
-    dbf = dr3.astype(BF)
-    ffn_out_w_grad = reduce_matrix(dot(act, dbf, TN).astype(BF))
-    dpre = (dot(dbf, ffn_out_w, NT) * slope).astype(BF)
-    ffn_in_w_grad = reduce_matrix(dot(h2b, dpre, TN).astype(BF))
-    dh2 = dr3 + dot(dpre, ffn_in_w, NT)
-    dr2, norm2_gain_grad, norm2_bias_grad = norm_back(dh2, n2, i2, norm2_gain)
-    dbc = dr2.astype(BF)
-    dco = dot(dbc, cross_out_w, NT).astype(BF)
-    dcq, dck, dcv = attention_back(cq, ckv, cross_cols, dco, cross_o, cross_lse, False)
-    dckv = jnp.concatenate([dck, dcv], 1)
-    cross_grads = reduce_matrix(
-        jnp.concatenate(
-            [
-                dot(cross_ob, dbc, TN).astype(BF),
-                dot(h1b, dcq, TN).astype(BF),
-                dot(flat_enc, dckv, TN).astype(BF),
-            ],
-            1,
+    hidden = ffn_in_w.shape[1]
+    h3b, act, dbf, h2b, dpre, dr2, dbc, dco, mid_sums, hid_sums = token_call(
+        functools.partial(middle_kernel, chunk=width), block,
+        (cross_ob, n1, upstream),
+        (
+            norm1_gain, norm1_bias, cross_out_w, cross_out_b, norm2_gain, norm2_bias,
+            ffn_in_w, ffn_in_b, ffn_out_w, ffn_out_b, norm3_gain, norm3_bias,
+        ),
+        [
+            (width, BF), (hidden, BF), (width, BF), (width, BF), (hidden, BF), (width, F32),
+            (width, BF), (width, BF), (8, width, F32), (8, hidden, F32),
+        ],
+        scratch=[pltpu.VMEM((block, hidden), F32)],
+        flops=2 * tokens * width * (4 * hidden + 2 * width),
+    )
+    got_out = send_back(h3b)
+
+    ra = Reduction([dot(act, dbf, TN).astype(BF)], X_FIRST)
+    sent_a = ra.send()
+    rb = Reduction(
+        [dot(h2b, dpre, TN).astype(BF), dot(cross_ob, dbc, TN).astype(BF)], Y_FIRST
+    )
+    sent_b = rb.send()
+    ra.take()
+    sent_a = ra.send()
+
+    pairs = width // LANES
+    cuts = 3 if pairs % 3 == 0 else 1
+    per = pairs // cuts
+
+    def cross_part(index, after):
+        return attention_back(
+            cq, ckv, cross_cols, dco, cross_o, cross_lse, False, index * per, per, after
         )
-    )
-    encoded_grad = give(dot(dckv, cross_kv_w, NT), F32)
-    dh1 = dr2 + dot(dcq, cross_q_w, NT)
-    dr1, norm1_gain_grad, norm1_bias_grad = norm_back(dh1, n1, i1, norm1_gain)
-    dba = dr1.astype(BF)
-    dso = dot(dba, self_out_w, NT).astype(BF)
-    dsq, dsk, dsv = attention_back(qkv, self_kv, self_cols, dso, self_o, self_lse, True)
-    dqkv = jnp.concatenate([dsq, dsk, dsv], 1)
-    self_grads = reduce_matrix(
-        jnp.concatenate(
-            [dot(self_ob, dba, TN).astype(BF), dot(flat_in, dqkv, TN).astype(BF)], 1
+
+    def self_part(index, dso, after):
+        return attention_back(
+            qkv, self_kv, self_cols, dso, self_o, self_lse, True, index * per, per, after
         )
-    )
-    target_grad = give(dr1 + dot(dqkv, self_qkv_w, NT), F32)
-
+
+    cross_parts = [cross_part(0, sent_a + sent_b)]
+    rb.take()
+    sent_b = rb.send()
+    for index in range(1, cuts):
+        cross_parts.append(cross_part(index, sent_b if index == 1 else got_out))
+    dcq, dck, dcv, csums = ([part[i] for part in cross_parts] for i in range(4))
+    ra.take()
+    sent_a = ra.send()
+    rb.take()
+    sent_b = rb.send()
+    dr1, dba, dso, low_sums = token_call(
+        functools.partial(before_self_kernel, parts=cuts), block,
+        (*dcq, dr2, n1, i1),
+        (cross_q_w, norm1_gain, self_out_w),
+        [(width, F32), (width, BF), (width, BF), (8, width, F32)],
+        flops=4 * tokens * width * width, after=sent_a + sent_b,
+    )
+    dckv = jnp.concatenate(dck + dcv, 1)
+    enc_grad = dot(dckv, cross_kv_w, NT)
+    got_enc = send_back(enc_grad)
+    rc = Reduction(
+        [dot(h1b, x, TN).astype(BF) for x in dcq]
+        + [dot(flat_enc, x, TN).astype(BF) for x in dck + dcv]
+        + [dot(self_ob, dba, TN).astype(BF)],
+        Y_FIRST,
+    )
+    sent_c = rc.send()
+    ra.take()
+    sent_a = ra.send()
+    rb.take()
+    sent_b = rb.send()
+    self_parts = [self_part(0, dso, sent_a + sent_b + sent_c)]
+    for r in (ra, rb, rc):
+        r.take()
+    sent = ra.send() + rb.send() + rc.send()
+    self_parts.append(self_part(1, dso, sent)) if cuts > 1 else None
+    for index in range(2, cuts):
+        self_parts.append(self_part(index, dso, got_enc))
+    dsq, dsk, dsv, ssums = ([part[i] for part in self_parts] for i in range(4))
+    dqkv = jnp.concatenate(dsq + dsk + dsv, 1)
+    rd = Reduction([dot(flat_in, dqkv, TN).astype(BF)], X_FIRST)
+    sent_d = rd.send()
+    in_grad = dr1 + dot(dqkv, self_qkv_w, NT)
+    got_in = send_back(in_grad)
+    if swapped:
+        for r in (ra, rb, rc, rd):
+            r.take()
+        left = [ra, rb, rc, rd]
+        while left:
+            left = [r for r in left if r.steps]
+            for r in left:
+                r.send()
+            for r in left:
+                r.take()
+    layer_out = give(h3b, got_out, BF)
+    encoded_grad = give(enc_grad, got_enc, F32)
+    target_grad = give(in_grad, got_in, F32)
+    grad_a, grad_b, grad_c, grad_d = (r.result() for r in (ra, rb, rc, rd))
+
+    csums, ssums = (jnp.concatenate(x, 1) for x in (csums, ssums))
     (
         self_q_b_grad, self_v_b_grad, self_out_b_grad, norm1_gain_grad, norm1_bias_grad,
         cross_q_b_grad, cross_v_b_grad, cross_out_b_grad, norm2_gain_grad, norm2_bias_grad,
         ffn_in_b_grad, ffn_out_b_grad, norm3_gain_grad, norm3_bias_grad,
     ) = reduce_vectors(
         [
-            column_sum(dsq), column_sum(dsv), column_sum(dba), norm1_gain_grad, norm1_bias_grad,
-            column_sum(dcq), column_sum(dcv), column_sum(dbc), norm2_gain_grad, norm2_bias_grad,
-            column_sum(dpre), column_sum(dbf), norm3_gain_grad, norm3_bias_grad,
+            ssums[0], ssums[1], low_sums[2], low_sums[0], low_sums[1],
+            csums[0], csums[1], mid_sums[5], mid_sums[3], mid_sums[4],
+            hid_sums[0], mid_sums[2], mid_sums[0], mid_sums[1],
         ]
     )
     return (
         layer_out, target_grad, encoded_grad,
-        self_grads[:, width:], self_q_b_grad, self_v_b_grad,
-        self_grads[:, :width], self_out_b_grad, norm1_gain_grad, norm1_bias_grad,
-        cross_grads[:, width : 2 * width], cross_q_b_grad,
-        cross_grads[:, 2 * width :], cross_v_b_grad,
-        cross_grads[:, :width], cross_out_b_grad, norm2_gain_grad, norm2_bias_grad,
-        ffn_in_w_grad, ffn_in_b_grad, ffn_out_w_grad, ffn_out_b_grad,
+        grad_d, self_q_b_grad, self_v_b_grad,
+        grad_c[:, 3 * width :], self_out_b_grad, norm1_gain_grad, norm1_bias_grad,
+        grad_c[:, :width], cross_q_b_grad,
+        grad_c[:, width : 3 * width], cross_v_b_grad,
+        grad_b[:, hidden:], cross_out_b_grad, norm2_gain_grad, norm2_bias_grad,
+        grad_b[:, :hidden], ffn_in_b_grad, grad_a, ffn_out_b_grad,
         norm3_gain_grad, norm3_bias_grad,
     )
 

time: 744 us -> 570 us (0.77)
  waiting for transfers between devices: 272 us -> 125 us
  matrix products: 149 us -> 63.3 us
  Pallas kernels: 107 us -> 172 us
  other arithmetic: 70.7 us -> 48.3 us
  local copies, waits for them, and re-layouts: 96.3 us -> 113 us
    ppermute x40 -> x44, waiting for transfers between devices: 272 us -> 125 us  [partner(): return lax.ppermute(x, axis, [(i, i ^ bit) for i in range(count)])]
    dot_general x21 -> x18, matrix products: 149 us -> 63.3 us  [dot(): return lax.dot_general(a, b, dims, preferred_element_type=F32)]
    pallas_call x4 -> x11, Pallas kernels: 107 us -> 172 us  [the longest x6 69.1 us: attend_back(): pl.pallas_call(skip_refs(kernel, 9, len(after)), grid_spec=pltpu.Prefetch...]
    reduce_sum x11 -> x0, other arithmetic: 17.1 us -> none  [the longest x7 12.3 us: column_sum(): return jnp.sum(x.astype(F32), 0)]
    unnamed x212 -> x193, local copies, waits for them, and re-layouts: 41.4 us -> 55.6 us
    dynamic_slice x14 -> x0, local copies, waits for them, and re-layouts: 9.96 us -> none  [the longest x12 5.38 us: halve(): sent = lax.dynamic_slice_in_dim(x, (1 - index) * half, half, 0)]
    another operation x0 -> x14, local copies, waits for them, and re-layouts: none -> 9.23 us  [reduce_vectors(): x = jnp.concatenate([v.reshape(wide, -1) for v in vectors], 1)]
    squeeze x0 -> x16, local copies, waits for them, and re-layouts: none -> 9.02 us  [pick(): return lax.dynamic_index_in_dim(x, index, axis, keepdims=False)]
  transfers between devices with their start and end apart: 40 -> 44, of which waited for: 16 -> 18; matrix products, arithmetic and copies ran while one was open for 31% -> 35% of each run, Pallas kernels for 9% -> 23%
where the time goes in v2:
time: 570 us; the launch traced here: 560 us
  Pallas kernels  172 us (30%)
  waiting for transfers between devices  125 us (22%)
  local copies, waits for them, and re-layouts  113 us (20%)
  matrix products  63.3 us (11%)
  other arithmetic  48.3 us (8%)
  starting transfers between devices  36.1 us (6%)
    ppermute x44, waiting for transfers between devices, partner(): return lax.ppermute(x, axis, [(i, i ^ bit) for i in range(count)])  125 us
    pallas_call x6, Pallas kernels, attend_back(): pl.pallas_call(skip_refs(kernel, 9, len(after)), grid_spec=pltpu.Prefetch...  69.1 us
    dot_general x18, matrix products, dot(): return lax.dot_general(a, b, dims, preferred_element_type=F32)  63.3 us
    pallas_call x3, Pallas kernels, token_call(): pl.pallas_call(run, grid=(tokens // block,), in_specs=in_specs, out_specs...  60.5 us
    unnamed x193, local copies, waits for them, and re-layouts  55.6 us
    pallas_call x2, Pallas kernels, attend(): pl.pallas_call(skip_refs(kernel, 6, len(after)), grid_spec=pltpu.Prefetch...  42.1 us
    ppermute x44, starting transfers between devices, partner(): return lax.ppermute(x, axis, [(i, i ^ bit) for i in range(count)])  36.1 us
    add x16, other arithmetic, take(): self.acc = [kept + self.got]  14 us
  transfers between devices with their start and end apart: 44, of which 18 were waited for; matrix products, arithmetic and copies ran while one was open for 35% of the time, Pallas kernels for 23%

profile of v2, /device:TPU:0, one launch (start us, length us, event | category | flops | bytes accessed | tf_op | source)
XLA Modules:
  0.0 559.7 jit_solution(14247307574028021782)
XLA Ops:
  0.7 2.8 dynamic-slice_bitcast_fusion.13
  3.5 2.9 collective-permute-start
  8.3 2.0 collective-permute-start.2
  29.0 7.4 %fusion.refs_1_.refs_2_.refs_3_ = bf16[1,1024,2304]{2,1,0:T(8,128)(2,1)} fusion(bf16[768,2304]{1,0:T(8,128)(2,1)S(1)} %copy-done, f32[2304]{0:T(1024)} %constant.246.clone.1, f32[2304]{0:T(1024)S(1)} %pad_maximum_fusion.19, bf16[512,768]{1,0:T(8,128)(2,1)} %collective-permute-done, bf16[512,768]{1,0:T(8,128)(2,1)} %get-tuple-element.153), kind=kOutput, calls=%fused_computation.5 | convolution fusion | flops 3634102272 | bytes 9848832 | tf_op jit(solution)/shard_map/dot_general | solution.py:23
  36.4 19.8 %shard_map.424 = (bf16[1,1024,768]{2,1,0:T(8,128)(2,1)S(1)}, f32[1,1024,128]{2,1,0:T(8,128)S(1)}) custom-call(s32[1]{0:T(128)} %bitcast.refs_0_, bf16[1,1024,2304]{2,1,0:T(8,128)(2,1)} %fusion.refs_1_.refs_2_.refs_3_, bf16[1,1024,2304]{2,1,0:T(8,128)(2,1)} %fusion.refs_1_.refs_2_.refs_3_, bf16[1,1024,2304]{2,1,0:T(8,128)(2,1)} %fusion.refs_1_.refs_2_.refs_3_, ...), custom_call_target="tpu_custom_call" | custom-call | flops 20132659200 | bytes 6291456 | tf_op jit(solution)/shard_map/pallas_call | solution.py:217
  56.3 3.0 pad_maximum_fusion.7.refs_1_
  59.3 2.4 pad_maximum_fusion.8.refs_8_
  61.7 8.3 %shard_map.425 = (f32[1024,768]{1,0:T(8,128)}, f32[1024,128]{1,0:T(8,128)}, bf16[1024,768]{1,0:T(8,128)(2,1)}, bf16[1024,768]{1,0:T(8,128)(2,1)}) custom-call(bf16[1024,768]{1,0:T(8,128)(2,1)} %bitcast.376, bf16[1024,768]{1,0:T(8,128)(2,1)} %pad_maximum_fusion.7.refs_1_, bf16[768,768]{1,0:T(8,128)(2,1)} %refs_8_.1, f32[1,768]{1,0:T(1,128)} %reshape.455.refs_3_, ...), custom_call_target="tpu_custom_call" | custom-call | flops 2415919104 | bytes 12333056 | tf_op jit(solution)/shard_map/pallas_call | solution.py:405
  70.0 5.2 fusion.1.refs_2_.refs_3_
  75.2 22.3 %shard_map.426 = (bf16[1,1024,768]{2,1,0:T(8,128)(2,1)S(1)}, f32[1,1024,128]{2,1,0:T(8,128)S(1)}) custom-call(s32[1]{0:T(128)} %bitcast.refs_0_, bf16[1,1024,768]{2,1,0:T(8,128)(2,1)S(1)} %bitcast.377, bf16[1,1024,1536]{2,1,0:T(8,128)(2,1)} %fusion.1.refs_2_.refs_3_, bf16[1,1024,1536]{2,1,0:T(8,128)(2,1)} %fusion.1.refs_2_.refs_3_, ...), custom_call_target="tpu_custom_call" | custom-call | flops 20132659200 | bytes 6291456 | tf_op jit(solution)/shard_map/pallas_call | solution.py:217
  99.5 2.4 pad_maximum_fusion.9.refs_2_
  101.9 42.9 %shard_map.427 = (bf16[1024,768]{1,0:T(8,128)(2,1)}, bf16[1024,3072]{1,0:T(8,128)(2,1)}, bf16[1024,768]{1,0:T(8,128)(2,1)}, bf16[1024,768]{1,0:T(8,128)(2,1)}, b...) custom-call(bf16[1024,768]{1,0:T(8,128)(2,1)} %bitcast.381, ...), custom_call_target="tpu_custom_call" | custom-call | flops 21743271936 | bytes 40660992 | tf_op jit(solution)/shard_map/pallas_call | solution.py:405
  144.8 2.2 slice.120
  147.0 2.0 collective-permute-start.4
  149.1 8.0 %convolution_convert_fusion.1 = bf16[3072,768]{1,0:T(8,128)(2,1)S(1)} fusion(bf16[1024,3072]{1,0:T(8,128)(2,1)} %get-tuple-element.77, bf16[1024,768]{1,0:T(8,128)(2,1)} %get-tuple-element.78), kind=kOutput, calls=%fused_computation.3 | convolution fusion | flops 4834197504 | bytes 12582912 | tf_op jit(solution)/shard_map/dot_general | solution.py:23
  162.8 5.4 convolution_convert_fusion
  183.5 13.4 %shard_map.430 = (bf16[1,1024,256]{2,1,0:T(8,128)(2,1)S(1)}, bf16[1,1024,256]{2,1,0:T(8,128)(2,1)S(1)}, bf16[1,1024,256]{2,1,0:T(8,128)(2,1)S(1)}, f32[1,8,256]{2,1,0:T(8,128)S(1)}) custom-call(s32[1]{0:T(128)} %bitcast.refs_0_, bf16[1,1024,768]{2,1,0:T(8,128)(2,1)S(1)} %bitcast.378, bf16[1,1024,1536]{2,1,0:T(8,128)(2,1)} %fusion.1.refs_2_.refs_3_, ...), custom_call_target="tpu_custom_call" | custom-call | flops 10905190400 | bytes 4194304 | tf_op jit(solution)/shard_map/pallas_call | solution.py:247
  196.9 2.0 convolution_convert_fusion.8
  199.0 2.7 convolution_convert_fusion.5
  203.0 1.9 bitcast_add_fusion
  205.1 13.1 %shard_map.428 = (bf16[1,1024,256]{2,1,0:T(8,128)(2,1)S(1)}, bf16[1,1024,256]{2,1,0:T(8,128)(2,1)S(1)}, bf16[1,1024,256]{2,1,0:T(8,128)(2,1)S(1)}, f32[1,8,256]{2,1,0:T(8,128)S(1)}) custom-call(s32[1]{0:T(128)} %bitcast.refs_0_, bf16[1,1024,768]{2,1,0:T(8,128)(2,1)S(1)} %bitcast.379, bf16[1,1024,1536]{2,1,0:T(8,128)(2,1)} %fusion.1.refs_2_.refs_3_, ...), custom_call_target="tpu_custom_call" | custom-call | flops 10905190400 | bytes 4194304 | tf_op jit(solution)/shard_map/pallas_call | solution.py:247
  220.7 2.5 convolution_convert_fusion.10
  223.2 2.7 convolution_convert_fusion.7
  225.9 2.6 maximum_add_fusion
  231.4 13.5 %shard_map.429 = (bf16[1,1024,256]{2,1,0:T(8,128)(2,1)S(1)}, bf16[1,1024,256]{2,1,0:T(8,128)(2,1)S(1)}, bf16[1,1024,256]{2,1,0:T(8,128)(2,1)S(1)}, f32[1,8,256]{2,1,0:T(8,128)S(1)}) custom-call(s32[1]{0:T(128)} %bitcast.refs_0_, bf16[1,1024,768]{2,1,0:T(8,128)(2,1)S(1)} %bitcast.380, bf16[1,1024,1536]{2,1,0:T(8,128)(2,1)} %fusion.1.refs_2_.refs_3_, ...), custom_call_target="tpu_custom_call" | custom-call | flops 10905190400 | bytes 4194304 | tf_op jit(solution)/shard_map/pallas_call | solution.py:247
  244.9 2.1 collective-permute-start.8
  251.1 4.6 fusion.23
  263.2 2.5 convolution_convert_fusion.6
  270.1 2.0 bitcast_dynamic-update-slice_fusion.19
  275.8 16.9 %collective-permute-done.9 = bf16[2,192,768]{2,1,0:T(8,128)(2,1)} collective-permute-done((bf16[2,192,768]{2,1,0:T(8,128)(2,1)}, bf16[2,192,768]{2,1,0:T(8,128)(2,1)}, u32[]{:S(2)}, u32[]{:S(2)}) %collective-permute-start.9) | collective-permute-done | bytes 589856 | tf_op jit(solution)/shard_map/ppermute | solution.py:419
  297.1 1.9 pad_maximum_fusion.1
  299.0 3.6 collective-permute-done.11
  303.3 2.5 collective-permute-start.40
  309.8 9.3 %shard_map.431 = (f32[1024,768]{1,0:T(8,128)}, bf16[1024,768]{1,0:T(8,128)(2,1)}, bf16[1024,768]{1,0:T(8,128)(2,1)}, f32[8,768]{1,0:T(8,128)}) custom-call(bf16[1024,256]{1,0:T(8,128)(2,1)} %bitcast.365, bf16[1024,256]{1,0:T(8,128)(2,1)} %bitcast.366, bf16[1024,256]{1,0:T(8,128)(2,1)} %bitcast.364, f32[1024,768]{1,0:T(8,128)} %get-tuple-element.85.refs_3_, ...), custom_call_target="tpu_custom_call" | custom-call | flops 2415919104 | bytes 17067008 | tf_op jit(solution)/shard_map/pallas_call | solution.py:405
  319.1 2.9 convolution_convert_fusion.3
  324.0 9.6 %shard_map.434 = (bf16[1,1024,256]{2,1,0:T(8,128)(2,1)S(1)}, bf16[1,1024,256]{2,1,0:T(8,128)(2,1)S(1)}, bf16[1,1024,256]{2,1,0:T(8,128)(2,1)S(1)}, f32[1,8,256]{2,1,0:T(8,128)S(1)}) custom-call(s32[1]{0:T(128)} %bitcast.refs_0_, bf16[1,1024,2304]{2,1,0:T(8,128)(2,1)} %fusion.refs_1_.refs_2_.refs_3_, bf16[1,1024,2304]{2,1,0:T(8,128)(2,1)} %fusion.refs_1_.refs_2_.refs_3_, ...), custom_call_target="tpu_custom_call" | custom-call | flops 10905190400 | bytes 4194304 | tf_op jit(solution)/shard_map/pallas_call | solution.py:247
  344.8 6.3 %collective-permute-done.41 = bf16[192,768]{1,0:T(8,128)(2,1)S(1)} collective-permute-done((bf16[192,768]{1,0:T(8,128)(2,1)S(1)}, bf16[192,768]{1,0:T(8,128)(2,1)S(1)}, u32[]{:S(2)}, u32[]{:S(2)}) %collective-permute-start.41) | collective-permute-done | bytes 294944 | tf_op jit(solution)/shard_map/ppermute | solution.py:419
  352.8 4.9 collective-permute-done.12
  358.2 9.9 %shard_map.432 = (bf16[1,1024,256]{2,1,0:T(8,128)(2,1)S(1)}, bf16[1,1024,256]{2,1,0:T(8,128)(2,1)S(1)}, bf16[1,1024,256]{2,1,0:T(8,128)(2,1)S(1)}, f32[1,8,256]{2,1,0:T(8,128)S(1)}) custom-call(s32[1]{0:T(128)} %bitcast.refs_0_, bf16[1,1024,2304]{2,1,0:T(8,128)(2,1)} %fusion.refs_1_.refs_2_.refs_3_, bf16[1,1024,2304]{2,1,0:T(8,128)(2,1)} %fusion.refs_1_.refs_2_.refs_3_, ...), custom_call_target="tpu_custom_call" | custom-call | flops 10905190400 | bytes 4194304 | tf_op jit(solution)/shard_map/pallas_call | solution.py:247
  369.1 7.0 %collective-permute-done.36 = bf16[48,3840]{1,0:T(8,128)(2,1)S(1)} collective-permute-done((bf16[48,3840]{1,0:T(8,128)(2,1)S(1)}, bf16[48,3840]{1,0:T(8,128)(2,1)S(1)}, u32[]{:S(2)}, u32[]{:S(2)}) %collective-permute-start.36) | collective-permute-done | bytes 368672 | tf_op jit(solution)/shard_map/ppermute | solution.py:419
  376.5 9.1 %collective-permute-done.37 = bf16[48,3840]{1,0:T(8,128)(2,1)S(1)} collective-permute-done((bf16[48,3840]{1,0:T(8,128)(2,1)S(1)}, bf16[48,3840]{1,0:T(8,128)(2,1)S(1)}, u32[]{:S(2)}, u32[]{:S(2)}) %collective-permute-start.37) | collective-permute-done | bytes 368672 | tf_op jit(solution)/shard_map/ppermute | solution.py:419
  388.6 2.7 bitcast_convert_fusion.1
  391.3 2.6 add.259
  396.4 9.6 %shard_map.433 = (bf16[1,1024,256]{2,1,0:T(8,128)(2,1)S(1)}, bf16[1,1024,256]{2,1,0:T(8,128)(2,1)S(1)}, bf16[1,1024,256]{2,1,0:T(8,128)(2,1)S(1)}, f32[1,8,256]{2,1,0:T(8,128)S(1)}) custom-call(s32[1]{0:T(128)} %bitcast.refs_0_, bf16[1,1024,2304]{2,1,0:T(8,128)(2,1)} %fusion.refs_1_.refs_2_.refs_3_, bf16[1,1024,2304]{2,1,0:T(8,128)(2,1)} %fusion.refs_1_.refs_2_.refs_3_, ...), custom_call_target="tpu_custom_call" | custom-call | flops 10905190400 | bytes 4194304 | tf_op jit(solution)/shard_map/pallas_call | solution.py:247
  425.3 1.9 bitcast_dynamic-update-slice_fusion.9
  427.3 2.0 bitcast_dynamic-update-slice_fusion.8
  436.3 5.7 %fusion.24 = f32[1024,768]{1,0:T(8,128)S(1)} fusion(bf16[1024,2304]{1,0:T(8,128)(2,1)} %bitcast_dynamic-update-slice_fusion.2, bf16[768,2304]{1,0:T(8,128)(2,1)S(1)} %copy-done), kind=kOutput, calls=%fused_computation.212 | convolution fusion | flops 3623878656 | bytes 11403264 | tf_op jit(solution)/shard_map/dot_general | solution.py:23
  444.6 5.8 %convolution_convert_fusion.2 = bf16[768,2304]{1,0:T(8,128)(2,1)S(1)} fusion(bf16[1024,2304]{1,0:T(8,128)(2,1)S(1)} %copy-done.65, bf16[512,768]{1,0:T(8,128)(2,1)} %collective-permute-done, bf16[512,768]{1,0:T(8,128)(2,1)S(1)} %copy-done.52), kind=kOutput, calls=%fused_computation.4 | convolution fusion | flops 3628793856 | bytes 9830400 | tf_op jit(solution)/shard_map/dot_general | solution.py:23
  452.2 4.0 collective-permute-done.27
  458.4 4.5 collective-permute-done.28
  464.4 1.9 pad_maximum_fusion
  469.6 13.8 %collective-permute-done.30 = bf16[2,48,3072]{2,1,0:T(8,128)(2,1)S(1)} collective-permute-done((bf16[2,48,3072]{2,1,0:T(8,128)(2,1)S(1)}, bf16[2,48,3072]{2,1,0:T(8,128)(2,1)S(1)}, u32[]{:S(2)}, u32[]{:S(2)}) %collective-permute-start.30) | collective-permute-done | bytes 589856 | tf_op jit(solution)/shard_map/ppermute | solution.py:419
  484.7 6.3 %collective-permute-done.31 = bf16[48,3072]{1,0:T(8,128)(2,1)S(1)} collective-permute-done((bf16[48,3072]{1,0:T(8,128)(2,1)S(1)}, bf16[48,3072]{1,0:T(8,128)(2,1)S(1)}, u32[]{:S(2)}, u32[]{:S(2)}) %collective-permute-start.31) | collective-permute-done | bytes 294944 | tf_op jit(solution)/shard_map/ppermute | solution.py:419
  492.5 12.0 %collective-permute-done.32 = bf16[48,3072]{1,0:T(8,128)(2,1)S(1)} collective-permute-done((bf16[48,3072]{1,0:T(8,128)(2,1)S(1)}, bf16[48,3072]{1,0:T(8,128)(2,1)S(1)}, u32[]{:S(2)}, u32[]{:S(2)}) %collective-permute-start.32) | collective-permute-done | bytes 294944 | tf_op jit(solution)/shard_map/ppermute | solution.py:419
  505.1 8.3 %collective-permute-done.33 = bf16[48,3072]{1,0:T(8,128)(2,1)S(1)} collective-permute-done((bf16[48,3072]{1,0:T(8,128)(2,1)S(1)}, bf16[48,3072]{1,0:T(8,128)(2,1)S(1)}, u32[]{:S(2)}, u32[]{:S(2)}) %collective-permute-start.33) | collective-permute-done | bytes 294944 | tf_op jit(solution)/shard_map/ppermute | solution.py:419
  513.5 3.4 collective-permute-done.18
  519.1 4.2 collective-permute-done.19
  523.3 2.3 collective-permute-start.20
  525.7 6.8 %collective-permute-done.34 = bf16[96,3072]{1,0:T(8,128)(2,1)S(1)} collective-permute-done((bf16[96,3072]{1,0:T(8,128)(2,1)S(1)}, bf16[96,3072]{1,0:T(8,128)(2,1)S(1)}, u32[]{:S(2)}, u32[]{:S(2)}) %collective-permute-start.34) | collective-permute-done | bytes 589856 | tf_op jit(solution)/shard_map/ppermute | solution.py:419
  532.6 1.9 collective-permute-done.20
  534.8 6.6 %collective-permute-done.21 = bf16[48,2304]{1,0:T(8,128)(2,1)S(1)} collective-permute-done((bf16[48,2304]{1,0:T(8,128)(2,1)S(1)}, bf16[48,2304]{1,0:T(8,128)(2,1)S(1)}, u32[]{:S(2)}, u32[]{:S(2)}) %collective-permute-start.21) | collective-permute-done | bytes 221216 | tf_op jit(solution)/shard_map/ppermute | solution.py:419
  543.7 2.8 slice.176
  546.5 5.6 collective-permute-done.22
  557.1 2.1 bitcast_convert_fusion.3
  (382 shorter events, 152.1 us)
Async XLA Ops:
  0.7 28.3 %copy-start = (bf16[768,2304]{1,0:T(8,128)(2,1)S(1)}, bf16[768,2304]{1,0:T(8,128)(2,1)}, u32[]{:S(2)}) copy-start(bf16[768,2304]{1,0:T(8,128)(2,1)} %param.29) | copy-start | bytes 10616836
  3.5 25.5 %collective-permute-start = (bf16[512,768]{1,0:T(8,128)(2,1)}, bf16[512,768]{1,0:T(8,128)(2,1)}, u32[]{:S(2)}, u32[]{:S(2)}) collective-permute-start(bf16[512,768]{1,0:T(8,128)(2,1)} %get-tuple-element.154), channel_id=1, source_target_pairs={{0,16},{16,0},{1,17},{17,1},{2,18},{18,2},{3,19},{19,3},{4,20},{20... | collective-permute-start | bytes 2359304 | tf_op jit(solution)/shard_map/ppermute | solution.py:419
  7.0 20.3 %collective-permute-start.1 = (s32[512]{0:T(512)}, s32[512]{0:T(512)}, u32[]{:S(2)}, u32[]{:S(2)}) collective-permute-start(s32[512]{0:T(512)} %bitcast.5), channel_id=1, source_target_pairs={{0,16},{16,0},{1,17},{17,1},{2,18},{18,2},{3,19},{19,3},{4,20},{20... | collective-permute-start | bytes 6152 | tf_op jit(solution)/shard_map/ppermute | solution.py:419
  8.3 51.0 %collective-permute-start.2 = (bf16[512,768]{1,0:T(8,128)(2,1)}, bf16[512,768]{1,0:T(8,128)(2,1)}, u32[]{:S(2)}, u32[]{:S(2)}) collective-permute-start(bf16[512,768]{1,0:T(8,128)(2,1)} %get-tuple-element.152), channel_id=1, source_target_pairs={{0,16},{16,0},{1,17},{17,1},{2,18},{18,2},{3,19},{19,3},{4,20},{20... | collective-permute-start | bytes 2359304 | tf_op jit(solution)/shard_map/ppermute | solution.py:419
  11.5 88.0 %collective-permute-start.3 = (bf16[512,768]{1,0:T(8,128)(2,1)}, bf16[512,768]{1,0:T(8,128)(2,1)}, u32[]{:S(2)}, u32[]{:S(2)}) collective-permute-start(bf16[512,768]{1,0:T(8,128)(2,1)} %get-tuple-element.150), channel_id=1, source_target_pairs={{0,16},{16,0},{1,17},{17,1},{2,18},{18,2},{3,19},{19,3},{4,20},{20... | collective-permute-start | bytes 2359304 | tf_op jit(solution)/shard_map/ppermute | solution.py:419
  29.0 46.3 %copy-start.20 = (bf16[1,1024,128]{2,1,0:T(8,128)(2,1)}, bf16[1,1024,128]{2,1,0:T(8,128)(2,1)S(1)}, u32[]{:S(2)}) copy-start(bf16[1,1024,128]{2,1,0:T(8,128)(2,1)S(1)} %get-tuple-element.206.refs_5_.refs_7_) | copy-start | bytes 786436
  29.0 46.2 %copy-start.24 = (bf16[1,1024,128]{2,1,0:T(8,128)(2,1)}, bf16[1,1024,128]{2,1,0:T(8,128)(2,1)S(1)}, u32[]{:S(2)}) copy-start(bf16[1,1024,128]{2,1,0:T(8,128)(2,1)S(1)} %get-tuple-element.207.refs_4_.refs_6_) | copy-start | bytes 786436
  36.4 19.8 %copy-start.51 = (bf16[512,768]{1,0:T(8,128)(2,1)S(1)}, bf16[512,768]{1,0:T(8,128)(2,1)}, u32[]{:S(2)}) copy-start(bf16[512,768]{1,0:T(8,128)(2,1)} %get-tuple-element.153) | copy-start | bytes 2359300
  75.2 24.3 %copy-start.55 = (bf16[512,768]{1,0:T(8,128)(2,1)S(1)}, bf16[512,768]{1,0:T(8,128)(2,1)}, u32[]{:S(2)}) copy-start(bf16[512,768]{1,0:T(8,128)(2,1)} %get-tuple-element.149) | copy-start | bytes 2359300
  144.8 17.9 %slice-start.2 = ((s8[6291456]{0:T(1024)(128)(4,1)}), s8[4194304]{0:T(1024)(128)(4,1)S(1)}, s32[]{:S(2)}) async-start(s8[6291456]{0:T(1024)(128)(4,1)} %bitcast.412), calls=%async_computation.2 | async-start | bytes 8388608
  147.0 32.8 %collective-permute-start.4 = (bf16[512,768]{1,0:T(8,128)(2,1)}, bf16[512,768]{1,0:T(8,128)(2,1)}, u32[]{:S(2)}, u32[]{:S(2)}) collective-permute-start(bf16[512,768]{1,0:T(8,128)(2,1)} %slice.120), channel_id=1, source_target_pairs={{0,16},{16,0},{1,17},{17,1},{2,18},{18,2},{3,19},{19,3},{4,20},{20... | collective-permute-start | bytes 2359304 | tf_op jit(solution)/shard_map/ppermute | solution.py:419
  149.1 13.7 %slice-start.3 = ((s8[6291456]{0:T(1024)(128)(4,1)}), s8[2097152]{0:T(1024)(128)(4,1)S(1)}, s32[]{:S(2)}) async-start(s8[6291456]{0:T(1024)(128)(4,1)} %bitcast.412), calls=%async_computation.3 | async-start | bytes 4194304
  160.6 42.5 %collective-permute-start.5 = (bf16[2,2,2,192,768]{4,3,2,1,0:T(8,128)(2,1)}, bf16[2,2,2,192,768]{4,3,2,1,0:T(8,128)(2,1)}, u32[]{:S(2)}, u32[]{:S(2)}) collective-permute-start(bf16[2,2,2,192,768]{4,3,2,1,0:T(8,128)(2,1)} %dynamic-slice_bitcast_fusion.2), channel_id=1, source_target_pairs={{0,1},{1,0},{2,3},{3,2},{4,5},{5,4},{6,7},{7,6},{8,9},{9,8},{10,11... | collective-permute-start | bytes 7077896 | tf_op jit(solution)/shard_map/ppermute | solution.py:419
  172.7 53.2 %collective-permute-start.6 = (bf16[2,2,2,48,3840]{4,3,2,1,0:T(8,128)(2,1)}, bf16[2,2,2,48,3840]{4,3,2,1,0:T(8,128)(2,1)}, u32[]{:S(2)}, u32[]{:S(2)}) collective-permute-start(bf16[2,2,2,48,3840]{4,3,2,1,0:T(8,128)(2,1)} %pad_maximum_fusion.2.refs_10_), channel_id=1, source_target_pairs={{0,1},{1,0},{2,3},{3,2},{4,5},{5,4},{6,7},{7,6},{8,9},{9,8},{10,11... | collective-permute-start | bytes 8847368 | tf_op jit(solution)/shard_map/ppermute | solution.py:419
  183.5 13.4 %copy-start.54 = (bf16[512,768]{1,0:T(8,128)(2,1)S(1)}, bf16[512,768]{1,0:T(8,128)(2,1)}, u32[]{:S(2)}) copy-start(bf16[512,768]{1,0:T(8,128)(2,1)} %get-tuple-element.151) | copy-start | bytes 2359300
  205.0 60.7 %collective-permute-start.7 = (bf16[2,2,192,768]{3,2,1,0:T(8,128)(2,1)S(1)}, bf16[2,2,192,768]{3,2,1,0:T(8,128)(2,1)S(1)}, u32[]{:S(2)}, u32[]{:S(2)}) collective-permute-start(bf16[2,2,192,768]{3,2,1,0:T(8,128)(2,1)S(1)} %dynamic-slice_bitcast_fusion.6.refs_9_), channel_id=1, source_target_pairs={{0,16},{16,0},{1,17},{17,1},{2,18},{18,2},{3,19},{19,3},{4,20},{20... | collective-permute-start | bytes 3538952 | tf_op jit(solution)/shard_map/ppermute | solution.py:419
  244.9 13.5 %copy-start.17 = (bf16[1,1024,256]{2,1,0:T(8,128)(2,1)}, bf16[1,1024,256]{2,1,0:T(8,128)(2,1)S(1)}, u32[]{:S(2)}) copy-start(bf16[1,1024,256]{2,1,0:T(8,128)(2,1)S(1)} %get-tuple-element.83) | copy-start | bytes 1572868
  244.9 60.8 %collective-permute-start.8 = (bf16[2,2,48,3840]{3,2,1,0:T(8,128)(2,1)}, bf16[2,2,48,3840]{3,2,1,0:T(8,128)(2,1)}, u32[]{:S(2)}, u32[]{:S(2)}) collective-permute-start(bf16[2,2,48,3840]{3,2,1,0:T(8,128)(2,1)} %dynamic-slice_bitcast_fusion.4.refs_9_), channel_id=1, source_target_pairs={{0,2},{2,0},{1,3},{3,1},{4,6},{6,4},{5,7},{7,5},{8,10},{10,8},{9,1... | collective-permute-start | bytes 4423688 | tf_op jit(solution)/shard_map/ppermute | solution.py:419
  256.9 38.8 %collective-permute-start.14 = (bf16[512,768]{1,0:T(8,128)(2,1)}, bf16[512,768]{1,0:T(8,128)(2,1)}, u32[]{:S(2)}, u32[]{:S(2)}) collective-permute-start(bf16[512,768]{1,0:T(8,128)(2,1)} %slice.200), channel_id=1, source_target_pairs={{0,16},{16,0},{1,17},{17,1},{2,18},{18,2},{3,19},{19,3},{4,20},{20... | collective-permute-start | bytes 2359304 | tf_op jit(solution)/shard_map/ppermute | solution.py:419
  266.8 25.9 %collective-permute-start.9 = (bf16[2,192,768]{2,1,0:T(8,128)(2,1)}, bf16[2,192,768]{2,1,0:T(8,128)(2,1)}, u32[]{:S(2)}, u32[]{:S(2)}) collective-permute-start(bf16[2,192,768]{2,1,0:T(8,128)(2,1)} %dynamic-slice_bitcast_fusion.16.refs_9_), channel_id=1, source_target_pairs={{0,2},{2,0},{1,3},{3,1},{4,6},{6,4},{5,7},{7,5},{8,10},{10,8},{9,1... | collective-permute-start | bytes 1769480 | tf_op jit(solution)/shard_map/ppermute | solution.py:419
  270.1 22.5 %copy-start.49 = (bf16[2,2,192,768]{3,2,1,0:T(8,128)(2,1)S(1)}, bf16[2,2,192,768]{3,2,1,0:T(8,128)(2,1)}, u32[]{:S(2)}) copy-start(bf16[2,2,192,768]{3,2,1,0:T(8,128)(2,1)} %copy-done.48) | copy-start | bytes 3538948
  270.1 25.5 %copy-start.59 = (f32[1024,768]{1,0:T(8,128)S(1)}, f32[1024,768]{1,0:T(8,128)}, u32[]{:S(2)}) copy-start(f32[1024,768]{1,0:T(8,128)} %copy-done.58) | copy-start | bytes 9437188
  293.8 8.7 %collective-permute-start.11 = (bf16[192,768]{1,0:T(8,128)(2,1)S(1)}, bf16[192,768]{1,0:T(8,128)(2,1)S(1)}, u32[]{:S(2)}, u32[]{:S(2)}) collective-permute-start(bf16[192,768]{1,0:T(8,128)(2,1)S(1)} %dynamic-slice_bitcast_fusion.22.refs_9_), channel_id=1, source_target_pairs={{0,4},{4,0},{8,12},{12,8},{1,5},{5,1},{9,13},{13,9},{2,6},{6,2},{1... | collective-permute-start | bytes 884744 | tf_op jit(solution)/shard_map/ppermute | solution.py:419
  303.3 36.7 %collective-permute-start.40 = (bf16[192,768]{1,0:T(8,128)(2,1)}, bf16[192,768]{1,0:T(8,128)(2,1)}, u32[]{:S(2)}, u32[]{:S(2)}) collective-permute-start(bf16[192,768]{1,0:T(8,128)(2,1)} %bitcast_add_fusion.12.refs_9_), channel_id=1, source_target_pairs={{0,8},{4,12},{8,0},{12,4},{1,9},{5,13},{9,1},{13,5},{2,10},{6,14},... | collective-permute-start | bytes 884744 | tf_op jit(solution)/shard_map/ppermute | solution.py:419
  308.3 34.5 %collective-permute-start.10 = (bf16[2,48,3840]{2,1,0:T(8,128)(2,1)}, bf16[2,48,3840]{2,1,0:T(8,128)(2,1)}, u32[]{:S(2)}, u32[]{:S(2)}) collective-permute-start(bf16[2,48,3840]{2,1,0:T(8,128)(2,1)} %dynamic-slice_bitcast_fusion.14.refs_10_), channel_id=1, source_target_pairs={{0,16},{16,0},{1,17},{17,1},{2,18},{18,2},{3,19},{19,3},{4,20},{20... | collective-permute-start | bytes 2211848 | tf_op jit(solution)/shard_map/ppermute | solution.py:419
  309.8 9.3 %copy-start.31 = (bf16[1,1024,768]{2,1,0:T(8,128)(2,1)S(1)}, bf16[1,1024,768]{2,1,0:T(8,128)(2,1)}, u32[]{:S(2)}) copy-start(bf16[1,1024,768]{2,1,0:T(8,128)(2,1)} %copy-done.30) | copy-start | bytes 4718596
  323.2 68.1 %collective-permute-start.13 = (bf16[2,2,2,48,3072]{4,3,2,1,0:T(8,128)(2,1)}, bf16[2,2,2,48,3072]{4,3,2,1,0:T(8,128)(2,1)}, u32[]{:S(2)}, u32[]{:S(2)}) collective-permute-start(bf16[2,2,2,48,3072]{4,3,2,1,0:T(8,128)(2,1)} %get-tuple-element.162.refs_11_), channel_id=1, source_target_pairs={{0,1},{1,0},{2,3},{3,2},{4,5},{5,4},{6,7},{7,6},{8,9},{9,8},{10,11... | collective-permute-start | bytes 7077896 | tf_op jit(solution)/shard_map/ppermute | solution.py:419
  341.1 10.0 %collective-permute-start.41 = (bf16[192,768]{1,0:T(8,128)(2,1)S(1)}, bf16[192,768]{1,0:T(8,128)(2,1)S(1)}, u32[]{:S(2)}, u32[]{:S(2)}) collective-permute-start(bf16[192,768]{1,0:T(8,128)(2,1)S(1)} %add.276), channel_id=1, source_target_pairs={{0,4},{4,0},{8,12},{12,8},{1,5},{5,1},{9,13},{13,9},{2,6},{6,2},{1... | collective-permute-start | bytes 884744 | tf_op jit(solution)/shard_map/ppermute | solution.py:419
  344.2 14.0 %copy-start.19 = (bf16[192,768]{1,0:T(8,128)(2,1)S(1)}, bf16[192,768]{1,0:T(8,128)(2,1)}, u32[]{:S(2)}) copy-start(bf16[192,768]{1,0:T(8,128)(2,1)} %copy-done.18) | copy-start | bytes 884740
  344.2 14.0 %copy-start.23 = (bf16[1,1024,128]{2,1,0:T(8,128)(2,1)S(1)}, bf16[1,1024,128]{2,1,0:T(8,128)(2,1)}, u32[]{:S(2)}) copy-start(bf16[1,1024,128]{2,1,0:T(8,128)(2,1)} %copy-done.20) | copy-start | bytes 786436
  344.2 14.0 %copy-start.27 = (bf16[1,1024,128]{2,1,0:T(8,128)(2,1)S(1)}, bf16[1,1024,128]{2,1,0:T(8,128)(2,1)}, u32[]{:S(2)}) copy-start(bf16[1,1024,128]{2,1,0:T(8,128)(2,1)} %copy-done.24) | copy-start | bytes 786436
  344.2 14.0 %copy-start.29 = (bf16[1024,768]{1,0:T(8,128)(2,1)S(1)}, bf16[1024,768]{1,0:T(8,128)(2,1)}, u32[]{:S(2)}) copy-start(bf16[1024,768]{1,0:T(8,128)(2,1)} %get-tuple-element.88) | copy-start | bytes 4718596
  344.2 14.0 %copy-start.38 = (f32[1,1024,128]{2,1,0:T(8,128)S(1)}, f32[1,1024,128]{2,1,0:T(8,128)}, u32[]{:S(2)}) copy-start(f32[1,1024,128]{2,1,0:T(8,128)} %copy-done.36) | copy-start | bytes 1572868
  344.3 13.5 %collective-permute-start.12 = (bf16[48,3840]{1,0:T(8,128)(2,1)S(1)}, bf16[48,3840]{1,0:T(8,128)(2,1)S(1)}, u32[]{:S(2)}, u32[]{:S(2)}) collective-permute-start(bf16[48,3840]{1,0:T(8,128)(2,1)S(1)} %dynamic-slice_bitcast_fusion.20.refs_10_), channel_id=1, source_target_pairs={{0,4},{4,0},{8,12},{12,8},{1,5},{5,1},{9,13},{13,9},{2,6},{6,2},{1... | collective-permute-start | bytes 1105928 | tf_op jit(solution)/shard_map/ppermute | solution.py:419
  351.2 25.0 %collective-permute-start.42 = (bf16[384,768]{1,0:T(8,128)(2,1)S(1)}, bf16[384,768]{1,0:T(8,128)(2,1)S(1)}, u32[]{:S(2)}, u32[]{:S(2)}) collective-permute-start(bf16[384,768]{1,0:T(8,128)(2,1)S(1)} %bitcast.393), channel_id=1, source_target_pairs={{0,2},{2,0},{1,3},{3,1},{4,6},{6,4},{5,7},{7,5},{8,10},{10,8},{9,1... | collective-permute-start | bytes 1769480 | tf_op jit(solution)/shard_map/ppermute | solution.py:419
  357.8 18.2 %collective-permute-start.36 = (bf16[48,3840]{1,0:T(8,128)(2,1)S(1)}, bf16[48,3840]{1,0:T(8,128)(2,1)S(1)}, u32[]{:S(2)}, u32[]{:S(2)}) collective-permute-start(bf16[48,3840]{1,0:T(8,128)(2,1)S(1)} %bitcast_add_fusion.10.refs_10_), channel_id=1, source_target_pairs={{0,8},{4,12},{8,0},{12,4},{1,9},{5,13},{9,1},{13,5},{2,10},{6,14},... | collective-permute-start | bytes 1105928 | tf_op jit(solution)/shard_map/ppermute | solution.py:419
  376.1 9.5 %collective-permute-start.37 = (bf16[48,3840]{1,0:T(8,128)(2,1)S(1)}, bf16[48,3840]{1,0:T(8,128)(2,1)S(1)}, u32[]{:S(2)}, u32[]{:S(2)}) collective-permute-start(bf16[48,3840]{1,0:T(8,128)(2,1)S(1)} %add.275), channel_id=1, source_target_pairs={{0,4},{4,0},{8,12},{12,8},{1,5},{5,1},{9,13},{13,9},{2,6},{6,2},{1... | collective-permute-start | bytes 1105928 | tf_op jit(solution)/shard_map/ppermute | solution.py:419
  376.5 11.7 %collective-permute-start.43 = (bf16[768,768]{1,0:T(8,128)(2,1)S(1)}, bf16[768,768]{1,0:T(8,128)(2,1)S(1)}, u32[]{:S(2)}, u32[]{:S(2)}) collective-permute-start(bf16[768,768]{1,0:T(8,128)(2,1)S(1)} %bitcast.388), channel_id=1, source_target_pairs={{0,1},{1,0},{2,3},{3,2},{4,5},{5,4},{6,7},{7,6},{8,9},{9,8},{10,11... | collective-permute-start | bytes 3538952 | tf_op jit(solution)/shard_map/ppermute | solution.py:419
  386.6 70.1 %collective-permute-start.38 = (bf16[96,3840]{1,0:T(8,128)(2,1)}, bf16[96,3840]{1,0:T(8,128)(2,1)}, u32[]{:S(2)}, u32[]{:S(2)}) collective-permute-start(bf16[96,3840]{1,0:T(8,128)(2,1)} %bitcast.134), channel_id=1, source_target_pairs={{0,2},{2,0},{1,3},{3,1},{4,6},{6,4},{5,7},{7,5},{8,10},{10,8},{9,1... | collective-permute-start | bytes 2211848 | tf_op jit(solution)/shard_map/ppermute | solution.py:419
  408.4 57.8 %collective-permute-start.29 = (bf16[2,2,48,3072]{3,2,1,0:T(8,128)(2,1)}, bf16[2,2,48,3072]{3,2,1,0:T(8,128)(2,1)}, u32[]{:S(2)}, u32[]{:S(2)}) collective-permute-start(bf16[2,2,48,3072]{3,2,1,0:T(8,128)(2,1)} %dynamic-slice_bitcast_fusion.5.refs_11_), channel_id=1, source_target_pairs={{0,2},{2,0},{1,3},{3,1},{4,6},{6,4},{5,7},{7,5},{8,10},{10,8},{9,1... | collective-permute-start | bytes 3538952 | tf_op jit(solution)/shard_map/ppermute | solution.py:419
  409.5 19.7 %copy-start.9 = (bf16[1,1024,256]{2,1,0:T(8,128)(2,1)S(1)}, bf16[1,1024,256]{2,1,0:T(8,128)(2,1)}, u32[]{:S(2)}) copy-start(bf16[1,1024,256]{2,1,0:T(8,128)(2,1)} %copy-done.8) | copy-start | bytes 1572868
  409.5 20.6 %copy-start.13 = (bf16[1,1024,256]{2,1,0:T(8,128)(2,1)S(1)}, bf16[1,1024,256]{2,1,0:T(8,128)(2,1)}, u32[]{:S(2)}) copy-start(bf16[1,1024,256]{2,1,0:T(8,128)(2,1)} %copy-done.12) | copy-start | bytes 1572868
  409.5 21.5 %copy-start.4 = (bf16[1,1024,256]{2,1,0:T(8,128)(2,1)S(1)}, bf16[1,1024,256]{2,1,0:T(8,128)(2,1)}, u32[]{:S(2)}) copy-start(bf16[1,1024,256]{2,1,0:T(8,128)(2,1)} %copy-done.3) | copy-start | bytes 1572868
  425.3 9.3 %collective-permute-start.24 = (f32[2,6528]{1,0:T(2,128)}, f32[2,6528]{1,0:T(2,128)S(1)}, u32[]{:S(2)}, u32[]{:S(2)}) collective-permute-start(f32[2,6528]{1,0:T(2,128)} %constant_dynamic-update-slice_fusion), channel_id=1, source_target_pairs={{0,1},{1,0},{2,3},{3,2},{4,5},{5,4},{6,7},{7,6},{8,9},{9,8},{10,11... | collective-permute-start | bytes 156680 | tf_op jit(solution)/shard_map/ppermute | solution.py:419
  434.7 8.4 %collective-permute-start.25 = (f32[2,6528]{1,0:T(2,128)S(1)}, f32[2,6528]{1,0:T(2,128)S(1)}, u32[]{:S(2)}, u32[]{:S(2)}) collective-permute-start(f32[2,6528]{1,0:T(2,128)S(1)} %add.266), channel_id=1, source_target_pairs={{0,2},{2,0},{1,3},{3,1},{4,6},{6,4},{5,7},{7,5},{8,10},{10,8},{9,1... | collective-permute-start | bytes 156680 | tf_op jit(solution)/shard_map/ppermute | solution.py:419
  442.5 21.6 %collective-permute-start.15 = (bf16[512,768]{1,0:T(8,128)(2,1)S(1)}, bf16[512,768]{1,0:T(8,128)(2,1)S(1)}, u32[]{:S(2)}, u32[]{:S(2)}) collective-permute-start(bf16[512,768]{1,0:T(8,128)(2,1)S(1)} %slice.199), channel_id=1, source_target_pairs={{0,16},{16,0},{1,17},{17,1},{2,18},{18,2},{3,19},{19,3},{4,20},{20... | collective-permute-start | bytes 2359304 | tf_op jit(solution)/shard_map/ppermute | solution.py:419
  443.2 7.3 %collective-permute-start.26 = (f32[2,6528]{1,0:T(2,128)S(1)}, f32[2,6528]{1,0:T(2,128)S(1)}, u32[]{:S(2)}, u32[]{:S(2)}) collective-permute-start(f32[2,6528]{1,0:T(2,128)S(1)} %add.267), channel_id=1, source_target_pairs={{0,4},{4,0},{8,12},{12,8},{1,5},{5,1},{9,13},{13,9},{2,6},{6,2},{1... | collective-permute-start | bytes 156680 | tf_op jit(solution)/shard_map/ppermute | solution.py:419
  450.5 5.8 %collective-permute-start.27 = (f32[2,6528]{1,0:T(2,128)S(1)}, f32[2,6528]{1,0:T(2,128)S(1)}, u32[]{:S(2)}, u32[]{:S(2)}) collective-permute-start(f32[2,6528]{1,0:T(2,128)S(1)} %add.268), channel_id=1, source_target_pairs={{0,8},{4,12},{8,0},{12,4},{1,9},{5,13},{9,1},{13,5},{2,10},{6,14},... | collective-permute-start | bytes 156680 | tf_op jit(solution)/shard_map/ppermute | solution.py:419
  452.2 31.7 %collective-permute-start.16 = (bf16[2,2,2,48,2304]{4,3,2,1,0:T(8,128)(2,1)S(1)}, bf16[2,2,2,48,2304]{4,3,2,1,0:T(8,128)(2,1)S(1)}, u32[]{:S(2)}, u32[]{:S(2)}) collective-permute-start(bf16[2,2,2,48,2304]{4,3,2,1,0:T(8,128)(2,1)S(1)} %dynamic-slice_bitcast_fusion.3), channel_id=1, source_target_pairs={{0,1},{1,0},{2,3},{3,2},{4,5},{5,4},{6,7},{7,6},{8,9},{9,8},{10,11... | collective-permute-start | bytes 5308424 | tf_op jit(solution)/shard_map/ppermute | solution.py:419
  456.4 6.5 %collective-permute-start.28 = (f32[6528]{0:T(1024)S(1)}, f32[6528]{0:T(1024)S(1)}, u32[]{:S(2)}, u32[]{:S(2)}) collective-permute-start(f32[6528]{0:T(1024)S(1)} %get-tuple-element.116), channel_id=1, source_target_pairs={{0,16},{16,0},{1,17},{17,1},{2,18},{18,2},{3,19},{19,3},{4,20},{20... | collective-permute-start | bytes 78344 | tf_op jit(solution)/shard_map/ppermute | solution.py:419
  458.3 11.0 %collective-permute-start.39 = (bf16[192,3840]{1,0:T(8,128)(2,1)S(1)}, bf16[192,3840]{1,0:T(8,128)(2,1)S(1)}, u32[]{:S(2)}, u32[]{:S(2)}) collective-permute-start(bf16[192,3840]{1,0:T(8,128)(2,1)S(1)} %bitcast.382), channel_id=1, source_target_pairs={{0,1},{1,0},{2,3},{3,2},{4,5},{5,4},{6,7},{7,6},{8,9},{9,8},{10,11... | collective-permute-start | bytes 4423688 | tf_op jit(solution)/shard_map/ppermute | solution.py:419
  468.7 14.7 %collective-permute-start.30 = (bf16[2,48,3072]{2,1,0:T(8,128)(2,1)S(1)}, bf16[2,48,3072]{2,1,0:T(8,128)(2,1)S(1)}, u32[]{:S(2)}, u32[]{:S(2)}) collective-permute-start(bf16[2,48,3072]{2,1,0:T(8,128)(2,1)S(1)} %dynamic-slice_bitcast_fusion.15), channel_id=1, source_target_pairs={{0,16},{16,0},{1,17},{17,1},{2,18},{18,2},{3,19},{19,3},{4,20},{20... | collective-permute-start | bytes 1769480 | tf_op jit(solution)/shard_map/ppermute | solution.py:419
  483.5 7.5 %collective-permute-start.31 = (bf16[48,3072]{1,0:T(8,128)(2,1)S(1)}, bf16[48,3072]{1,0:T(8,128)(2,1)S(1)}, u32[]{:S(2)}, u32[]{:S(2)}) collective-permute-start(bf16[48,3072]{1,0:T(8,128)(2,1)S(1)} %dynamic-slice_bitcast_fusion.21), channel_id=1, source_target_pairs={{0,4},{4,0},{8,12},{12,8},{1,5},{5,1},{9,13},{13,9},{2,6},{6,2},{1... | collective-permute-start | bytes 884744 | tf_op jit(solution)/shard_map/ppermute | solution.py:419
  484.1 20.5 %collective-permute-start.17 = (bf16[2,2,48,2304]{3,2,1,0:T(8,128)(2,1)S(1)}, bf16[2,2,48,2304]{3,2,1,0:T(8,128)(2,1)S(1)}, u32[]{:S(2)}, u32[]{:S(2)}) collective-permute-start(bf16[2,2,48,2304]{3,2,1,0:T(8,128)(2,1)S(1)} %dynamic-slice_bitcast_fusion.7), channel_id=1, source_target_pairs={{0,16},{16,0},{1,17},{17,1},{2,18},{18,2},{3,19},{19,3},{4,20},{20... | collective-permute-start | bytes 2654216 | tf_op jit(solution)/shard_map/ppermute | solution.py:419
  491.0 13.5 %collective-permute-start.32 = (bf16[48,3072]{1,0:T(8,128)(2,1)S(1)}, bf16[48,3072]{1,0:T(8,128)(2,1)S(1)}, u32[]{:S(2)}, u32[]{:S(2)}) collective-permute-start(bf16[48,3072]{1,0:T(8,128)(2,1)S(1)} %bitcast_add_fusion.11), channel_id=1, source_target_pairs={{0,8},{4,12},{8,0},{12,4},{1,9},{5,13},{9,1},{13,5},{2,10},{6,14},... | collective-permute-start | bytes 884744 | tf_op jit(solution)/shard_map/ppermute | solution.py:419
  504.6 8.9 %collective-permute-start.33 = (bf16[48,3072]{1,0:T(8,128)(2,1)S(1)}, bf16[48,3072]{1,0:T(8,128)(2,1)S(1)}, u32[]{:S(2)}, u32[]{:S(2)}) collective-permute-start(bf16[48,3072]{1,0:T(8,128)(2,1)S(1)} %add.274), channel_id=1, source_target_pairs={{0,4},{4,0},{8,12},{12,8},{1,5},{5,1},{9,13},{13,9},{2,6},{6,2},{1... | collective-permute-start | bytes 884744 | tf_op jit(solution)/shard_map/ppermute | solution.py:419
  504.8 12.0 %collective-permute-start.18 = (bf16[2,48,2304]{2,1,0:T(8,128)(2,1)S(1)}, bf16[2,48,2304]{2,1,0:T(8,128)(2,1)S(1)}, u32[]{:S(2)}, u32[]{:S(2)}) collective-permute-start(bf16[2,48,2304]{2,1,0:T(8,128)(2,1)S(1)} %dynamic-slice_bitcast_fusion.19), channel_id=1, source_target_pairs={{0,2},{2,0},{1,3},{3,1},{4,6},{6,4},{5,7},{7,5},{8,10},{10,8},{9,1... | collective-permute-start | bytes 1327112 | tf_op jit(solution)/shard_map/ppermute | solution.py:419
  516.9 6.4 %collective-permute-start.19 = (bf16[48,2304]{1,0:T(8,128)(2,1)S(1)}, bf16[48,2304]{1,0:T(8,128)(2,1)S(1)}, u32[]{:S(2)}, u32[]{:S(2)}) collective-permute-start(bf16[48,2304]{1,0:T(8,128)(2,1)S(1)} %dynamic-slice_bitcast_fusion.23), channel_id=1, source_target_pairs={{0,4},{4,0},{8,12},{12,8},{1,5},{5,1},{9,13},{13,9},{2,6},{6,2},{1... | collective-permute-start | bytes 663560 | tf_op jit(solution)/shard_map/ppermute | solution.py:419
  518.8 13.7 %collective-permute-start.34 = (bf16[96,3072]{1,0:T(8,128)(2,1)S(1)}, bf16[96,3072]{1,0:T(8,128)(2,1)S(1)}, u32[]{:S(2)}, u32[]{:S(2)}) collective-permute-start(bf16[96,3072]{1,0:T(8,128)(2,1)S(1)} %bitcast.394), channel_id=1, source_target_pairs={{0,2},{2,0},{1,3},{3,1},{4,6},{6,4},{5,7},{7,5},{8,10},{10,8},{9,1... | collective-permute-start | bytes 1769480 | tf_op jit(solution)/shard_map/ppermute | solution.py:419
  523.3 11.1 %collective-permute-start.20 = (bf16[48,2304]{1,0:T(8,128)(2,1)S(1)}, bf16[48,2304]{1,0:T(8,128)(2,1)S(1)}, u32[]{:S(2)}, u32[]{:S(2)}) collective-permute-start(bf16[48,2304]{1,0:T(8,128)(2,1)S(1)} %bitcast_add_fusion.13), channel_id=1, source_target_pairs={{0,8},{4,12},{8,0},{12,4},{1,9},{5,13},{9,1},{13,5},{2,10},{6,14},... | collective-permute-start | bytes 663560 | tf_op jit(solution)/shard_map/ppermute | solution.py:419
  534.5 6.8 %collective-permute-start.21 = (bf16[48,2304]{1,0:T(8,128)(2,1)S(1)}, bf16[48,2304]{1,0:T(8,128)(2,1)S(1)}, u32[]{:S(2)}, u32[]{:S(2)}) collective-permute-start(bf16[48,2304]{1,0:T(8,128)(2,1)S(1)} %add.265), channel_id=1, source_target_pairs={{0,4},{4,0},{8,12},{12,8},{1,5},{5,1},{9,13},{13,9},{2,6},{6,2},{1... | collective-permute-start | bytes 663560 | tf_op jit(solution)/shard_map/ppermute | solution.py:419
  534.7 17.6 %collective-permute-start.35 = (bf16[192,3072]{1,0:T(8,128)(2,1)S(1)}, bf16[192,3072]{1,0:T(8,128)(2,1)S(1)}, u32[]{:S(2)}, u32[]{:S(2)}) collective-permute-start(bf16[192,3072]{1,0:T(8,128)(2,1)S(1)} %bitcast.387), channel_id=1, source_target_pairs={{0,1},{1,0},{2,3},{3,2},{4,5},{5,4},{6,7},{7,6},{8,9},{9,8},{10,11... | collective-permute-start | bytes 3538952 | tf_op jit(solution)/shard_map/ppermute | solution.py:419
  541.4 10.6 %collective-permute-start.22 = (bf16[96,2304]{1,0:T(8,128)(2,1)S(1)}, bf16[96,2304]{1,0:T(8,128)(2,1)S(1)}, u32[]{:S(2)}, u32[]{:S(2)}) collective-permute-start(bf16[96,2304]{1,0:T(8,128)(2,1)S(1)} %bitcast.395), channel_id=1, source_target_pairs={{0,2},{2,0},{1,3},{3,1},{4,6},{6,4},{5,7},{7,5},{8,10},{10,8},{9,1... | collective-permute-start | bytes 1327112 | tf_op jit(solution)/shard_map/ppermute | solution.py:419
  552.3 4.5 collective-permute-start.23
  (59 other events, 202.1 us)

commit v3 on v1

v3 whole, which is shorter than its diff:
```python
import functools

import jax
import jax.numpy as jnp
from jax import lax
from jax.experimental import pallas as pl
from jax.experimental.pallas import tpu as pltpu
from jax.sharding import Mesh, PartitionSpec as P

HD = 64
LANES = 128
norm_epsilon = 1e-05
masked_score = -1e9
BF = jnp.bfloat16
F32 = jnp.float32

NN = (((1,), (0,)), ((), ()))
NT = (((1,), (1,)), ((), ()))
TN = (((0,), (0,)), ((), ()))


def dot(a, b, dims=NN):
    return lax.dot_general(a, b, dims, preferred_element_type=F32)


def segment_terms(seg):
    lane = jnp.arange(LANES) % HD
    same = seg[..., None] == lane
    query_terms = jnp.where((lane < 4) & ~same, masked_score, 0.0).astype(BF)
    key_terms = jnp.where(((lane < 4) & same) | ((lane >= 4) & (lane < 7)), 1.0, 0.0).astype(BF)
    return query_terms, key_terms


def head_lanes(shape, head):
    lane = lax.broadcasted_iota(jnp.int32, shape, 1)
    return (lane < HD) if head == 0 else (lane >= HD)


def causal_scores(scores, causal, first_query, block, query_axis):
    if causal == "block":
        queries = lax.broadcasted_iota(jnp.int32, (block, block), query_axis)
        keys = lax.broadcasted_iota(jnp.int32, (block, block), 1 - query_axis)
        count = scores.shape[1 - query_axis]
        before = lax.slice_in_dim(scores, 0, count - block, axis=1 - query_axis)
        corner = lax.slice_in_dim(scores, count - block, count, axis=1 - query_axis)
        corner = jnp.where(keys <= queries, corner, masked_score)
        if count == block:
            return corner
        return jnp.concatenate([before, corner], 1 - query_axis)
    if causal == "mask":
        queries = first_query + lax.broadcasted_iota(jnp.int32, scores.shape, query_axis)
        keys = lax.broadcasted_iota(jnp.int32, scores.shape, 1 - query_axis)
        return jnp.where(keys <= queries, scores, masked_score)
    return scores


def part_places(parts, shift):
    if len(parts) == 1:
        return [slice(0, parts[0].shape[0])]
    half = parts[0].shape[0]
    count = half * len(parts)
    return [
        pl.ds(pl.multiple_of(lax.rem(part * half + shift, count), half), half)
        for part in range(len(parts))
    ]


def array_places(count, shift, swapped):
    if not swapped:
        return [(slice(0, count), slice(0, count))]
    half = count // 2
    return [
        (
            slice(part * half, (part + 1) * half),
            pl.ds(pl.multiple_of(lax.rem(part * half + shift, count), half), half),
        )
        for part in (0, 1)
    ]


def row_block(index, block, count, shift, swapped):
    if not swapped:
        return pl.ds(index * block, block)
    return pl.ds(pl.multiple_of(lax.rem(index * block + shift, count), block), block)


def forward_kernel(*refs, parts, skipped, causal, block, swapped):
    scalars, refs = refs[0], refs[1:]
    q_parts, k_parts, v_parts = refs[:parts], refs[parts : 2 * parts], refs[2 * parts : 3 * parts]
    qt_ref, kt_ref = refs[3 * parts : 3 * parts + 2]
    o_ref, lse_ref, ka, va, qa = refs[3 * parts + 2 + skipped :]
    tq, ts = qa.shape[1], ka.shape[1]
    pair = pl.program_id(1)
    shift = scalars[0]
    extra = kt_ref[...]
    for part, here in enumerate(part_places(k_parts, shift)):
        k, v = k_parts[part][...], v_parts[part][...]
        extra = kt_ref[part * k.shape[0] : (part + 1) * k.shape[0], :]
        for head in (0, 1):
            own = head_lanes(k.shape, head)
            ka[head, here, :] = jnp.where(own, k, extra)
            va[head, here, :] = jnp.where(own, v, extra)
    for part, here in enumerate(part_places(q_parts, shift)):
        q = q_parts[part][...]
        extra = qt_ref[part * q.shape[0] : (part + 1) * q.shape[0], :]
        for head in (0, 1):
            qa[head, here, :] = jnp.where(head_lanes(q.shape, head), q, extra)
    lane = lax.broadcasted_iota(jnp.int32, (block, LANES), 1)
    for index in range(tq // block):
        count = (index + 1) * block if causal == "block" else ts
        outs, lses = [], []
        for head in (0, 1):
            scores = dot(qa[head, index * block : (index + 1) * block, :], ka[head, :count, :], NT)
            scores = causal_scores(scores, causal, shift + index * block, block, 0)
            top = jnp.max(scores, 1, keepdims=True)
            weights = jnp.exp(scores - top).astype(BF)
            sums = dot(weights, va[head, :count, :])
            ones_lane = HD + 6 if head == 0 else 6
            total = sums[:, ones_lane : ones_lane + 1]
            outs.append(sums / total)
            lses.append(top + jnp.log(total))
        there = row_block(index, block, tq, shift, swapped)
        o_ref[there, :] = jnp.where(lane < HD, outs[0], outs[1]).astype(BF)
        lse_ref[there, :] = jnp.where(
            lane == 2 * pair, lses[0], jnp.where(lane == 2 * pair + 1, lses[1], lse_ref[there, :])
        )


def three_parts(x):
    parts = []
    for _ in range(3):
        part = x.astype(BF).astype(F32)
        parts.append(part)
        x = x - part
    return parts


def backward_kernel(*refs, parts, skipped, causal, block, swapped, scaling, first):
    scalars, refs = refs[0], refs[1:]
    q_parts, k_parts, v_parts = refs[:parts], refs[parts : 2 * parts], refs[2 * parts : 3 * parts]
    g_ref, o_ref, qt_ref, kt_ref, lse_ref = refs[3 * parts : 3 * parts + 5]
    (
        dq_ref, dk_ref, dv_ref, ka, va, qa, ga, k_turned, dk_sum, dv_sum, dq_turned,
    ) = refs[3 * parts + 5 + skipped :]
    tq, ts = qa.shape[1], ka.shape[1]
    pair = pl.program_id(1) + first
    shift = scalars[0]
    for part, here in enumerate(part_places(k_parts, shift)):
        k, v = k_parts[part][...], v_parts[part][...]
        extra = kt_ref[part * k.shape[0] : (part + 1) * k.shape[0], :]
        for head in (0, 1):
            own = head_lanes(k.shape, head)
            ka[head, here, :] = jnp.where(own, k, extra)
            va[head, here, :] = jnp.where(own, v, extra)
    for here in [s for s, _ in array_places(ts, shift, swapped)]:
        k = jnp.where(head_lanes((here.stop - here.start, LANES), 0), ka[0, here, :], ka[1, here, :])
        k_turned[:, here] = k.astype(F32).T.astype(BF)
    for part, here in enumerate(part_places(q_parts, shift)):
        q = q_parts[part][...]
        there = slice(part * q.shape[0], (part + 1) * q.shape[0])
        g, extra = g_ref[there, :], qt_ref[there, :]
        products = g.astype(F32) * o_ref[there, :].astype(F32)
        lse = lse_ref[there, :]
        lane = lax.broadcasted_iota(jnp.int32, q.shape, 1)
        for head in (0, 1):
            own = head_lanes(q.shape, head)
            at = HD + 4 if head == 0 else 4
            delta = three_parts(-jnp.sum(jnp.where(own, products, 0.0), 1, keepdims=True))
            lse_col = three_parts(
                -jnp.sum(jnp.where(lane == 2 * pair + head, lse, 0.0), 1, keepdims=True)
            )
            q_extra, g_extra = extra.astype(F32), jnp.zeros(q.shape, F32)
            for i in range(3):
                q_extra = jnp.where(lane == at + i, lse_col[i], q_extra)
                g_extra = jnp.where(lane == at + i, delta[i], g_extra)
            qa[head, here, :] = jnp.where(own, q, q_extra.astype(BF))
            ga[head, here, :] = jnp.where(own, g, g_extra.astype(BF))
    blocks = tq // block
    for index in reversed(range(blocks)):
        count = (index + 1) * block if causal == "block" else ts
        rows = slice(index * block, (index + 1) * block)
        for head in (0, 1):
            q, g = qa[head, rows, :], ga[head, rows, :]
            scores = dot(ka[head, :count, :], q, NT)
            scores = causal_scores(scores, causal, shift + index * block, block, 1)
            probs = jnp.exp(scores)
            grads = (probs * dot(va[head, :count, :], g, NT)).astype(BF)
            dv, dk = dot(probs.astype(BF), g), dot(grads, q)
            if index == blocks - 1:
                dv_sum[head, :count, :] = dv
                dk_sum[head, :count, :] = dk
            else:
                dv_sum[head, :count, :] += dv
                dk_sum[head, :count, :] += dk
            own_rows = slice(HD * head, HD * (head + 1))
            dq_turned[own_rows, rows] = dot(k_turned[own_rows, :count], grads)
        there = row_block(index, block, tq, shift, swapped)
        dq_ref[there, :] = dq_turned[:, rows].T.astype(BF) * jnp.asarray(scaling, BF)
    for here, there in array_places(ts, shift, swapped):
        own = head_lanes((here.stop - here.start, LANES), 0)
        dk_ref[there, :] = jnp.where(own, dk_sum[0, here, :], dk_sum[1, here, :]).astype(BF)
        dv_ref[there, :] = jnp.where(own, dv_sum[0, here, :], dv_sum[1, here, :]).astype(BF)


ANYWHERE = pl.BlockSpec(memory_space=pl.ANY)


def head_spec(count, start):
    return pl.BlockSpec((pl.Squeezed(), count, LANES), lambda row, pair, _: (row, 0, start + pair))


def shared_spec(count):
    return pl.BlockSpec((pl.Squeezed(), count, LANES), lambda row, pair, _: (row, 0, 0))


def part_specs(q, k, v, first):
    specs, arrays = [], []
    for parts, column in (q, k, v):
        for x in parts:
            specs.append(head_spec(x.shape[1], column // LANES + first))
            arrays.append(x)
    return specs, arrays


def attend(q, k, v, terms, shift, width, causal, block, swapped, after=()):
    specs, arrays = part_specs(q, k, v, 0)
    rows = arrays[0].shape[0]
    tq, ts = (sum(x.shape[1] for x in one[0]) for one in (q, k))
    pairs = width // LANES
    elements = rows * pairs * 2 * tq * ts
    return pl.pallas_call(
        functools.partial(
            forward_kernel, parts=len(q[0]), skipped=len(after), causal=causal, block=block,
            swapped=swapped,
        ),
        grid_spec=pltpu.PrefetchScalarGridSpec(
            num_scalar_prefetch=1,
            grid=(rows, pairs),
            in_specs=specs + [shared_spec(tq), shared_spec(ts)] + [ANYWHERE] * len(after),
            out_specs=[head_spec(tq, 0), shared_spec(tq)],
            scratch_shapes=[pltpu.VMEM((2, n, LANES), BF) for n in (ts, ts, tq)],
        ),
        out_shape=[
            jax.ShapeDtypeStruct((rows, tq, width), BF),
            jax.ShapeDtypeStruct((rows, tq, LANES), F32),
        ],
        compiler_params=pltpu.CompilerParams(vmem_limit_bytes=48 * 2**20),
        cost_estimate=pl.CostEstimate(
            flops=elements * 1600, bytes_accessed=rows * (tq + ts) * width * 4, transcendentals=0
        ),
    )(shift, *arrays, *terms, *after)


def attend_back(
    q, k, v, g, o, lse, terms, shift, first, pairs, causal, block, swapped, held=(), after=()
):
    specs, arrays = part_specs(q, k, v, first)
    rows, _, width = o.shape
    tq, ts = (sum(x.shape[1] for x in one[0]) for one in (q, k))
    elements = rows * pairs * 2 * tq * ts
    skipped = len(held) + len(after)
    count = len(arrays) + 5
    return pl.pallas_call(
        functools.partial(
            backward_kernel, parts=len(q[0]), skipped=skipped, causal=causal, block=block,
            swapped=swapped, scaling=HD**-0.5, first=first,
        ),
        grid_spec=pltpu.PrefetchScalarGridSpec(
            num_scalar_prefetch=1,
            grid=(rows, pairs),
            in_specs=specs
            + [head_spec(tq, first)] * 2
            + [shared_spec(tq), shared_spec(ts), shared_spec(tq)]
            + [ANYWHERE] * skipped,
            out_specs=[head_spec(tq, first), head_spec(ts, first), head_spec(ts, first)],
            scratch_shapes=[pltpu.VMEM((2, n, LANES), BF) for n in (ts, ts, tq, tq)]
            + [
                pltpu.VMEM((LANES, ts), BF),
                pltpu.VMEM((2, ts, LANES), F32),
                pltpu.VMEM((2, ts, LANES), F32),
                pltpu.VMEM((LANES, tq), F32),
            ],
        ),
        out_shape=[jax.ShapeDtypeStruct((rows, n, width), BF) for n in (tq, ts, ts)],
        input_output_aliases={1 + count + i: i for i in range(len(held))},
        compiler_params=pltpu.CompilerParams(vmem_limit_bytes=48 * 2**20),
        cost_estimate=pl.CostEstimate(
            flops=elements * 2600, bytes_accessed=rows * (tq + ts) * pairs * 1024, transcendentals=0
        ),
    )(shift, *arrays, g, o, *terms, lse, *held, *after)


def norm(resid):
    center = resid - jnp.mean(resid, -1, keepdims=True)
    inverse = lax.rsqrt(jnp.mean(center * center, -1, keepdims=True) + norm_epsilon)
    return center * inverse, inverse


def norm_back(upstream, normed, inverse, gain_vec):
    w = upstream * gain_vec
    return (
        w - jnp.mean(w, -1, keepdims=True) - normed * jnp.mean(w * normed, -1, keepdims=True)
    ) * inverse


def gelu_parts(pre):
    bell = jnp.exp(pre * pre * -0.5)
    t = 1.0 / (1.0 + jnp.abs(pre) * (0.3275911 * 0.5**0.5))
    poly = 0.5 * 1.061405429
    for c in (-1.453152027, 1.421413741, -0.284496736, 0.254829592):
        poly = poly * t + 0.5 * c
    tail = poly * t * bell
    phi_sum = jnp.where(pre >= 0, 1.0 - tail, tail)
    return pre * phi_sum, phi_sum + pre * (bell * 0.3989422804014327)


def add_rows(sums_ref, first, rows):
    for index, value in enumerate(rows):
        here = slice(first + index, first + index + 1)
        sums_ref[here, :] += jnp.sum(value.astype(F32), 0, keepdims=True)


def finish_rows(sums_ref, out_ref):
    @pl.when(pl.program_id(0) == pl.num_programs(0) - 1)
    def _():
        out_ref[...] = sums_ref[...].T


def clear(ref):
    @pl.when(pl.program_id(0) == 0)
    def _():
        ref[...] = jnp.zeros_like(ref)


def row(ref):
    return ref[...][None, :]


def project_kernel(x_ref, w_ref, b_ref, out_ref, *, scaled):
    width = b_ref.shape[0] // 3
    y = dot(x_ref[...], w_ref[...]) + row(b_ref)
    if scaled:
        out_ref[:, :width] = (y[:, :width] * HD**-0.5).astype(BF)
        out_ref[:, width:] = y[:, width:].astype(BF)
    else:
        out_ref[...] = y.astype(BF)


def after_self_kernel(
    o_ref, x_ref, w_ref, b_ref, gain_ref, bias_ref, qw_ref, qb_ref, n1_ref, i1_ref, h1b_ref, cq_ref,
):
    resid = x_ref[...].astype(F32) + (dot(o_ref[...], w_ref[...]) + row(b_ref))
    n1, i1 = norm(resid)
    h1b = (n1 * row(gain_ref) + row(bias_ref)).astype(BF)
    n1_ref[...] = n1
    i1_ref[...] = jnp.broadcast_to(i1, i1_ref.shape)
    h1b_ref[...] = h1b
    cq_ref[...] = ((dot(h1b, qw_ref[...]) + row(qb_ref)) * HD**-0.5).astype(BF)


def middle_kernel(
    o_ref, n1_ref, up_ref, g1_ref, s1_ref, ow_ref, ob_ref, g2_ref, s2_ref,
    w1_ref, b1_ref, w2_ref, b2_ref, g3_ref, s3_ref,
    *refs, chunk, kept_blocks,
):
    if kept_blocks is None:
        out_ref, *refs = refs
    else:
        out_ref, sent_ref, *refs = refs
    act_ref, dbf_ref, h2b_ref, dpre_ref, dr2_ref, dbc_ref, dco_ref, sums_ref, slope, sums = refs
    clear(sums)
    h1 = n1_ref[...] * row(g1_ref) + row(s1_ref)
    n2, i2 = norm(h1 + (dot(o_ref[...], ow_ref[...]) + row(ob_ref)))
    h2 = n2 * row(g2_ref) + row(s2_ref)
    h2b = h2.astype(BF)
    h2b_ref[...] = h2b
    hidden = w1_ref.shape[1]
    cols = [slice(c, c + chunk) for c in range(0, hidden, chunk)]
    bias1 = row(b1_ref)
    branch = row(b2_ref)
    for c in cols:
        pre = dot(h2b, w1_ref[:, c]) + bias1[:, c]
        value, slope_c = gelu_parts(pre)
        slope[:, c] = slope_c
        act_c = value.astype(BF)
        act_ref[:, c] = act_c
        branch = branch + dot(act_c, w2_ref[c, :])
    n3, i3 = norm(h2 + branch)
    out = (n3 * row(g3_ref) + row(s3_ref)).astype(BF)
    if kept_blocks is None:
        out_ref[...] = out
    else:
        step = pl.program_id(0)

        @pl.when(step < kept_blocks)
        def _():
            out_ref[...] = out

        @pl.when(step >= kept_blocks)
        def _():
            sent_ref[...] = out

    up = up_ref[...].astype(F32)
    dr3 = norm_back(up, n3, i3, row(g3_ref))
    dbf = dr3.astype(BF)
    dbf_ref[...] = dbf
    dh2 = dr3
    for c in cols:
        dpre_c = (dot(dbf, w2_ref[c, :], NT) * slope[:, c]).astype(BF)
        dpre_ref[:, c] = dpre_c
        dh2 = dh2 + dot(dpre_c, w1_ref[:, c], NT)
    dr2 = norm_back(dh2, n2, i2, row(g2_ref))
    dbc = dr2.astype(BF)
    dr2_ref[...] = dr2
    dbc_ref[...] = dbc
    dco_ref[...] = dot(dbc, ow_ref[...], NT).astype(BF)
    add_rows(sums, MID_ROWS, (up * n3, up, dbf, dh2 * n2, dh2))
    finish_rows(sums, sums_ref)


def before_self_kernel(
    dcq_ref, dr2_ref, n1_ref, i1_ref, qw_ref, g1_ref, ow_ref, dr1_ref, dba_ref, dso_ref, sums_ref,
    sums,
):
    clear(sums)
    n1 = n1_ref[...]
    dh1 = dr2_ref[...] + dot(dcq_ref[...], qw_ref[...], NT)
    dr1 = norm_back(dh1, n1, i1_ref[:, 0:1], row(g1_ref))
    dba = dr1.astype(BF)
    dr1_ref[...] = dr1
    dba_ref[...] = dba
    dso_ref[...] = dot(dba, ow_ref[...], NT).astype(BF)
    add_rows(sums, LOW_ROWS, (dh1 * n1, dh1))
    finish_rows(sums, sums_ref)


def input_grad_kernel(*refs, count, start):
    grads, w_ref, out_ref = refs[:count], refs[count + start], refs[count + start + 1]
    total = refs[count][...] if start else None
    width = grads[0].shape[-1]
    for index, ref in enumerate(grads):
        part = dot(ref[...], w_ref[:, index * width : (index + 1) * width], NT)
        total = part if total is None else total + part
    out_ref[...] = total.astype(out_ref.dtype)


class Joined:
    def __init__(self, kept, got, use_kept):
        self.kept, self.got, self.use_kept = kept, got, use_kept

    def __getitem__(self, index):
        return jnp.where(self.use_kept, self.kept[index], self.got[index])


def token_call(kernel, block, blocked, whole, outs, place, scratch=(), flops=0, after=(), span=None):
    def length(x):
        return x.shape[0] if not isinstance(x, tuple) else x[0].shape[1] * (1 if x[1] is None else 2)

    tokens = length(blocked[0])
    half = tokens // block // 2
    first, count = span if span is not None else (0, tokens // block)
    in_specs, arrays, kinds = [], [], []
    for x in blocked:
        if not isinstance(x, tuple):
            in_specs.append(pl.BlockSpec((block, x.shape[1]), lambda i, _: (i + first, 0)))
            arrays.append(x)
            kinds.append(1)
            continue
        stack, got = x
        shape = (pl.Squeezed(), block, stack.shape[2])
        if got is None:
            in_specs.append(pl.BlockSpec(shape, lambda i, p: (p[0], i, 0)))
            arrays.append(stack)
            kinds.append(1)
        else:
            in_specs.append(pl.BlockSpec(shape, lambda i, p: (p[0], jnp.minimum(i, half - 1), 0)))
            in_specs.append(
                pl.BlockSpec(shape[1:], lambda i, p: (jnp.maximum(i - half, 0), 0))
            )
            arrays += [stack, got]
            kinds.append(2)
    for x in whole:
        zeros = (0,) * x.ndim
        in_specs.append(
            pl.BlockSpec(x.shape, lambda i, _, z=zeros: z, pipeline_mode=pl.Buffered(1))
        )
    in_specs += [ANYWHERE] * len(after)
    out_specs, out_shape = [], []
    for out in outs:
        if out[0] == "whole":
            out_specs.append(pl.BlockSpec(out[1:3], lambda i, _: (0, 0)))
            shape = out[1:3]
        elif out[0] == "kept":
            shape = (out[1], tokens // 2, out[2])
            out_specs.append(
                pl.BlockSpec(
                    (pl.Squeezed(), block, out[2]),
                    lambda i, p: (p[0], jnp.minimum(i, half - 1), 0),
                )
            )
        elif out[0] == "sent":
            shape = (tokens // 2, out[1])
            out_specs.append(
                pl.BlockSpec(
                    (block, out[1]), lambda i, _: (jnp.maximum(i + first - half, 0), 0)
                )
            )
        else:
            shape = (count * block, out[0])
            out_specs.append(pl.BlockSpec((block, out[0]), lambda i, _: (i, 0)))
        out_shape.append(jax.ShapeDtypeStruct(shape, out[-1]))

    def run(_, *refs):
        used = []
        for kind in kinds:
            if kind == 1:
                used.append(refs[0])
            else:
                used.append(Joined(refs[0], refs[1], pl.program_id(0) < half))
            refs = refs[kind:]
        kernel(*used, *refs[: len(whole)], *refs[len(whole) + len(after) :])

    moved = sum(a.size * a.dtype.itemsize for a in (*arrays, *whole, *out_shape))
    return pl.pallas_call(
        run,
        grid_spec=pltpu.PrefetchScalarGridSpec(
            num_scalar_prefetch=1,
            grid=(count,),
            in_specs=in_specs,
            out_specs=out_specs,
            scratch_shapes=list(scratch),
        ),
        out_shape=out_shape,
        compiler_params=pltpu.CompilerParams(vmem_limit_bytes=56 * 2**20),
        cost_estimate=pl.CostEstimate(
            flops=flops * count * block // tokens, bytes_accessed=moved, transcendentals=0
        ),
    )(place, *arrays, *whole, *after)


def store_kernel(_, got_ref, __, out_ref):
    out_ref[...] = got_ref[...].astype(out_ref.dtype)


def store_other(held, got, place):
    n, c = got.shape
    return pl.pallas_call(
        store_kernel,
        grid_spec=pltpu.PrefetchScalarGridSpec(
            num_scalar_prefetch=1,
            grid=(2,),
            in_specs=[pl.BlockSpec((n // 2, c), lambda i, _: (i, 0)), ANYWHERE],
            out_specs=pl.BlockSpec((pl.Squeezed(), n // 2, c), lambda i, p: (1 - p[0], i, 0)),
        ),
        out_shape=jax.ShapeDtypeStruct(held.shape, held.dtype),
        input_output_aliases={2: 0},
        cost_estimate=pl.CostEstimate(flops=0, bytes_accessed=n * c * 6, transcendentals=0),
    )(place, got, held)


MID_ROWS, LOW_ROWS = 8, 16


def weight_grads(items, extras, place, wide, order, after=()):
    width = items[0][0].shape[-1] if not isinstance(items[0][0], tuple) else items[0][0][0].shape[-1]
    specs, arrays, lefts, steps = [], [], [], []
    known = {}
    for left, right, sum_row in items:
        if id(left) not in known:
            where = len(arrays)
            if isinstance(left, tuple):
                stack, got = left
                specs.append(
                    pl.BlockSpec(
                        (pl.Squeezed(),) + stack.shape[1:], lambda j, p: (p[0], 0, 0),
                        pipeline_mode=pl.Buffered(1),
                    )
                )
                specs.append(
                    pl.BlockSpec(got.shape, lambda j, p: (0, 0), pipeline_mode=pl.Buffered(1))
                )
                arrays += [stack, got]
            else:
                specs.append(
                    pl.BlockSpec(left.shape, lambda j, p: (0, 0), pipeline_mode=pl.Buffered(1))
                )
                arrays.append(left)
            known[id(left)] = (where, isinstance(left, tuple))
        begin, blocks = len(steps), right.shape[1] // width
        where = len(arrays)
        specs.append(
            pl.BlockSpec(
                (right.shape[0], width),
                lambda j, p, b=begin, n=blocks: (0, jnp.clip(j - b, 0, n - 1)),
            )
        )
        arrays.append(right)
        for index in range(blocks):
            steps.append((known[id(left)], where, sum_row, index, blocks))
    for extra in extras:
        specs.append(
            pl.BlockSpec(extra.shape, lambda j, p: (0, 0), pipeline_mode=pl.Buffered(1))
        )
    slab = width // len(order)
    size = width // wide

    def kernel(_, *refs):
        ins, rest = refs[: len(arrays)], refs[len(arrays) :]
        extra_refs, (out_ref, sums) = rest[: len(extras)], rest[len(extras) + len(after) :]
        clear(sums)
        step = pl.program_id(0)

        def store(value):
            for to, source in enumerate(order):
                out_ref[to * slab : (to + 1) * slab, :] = value[
                    source * slab : (source + 1) * slab
                ].astype(BF)

        for index, ((left, split), right, sum_row, part, parts) in enumerate(steps):

            @pl.when(step == index)
            def _():
                grad = ins[right][...]
                if split:
                    half = ins[left].shape[0]
                    value = dot(ins[left][...], grad[:half], TN)
                    value = value + dot(ins[left + 1][...], grad[half:], TN)
                else:
                    value = dot(ins[left][...], grad, TN)
                store(value)
                if sum_row is not None:
                    total = jnp.sum(grad.astype(F32), 0, keepdims=True)
                    if parts == 1:
                        sums[sum_row : sum_row + 1, :] = total
                    else:
                        for piece in range(wide):
                            w, k = divmod(wide * part + piece, parts)
                            sums[sum_row + k : sum_row + k + 1, w * size : (w + 1) * size] = total[
                                :, piece * size : (piece + 1) * size
                            ]

        @pl.when(step == len(steps))
        def _():
            value = sums[...].T
            for ref in extra_refs:
                value = value + ref[...]
            store(jnp.concatenate([value, jnp.zeros((width, width - LANES), F32)], 1))

    columns = width * len(steps) + LANES
    tokens = items[0][1].shape[0]
    return pl.pallas_call(
        kernel,
        grid_spec=pltpu.PrefetchScalarGridSpec(
            num_scalar_prefetch=1,
            grid=(len(steps) + 1,),
            in_specs=specs + [ANYWHERE] * len(after),
            out_specs=pl.BlockSpec((width, width), lambda j, _: (0, j)),
            scratch_shapes=[pltpu.VMEM((LANES, width), F32)],
        ),
        out_shape=jax.ShapeDtypeStruct((width, columns), BF),
        compiler_params=pltpu.CompilerParams(vmem_limit_bytes=48 * 2**20),
        cost_estimate=pl.CostEstimate(
            flops=2 * tokens * width * columns,
            bytes_accessed=sum(a.size * 2 for a in arrays) + width * columns * 2,
            transcendentals=0,
        ),
    )(place, *arrays, *extras, *after)


def tall_grad(left, right, place, order, after=()):
    tokens, rows = left.shape
    width = right.shape[1]
    slabs = len(order)
    size = rows // slabs

    def out_row(j):
        to = 0
        for at, source in enumerate(order):
            to = jnp.where(j == source, at, to)
        return to

    def kernel(_, left_ref, right_ref, *refs):
        refs[-1][...] = dot(left_ref[...], right_ref[...], TN).astype(BF)

    return pl.pallas_call(
        kernel,
        grid_spec=pltpu.PrefetchScalarGridSpec(
            num_scalar_prefetch=1,
            grid=(slabs,),
            in_specs=[
                pl.BlockSpec((tokens, size), lambda j, _: (0, j)),
                pl.BlockSpec(right.shape, lambda j, _: (0, 0), pipeline_mode=pl.Buffered(1)),
            ]
            + [ANYWHERE] * len(after),
            out_specs=pl.BlockSpec((size, width), lambda j, _: (out_row(j), 0)),
        ),
        out_shape=jax.ShapeDtypeStruct((rows, width), BF),
        compiler_params=pltpu.CompilerParams(vmem_limit_bytes=48 * 2**20),
        cost_estimate=pl.CostEstimate(
            flops=2 * tokens * rows * width,
            bytes_accessed=2 * (left.size + right.size + rows * width),
            transcendentals=0,
        ),
    )(place, left, right, *after)


def vectors_kernel(x_ref, *outs, columns):
    turned = x_ref[...].astype(F32).T
    for (start, count), out in zip(columns, outs):
        rows = [turned[start + i] for i in range(count)]
        out[...] = rows[0] if count == 1 else jnp.concatenate(rows)


def vectors_of(x, columns):
    return pl.pallas_call(
        functools.partial(vectors_kernel, columns=columns),
        out_shape=[jax.ShapeDtypeStruct((count * x.shape[0],), F32) for _, count in columns],
    )(x)


def partner(x, axis, bit=1):
    count = lax.axis_size(axis)
    return lax.ppermute(x, axis, [(i, i ^ bit) for i in range(count)])


ROWS = ("far", "near", "side", "core")


def pick(x, index):
    half = x.shape[0] // 2
    return lax.dynamic_slice_in_dim(x, index * half, half, 0)


class Reduction:
    def __init__(self, x, order):
        self.split = all(lax.axis_size(a) == 2 for a in ("wide", "side", "near", "core"))
        self.x = x
        self.steps = list(order) if self.split else []
        self.terms = [x]
        self.got = None

    def total(self, terms):
        value = sum(t.astype(F32) for t in terms)
        return value.astype(BF)

    def send(self):
        if not self.steps:
            return ()
        step = self.steps[0]
        if step == "core_sum":
            self.got = lax.psum_scatter(self.x, "core", scatter_dimension=0, tiled=True)
            return ()
        if step == "gather":
            self.got = lax.all_gather(self.total(self.terms), ("core", "side", "near"), axis=0, tiled=True)
            return ()
        if step in ("core", "wide", "side", "near"):
            sent = self.total([pick(t, 1 - lax.axis_index(step)) for t in self.terms])
            axis = step
        elif step == "far":
            sent = self.total(self.terms)
            axis = step
        else:
            sent = self.total(self.terms)
            self.terms = [sent]
            axis = step[5:]
        if step == "far":
            self.got = []
            count, bit = lax.axis_size("far"), 1
            assert count <= 2
            while bit < count:
                self.got.append(partner(sent, "far", bit))
                bit *= 2
        else:
            self.got = [partner(sent, axis)]
        return (sent,)

    def take(self):
        if not self.steps:
            return
        step = self.steps.pop(0)
        if step in ("core_sum", "gather"):
            self.terms = [self.got]
        elif step in ("core", "wide", "side", "near"):
            self.terms = [pick(t, lax.axis_index(step)) for t in self.terms] + self.got
        elif step == "far":
            self.terms = self.terms + self.got
        else:
            x, got = self.terms[0], self.got[0]
            first = lax.axis_index(step[5:]) == 0
            self.terms = [
                jnp.concatenate([jnp.where(first, x, got), jnp.where(first, got, x)], 0)
            ]

    def result(self):
        assert not self.steps
        if self.split:
            return self.terms[0]
        x = lax.psum_scatter(self.x, "wide", scatter_dimension=0, tiled=True)
        return lax.psum(x, ROWS)


CORE_WIDE = (0, 2, 1, 3)
CORE_SIDE = (0, 4, 1, 5, 2, 6, 3, 7)
JOINS = ("join_near", "join_side", "join_core")
X_FIRST = ("core", "wide", "side", "near", "far") + JOINS
Y_FIRST = ("core", "side", "wide", "near", "far") + JOINS


def body(
    target, encoded, segments, out_grad,
    self_qkv_w, self_q_b, self_v_b, self_out_w, self_out_b, norm1_gain, norm1_bias,
    cross_q_w, cross_q_b, cross_kv_w, cross_v_b, cross_out_w, cross_out_b, norm2_gain, norm2_bias,
    ffn_in_w, ffn_in_b, ffn_out_w, ffn_out_b, norm3_gain, norm3_bias,
):
    row_count, tok_count, width = target.shape
    hidden = ffn_in_w.shape[1]
    wide = lax.axis_size("wide")
    index = lax.axis_index("wide").astype(jnp.int32)
    place = index.reshape(1)
    shift = (index * tok_count).reshape(1)
    swapped = wide == 2 and row_count == 2
    split = all(lax.axis_size(a) == 2 for a in ("wide", "side", "near", "core"))
    core_wide = CORE_WIDE if split else (0, 1, 2, 3)
    core_side = CORE_SIDE if split else (0,)
    tokens = row_count * tok_count
    block = min(256, tok_count)

    if swapped:
        def bring(x):
            sent = lax.dynamic_index_in_dim(x, 1 - index, 0, keepdims=False)
            return x, partner(sent, "wide")

        causal, block_f, block_b = "block", 2 * block, block
        seg_kept, seg_got = bring(segments)
        seg = jnp.concatenate(
            [lax.dynamic_index_in_dim(seg_kept, index, 0, keepdims=False), seg_got]
        )[None]
        key_seg = seg
        row_tokens = tokens
    else:
        def bring(x):
            return x.reshape(tokens, -1)

        causal, block_f, block_b = "mask", block, block
        seg = segments
        key_seg = lax.all_gather(segments, "wide", axis=1, tiled=True)
        row_tokens = tok_count
    terms = (segment_terms(seg)[0], segment_terms(key_seg)[1])

    def by_row(x):
        return x.reshape(-1, row_tokens, x.shape[-1])

    def flat(x):
        return x.reshape(-1, x.shape[-1])

    def keys_of(x):
        return lax.all_gather(x, "wide", axis=1, tiled=True)

    def key_grads(x):
        return x if swapped else lax.psum_scatter(x, "wide", scatter_dimension=1, tiled=True)

    def project(x, w, bias, scaled, after=()):
        if not swapped:
            parts = [(x, None)]
        else:
            parts = [((x[0], None), None), (x[1], after)]
        outs = []
        for part, deps in parts:
            (out,) = token_call(
                functools.partial(project_kernel, scaled=scaled), block, (part,), (w, bias),
                [(w.shape[1], BF)], place, flops=2 * tokens * width * w.shape[1],
                after=deps or (),
            )
            outs.append(out[None] if swapped else by_row(out))
        return outs

    def attention(q, k, v, is_causal, after=()):
        return attend(
            q, k, v, terms, shift, width, causal if is_causal else "no", block_f, swapped, after
        )

    def attention_back(q, k, v, g, o, lse, is_causal, cuts, after):
        held = ()
        pairs = width // LANES
        per = pairs // cuts
        for cut in range(cuts):
            held = attend_back(
                q, k, v, by_row(g), o, lse, terms, shift, cut * per, per,
                causal if is_causal else "no", block_b, swapped, held, after[cut](),
            )
        dq, dk, dv = held
        return flat(dq), flat(key_grads(dk)), flat(key_grads(dv))

    def input_grad(grads, w, start=None, after=()):
        blocked = list(grads) + ([] if start is None else [start])
        kernel = functools.partial(
            input_grad_kernel, count=len(grads), start=0 if start is None else 1
        )
        flops = 2 * tokens * width * w.shape[1]
        if not swapped:
            return token_call(kernel, block, blocked, (w,), [(width, F32)], place, flops=flops)[0], None
        half = tokens // block // 2
        (sent,) = token_call(
            kernel, block, blocked, (w,), [("sent", width, BF)], place, flops=flops,
            span=(half, half), after=after,
        )
        (kept,) = token_call(
            kernel, block, blocked, (w,), [("kept", 2, width, F32)], place, flops=flops,
            span=(0, half), after=(sent,),
        )
        return kept, sent

    def give(out, got):
        if not swapped:
            return out.reshape(row_count, tok_count, width)
        return store_other(out, got, place)

    def send_back(x):
        return partner(x, "wide") if swapped else None

    zeros = jnp.zeros_like(self_q_b)
    x_in = bring(target)
    x_enc = bring(encoded)
    qkv = project(x_in, self_qkv_w, jnp.concatenate([self_q_b, zeros, self_v_b]), True)
    if swapped:
        self_q, self_k, self_v = (qkv, 0), (qkv, width), (qkv, 2 * width)
    else:
        both = [keys_of(qkv[0][..., width:])]
        self_q, self_k, self_v = (qkv, 0), (both, 0), (both, width)
    self_o, self_lse = attention(self_q, self_k, self_v, True)
    self_ob = flat(self_o)
    n1, i1, h1b, cq = token_call(
        after_self_kernel, block, (self_ob, x_in),
        (self_out_w, self_out_b, norm1_gain, norm1_bias, cross_q_w, cross_q_b),
        [(width, F32), (LANES, F32), (width, BF), (width, BF)], place,
        flops=4 * tokens * width * width,
    )
    ckv = project(
        x_enc, cross_kv_w, jnp.concatenate([zeros, cross_v_b]), False, (h1b,)
    )
    upstream = bring(out_grad)
    cross_q = ([by_row(cq)], 0)
    if swapped:
        half = row_tokens // 2
        cross_q = ([by_row(cq)[:, :half], by_row(cq)[:, half:]], 0)
        cross_k, cross_v = (ckv, 0), (ckv, width)
    else:
        both = [keys_of(ckv[0])]
        cross_k, cross_v = (both, 0), (both, width)
    cross_o, cross_lse = attention(cross_q, cross_k, cross_v, False)
    cross_ob = flat(cross_o)
    outs = [("kept", 2, width, BF), ("sent", width, BF)] if swapped else [(width, BF)]
    *h3, act, dbf, h2b, dpre, dr2, dbc, dco, mid_sums = token_call(
        functools.partial(
            middle_kernel, chunk=width, kept_blocks=tok_count // block if swapped else None
        ),
        block, (cross_ob, n1, upstream),
        (
            norm1_gain, norm1_bias, cross_out_w, cross_out_b, norm2_gain, norm2_bias,
            ffn_in_w, ffn_in_b, ffn_out_w, ffn_out_b, norm3_gain, norm3_bias,
        ),
        outs
        + [
            (hidden, BF), (width, BF), (width, BF), (hidden, BF), (width, F32),
            (width, BF), (width, BF), ("whole", width, LANES, F32),
        ],
        place,
        scratch=[pltpu.VMEM((block, hidden), F32), pltpu.VMEM((LANES, width), F32)],
        flops=2 * tokens * width * (4 * hidden + 2 * width),
    )
    got_out = send_back(h3[-1])

    ra = Reduction(tall_grad(act, dbf, place, core_wide), X_FIRST)
    sent_a = ra.send()
    rb = Reduction(
        weight_grads(
            [(h2b, dpre, 0), (cross_ob, dbc, 4)], [mid_sums], place, wide, core_side, sent_a
        ),
        Y_FIRST,
    )
    sent_b = rb.send()
    ra.take()
    sent_a = ra.send()

    def step(*reductions):
        for r in reductions:
            r.take()
        return sum((r.send() for r in reductions), ())

    dcq, dck, dcv = attention_back(
        cross_q, cross_k, cross_v, dco, cross_o, cross_lse, False, 2,
        [lambda: sent_a + sent_b, lambda: step(rb)],
    )
    sent = step(ra, rb)
    dr1, dba, dso, low_sums = token_call(
        before_self_kernel, block, (dcq, dr2, n1, i1), (cross_q_w, norm1_gain, self_out_w),
        [(width, F32), (width, BF), (width, BF), ("whole", width, LANES, F32)], place,
        scratch=[pltpu.VMEM((LANES, width), F32)],
        flops=4 * tokens * width * width, after=sent,
    )
    rc = Reduction(
        weight_grads(
            [(h1b, dcq, 0), (x_enc, dck, None), (x_enc, dcv, 1), (self_ob, dba, 2)],
            [low_sums], place, wide, core_side,
        ),
        Y_FIRST,
    )
    sent_c = rc.send()
    enc_kept, enc_sent = input_grad([dck, dcv], cross_kv_w)
    got_enc = send_back(enc_sent)
    out_first = (got_out,) if swapped else ()
    dsq, dsk, dsv = attention_back(
        self_q, self_k, self_v, dso, self_o, self_lse, True, 2,
        [lambda: step(ra, rb) + sent_c + out_first, lambda: step(ra, rb, rc)],
    )
    sent = step(ra, rb, rc)
    rd = Reduction(
        weight_grads(
            [(x_in, dsq, 0), (x_in, dsk, None), (x_in, dsv, 1)], [], place, wide, core_wide, sent
        ),
        X_FIRST,
    )
    sent = rd.send()
    in_kept, in_sent = input_grad([dsq, dsk, dsv], self_qkv_w, dr1, sent)
    got_in = send_back(in_sent)
    while any(r.steps for r in (ra, rb, rc, rd)):
        step(ra, rb, rc, rd)
    layer_out = give(h3[0], got_out)
    encoded_grad = give(enc_kept, got_enc)
    target_grad = give(in_kept, got_in)
    grad_a, grad_b, grad_c, grad_d = (r.result() for r in (ra, rb, rc, rd))

    def matrix(x, first, count):
        return x[:, first * width : (first + count) * width].astype(F32)

    parts = hidden // width
    (
        ffn_in_b_grad, cross_out_b_grad, norm3_gain_grad, norm3_bias_grad, ffn_out_b_grad,
        norm2_gain_grad, norm2_bias_grad,
    ) = vectors_of(
        grad_b[:, -LANES:], [(0, parts), (parts, 1)] + [(MID_ROWS + i, 1) for i in range(5)]
    )
    cross_q_b_grad, cross_v_b_grad, self_out_b_grad, norm1_gain_grad, norm1_bias_grad = vectors_of(
        grad_c[:, -LANES:], [(0, 1), (1, 1), (2, 1), (LOW_ROWS, 1), (LOW_ROWS + 1, 1)]
    )
    self_q_b_grad, self_v_b_grad = vectors_of(grad_d[:, -LANES:], [(0, 1), (1, 1)])
    return (
        layer_out, target_grad, encoded_grad,
        matrix(grad_d, 0, 3), self_q_b_grad, self_v_b_grad,
        matrix(grad_c, 3, 1), self_out_b_grad, norm1_gain_grad, norm1_bias_grad,
        matrix(grad_c, 0, 1), cross_q_b_grad,
        matrix(grad_c, 1, 2), cross_v_b_grad,
        matrix(grad_b, parts, 1), cross_out_b_grad, norm2_gain_grad, norm2_bias_grad,
        matrix(grad_b, 0, parts), ffn_in_b_grad, grad_a.astype(F32), ffn_out_b_grad,
        norm3_gain_grad, norm3_bias_grad,
    )


def solution(mesh):
    wide, narrow = mesh.shape["wide"], mesh.shape["narrow"]
    core = 2 if narrow % 2 == 0 else 1
    side = 2 if narrow % (2 * core) == 0 else 1
    near = 2 if narrow % (2 * core * side) == 0 else 1
    devices = mesh.devices.reshape(wide, narrow // (near * side * core), near, side, core)
    split = Mesh(devices, ("wide",) + ROWS)
    token_spec = P(ROWS, "wide", None)
    in_specs = (token_spec, token_spec, P(ROWS, "wide"), token_spec) + (P(),) * 21
    matrix, vector = P("wide", None), P("wide")
    out_specs = (token_spec,) * 3 + (
        matrix, vector, vector, matrix, vector, vector, vector,
        matrix, vector, matrix, vector, matrix, vector, vector, vector,
        matrix, vector, matrix, vector, vector, vector,
    )
    return jax.shard_map(body, mesh=split, in_specs=in_specs, out_specs=out_specs, check_vma=False)
```

time: 744 us -> 539 us (0.72)
  Pallas kernels: 107 us -> 274 us
  matrix products: 149 us -> 0 us
  waiting for transfers between devices: 272 us -> 134 us
  local copies, waits for them, and re-layouts: 96.3 us -> 28 us
  other arithmetic: 70.7 us -> 60.3 us
    pallas_call x4 -> x27, Pallas kernels: 107 us -> 274 us  [the longest x11 104 us: token_call(): pl.pallas_call(run, grid_spec=pltpu.PrefetchScalarGridSpec(num_scalar_pre...]
    dot_general x21 -> x0, matrix products: 149 us -> none  [dot(): return lax.dot_general(a, b, dims, preferred_element_type=F32)]
    ppermute x40 -> x39, waiting for transfers between devices: 272 us -> 134 us  [partner(): return lax.ppermute(x, axis, [(i, i ^ bit) for i in range(count)])]
    convert_element_type x4 -> x26, other arithmetic: 6.42 us -> 46.2 us  [the longest x20 34.3 us: total(): return value.astype(BF)]
    unnamed x212 -> x114, local copies, waits for them, and re-layouts: 41.4 us -> 9.06 us
    add x25 -> x0, other arithmetic: 20.3 us -> none  [the longest x12 11.8 us: halve(): return lax.dynamic_slice_in_dim(x, index * half, half, 0) + got]
    reduce_sum x11 -> x0, other arithmetic: 17.1 us -> none  [the longest x7 12.3 us: column_sum(): return jnp.sum(x.astype(F32), 0)]
    reshape x14 -> x0, local copies, waits for them, and re-layouts: 13.9 us -> none  [reduce_vectors(): x = jnp.concatenate([v.reshape(wide, -1) for v in vectors], 1)]
  transfers between devices with their start and end apart: 40 -> 39, of which waited for: 16 -> 17; matrix products, arithmetic and copies ran while one was open for 31% -> 13% of each run, Pallas kernels for 9% -> 41%
where the time goes in v3:
time: 539 us; the launch traced here: 530 us
  Pallas kernels  274 us (51%)
  waiting for transfers between devices  134 us (25%)
  other arithmetic  60.3 us (11%)
  starting transfers between devices  32.4 us (6%)
  local copies, waits for them, and re-layouts  28 us (5%)
    ppermute x39, waiting for transfers between devices, partner(): return lax.ppermute(x, axis, [(i, i ^ bit) for i in range(count)])  134 us
    pallas_call x11, Pallas kernels, token_call(): pl.pallas_call(run, grid_spec=pltpu.PrefetchScalarGridSpec(num_scalar_pre...  104 us
    pallas_call x4, Pallas kernels, attend_back(): pl.pallas_call(functools.partial(backward_kernel, parts=len(q[0]), skippe...  77.9 us
    pallas_call x2, Pallas kernels, attend(): pl.pallas_call(functools.partial(forward_kernel, parts=len(q[0]), skipped...  43.3 us
    convert_element_type x20, other arithmetic, total(): return value.astype(BF)  34.3 us
    ppermute x39, starting transfers between devices, partner(): return lax.ppermute(x, axis, [(i, i ^ bit) for i in range(count)])  32.4 us
    pallas_call x3, Pallas kernels, weight_grads(): pl.pallas_call(kernel, grid_spec=pltpu.PrefetchScalarGridSpec(num_scalar_...  28.5 us
    dynamic_slice x4, local copies, waits for them, and re-layouts, pick(): return lax.dynamic_slice_in_dim(x, index * half, half, 0)  12.1 us
  transfers between devices with their start and end apart: 39, of which 17 were waited for; matrix products, arithmetic and copies ran while one was open for 13% of the time, Pallas kernels for 41%

profile of v3, /device:TPU:0, one launch (start us, length us, event | category | flops | bytes accessed | tf_op | source)
XLA Modules:
  0.0 529.5 jit_solution(13438031048962755412)
XLA Ops:
  1.5 3.0 collective-permute-start.1
  4.5 2.1 dynamic-slice_bitcast_fusion.2
  7.6 1.9 collective-permute-start.2
  11.8 4.3 shard_map.428
  16.1 5.4 %shard_map.424 = bf16[512,2304]{1,0:T(8,128)(2,1)} custom-call(s32[1]{0:T(128)} %bitcast._, bf16[2,512,768]{2,1,0:T(8,128)(2,1)} %refs_0_.5, bf16[768,2304]{1,0:T(8,128)(2,1)} %refs_4_.9, f32[2304]{0:T(1024)} %pad_maximum_fusion.13.refs_2_), custom_call_target="tpu_custom_call" | custom-call | flops 3623878656 | bytes 7480320 | tf_op jit(solution)/shard_map/pallas_call | solution.py:524
  21.8 5.4 %collective-permute-done.refs_0_.refs_2_.refs_1_ = bf16[512,768]{1,0:T(8,128)(2,1)S(1)} collective-permute-done((bf16[512,768]{1,0:T(8,128)(2,1)}, bf16[512,768]{1,0:T(8,128)(2,1)S(1)}, u32[]{:S(2)}, u32[]{:S(2)}) %collective-permute-start) | collective-permute-done | bytes 786464 | tf_op jit(solution)/shard_map/ppermute | solution.py:723
  28.1 5.4 %shard_map.425 = bf16[512,2304]{1,0:T(8,128)(2,1)} custom-call(s32[1]{0:T(128)} %bitcast._, bf16[512,768]{1,0:T(8,128)(2,1)} %copy-done.14, bf16[768,2304]{1,0:T(8,128)(2,1)} %refs_4_.9, f32[2304]{0:T(1024)} %pad_maximum_fusion.13.refs_2_), custom_call_target="tpu_custom_call" | custom-call | flops 3623878656 | bytes 6693888 | tf_op jit(solution)/shard_map/pallas_call | solution.py:524
  33.5 20.4 %shard_map.426 = (bf16[1,1024,768]{2,1,0:T(8,128)(2,1)S(1)}, f32[1,1024,128]{2,1,0:T(8,128)S(1)}) custom-call(s32[1]{0:T(128)} %bitcast.1.refs_0_, bf16[1,512,2304]{2,1,0:T(8,128)(2,1)S(1)} %bitcast.39, bf16[1,512,2304]{2,1,0:T(8,128)(2,1)} %bitcast.66, bf16[1,512,2304]{2,1,0:T(8,128)(2,1)S(1)} %bitcast.40, bf16[1,512,2304]{2,1,0:T(8,128)(2,1)} %bitcast.67, ...), custom_call_target="tpu_custom_call" | custom-call | flops 20132659200 | bytes 6291456 | tf_op jit(solution)/shard_map/pallas_call | solution.py:231
  55.0 8.6 %shard_map.427 = (f32[1024,768]{1,0:T(8,128)}, f32[1024,128]{1,0:T(8,128)}, bf16[1024,768]{1,0:T(8,128)(2,1)}, bf16[1024,768]{1,0:T(8,128)(2,1)}) custom-call(s32[1]{0:T(128)} %bitcast._, bf16[1024,768]{1,0:T(8,128)(2,1)} %bitcast.42, bf16[2,512,768]{2,1,0:T(8,128)(2,1)} %refs_0_.5, bf16[512,768]{1,0:T(8,128)(2,1)} %copy-done.14, bf16[768,768]{1,0:T(8,128)(2,1)} %refs_6_.5, ...), custom_call_target="tpu_custom_call" | custom-call | flops 2415919104 | bytes 13119488 | tf_op jit(solution)/shard_map/pallas_call | solution.py:524
  66.1 4.4 shard_map.429
  70.4 23.0 %shard_map.430 = (bf16[1,1024,768]{2,1,0:T(8,128)(2,1)S(1)}, f32[1,1024,128]{2,1,0:T(8,128)S(1)}) custom-call(s32[1]{0:T(128)} %bitcast.1.refs_0_, bf16[1,512,768]{2,1,0:T(8,128)(2,1)S(1)} %get-tuple-element.131.refs_1_, bf16[1,512,768]{2,1,0:T(8,128)(2,1)S(1)} %get-tuple-element.130.refs_2_, bf16[1,512,1536]{2,1,0:T(8,128)(2,1)S(1)} %bitcast.48, ...), custom_call_target="tpu_custom_call" | custom-call | flops 20132659200 | bytes 6291456 | tf_op jit(solution)/shard_map/pallas_call | solution.py:231
  95.4 45.0 %shard_map.431 = (bf16[2,512,768]{2,1,0:T(8,128)(2,1)}, bf16[512,768]{1,0:T(8,128)(2,1)}, bf16[1024,3072]{1,0:T(8,128)(2,1)}, bf16[1024,768]{1,0:T(8,128)(2,1)},...) custom-call(s32[1]{0:T(128)} %bitcast._, ...), custom_call_target="tpu_custom_call" | custom-call | flops 21743271936 | bytes 42504192 | tf_op jit(solution)/shard_map/pallas_call | solution.py:524
  141.8 8.7 %shard_map.433 = bf16[3072,768]{1,0:T(8,128)(2,1)} custom-call(s32[1]{0:T(128)} %bitcast._, bf16[1024,3072]{1,0:T(8,128)(2,1)} %get-tuple-element.81.left_ref, bf16[1024,768]{1,0:T(8,128)(2,1)S(1)} %copy-done.27), custom_call_target="tpu_custom_call" | custom-call | flops 4831838208 | bytes 12582912 | tf_op jit(solution)/shard_map/pallas_call | solution.py:685
  150.6 3.4 constant_dynamic-slice_fusion.3.refs_5_
  154.0 10.8 %shard_map.434 = bf16[768,3968]{1,0:T(8,128)(2,1)} custom-call(s32[1]{0:T(128)} %bitcast._, bf16[1024,768]{1,0:T(8,128)(2,1)S(1)} %copy-done.25, bf16[1024,3072]{1,0:T(8,128)(2,1)} %get-tuple-element.84.refs_1_, bf16[1024,768]{1,0:T(8,128)(2,1)S(1)} %bitcast.51, bf16[1024,768]{1,0:T(8,128)(2,1)S(1)} %copy-done.26, f32[768,128]{1,0:T(8,128)S(1)} %copy-done.28, ...), custom_call_target="tpu_custom_call" | custom-call | flops 6241124352 | bytes 17104896 | tf_op jit(solution)/shard_map/pallas_call | solution.py:651
  164.8 3.7 constant_dynamic-slice_fusion.2.refs_13_
  169.1 2.1 add_convert_fusion.2.refs_12_
  171.2 2.0 collective-permute-start.7
  173.1 21.9 %shard_map.435 = (bf16[1,1024,768]{2,1,0:T(8,128)(2,1)S(1)}, bf16[1,1024,768]{2,1,0:T(8,128)(2,1)}, bf16[1,1024,768]{2,1,0:T(8,128)(2,1)}) custom-call(s32[1]{0:T(128)} %bitcast.1.refs_0_, bf16[1,512,768]{2,1,0:T(8,128)(2,1)S(1)} %get-tuple-element.131.refs_1_, bf16[1,512,768]{2,1,0:T(8,128)(2,1)S(1)} %get-tuple-element.130.refs_2_, ...), custom_call_target="tpu_custom_call" | custom-call | flops 16357785600 | bytes 6291456 | tf_op jit(solution)/shard_map/pallas_call | solution.py:263
  195.1 2.4 add_convert_fusion.refs_15_
  199.1 14.9 %collective-permute-done.7 = bf16[768,768]{1,0:T(8,128)(2,1)S(1)} collective-permute-done((bf16[768,768]{1,0:T(8,128)(2,1)S(1)}, bf16[768,768]{1,0:T(8,128)(2,1)S(1)}, u32[]{:S(2)}, u32[]{:S(2)}) %collective-permute-start.7) | collective-permute-done | bytes 1179680 | tf_op jit(solution)/shard_map/ppermute | solution.py:723
  214.0 2.0 add_convert_fusion.6.refs_7_
  217.6 21.9 %shard_map.436 = (bf16[1,1024,768]{2,1,0:T(8,128)(2,1)S(1)}, bf16[1,1024,768]{2,1,0:T(8,128)(2,1)}, bf16[1,1024,768]{2,1,0:T(8,128)(2,1)}) custom-call(s32[1]{0:T(128)} %bitcast.1.refs_0_, bf16[1,512,768]{2,1,0:T(8,128)(2,1)S(1)} %copy-done.7, bf16[1,512,768]{2,1,0:T(8,128)(2,1)S(1)} %copy-done.5, ...), custom_call_target="tpu_custom_call", output_to_operand_aliasing={{0}: (12, {}), {1}: (13, {}), {2}: (14, {})} | custom-call | flops 16357785600 | bytes 6291456 | tf_op jit(solution)/shard_map/pallas_call | solution.py:263
  239.6 4.9 shard_map.445.refs_3_
  248.3 1.9 shard_map.432
  250.2 4.4 shard_map.446.__
  254.6 8.7 %collective-permute-done.18.got_ref = bf16[512,768]{1,0:T(8,128)(2,1)} collective-permute-done((bf16[512,768]{1,0:T(8,128)(2,1)}, bf16[512,768]{1,0:T(8,128)(2,1)}, u32[]{:S(2)}, u32[]{:S(2)}) %collective-permute-start.18) | collective-permute-done | bytes 786464 | tf_op jit(solution)/shard_map/ppermute | solution.py:723
  263.3 2.2 shard_map.447
  266.9 2.7 collective-permute-start.14
  269.6 2.1 add_convert_fusion.4.refs_8_
  272.6 10.2 %shard_map.437 = (f32[1024,768]{1,0:T(8,128)}, bf16[1024,768]{1,0:T(8,128)(2,1)}, bf16[1024,768]{1,0:T(8,128)(2,1)}, f32[768,128]{1,0:T(8,128)}) custom-call(s32[1]{0:T(128)} %bitcast._, bf16[1024,768]{1,0:T(8,128)(2,1)} %bitcast.31, f32[1024,768]{1,0:T(8,128)} %get-tuple-element.91.refs_1_, f32[1024,768]{1,0:T(8,128)} %get-tuple-element.76.refs_1_.refs_2_, ...), custom_call_target="tpu_custom_call" | custom-call | flops 2415919104 | bytes 17435648 | tf_op jit(solution)/shard_map/pallas_call | solution.py:524
  283.9 10.2 %shard_map.438 = bf16[768,3200]{1,0:T(8,128)(2,1)} custom-call(s32[1]{0:T(128)} %bitcast._, bf16[1024,768]{1,0:T(8,128)(2,1)S(1)} %copy-done.24, bf16[1024,768]{1,0:T(8,128)(2,1)S(1)} %bitcast.32, bf16[2,512,768]{2,1,0:T(8,128)(2,1)S(1)} %copy-done.9, bf16[512,768]{1,0:T(8,128)(2,1)S(1)} %copy-done.17, bf16[1024,768]{1,0:T(8,128)(2,1)} %bitcast.54, ...), custom_call_target="tpu_custom_call" | custom-call | flops 5033164800 | bytes 16711680 | tf_op jit(solution)/shard_map/pallas_call | solution.py:651
  294.1 3.4 constant_dynamic-slice_fusion.1.refs_14_
  300.6 1.7 add_convert_fusion.9.refs_13_
  302.9 6.0 %collective-permute-done.36 = bf16[192,768]{1,0:T(8,128)(2,1)S(1)} collective-permute-done((bf16[192,768]{1,0:T(8,128)(2,1)S(1)}, bf16[192,768]{1,0:T(8,128)(2,1)S(1)}, u32[]{:S(2)}, u32[]{:S(2)}) %collective-permute-start.36) | collective-permute-done | bytes 294944 | tf_op jit(solution)/shard_map/ppermute | solution.py:723
  309.5 7.1 %collective-permute-done.12 = bf16[48,3968]{1,0:T(8,128)(2,1)S(1)} collective-permute-done((bf16[48,3968]{1,0:T(8,128)(2,1)S(1)}, bf16[48,3968]{1,0:T(8,128)(2,1)S(1)}, u32[]{:S(2)}, u32[]{:S(2)}) %collective-permute-start.12) | collective-permute-done | bytes 380960 | tf_op jit(solution)/shard_map/ppermute | solution.py:723
  316.6 1.8 fusion.9.refs_16_
  318.8 17.2 %shard_map.439 = (bf16[1,1024,768]{2,1,0:T(8,128)(2,1)S(1)}, bf16[1,1024,768]{2,1,0:T(8,128)(2,1)S(1)}, bf16[1,1024,768]{2,1,0:T(8,128)(2,1)}) custom-call(s32[1]{0:T(128)} %bitcast.1.refs_0_, bf16[1,512,2304]{2,1,0:T(8,128)(2,1)} %bitcast.33, bf16[1,512,2304]{2,1,0:T(8,128)(2,1)} %bitcast.69, bf16[1,512,2304]{2,1,0:T(8,128)(2,1)} %bitcast.34, ...), custom_call_target="tpu_custom_call" | custom-call | flops 16357785600 | bytes 6291456 | tf_op jit(solution)/shard_map/pallas_call | solution.py:263
  336.0 2.0 collective-permute-done.15
  338.0 1.9 add_convert_fusion.8.refs_6_
  340.4 9.3 %collective-permute-done.33 = bf16[48,3968]{1,0:T(8,128)(2,1)S(1)} collective-permute-done((bf16[48,3968]{1,0:T(8,128)(2,1)S(1)}, bf16[48,3968]{1,0:T(8,128)(2,1)S(1)}, u32[]{:S(2)}, u32[]{:S(2)}) %collective-permute-start.33) | collective-permute-done | bytes 380960 | tf_op jit(solution)/shard_map/ppermute | solution.py:723
  350.9 2.7 add_convert_fusion.1.refs_17_
  355.2 16.9 %shard_map.440 = (bf16[1,1024,768]{2,1,0:T(8,128)(2,1)S(1)}, bf16[1,1024,768]{2,1,0:T(8,128)(2,1)S(1)}, bf16[1,1024,768]{2,1,0:T(8,128)(2,1)}) custom-call(s32[1]{0:T(128)} %bitcast.1.refs_0_, bf16[1,512,2304]{2,1,0:T(8,128)(2,1)} %bitcast.36, bf16[1,512,2304]{2,1,0:T(8,128)(2,1)} %bitcast.72, ...), custom_call_target="tpu_custom_call", output_to_operand_aliasing={{0}: (12, {}), {1}: (13, {}), {2}: (14, {})} | custom-call | flops 16357785600 | bytes 6291456 | tf_op jit(solution)/shard_map/pallas_call | solution.py:263
  373.7 19.5 %collective-permute-done.16 = bf16[192,3200]{1,0:T(8,128)(2,1)S(1)} collective-permute-done((bf16[192,3200]{1,0:T(8,128)(2,1)S(1)}, bf16[192,3200]{1,0:T(8,128)(2,1)S(1)}, u32[]{:S(2)}, u32[]{:S(2)}) %collective-permute-start.16) | collective-permute-done | bytes 1228832 | tf_op jit(solution)/shard_map/ppermute | solution.py:723
  393.2 2.1 add_convert_fusion.5.refs_7_
  395.4 7.5 %shard_map.441 = bf16[768,2432]{1,0:T(8,128)(2,1)} custom-call(s32[1]{0:T(128)} %bitcast._, bf16[2,512,768]{2,1,0:T(8,128)(2,1)S(1)} %copy-done.10, bf16[512,768]{1,0:T(8,128)(2,1)S(1)} %copy-done.15, bf16[1024,768]{1,0:T(8,128)(2,1)S(1)} %bitcast.25, bf16[1024,768]{1,0:T(8,128)(2,1)} %bitcast.28, bf16[1024,768]{1,0:T(8,128)(2,1)} %bitcast.58, ...), custom_call_target="tpu_custom_call" | custom-call | flops 3825205248 | bytes 10813440 | tf_op jit(solution)/shard_map/pallas_call | solution.py:651
  404.7 2.7 maximum_convert_fusion
  408.6 5.8 %shard_map.442.refs_5_ = bf16[512,768]{1,0:T(8,128)(2,1)} custom-call(s32[1]{0:T(128)} %bitcast._, bf16[1024,768]{1,0:T(8,128)(2,1)} %bitcast.26, bf16[1024,768]{1,0:T(8,128)(2,1)} %bitcast.29, bf16[1024,768]{1,0:T(8,128)(2,1)} %bitcast.59, f32[1024,768]{1,0:T(8,128)} %get-tuple-element.105.refs_3_, bf16[768,2304]{1,0:T(8,128)(2,1)} %refs_4_.9, ...), custom_call_target="tpu_custom_call" | custom-call | flops 1811939328 | bytes 12189696 | tf_op jit(solution)/shard_map/pallas_call | solution.py:524
  415.2 6.0 %shard_map.443.__ = f32[2,512,768]{2,1,0:T(8,128)} custom-call(s32[1]{0:T(128)} %bitcast._, bf16[1024,768]{1,0:T(8,128)(2,1)} %bitcast.27, bf16[1024,768]{1,0:T(8,128)(2,1)} %bitcast.30, bf16[1024,768]{1,0:T(8,128)(2,1)} %bitcast.60, f32[1024,768]{1,0:T(8,128)} %get-tuple-element.105.refs_3_, bf16[768,2304]{1,0:T(8,128)(2,1)} %refs_4_.9, ...), custom_call_target="tpu_custom_call" | custom-call | flops 1811939328 | bytes 14548992 | tf_op jit(solution)/shard_map/pallas_call | solution.py:524
  421.3 2.1 broadcast_select_fusion.1
  428.9 2.8 fusion
  431.7 2.1 collective-permute-done.28
  435.2 1.8 collective-permute-start.29
  437.1 23.3 %collective-permute-done.20 = bf16[192,2432]{1,0:T(8,128)(2,1)S(1)} collective-permute-done((bf16[192,2432]{1,0:T(8,128)(2,1)S(1)}, bf16[192,2432]{1,0:T(8,128)(2,1)S(1)}, u32[]{:S(2)}, u32[]{:S(2)}) %collective-permute-start.20) | collective-permute-done | bytes 933920 | tf_op jit(solution)/shard_map/ppermute | solution.py:723
  464.3 9.5 %collective-permute-done.21 = bf16[96,2432]{1,0:T(8,128)(2,1)S(1)} collective-permute-done((bf16[96,2432]{1,0:T(8,128)(2,1)S(1)}, bf16[96,2432]{1,0:T(8,128)(2,1)S(1)}, u32[]{:S(2)}, u32[]{:S(2)}) %collective-permute-start.21) | collective-permute-done | bytes 466976 | tf_op jit(solution)/shard_map/ppermute | solution.py:723
  475.7 5.6 %collective-permute-done.22 = bf16[48,2432]{1,0:T(8,128)(2,1)S(1)} collective-permute-done((bf16[48,2432]{1,0:T(8,128)(2,1)S(1)}, bf16[48,2432]{1,0:T(8,128)(2,1)S(1)}, u32[]{:S(2)}, u32[]{:S(2)}) %collective-permute-start.22) | collective-permute-done | bytes 233504 | tf_op jit(solution)/shard_map/ppermute | solution.py:723
  482.5 1.8 collective-permute-start.23
  485.0 8.8 %collective-permute-done.23 = bf16[48,2432]{1,0:T(8,128)(2,1)S(1)} collective-permute-done((bf16[48,2432]{1,0:T(8,128)(2,1)S(1)}, bf16[48,2432]{1,0:T(8,128)(2,1)S(1)}, u32[]{:S(2)}, u32[]{:S(2)}) %collective-permute-start.23) | collective-permute-done | bytes 233504 | tf_op jit(solution)/shard_map/ppermute | solution.py:723
  495.2 2.7 collective-permute-done.31
  498.1 3.9 collective-permute-done.24
  507.8 2.2 shard_map.444
  510.0 4.1 collective-permute-done.25
  516.4 1.7 broadcast_select_fusion.3
  525.7 2.0 fusion.2
  (220 shorter events, 70.1 us)
Async XLA Ops:
  1.5 8.0 %copy-start.53 = (bf16[2,512,768]{2,1,0:T(8,128)(2,1)S(1)}, bf16[2,512,768]{2,1,0:T(8,128)(2,1)}, u32[]{:S(2)}) copy-start(bf16[2,512,768]{2,1,0:T(8,128)(2,1)} %refs_2_.4) | copy-start | bytes 4718596
  1.5 20.0 %collective-permute-start.1 = (s32[512]{0:T(512)S(1)}, s32[512]{0:T(512)S(1)}, u32[]{:S(2)}, u32[]{:S(2)}) collective-permute-start(s32[512]{0:T(512)S(1)} %bitcast.63), channel_id=1, source_target_pairs={{0,16},{16,0},{1,17},{17,1},{2,18},{18,2},{3,19},{19,3},{4,20},{20... | collective-permute-start | bytes 6152 | tf_op jit(solution)/shard_map/ppermute | solution.py:723
  6.6 20.7 %collective-permute-start = (bf16[512,768]{1,0:T(8,128)(2,1)}, bf16[512,768]{1,0:T(8,128)(2,1)S(1)}, u32[]{:S(2)}, u32[]{:S(2)}) collective-permute-start(bf16[512,768]{1,0:T(8,128)(2,1)} %dynamic-slice_bitcast_fusion.2), channel_id=1, source_target_pairs={{0,16},{16,0},{1,17},{17,1},{2,18},{18,2},{3,19},{19,3},{4,20},{20... | collective-permute-start | bytes 2359304 | tf_op jit(solution)/shard_map/ppermute | solution.py:723
  7.6 57.5 %collective-permute-start.2 = (bf16[512,768]{1,0:T(8,128)(2,1)}, bf16[512,768]{1,0:T(8,128)(2,1)S(1)}, u32[]{:S(2)}, u32[]{:S(2)}) collective-permute-start(bf16[512,768]{1,0:T(8,128)(2,1)} %dynamic-slice_bitcast_fusion.1), channel_id=1, source_target_pairs={{0,16},{16,0},{1,17},{17,1},{2,18},{18,2},{3,19},{19,3},{4,20},{20... | collective-permute-start | bytes 2359304 | tf_op jit(solution)/shard_map/ppermute | solution.py:723
  10.5 85.0 %collective-permute-start.3 = (bf16[512,768]{1,0:T(8,128)(2,1)}, bf16[512,768]{1,0:T(8,128)(2,1)}, u32[]{:S(2)}, u32[]{:S(2)}) collective-permute-start(bf16[512,768]{1,0:T(8,128)(2,1)} %dynamic-slice_bitcast_fusion), channel_id=1, source_target_pairs={{0,16},{16,0},{1,17},{17,1},{2,18},{18,2},{3,19},{19,3},{4,20},{20... | collective-permute-start | bytes 2359304 | tf_op jit(solution)/shard_map/ppermute | solution.py:723
  21.8 48.6 %copy-start.11 = (bf16[1,1024,128]{2,1,0:T(8,128)(2,1)}, bf16[1,1024,128]{2,1,0:T(8,128)(2,1)S(1)}, u32[]{:S(2)}) copy-start(bf16[1,1024,128]{2,1,0:T(8,128)(2,1)S(1)} %get-tuple-element.149.refs_7_.refs_9_) | copy-start | bytes 786436
  21.8 11.7 %copy-start.19 = (bf16[512,2304]{1,0:T(8,128)(2,1)S(1)}, bf16[512,2304]{1,0:T(8,128)(2,1)}, u32[]{:S(2)}) copy-start(bf16[512,2304]{1,0:T(8,128)(2,1)} %shard_map.424) | copy-start | bytes 7077892
  55.0 8.6 %copy-start.29 = (f32[1,1024,128]{2,1,0:T(8,128)}, f32[1,1024,128]{2,1,0:T(8,128)S(1)}, u32[]{:S(2)}) copy-start(f32[1,1024,128]{2,1,0:T(8,128)S(1)} %get-tuple-element.94.refs_11_) | copy-start | bytes 1572868
  65.1 108.0 %copy-start.4 = (bf16[1,512,768]{2,1,0:T(8,128)(2,1)}, bf16[1,512,768]{2,1,0:T(8,128)(2,1)S(1)}, u32[]{:S(2)}) copy-start(bf16[1,512,768]{2,1,0:T(8,128)(2,1)S(1)} %get-tuple-element.130.refs_2_) | copy-start | bytes 2359300
  65.1 108.0 %copy-start.6 = (bf16[1,512,768]{2,1,0:T(8,128)(2,1)}, bf16[1,512,768]{2,1,0:T(8,128)(2,1)S(1)}, u32[]{:S(2)}) copy-start(bf16[1,512,768]{2,1,0:T(8,128)(2,1)S(1)} %get-tuple-element.131.refs_1_) | copy-start | bytes 2359300
  141.8 12.1 %copy-start.28 = (f32[768,128]{1,0:T(8,128)S(1)}, f32[768,128]{1,0:T(8,128)}, u32[]{:S(2)}) copy-start(f32[768,128]{1,0:T(8,128)} %get-tuple-element.86.refs_4_) | copy-start | bytes 1179652
  153.9 15.1 %collective-permute-start.5 = (bf16[1536,768]{1,0:T(8,128)(2,1)}, bf16[1536,768]{1,0:T(8,128)(2,1)}, u32[]{:S(2)}, u32[]{:S(2)}) collective-permute-start(bf16[1536,768]{1,0:T(8,128)(2,1)} %constant_dynamic-slice_fusion.3.refs_5_), channel_id=1, source_target_pairs={{0,1},{1,0},{2,3},{3,2},{4,5},{5,4},{6,7},{7,6},{8,9},{9,8},{10,11... | collective-permute-start | bytes 7077896 | tf_op jit(solution)/shard_map/ppermute | solution.py:723
  168.5 26.6 %collective-permute-start.6 = (bf16[384,3968]{1,0:T(8,128)(2,1)}, bf16[384,3968]{1,0:T(8,128)(2,1)}, u32[]{:S(2)}, u32[]{:S(2)}) collective-permute-start(bf16[384,3968]{1,0:T(8,128)(2,1)} %constant_dynamic-slice_fusion.2.refs_13_), channel_id=1, source_target_pairs={{0,1},{1,0},{2,3},{3,2},{4,5},{5,4},{6,7},{7,6},{8,9},{9,8},{10,11... | collective-permute-start | bytes 9142280 | tf_op jit(solution)/shard_map/ppermute | solution.py:723
  169.0 79.3 %collective-permute-start.4 = (bf16[512,768]{1,0:T(8,128)(2,1)}, bf16[512,768]{1,0:T(8,128)(2,1)}, u32[]{:S(2)}, u32[]{:S(2)}) collective-permute-start(bf16[512,768]{1,0:T(8,128)(2,1)} %get-tuple-element.77), channel_id=1, source_target_pairs={{0,16},{16,0},{1,17},{17,1},{2,18},{18,2},{3,19},{19,3},{4,20},{20... | collective-permute-start | bytes 2359304 | tf_op jit(solution)/shard_map/ppermute | solution.py:723
  171.2 42.8 %collective-permute-start.7 = (bf16[768,768]{1,0:T(8,128)(2,1)S(1)}, bf16[768,768]{1,0:T(8,128)(2,1)S(1)}, u32[]{:S(2)}, u32[]{:S(2)}) collective-permute-start(bf16[768,768]{1,0:T(8,128)(2,1)S(1)} %add_convert_fusion.2.refs_12_), channel_id=1, source_target_pairs={{0,16},{16,0},{1,17},{17,1},{2,18},{18,2},{3,19},{19,3},{4,20},{20... | collective-permute-start | bytes 3538952 | tf_op jit(solution)/shard_map/ppermute | solution.py:723
  197.5 20.1 %copy-start.5 = (bf16[1,512,768]{2,1,0:T(8,128)(2,1)S(1)}, bf16[1,512,768]{2,1,0:T(8,128)(2,1)}, u32[]{:S(2)}) copy-start(bf16[1,512,768]{2,1,0:T(8,128)(2,1)} %copy-done.4) | copy-start | bytes 2359300
  197.5 20.1 %copy-start.7 = (bf16[1,512,768]{2,1,0:T(8,128)(2,1)S(1)}, bf16[1,512,768]{2,1,0:T(8,128)(2,1)}, u32[]{:S(2)}) copy-start(bf16[1,512,768]{2,1,0:T(8,128)(2,1)} %copy-done.6) | copy-start | bytes 2359300
  197.5 72.1 %collective-permute-start.8 = (bf16[192,3968]{1,0:T(8,128)(2,1)S(1)}, bf16[192,3968]{1,0:T(8,128)(2,1)}, u32[]{:S(2)}, u32[]{:S(2)}) collective-permute-start(bf16[192,3968]{1,0:T(8,128)(2,1)S(1)} %add_convert_fusion.refs_15_), channel_id=1, source_target_pairs={{0,2},{2,0},{1,3},{3,1},{4,6},{6,4},{5,7},{7,5},{8,10},{10,8},{9,1... | collective-permute-start | bytes 4571144 | tf_op jit(solution)/shard_map/ppermute | solution.py:723
  214.0 25.6 %copy-start.50 = (bf16[768,768]{1,0:T(8,128)(2,1)}, bf16[768,768]{1,0:T(8,128)(2,1)S(1)}, u32[]{:S(2)}) copy-start(bf16[768,768]{1,0:T(8,128)(2,1)S(1)} %collective-permute-done.7) | copy-start | bytes 3538948
  216.0 23.5 %copy-start.47 = (bf16[384,768]{1,0:T(8,128)(2,1)}, bf16[384,768]{1,0:T(8,128)(2,1)S(1)}, u32[]{:S(2)}) copy-start(bf16[384,768]{1,0:T(8,128)(2,1)S(1)} %add_convert_fusion.6.refs_7_) | copy-start | bytes 1769476
  216.0 29.0 %collective-permute-start.9 = (bf16[384,768]{1,0:T(8,128)(2,1)S(1)}, bf16[384,768]{1,0:T(8,128)(2,1)S(1)}, u32[]{:S(2)}, u32[]{:S(2)}) collective-permute-start(bf16[384,768]{1,0:T(8,128)(2,1)S(1)} %add_convert_fusion.6.refs_7_), channel_id=1, source_target_pairs={{0,2},{2,0},{1,3},{3,1},{4,6},{6,4},{5,7},{7,5},{8,10},{10,8},{9,1... | collective-permute-start | bytes 1769480 | tf_op jit(solution)/shard_map/ppermute | solution.py:723
  244.5 18.8 %collective-permute-start.18 = (bf16[512,768]{1,0:T(8,128)(2,1)}, bf16[512,768]{1,0:T(8,128)(2,1)}, u32[]{:S(2)}, u32[]{:S(2)}) collective-permute-start(bf16[512,768]{1,0:T(8,128)(2,1)} %shard_map.445.refs_3_), channel_id=1, source_target_pairs={{0,16},{16,0},{1,17},{17,1},{2,18},{18,2},{3,19},{19,3},{4,20},{20... | collective-permute-start | bytes 2359304 | tf_op jit(solution)/shard_map/ppermute | solution.py:723
  245.0 20.5 %copy-start.51 = (bf16[384,768]{1,0:T(8,128)(2,1)}, bf16[384,768]{1,0:T(8,128)(2,1)S(1)}, u32[]{:S(2)}) copy-start(bf16[384,768]{1,0:T(8,128)(2,1)S(1)} %collective-permute-done.9) | copy-start | bytes 1769476
  246.6 18.8 %collective-permute-start.11 = (bf16[192,768]{1,0:T(8,128)(2,1)S(1)}, bf16[192,768]{1,0:T(8,128)(2,1)S(1)}, u32[]{:S(2)}, u32[]{:S(2)}) collective-permute-start(bf16[192,768]{1,0:T(8,128)(2,1)S(1)} %add_convert_fusion.13.refs_12_), channel_id=1, source_target_pairs={{0,4},{4,0},{1,5},{5,1},{2,6},{6,2},{3,7},{7,3},{8,12},{12,8},{9,1... | collective-permute-start | bytes 884744 | tf_op jit(solution)/shard_map/ppermute | solution.py:723
  266.9 30.5 %collective-permute-start.14 = (bf16[192,768]{1,0:T(8,128)(2,1)S(1)}, bf16[192,768]{1,0:T(8,128)(2,1)S(1)}, u32[]{:S(2)}, u32[]{:S(2)}) collective-permute-start(bf16[192,768]{1,0:T(8,128)(2,1)S(1)} %fusion.7.refs_15_), channel_id=1, source_target_pairs={{0,8},{8,0},{1,9},{9,1},{2,10},{10,2},{3,11},{11,3},{4,12},{12,4},... | collective-permute-start | bytes 884744 | tf_op jit(solution)/shard_map/ppermute | solution.py:723
  271.7 28.9 %collective-permute-start.10 = (bf16[96,3968]{1,0:T(8,128)(2,1)S(1)}, bf16[96,3968]{1,0:T(8,128)(2,1)}, u32[]{:S(2)}, u32[]{:S(2)}) collective-permute-start(bf16[96,3968]{1,0:T(8,128)(2,1)S(1)} %add_convert_fusion.4.refs_8_), channel_id=1, source_target_pairs={{0,16},{16,0},{1,17},{17,1},{2,18},{18,2},{3,19},{19,3},{4,20},{20... | collective-permute-start | bytes 2285576 | tf_op jit(solution)/shard_map/ppermute | solution.py:723
  272.6 10.2 %copy-start.3 = (bf16[1,1024,768]{2,1,0:T(8,128)(2,1)S(1)}, bf16[1,1024,768]{2,1,0:T(8,128)(2,1)}, u32[]{:S(2)}) copy-start(bf16[1,1024,768]{2,1,0:T(8,128)(2,1)} %copy-done.2) | copy-start | bytes 4718596
  272.6 10.2 %copy-start.9 = (bf16[2,512,768]{2,1,0:T(8,128)(2,1)S(1)}, bf16[2,512,768]{2,1,0:T(8,128)(2,1)}, u32[]{:S(2)}) copy-start(bf16[2,512,768]{2,1,0:T(8,128)(2,1)} %refs_2_.5) | copy-start | bytes 4718596
  272.6 10.2 %copy-start.17 = (bf16[512,768]{1,0:T(8,128)(2,1)S(1)}, bf16[512,768]{1,0:T(8,128)(2,1)}, u32[]{:S(2)}) copy-start(bf16[512,768]{1,0:T(8,128)(2,1)} %copy-done.16) | copy-start | bytes 2359300
  272.6 10.3 %copy-start.24 = (bf16[1024,768]{1,0:T(8,128)(2,1)S(1)}, bf16[1024,768]{1,0:T(8,128)(2,1)}, u32[]{:S(2)}) copy-start(bf16[1024,768]{1,0:T(8,128)(2,1)} %get-tuple-element.74.refs_3_.refs_0_) | copy-start | bytes 4718596
  297.4 53.4 %collective-permute-start.13 = (bf16[384,3200]{1,0:T(8,128)(2,1)}, bf16[384,3200]{1,0:T(8,128)(2,1)S(1)}, u32[]{:S(2)}, u32[]{:S(2)}) collective-permute-start(bf16[384,3200]{1,0:T(8,128)(2,1)} %constant_dynamic-slice_fusion.1.refs_14_), channel_id=1, source_target_pairs={{0,1},{1,0},{2,3},{3,2},{4,5},{5,4},{6,7},{7,6},{8,9},{9,8},{10,11... | collective-permute-start | bytes 7372808 | tf_op jit(solution)/shard_map/ppermute | solution.py:723
  299.0 9.9 %collective-permute-start.36 = (bf16[192,768]{1,0:T(8,128)(2,1)S(1)}, bf16[192,768]{1,0:T(8,128)(2,1)S(1)}, u32[]{:S(2)}, u32[]{:S(2)}) collective-permute-start(bf16[192,768]{1,0:T(8,128)(2,1)S(1)} %add_convert_fusion.12.refs_5_), channel_id=1, source_target_pairs={{0,4},{4,0},{1,5},{5,1},{2,6},{6,2},{3,7},{7,3},{8,12},{12,8},{9,1... | collective-permute-start | bytes 884744 | tf_op jit(solution)/shard_map/ppermute | solution.py:723
  302.4 14.2 %collective-permute-start.12 = (bf16[48,3968]{1,0:T(8,128)(2,1)S(1)}, bf16[48,3968]{1,0:T(8,128)(2,1)S(1)}, u32[]{:S(2)}, u32[]{:S(2)}) collective-permute-start(bf16[48,3968]{1,0:T(8,128)(2,1)S(1)} %add_convert_fusion.9.refs_13_), channel_id=1, source_target_pairs={{0,4},{4,0},{1,5},{5,1},{2,6},{6,2},{3,7},{7,3},{8,12},{12,8},{9,1... | collective-permute-start | bytes 1142792 | tf_op jit(solution)/shard_map/ppermute | solution.py:723
  308.9 9.9 %copy-start.13 = (bf16[1,1024,128]{2,1,0:T(8,128)(2,1)S(1)}, bf16[1,1024,128]{2,1,0:T(8,128)(2,1)}, u32[]{:S(2)}) copy-start(bf16[1,1024,128]{2,1,0:T(8,128)(2,1)} %copy-done.11) | copy-start | bytes 786436
  308.9 9.9 %copy-start.30 = (f32[1,1024,128]{2,1,0:T(8,128)S(1)}, f32[1,1024,128]{2,1,0:T(8,128)}, u32[]{:S(2)}) copy-start(f32[1,1024,128]{2,1,0:T(8,128)} %copy-done.29) | copy-start | bytes 1572868
  309.0 31.0 %collective-permute-start.37 = (bf16[384,768]{1,0:T(8,128)(2,1)S(1)}, bf16[384,768]{1,0:T(8,128)(2,1)S(1)}, u32[]{:S(2)}, u32[]{:S(2)}) collective-permute-start(bf16[384,768]{1,0:T(8,128)(2,1)S(1)} %pad_maximum_fusion.8), channel_id=1, source_target_pairs={{0,2},{2,0},{1,3},{3,1},{4,6},{6,4},{5,7},{7,5},{8,10},{10,8},{9,1... | collective-permute-start | bytes 1769480 | tf_op jit(solution)/shard_map/ppermute | solution.py:723
  318.4 19.6 %collective-permute-start.15 = (bf16[48,3968]{1,0:T(8,128)(2,1)S(1)}, bf16[48,3968]{1,0:T(8,128)(2,1)S(1)}, u32[]{:S(2)}, u32[]{:S(2)}) collective-permute-start(bf16[48,3968]{1,0:T(8,128)(2,1)S(1)} %fusion.9.refs_16_), channel_id=1, source_target_pairs={{0,8},{8,0},{1,9},{9,1},{2,10},{10,2},{3,11},{11,3},{4,12},{12,4},... | collective-permute-start | bytes 1142792 | tf_op jit(solution)/shard_map/ppermute | solution.py:723
  339.9 9.8 %collective-permute-start.33 = (bf16[48,3968]{1,0:T(8,128)(2,1)S(1)}, bf16[48,3968]{1,0:T(8,128)(2,1)S(1)}, u32[]{:S(2)}, u32[]{:S(2)}) collective-permute-start(bf16[48,3968]{1,0:T(8,128)(2,1)S(1)} %add_convert_fusion.8.refs_6_), channel_id=1, source_target_pairs={{0,4},{4,0},{1,5},{5,1},{2,6},{6,2},{3,7},{7,3},{8,12},{12,8},{9,1... | collective-permute-start | bytes 1142792 | tf_op jit(solution)/shard_map/ppermute | solution.py:723
  340.3 10.1 %collective-permute-start.38 = (bf16[768,768]{1,0:T(8,128)(2,1)S(1)}, bf16[768,768]{1,0:T(8,128)(2,1)S(1)}, u32[]{:S(2)}, u32[]{:S(2)}) collective-permute-start(bf16[768,768]{1,0:T(8,128)(2,1)S(1)} %pad_maximum_fusion.4), channel_id=1, source_target_pairs={{0,1},{1,0},{2,3},{3,2},{4,5},{5,4},{6,7},{7,6},{8,9},{9,8},{10,11... | collective-permute-start | bytes 3538952 | tf_op jit(solution)/shard_map/ppermute | solution.py:723
  349.8 22.3 %collective-permute-start.34 = (bf16[96,3968]{1,0:T(8,128)(2,1)S(1)}, bf16[96,3968]{1,0:T(8,128)(2,1)S(1)}, u32[]{:S(2)}, u32[]{:S(2)}) collective-permute-start(bf16[96,3968]{1,0:T(8,128)(2,1)S(1)} %pad_maximum_fusion.6), channel_id=1, source_target_pairs={{0,2},{2,0},{1,3},{3,1},{4,6},{6,4},{5,7},{7,5},{8,10},{10,8},{9,1... | collective-permute-start | bytes 2285576 | tf_op jit(solution)/shard_map/ppermute | solution.py:723
  353.6 39.6 %collective-permute-start.16 = (bf16[192,3200]{1,0:T(8,128)(2,1)S(1)}, bf16[192,3200]{1,0:T(8,128)(2,1)S(1)}, u32[]{:S(2)}, u32[]{:S(2)}) collective-permute-start(bf16[192,3200]{1,0:T(8,128)(2,1)S(1)} %add_convert_fusion.1.refs_17_), channel_id=1, source_target_pairs={{0,2},{2,0},{1,3},{3,1},{4,6},{6,4},{5,7},{7,5},{8,10},{10,8},{9,1... | collective-permute-start | bytes 3686408 | tf_op jit(solution)/shard_map/ppermute | solution.py:723
  372.1 23.2 %copy-start = (bf16[1,1024,768]{2,1,0:T(8,128)(2,1)}, bf16[1,1024,768]{2,1,0:T(8,128)(2,1)S(1)}, u32[]{:S(2)}) copy-start(bf16[1,1024,768]{2,1,0:T(8,128)(2,1)S(1)} %get-tuple-element.102) | copy-start | bytes 4718596
  373.7 21.6 %copy-start.10 = (bf16[2,512,768]{2,1,0:T(8,128)(2,1)S(1)}, bf16[2,512,768]{2,1,0:T(8,128)(2,1)}, u32[]{:S(2)}) copy-start(bf16[2,512,768]{2,1,0:T(8,128)(2,1)} %refs_0_.5) | copy-start | bytes 4718596
  373.7 21.7 %copy-start.15 = (bf16[512,768]{1,0:T(8,128)(2,1)S(1)}, bf16[512,768]{1,0:T(8,128)(2,1)}, u32[]{:S(2)}) copy-start(bf16[512,768]{1,0:T(8,128)(2,1)} %copy-done.14) | copy-start | bytes 2359300
  373.7 47.5 %collective-permute-start.35 = (bf16[192,3968]{1,0:T(8,128)(2,1)S(1)}, bf16[192,3968]{1,0:T(8,128)(2,1)}, u32[]{:S(2)}, u32[]{:S(2)}) collective-permute-start(bf16[192,3968]{1,0:T(8,128)(2,1)S(1)} %pad_maximum_fusion.1), channel_id=1, source_target_pairs={{0,1},{1,0},{2,3},{3,2},{4,5},{5,4},{6,7},{7,6},{8,9},{9,8},{10,11... | collective-permute-start | bytes 4571144 | tf_op jit(solution)/shard_map/ppermute | solution.py:723
  393.2 9.7 %copy-start.48 = (bf16[192,3200]{1,0:T(8,128)(2,1)}, bf16[192,3200]{1,0:T(8,128)(2,1)S(1)}, u32[]{:S(2)}) copy-start(bf16[192,3200]{1,0:T(8,128)(2,1)S(1)} %collective-permute-done.16) | copy-start | bytes 3686404
  404.6 21.5 %collective-permute-start.19 = (bf16[384,2432]{1,0:T(8,128)(2,1)S(1)}, bf16[384,2432]{1,0:T(8,128)(2,1)}, u32[]{:S(2)}, u32[]{:S(2)}) collective-permute-start(bf16[384,2432]{1,0:T(8,128)(2,1)S(1)} %constant_dynamic-slice_fusion.refs_5_), channel_id=1, source_target_pairs={{0,1},{1,0},{2,3},{3,2},{4,5},{5,4},{6,7},{7,6},{8,9},{9,8},{10,11... | collective-permute-start | bytes 5603336 | tf_op jit(solution)/shard_map/ppermute | solution.py:723
  407.4 16.7 %collective-permute-start.27 = (bf16[96,3200]{1,0:T(8,128)(2,1)S(1)}, bf16[96,3200]{1,0:T(8,128)(2,1)S(1)}, u32[]{:S(2)}, u32[]{:S(2)}) collective-permute-start(bf16[96,3200]{1,0:T(8,128)(2,1)S(1)} %add_convert_fusion.5.refs_7_), channel_id=1, source_target_pairs={{0,16},{16,0},{1,17},{17,1},{2,18},{18,2},{3,19},{19,3},{4,20},{20... | collective-permute-start | bytes 1843208 | tf_op jit(solution)/shard_map/ppermute | solution.py:723
  414.4 6.9 %copy-start.35 = (bf16[96,3968]{1,0:T(8,128)(2,1)S(1)}, bf16[96,3968]{1,0:T(8,128)(2,1)}, u32[]{:S(2)}) copy-start(bf16[96,3968]{1,0:T(8,128)(2,1)} %copy-done.34) | copy-start | bytes 2285572
  414.4 6.9 %copy-start.37 = (bf16[96,3968]{1,0:T(8,128)(2,1)S(1)}, bf16[96,3968]{1,0:T(8,128)(2,1)}, u32[]{:S(2)}) copy-start(bf16[96,3968]{1,0:T(8,128)(2,1)} %copy-done.36) | copy-start | bytes 2285572
  414.4 93.4 %collective-permute-start.17 = (bf16[512,768]{1,0:T(8,128)(2,1)}, bf16[512,768]{1,0:T(8,128)(2,1)}, u32[]{:S(2)}, u32[]{:S(2)}) collective-permute-start(bf16[512,768]{1,0:T(8,128)(2,1)} %shard_map.442.refs_5_), channel_id=1, source_target_pairs={{0,16},{16,0},{1,17},{17,1},{2,18},{18,2},{3,19},{19,3},{4,20},{20... | collective-permute-start | bytes 2359304 | tf_op jit(solution)/shard_map/ppermute | solution.py:723
  425.4 8.4 %collective-permute-start.28 = (bf16[48,3200]{1,0:T(8,128)(2,1)S(1)}, bf16[48,3200]{1,0:T(8,128)(2,1)S(1)}, u32[]{:S(2)}, u32[]{:S(2)}) collective-permute-start(bf16[48,3200]{1,0:T(8,128)(2,1)S(1)} %add_convert_fusion.11), channel_id=1, source_target_pairs={{0,4},{4,0},{1,5},{5,1},{2,6},{6,2},{3,7},{7,3},{8,12},{12,8},{9,1... | collective-permute-start | bytes 921608 | tf_op jit(solution)/shard_map/ppermute | solution.py:723
  427.6 32.7 %collective-permute-start.20 = (bf16[192,2432]{1,0:T(8,128)(2,1)S(1)}, bf16[192,2432]{1,0:T(8,128)(2,1)S(1)}, u32[]{:S(2)}, u32[]{:S(2)}) collective-permute-start(bf16[192,2432]{1,0:T(8,128)(2,1)S(1)} %add_convert_fusion.3), channel_id=1, source_target_pairs={{0,16},{16,0},{1,17},{17,1},{2,18},{18,2},{3,19},{19,3},{4,20},{20... | collective-permute-start | bytes 2801672 | tf_op jit(solution)/shard_map/ppermute | solution.py:723
  435.2 27.0 %collective-permute-start.29 = (bf16[48,3200]{1,0:T(8,128)(2,1)S(1)}, bf16[48,3200]{1,0:T(8,128)(2,1)S(1)}, u32[]{:S(2)}, u32[]{:S(2)}) collective-permute-start(bf16[48,3200]{1,0:T(8,128)(2,1)S(1)} %fusion.8), channel_id=1, source_target_pairs={{0,8},{8,0},{1,9},{9,1},{2,10},{10,2},{3,11},{11,3},{4,12},{12,4},... | collective-permute-start | bytes 921608 | tf_op jit(solution)/shard_map/ppermute | solution.py:723
  461.7 12.2 %collective-permute-start.21 = (bf16[96,2432]{1,0:T(8,128)(2,1)S(1)}, bf16[96,2432]{1,0:T(8,128)(2,1)S(1)}, u32[]{:S(2)}, u32[]{:S(2)}) collective-permute-start(bf16[96,2432]{1,0:T(8,128)(2,1)S(1)} %add_convert_fusion.7), channel_id=1, source_target_pairs={{0,2},{2,0},{1,3},{3,1},{4,6},{6,4},{5,7},{7,5},{8,10},{10,8},{9,1... | collective-permute-start | bytes 1400840 | tf_op jit(solution)/shard_map/ppermute | solution.py:723
  463.7 12.0 %collective-permute-start.30 = (bf16[48,3200]{1,0:T(8,128)(2,1)S(1)}, bf16[48,3200]{1,0:T(8,128)(2,1)S(1)}, u32[]{:S(2)}, u32[]{:S(2)}) collective-permute-start(bf16[48,3200]{1,0:T(8,128)(2,1)S(1)} %add_convert_fusion.10), channel_id=1, source_target_pairs={{0,4},{4,0},{1,5},{5,1},{2,6},{6,2},{3,7},{7,3},{8,12},{12,8},{9,1... | collective-permute-start | bytes 921608 | tf_op jit(solution)/shard_map/ppermute | solution.py:723
  475.1 6.3 %collective-permute-start.22 = (bf16[48,2432]{1,0:T(8,128)(2,1)S(1)}, bf16[48,2432]{1,0:T(8,128)(2,1)S(1)}, u32[]{:S(2)}, u32[]{:S(2)}) collective-permute-start(bf16[48,2432]{1,0:T(8,128)(2,1)S(1)} %add_convert_fusion.15), channel_id=1, source_target_pairs={{0,4},{4,0},{1,5},{5,1},{2,6},{6,2},{3,7},{7,3},{8,12},{12,8},{9,1... | collective-permute-start | bytes 700424 | tf_op jit(solution)/shard_map/ppermute | solution.py:723
  482.5 11.3 %collective-permute-start.23 = (bf16[48,2432]{1,0:T(8,128)(2,1)S(1)}, bf16[48,2432]{1,0:T(8,128)(2,1)S(1)}, u32[]{:S(2)}, u32[]{:S(2)}) collective-permute-start(bf16[48,2432]{1,0:T(8,128)(2,1)S(1)} %fusion.6), channel_id=1, source_target_pairs={{0,8},{8,0},{1,9},{9,1},{2,10},{10,2},{3,11},{11,3},{4,12},{12,4},... | collective-permute-start | bytes 700424 | tf_op jit(solution)/shard_map/ppermute | solution.py:723
  484.4 13.4 %collective-permute-start.31 = (bf16[96,3200]{1,0:T(8,128)(2,1)S(1)}, bf16[96,3200]{1,0:T(8,128)(2,1)S(1)}, u32[]{:S(2)}, u32[]{:S(2)}) collective-permute-start(bf16[96,3200]{1,0:T(8,128)(2,1)S(1)} %pad_maximum_fusion.7), channel_id=1, source_target_pairs={{0,2},{2,0},{1,3},{3,1},{4,6},{6,4},{5,7},{7,5},{8,10},{10,8},{9,1... | collective-permute-start | bytes 1843208 | tf_op jit(solution)/shard_map/ppermute | solution.py:723
  495.1 6.9 %collective-permute-start.24 = (bf16[48,2432]{1,0:T(8,128)(2,1)S(1)}, bf16[48,2432]{1,0:T(8,128)(2,1)S(1)}, u32[]{:S(2)}, u32[]{:S(2)}) collective-permute-start(bf16[48,2432]{1,0:T(8,128)(2,1)S(1)} %add_convert_fusion.14), channel_id=1, source_target_pairs={{0,4},{4,0},{1,5},{5,1},{2,6},{6,2},{3,7},{7,3},{8,12},{12,8},{9,1... | collective-permute-start | bytes 700424 | tf_op jit(solution)/shard_map/ppermute | solution.py:723
  502.8 11.3 %collective-permute-start.25 = (bf16[96,2432]{1,0:T(8,128)(2,1)}, bf16[96,2432]{1,0:T(8,128)(2,1)}, u32[]{:S(2)}, u32[]{:S(2)}) collective-permute-start(bf16[96,2432]{1,0:T(8,128)(2,1)} %pad_maximum_fusion.9), channel_id=1, source_target_pairs={{0,2},{2,0},{1,3},{3,1},{4,6},{6,4},{5,7},{7,5},{8,10},{10,8},{9,1... | collective-permute-start | bytes 1400840 | tf_op jit(solution)/shard_map/ppermute | solution.py:723
  504.5 11.9 %collective-permute-start.32 = (bf16[192,3200]{1,0:T(8,128)(2,1)}, bf16[192,3200]{1,0:T(8,128)(2,1)}, u32[]{:S(2)}, u32[]{:S(2)}) collective-permute-start(bf16[192,3200]{1,0:T(8,128)(2,1)} %pad_maximum_fusion.2), channel_id=1, source_target_pairs={{0,1},{1,0},{2,3},{3,2},{4,5},{5,4},{6,7},{7,6},{8,9},{9,8},{10,11... | collective-permute-start | bytes 3686408 | tf_op jit(solution)/shard_map/ppermute | solution.py:723
  510.0 6.4 %copy-start.41 = (bf16[96,3200]{1,0:T(8,128)(2,1)S(1)}, bf16[96,3200]{1,0:T(8,128)(2,1)}, u32[]{:S(2)}) copy-start(bf16[96,3200]{1,0:T(8,128)(2,1)} %copy-done.40) | copy-start | bytes 1843204
  516.4 7.2 %collective-permute-start.26 = (bf16[192,2432]{1,0:T(8,128)(2,1)}, bf16[192,2432]{1,0:T(8,128)(2,1)}, u32[]{:S(2)}, u32[]{:S(2)}) collective-permute-start(bf16[192,2432]{1,0:T(8,128)(2,1)} %pad_maximum_fusion.5), channel_id=1, source_target_pairs={{0,1},{1,0},{2,3},{3,2},{4,5},{5,4},{6,7},{7,6},{8,9},{9,8},{10,11... | collective-permute-start | bytes 2801672 | tf_op jit(solution)/shard_map/ppermute | solution.py:723
  (32 other events, 98.0 us)

commit v4 on v3

--- a/solution.py
+++ b/solution.py
@@ -9,6 +9,7 @@
 
 HD = 64
 LANES = 128
+VMEM = 56 * 2**20
 norm_epsilon = 1e-05
 masked_score = -1e9
 BF = jnp.bfloat16
@@ -54,15 +55,10 @@
     return scores
 
 
-def part_places(parts, shift):
+def in_order(parts, shift, half_index):
     if len(parts) == 1:
-        return [slice(0, parts[0].shape[0])]
-    half = parts[0].shape[0]
-    count = half * len(parts)
-    return [
-        pl.ds(pl.multiple_of(lax.rem(part * half + shift, count), half), half)
-        for part in range(len(parts))
-    ]
+        return parts[0]
+    return jnp.where(shift == 0, parts[half_index], parts[1 - half_index])
 
 
 def array_places(count, shift, swapped):
@@ -88,42 +84,40 @@
     scalars, refs = refs[0], refs[1:]
     q_parts, k_parts, v_parts = refs[:parts], refs[parts : 2 * parts], refs[2 * parts : 3 * parts]
     qt_ref, kt_ref = refs[3 * parts : 3 * parts + 2]
-    o_ref, lse_ref, ka, va, qa = refs[3 * parts + 2 + skipped :]
+    o_ref, qx_ref, ka, va, qa = refs[3 * parts + 2 + skipped :]
     tq, ts = qa.shape[1], ka.shape[1]
-    pair = pl.program_id(1)
     shift = scalars[0]
-    extra = kt_ref[...]
-    for part, here in enumerate(part_places(k_parts, shift)):
-        k, v = k_parts[part][...], v_parts[part][...]
-        extra = kt_ref[part * k.shape[0] : (part + 1) * k.shape[0], :]
+    for part, (here, there) in enumerate(array_places(ts, shift, swapped)):
+        k = in_order([ref[...] for ref in k_parts], shift, part)
+        v = in_order([ref[...] for ref in v_parts], shift, part)
+        extra = kt_ref[there, :]
         for head in (0, 1):
             own = head_lanes(k.shape, head)
             ka[head, here, :] = jnp.where(own, k, extra)
             va[head, here, :] = jnp.where(own, v, extra)
-    for part, here in enumerate(part_places(q_parts, shift)):
-        q = q_parts[part][...]
-        extra = qt_ref[part * q.shape[0] : (part + 1) * q.shape[0], :]
+    for part, (here, there) in enumerate(array_places(tq, shift, swapped)):
+        q = in_order([ref[...] for ref in q_parts], shift, part)
+        extra = qt_ref[there, :]
         for head in (0, 1):
             qa[head, here, :] = jnp.where(head_lanes(q.shape, head), q, extra)
     lane = lax.broadcasted_iota(jnp.int32, (block, LANES), 1)
     for index in range(tq // block):
         count = (index + 1) * block if causal == "block" else ts
-        outs, lses = [], []
+        there = row_block(index, block, tq, shift, swapped)
+        outs, extra = [], qt_ref[there, :].astype(F32)
         for head in (0, 1):
             scores = dot(qa[head, index * block : (index + 1) * block, :], ka[head, :count, :], NT)
             scores = causal_scores(scores, causal, shift + index * block, block, 0)
             top = jnp.max(scores, 1, keepdims=True)
             weights = jnp.exp(scores - top).astype(BF)
             sums = dot(weights, va[head, :count, :])
-            ones_lane = HD + 6 if head == 0 else 6
-            total = sums[:, ones_lane : ones_lane + 1]
+            at = HD + 4 if head == 0 else 4
+            total = sums[:, at + 2 : at + 3]
             outs.append(sums / total)
-            lses.append(top + jnp.log(total))
-        there = row_block(index, block, tq, shift, swapped)
+            for i, piece in enumerate(three_parts(-(top + jnp.log(total)))):
+                extra = jnp.where(lane == at + i, piece, extra)
         o_ref[there, :] = jnp.where(lane < HD, outs[0], outs[1]).astype(BF)
-        lse_ref[there, :] = jnp.where(
-            lane == 2 * pair, lses[0], jnp.where(lane == 2 * pair + 1, lses[1], lse_ref[there, :])
-        )
+        qx_ref[there, :] = extra.astype(BF)
 
 
 def three_parts(x):
@@ -135,46 +129,42 @@
     return parts
 
 
-def backward_kernel(*refs, parts, skipped, causal, block, swapped, scaling, first):
+def backward_kernel(*refs, parts, skipped, causal, block, swapped, scaling):
     scalars, refs = refs[0], refs[1:]
     q_parts, k_parts, v_parts = refs[:parts], refs[parts : 2 * parts], refs[2 * parts : 3 * parts]
-    g_ref, o_ref, qt_ref, kt_ref, lse_ref = refs[3 * parts : 3 * parts + 5]
+    g_ref, o_ref, qx_ref, kt_ref = refs[3 * parts : 3 * parts + 4]
     (
         dq_ref, dk_ref, dv_ref, ka, va, qa, ga, k_turned, dk_sum, dv_sum, dq_turned,
-    ) = refs[3 * parts + 5 + skipped :]
+    ) = refs[3 * parts + 4 + skipped :]
     tq, ts = qa.shape[1], ka.shape[1]
-    pair = pl.program_id(1) + first
     shift = scalars[0]
-    for part, here in enumerate(part_places(k_parts, shift)):
-        k, v = k_parts[part][...], v_parts[part][...]
-        extra = kt_ref[part * k.shape[0] : (part + 1) * k.shape[0], :]
+    for part, (here, there) in enumerate(array_places(ts, shift, swapped)):
+        k = in_order([ref[...] for ref in k_parts], shift, part)
+        v = in_order([ref[...] for ref in v_parts], shift, part)
+        extra = kt_ref[there, :]
         for head in (0, 1):
             own = head_lanes(k.shape, head)
             ka[head, here, :] = jnp.where(own, k, extra)
             va[head, here, :] = jnp.where(own, v, extra)
-    for here in [s for s, _ in array_places(ts, shift, swapped)]:
-        k = jnp.where(head_lanes((here.stop - here.start, LANES), 0), ka[0, here, :], ka[1, here, :])
         k_turned[:, here] = k.astype(F32).T.astype(BF)
-    for part, here in enumerate(part_places(q_parts, shift)):
-        q = q_parts[part][...]
-        there = slice(part * q.shape[0], (part + 1) * q.shape[0])
-        g, extra = g_ref[there, :], qt_ref[there, :]
+    source = lax.broadcasted_iota(jnp.int32, (LANES, LANES), 0)
+    target = lax.broadcasted_iota(jnp.int32, (LANES, LANES), 1)
+    rides = (target % HD >= 4) & (target % HD < 7) & ((source < HD) == (target >= HD))
+    spread = jnp.where(rides, -1.0, 0.0).astype(BF)
+    for part, (here, there) in enumerate(array_places(tq, shift, swapped)):
+        q = in_order([ref[...] for ref in q_parts], shift, part)
+        g, extra = g_ref[there, :], qx_ref[there, :]
         products = g.astype(F32) * o_ref[there, :].astype(F32)
-        lse = lse_ref[there, :]
-        lane = lax.broadcasted_iota(jnp.int32, q.shape, 1)
+        rough = products.astype(BF)
+        delta = dot(rough, spread) + dot((products - rough.astype(F32)).astype(BF), spread)
+        lane = lax.broadcasted_iota(jnp.int32, q.shape, 1) % HD
+        pieces = three_parts(delta)
+        g_extra = jnp.where(lane == 4, pieces[0], jnp.where(lane == 5, pieces[1], pieces[2]))
+        g_extra = g_extra.astype(BF)
         for head in (0, 1):
             own = head_lanes(q.shape, head)
-            at = HD + 4 if head == 0 else 4
-            delta = three_parts(-jnp.sum(jnp.where(own, products, 0.0), 1, keepdims=True))
-            lse_col = three_parts(
-                -jnp.sum(jnp.where(lane == 2 * pair + head, lse, 0.0), 1, keepdims=True)
-            )
-            q_extra, g_extra = extra.astype(F32), jnp.zeros(q.shape, F32)
-            for i in range(3):
-                q_extra = jnp.where(lane == at + i, lse_col[i], q_extra)
-                g_extra = jnp.where(lane == at + i, delta[i], g_extra)
-            qa[head, here, :] = jnp.where(own, q, q_extra.astype(BF))
-            ga[head, here, :] = jnp.where(own, g, g_extra.astype(BF))
+            qa[head, here, :] = jnp.where(own, q, extra)
+            ga[head, here, :] = jnp.where(own, g, g_extra)
     blocks = tq // block
     for index in reversed(range(blocks)):
         count = (index + 1) * block if causal == "block" else ts
@@ -237,14 +227,11 @@
             num_scalar_prefetch=1,
             grid=(rows, pairs),
             in_specs=specs + [shared_spec(tq), shared_spec(ts)] + [ANYWHERE] * len(after),
-            out_specs=[head_spec(tq, 0), shared_spec(tq)],
+            out_specs=[head_spec(tq, 0), head_spec(tq, 0)],
             scratch_shapes=[pltpu.VMEM((2, n, LANES), BF) for n in (ts, ts, tq)],
         ),
-        out_shape=[
-            jax.ShapeDtypeStruct((rows, tq, width), BF),
-            jax.ShapeDtypeStruct((rows, tq, LANES), F32),
-        ],
-        compiler_params=pltpu.CompilerParams(vmem_limit_bytes=48 * 2**20),
+        out_shape=[jax.ShapeDtypeStruct((rows, tq, width), BF)] * 2,
+        compiler_params=pltpu.CompilerParams(vmem_limit_bytes=VMEM),
         cost_estimate=pl.CostEstimate(
             flops=elements * 1600, bytes_accessed=rows * (tq + ts) * width * 4, transcendentals=0
         ),
@@ -252,25 +239,25 @@
 
 
 def attend_back(
-    q, k, v, g, o, lse, terms, shift, first, pairs, causal, block, swapped, held=(), after=()
+    q, k, v, g, o, extra, terms, shift, first, pairs, causal, block, swapped, held=(), after=()
 ):
     specs, arrays = part_specs(q, k, v, first)
     rows, _, width = o.shape
     tq, ts = (sum(x.shape[1] for x in one[0]) for one in (q, k))
     elements = rows * pairs * 2 * tq * ts
     skipped = len(held) + len(after)
-    count = len(arrays) + 5
+    count = len(arrays) + 4
     return pl.pallas_call(
         functools.partial(
             backward_kernel, parts=len(q[0]), skipped=skipped, causal=causal, block=block,
-            swapped=swapped, scaling=HD**-0.5, first=first,
+            swapped=swapped, scaling=HD**-0.5,
         ),
         grid_spec=pltpu.PrefetchScalarGridSpec(
             num_scalar_prefetch=1,
             grid=(rows, pairs),
             in_specs=specs
-            + [head_spec(tq, first)] * 2
-            + [shared_spec(tq), shared_spec(ts), shared_spec(tq)]
+            + [head_spec(tq, first)] * 3
+            + [shared_spec(ts)]
             + [ANYWHERE] * skipped,
             out_specs=[head_spec(tq, first), head_spec(ts, first), head_spec(ts, first)],
             scratch_shapes=[pltpu.VMEM((2, n, LANES), BF) for n in (ts, ts, tq, tq)]
@@ -283,11 +270,11 @@
         ),
         out_shape=[jax.ShapeDtypeStruct((rows, n, width), BF) for n in (tq, ts, ts)],
         input_output_aliases={1 + count + i: i for i in range(len(held))},
-        compiler_params=pltpu.CompilerParams(vmem_limit_bytes=48 * 2**20),
+        compiler_params=pltpu.CompilerParams(vmem_limit_bytes=VMEM),
         cost_estimate=pl.CostEstimate(
             flops=elements * 2600, bytes_accessed=rows * (tq + ts) * pairs * 1024, transcendentals=0
         ),
-    )(shift, *arrays, g, o, *terms, lse, *held, *after)
+    )(shift, *arrays, g, o, extra, terms[1], *held, *after)
 
 
 def norm(resid):
@@ -363,11 +350,7 @@
     w1_ref, b1_ref, w2_ref, b2_ref, g3_ref, s3_ref,
     *refs, chunk, kept_blocks,
 ):
-    if kept_blocks is None:
-        out_ref, *refs = refs
-    else:
-        out_ref, sent_ref, *refs = refs
-    act_ref, dbf_ref, h2b_ref, dpre_ref, dr2_ref, dbc_ref, dco_ref, sums_ref, slope, sums = refs
+    *outs, act_ref, dbf_ref, h2b_ref, dpre_ref, dr2_ref, dbc_ref, dco_ref, sums_ref, slope, sums = refs
     clear(sums)
     h1 = n1_ref[...] * row(g1_ref) + row(s1_ref)
     n2, i2 = norm(h1 + (dot(o_ref[...], ow_ref[...]) + row(ob_ref)))
@@ -387,19 +370,7 @@
         branch = branch + dot(act_c, w2_ref[c, :])
     n3, i3 = norm(h2 + branch)
     out = (n3 * row(g3_ref) + row(s3_ref)).astype(BF)
-    if kept_blocks is None:
-        out_ref[...] = out
-    else:
-        step = pl.program_id(0)
-
-        @pl.when(step < kept_blocks)
-        def _():
-            out_ref[...] = out
-
-        @pl.when(step >= kept_blocks)
-        def _():
-            sent_ref[...] = out
-
+    store_halves(outs, out, kept_blocks)
     up = up_ref[...].astype(F32)
     dr3 = norm_back(up, n3, i3, row(g3_ref))
     dbf = dr3.astype(BF)
@@ -434,14 +405,29 @@
     finish_rows(sums, sums_ref)
 
 
-def input_grad_kernel(*refs, count, start):
-    grads, w_ref, out_ref = refs[:count], refs[count + start], refs[count + start + 1]
+def input_grad_kernel(*refs, count, start, kept_blocks):
+    grads, w_ref, outs = refs[:count], refs[count + start], refs[count + start + 1 :]
     total = refs[count][...] if start else None
     width = grads[0].shape[-1]
     for index, ref in enumerate(grads):
         part = dot(ref[...], w_ref[:, index * width : (index + 1) * width], NT)
         total = part if total is None else total + part
-    out_ref[...] = total.astype(out_ref.dtype)
+    store_halves(outs, total, kept_blocks)
+
+
+def store_halves(outs, value, kept_blocks):
+    if kept_blocks is None:
+        outs[0][...] = value.astype(outs[0].dtype)
+        return
+    step = pl.program_id(0)
+
+    @pl.when(step < kept_blocks)
+    def _():
+        outs[0][...] = value.astype(outs[0].dtype)
+
+    @pl.when(step >= kept_blocks)
+    def _():
+        outs[1][...] = value.astype(outs[1].dtype)
 
 
 class Joined:
@@ -501,9 +487,7 @@
         elif out[0] == "sent":
             shape = (tokens // 2, out[1])
             out_specs.append(
-                pl.BlockSpec(
-                    (block, out[1]), lambda i, _: (jnp.maximum(i + first - half, 0), 0)
-                )
+                pl.BlockSpec((block, out[1]), lambda i, _: (jnp.maximum(i - half, 0), 0))
             )
         else:
             shape = (count * block, out[0])
@@ -531,7 +515,7 @@
             scratch_shapes=list(scratch),
         ),
         out_shape=out_shape,
-        compiler_params=pltpu.CompilerParams(vmem_limit_bytes=56 * 2**20),
+        compiler_params=pltpu.CompilerParams(vmem_limit_bytes=VMEM),
         cost_estimate=pl.CostEstimate(
             flops=flops * count * block // tokens, bytes_accessed=moved, transcendentals=0
         ),
@@ -561,13 +545,17 @@
 MID_ROWS, LOW_ROWS = 8, 16
 
 
-def weight_grads(items, extras, place, wide, order, after=()):
-    width = items[0][0].shape[-1] if not isinstance(items[0][0], tuple) else items[0][0][0].shape[-1]
-    specs, arrays, lefts, steps = [], [], [], []
+def weight_grads(items, extras, scalars, wide, order, after=()):
+    first_left = items[0][0]
+    m = (first_left[0] if isinstance(first_left, tuple) else first_left).shape[-1]
+    block = min(item[3] for item in items)
+    block = min(block, m)
+    specs, arrays, steps = [], [], []
     known = {}
-    for left, right, sum_row in items:
-        if id(left) not in known:
-            where = len(arrays)
+    for left, right, start, columns, sum_row in items:
+        key = id(left)
+        if key not in known:
+            known[key] = (len(arrays), isinstance(left, tuple))
             if isinstance(left, tuple):
                 stack, got = left
                 specs.append(
@@ -576,47 +564,53 @@
                         pipeline_mode=pl.Buffered(1),
                     )
                 )
-                specs.append(
-                    pl.BlockSpec(got.shape, lambda j, p: (0, 0), pipeline_mode=pl.Buffered(1))
-                )
-                arrays += [stack, got]
-            else:
-                specs.append(
-                    pl.BlockSpec(left.shape, lambda j, p: (0, 0), pipeline_mode=pl.Buffered(1))
-                )
-                arrays.append(left)
-            known[id(left)] = (where, isinstance(left, tuple))
-        begin, blocks = len(steps), right.shape[1] // width
+                arrays.append(stack)
+                left = got
+            specs.append(
+                pl.BlockSpec(left.shape, lambda j, p: (0, 0), pipeline_mode=pl.Buffered(1))
+            )
+            arrays.append(left)
+        begin, blocks = len(steps), columns // block
         where = len(arrays)
         specs.append(
             pl.BlockSpec(
-                (right.shape[0], width),
-                lambda j, p, b=begin, n=blocks: (0, jnp.clip(j - b, 0, n - 1)),
+                (right.shape[0], block),
+                lambda j, p, b=begin, n=blocks, f=start // block: (0, f + jnp.clip(j - b, 0, n - 1)),
             )
         )
         arrays.append(right)
         for index in range(blocks):
-            steps.append((known[id(left)], where, sum_row, index, blocks))
+            steps.append((known[key], where, sum_row, start + index * block, right.shape[1]))
     for extra in extras:
         specs.append(
             pl.BlockSpec(extra.shape, lambda j, p: (0, 0), pipeline_mode=pl.Buffered(1))
         )
-    slab = width // len(order)
-    size = width // wide
-
-    def kernel(_, *refs):
+    slab = m // len(order)
+    size = m // wide
+    apart = len(order) > 1
+    slabs = len(order) // 2
+
+    def kernel(scalar_ref, *refs):
         ins, rest = refs[: len(arrays)], refs[len(arrays) :]
-        extra_refs, (out_ref, sums) = rest[: len(extras)], rest[len(extras) + len(after) :]
+        extra_refs, (*outs, sums) = rest[: len(extras)], rest[len(extras) + len(after) :]
         clear(sums)
         step = pl.program_id(0)
 
         def store(value):
-            for to, source in enumerate(order):
-                out_ref[to * slab : (to + 1) * slab, :] = value[
-                    source * slab : (source + 1) * slab
-                ].astype(BF)
-
-        for index, ((left, split), right, sum_row, part, parts) in enumerate(steps):
+            if not apart:
+                outs[0][...] = value.astype(BF)
+                return
+            core = scalar_ref[1]
+            for to in range(slabs):
+                halves = [
+                    value[order[at] * slab : (order[at] + 1) * slab].astype(BF)
+                    for at in (to, slabs + to)
+                ]
+                here = slice(to * slab, (to + 1) * slab)
+                outs[0][here, :] = jnp.where(core == 0, halves[1], halves[0])
+                outs[1][here, :] = jnp.where(core == 0, halves[0], halves[1])
+
+        for index, ((left, split), right, sum_row, column, columns) in enumerate(steps):
 
             @pl.when(step == index)
             def _():
@@ -628,87 +622,119 @@
                 else:
                     value = dot(ins[left][...], grad, TN)
                 store(value)
-                if sum_row is not None:
-                    total = jnp.sum(grad.astype(F32), 0, keepdims=True)
-                    if parts == 1:
-                        sums[sum_row : sum_row + 1, :] = total
-                    else:
-                        for piece in range(wide):
-                            w, k = divmod(wide * part + piece, parts)
-                            sums[sum_row + k : sum_row + k + 1, w * size : (w + 1) * size] = total[
-                                :, piece * size : (piece + 1) * size
-                            ]
+                if sum_row is None:
+                    return
+                total = jnp.sum(grad.astype(F32), 0, keepdims=True)
+                if columns == m:
+                    sums[sum_row : sum_row + 1, column : column + block] = total
+                    return
+                for piece in range(block // size):
+                    w, k = divmod(column // size + piece, columns // m)
+                    sums[sum_row + k : sum_row + k + 1, w * size : (w + 1) * size] = total[
+                        :, piece * size : (piece + 1) * size
+                    ]
 
         @pl.when(step == len(steps))
         def _():
             value = sums[...].T
             for ref in extra_refs:
                 value = value + ref[...]
-            store(jnp.concatenate([value, jnp.zeros((width, width - LANES), F32)], 1))
-
-    columns = width * len(steps) + LANES
+            store(jnp.concatenate([value, jnp.zeros((m, block - LANES), F32)], 1))
+
+    n = block * len(steps) + LANES
     tokens = items[0][1].shape[0]
+    rows = m // 2 if apart else m
     return pl.pallas_call(
         kernel,
         grid_spec=pltpu.PrefetchScalarGridSpec(
             num_scalar_prefetch=1,
             grid=(len(steps) + 1,),
             in_specs=specs + [ANYWHERE] * len(after),
-            out_specs=pl.BlockSpec((width, width), lambda j, _: (0, j)),
-            scratch_shapes=[pltpu.VMEM((LANES, width), F32)],
-        ),
-        out_shape=jax.ShapeDtypeStruct((width, columns), BF),
-        compiler_params=pltpu.CompilerParams(vmem_limit_bytes=48 * 2**20),
+            out_specs=[pl.BlockSpec((rows, block), lambda j, _: (0, j))] * (m // rows),
+            scratch_shapes=[pltpu.VMEM((LANES, m), F32)],
+        ),
+        out_shape=[jax.ShapeDtypeStruct((rows, n), BF)] * (m // rows),
+        compiler_params=pltpu.CompilerParams(vmem_limit_bytes=VMEM),
         cost_estimate=pl.CostEstimate(
-            flops=2 * tokens * width * columns,
-            bytes_accessed=sum(a.size * 2 for a in arrays) + width * columns * 2,
+            flops=2 * tokens * m * n,
+            bytes_accessed=sum(a.size * 2 for a in arrays) + m * n * 2,
             transcendentals=0,
         ),
-    )(place, *arrays, *extras, *after)
-
-
-def tall_grad(left, right, place, order, after=()):
+    )(scalars, *arrays, *extras, *after)
+
+
+def tall_grad(left, right, scalars, order, after=()):
     tokens, rows = left.shape
     width = right.shape[1]
-    slabs = len(order)
-    size = rows // slabs
-
-    def out_row(j):
-        to = 0
-        for at, source in enumerate(order):
-            to = jnp.where(j == source, at, to)
-        return to
+    apart = len(order) > 1
+    blocks = len(order) if apart else 4
+    size = rows // blocks
+    half = blocks // 2
+
+    def source(j, s):
+        if not apart:
+            return j
+        to = jnp.where(s[1] == 0, (j + half) % blocks, j)
+        block = 0
+        for at, slab in enumerate(order):
+            block = jnp.where(to == at, slab, block)
+        return block
 
     def kernel(_, left_ref, right_ref, *refs):
-        refs[-1][...] = dot(left_ref[...], right_ref[...], TN).astype(BF)
-
+        value = dot(left_ref[...], right_ref[...], TN).astype(BF)
+        if not apart:
+            refs[-1][...] = value
+            return
+        other, own = refs[-2:]
+
+        @pl.when(pl.program_id(0) < half)
+        def _():
+            other[...] = value
+
+        @pl.when(pl.program_id(0) >= half)
+        def _():
+            own[...] = value
+
+    if apart:
+        out_specs = [
+            pl.BlockSpec((size, width), lambda j, _: (jnp.minimum(j, half - 1), 0)),
+            pl.BlockSpec((size, width), lambda j, _: (jnp.maximum(j - half, 0), 0)),
+        ]
+        out_shape = [jax.ShapeDtypeStruct((rows // 2, width), BF)] * 2
+    else:
+        out_specs = [pl.BlockSpec((size, width), lambda j, _: (j, 0))]
+        out_shape = [jax.ShapeDtypeStruct((rows, width), BF)]
     return pl.pallas_call(
         kernel,
         grid_spec=pltpu.PrefetchScalarGridSpec(
             num_scalar_prefetch=1,
-            grid=(slabs,),
+            grid=(blocks,),
             in_specs=[
-                pl.BlockSpec((tokens, size), lambda j, _: (0, j)),
+                pl.BlockSpec((tokens, size), lambda j, s: (0, source(j, s))),
                 pl.BlockSpec(right.shape, lambda j, _: (0, 0), pipeline_mode=pl.Buffered(1)),
             ]
             + [ANYWHERE] * len(after),
-            out_specs=pl.BlockSpec((size, width), lambda j, _: (out_row(j), 0)),
-        ),
-        out_shape=jax.ShapeDtypeStruct((rows, width), BF),
-        compiler_params=pltpu.CompilerParams(vmem_limit_bytes=48 * 2**20),
+            out_specs=out_specs,
+        ),
+        out_shape=out_shape,
+        compiler_params=pltpu.CompilerParams(vmem_limit_bytes=VMEM),
         cost_estimate=pl.CostEstimate(
             flops=2 * tokens * rows * width,
             bytes_accessed=2 * (left.size + right.size + rows * width),
             transcendentals=0,
         ),
-    )(place, left, right, *after)
-
-
-def vectors_kernel(x_ref, *outs, columns):
-    turned = x_ref[...].astype(F32).T
+    )(scalars, left, right, *after)
+
+
+def vector_rows(x, columns, outs):
+    turned = x.astype(F32).T
     for (start, count), out in zip(columns, outs):
         rows = [turned[start + i] for i in range(count)]
         out[...] = rows[0] if count == 1 else jnp.concatenate(rows)
+
+
+def vectors_kernel(x_ref, *outs, columns):
+    vector_rows(x_ref[...], columns, outs)
 
 
 def vectors_of(x, columns):
@@ -718,6 +744,28 @@
     )(x)
 
 
+def widen_kernel(*refs, count, pieces, columns):
+    ins, outs = refs[:count], refs[count:]
+    vectors = outs[len(pieces) :]
+    for out, parts in zip(outs, pieces):
+        at = 0
+        for which, start, size in parts:
+            out[:, at : at + size] = ins[which][:, start : start + size].astype(F32)
+            at += size
+    extra = sum(ref[:, ref.shape[1] - LANES :].astype(F32) for ref in ins)
+    vector_rows(extra, columns, vectors)
+
+
+def widen(arrays, pieces, columns):
+    rows = arrays[0].shape[0]
+    return pl.pallas_call(
+        functools.partial(widen_kernel, count=len(arrays), pieces=pieces, columns=columns),
+        out_shape=[jax.ShapeDtypeStruct((rows, sum(p[2] for p in parts)), F32) for parts in pieces]
+        + [jax.ShapeDtypeStruct((count * rows,), F32) for _, count in columns],
+        compiler_params=pltpu.CompilerParams(vmem_limit_bytes=VMEM),
+    )(*arrays)
+
+
 def partner(x, axis, bit=1):
     count = lax.axis_size(axis)
     return lax.ppermute(x, axis, [(i, i ^ bit) for i in range(count)])
@@ -732,78 +780,62 @@
 
 
 class Reduction:
-    def __init__(self, x, order):
-        self.split = all(lax.axis_size(a) == 2 for a in ("wide", "side", "near", "core"))
-        self.x = x
+    def __init__(self, arrays, order):
+        self.split = len(arrays) == 2
+        self.arrays = arrays
         self.steps = list(order) if self.split else []
-        self.terms = [x]
+        self.terms = []
         self.got = None
 
     def total(self, terms):
-        value = sum(t.astype(F32) for t in terms)
-        return value.astype(BF)
+        return sum(t.astype(F32) for t in terms).astype(BF)
 
     def send(self):
         if not self.steps:
             return ()
         step = self.steps[0]
-        if step == "core_sum":
-            self.got = lax.psum_scatter(self.x, "core", scatter_dimension=0, tiled=True)
-            return ()
         if step == "gather":
-            self.got = lax.all_gather(self.total(self.terms), ("core", "side", "near"), axis=0, tiled=True)
-            return ()
-        if step in ("core", "wide", "side", "near"):
-            sent = self.total([pick(t, 1 - lax.axis_index(step)) for t in self.terms])
-            axis = step
+            sent = self.total(self.terms)
+            self.got = lax.all_gather(sent, ("core", "side", "near"), axis=0, tiled=True)
+            return (sent,)
+        if step == "core":
+            sent = self.arrays[0]
         elif step == "far":
             sent = self.total(self.terms)
-            axis = step
+            assert lax.axis_size("far") <= 2
+            if lax.axis_size("far") == 1:
+                return ()
         else:
-            sent = self.total(self.terms)
-            self.terms = [sent]
-            axis = step[5:]
-        if step == "far":
-            self.got = []
-            count, bit = lax.axis_size("far"), 1
-            assert count <= 2
-            while bit < count:
-                self.got.append(partner(sent, "far", bit))
-                bit *= 2
-        else:
-            self.got = [partner(sent, axis)]
+            sent = self.total([pick(t, 1 - lax.axis_index(step)) for t in self.terms])
+        self.got = partner(sent, step)
         return (sent,)
 
     def take(self):
         if not self.steps:
             return
         step = self.steps.pop(0)
-        if step in ("core_sum", "gather"):
+        if step == "gather":
             self.terms = [self.got]
-        elif step in ("core", "wide", "side", "near"):
-            self.terms = [pick(t, lax.axis_index(step)) for t in self.terms] + self.got
+        elif step == "core":
+            self.terms = [self.arrays[1], self.got]
         elif step == "far":
-            self.terms = self.terms + self.got
+            if lax.axis_size("far") == 2:
+                self.terms.append(self.got)
         else:
-            x, got = self.terms[0], self.got[0]
-            first = lax.axis_index(step[5:]) == 0
-            self.terms = [
-                jnp.concatenate([jnp.where(first, x, got), jnp.where(first, got, x)], 0)
-            ]
+            self.terms = [pick(t, lax.axis_index(step)) for t in self.terms] + [self.got]
 
     def result(self):
         assert not self.steps
         if self.split:
             return self.terms[0]
-        x = lax.psum_scatter(self.x, "wide", scatter_dimension=0, tiled=True)
+        x = lax.psum_scatter(self.arrays[0], "wide", scatter_dimension=0, tiled=True)
         return lax.psum(x, ROWS)
 
 
 CORE_WIDE = (0, 2, 1, 3)
 CORE_SIDE = (0, 4, 1, 5, 2, 6, 3, 7)
-JOINS = ("join_near", "join_side", "join_core")
-X_FIRST = ("core", "wide", "side", "near", "far") + JOINS
-Y_FIRST = ("core", "side", "wide", "near", "far") + JOINS
+X_FIRST = ("core", "wide", "side", "near", "far", "gather")
+Y_FIRST = ("core", "side", "wide", "near", "far", "gather")
 
 
 def body(
@@ -814,13 +846,14 @@
 ):
     row_count, tok_count, width = target.shape
     hidden = ffn_in_w.shape[1]
+    parts = hidden // width
     wide = lax.axis_size("wide")
     index = lax.axis_index("wide").astype(jnp.int32)
-    place = index.reshape(1)
+    place = jnp.stack([index, lax.axis_index("core").astype(jnp.int32)])
     shift = (index * tok_count).reshape(1)
     swapped = wide == 2 and row_count == 2
     split = all(lax.axis_size(a) == 2 for a in ("wide", "side", "near", "core"))
-    core_wide = CORE_WIDE if split else (0, 1, 2, 3)
+    core_wide = CORE_WIDE if split else (0,)
     core_side = CORE_SIDE if split else (0,)
     tokens = row_count * tok_count
     block = min(256, tok_count)
@@ -845,6 +878,7 @@
         seg = segments
         key_seg = lax.all_gather(segments, "wide", axis=1, tiled=True)
         row_tokens = tok_count
+    kept_blocks = tok_count // block if swapped else None
     terms = (segment_terms(seg)[0], segment_terms(key_seg)[1])
 
     def by_row(x):
@@ -855,6 +889,9 @@
 
     def keys_of(x):
         return lax.all_gather(x, "wide", axis=1, tiled=True)
+
+    def by_keys(x):
+        return x.reshape(row_count, -1, width)
 
     def key_grads(x):
         return x if swapped else lax.psum_scatter(x, "wide", scatter_dimension=1, tiled=True)
@@ -879,36 +916,24 @@
             q, k, v, terms, shift, width, causal if is_causal else "no", block_f, swapped, after
         )
 
-    def attention_back(q, k, v, g, o, lse, is_causal, cuts, after):
-        held = ()
-        pairs = width // LANES
-        per = pairs // cuts
-        for cut in range(cuts):
-            held = attend_back(
-                q, k, v, by_row(g), o, lse, terms, shift, cut * per, per,
-                causal if is_causal else "no", block_b, swapped, held, after[cut](),
-            )
-        dq, dk, dv = held
-        return flat(dq), flat(key_grads(dk)), flat(key_grads(dv))
+    def attention_back(q, k, v, g, o, extra, is_causal, first, pairs, held, after):
+        return attend_back(
+            q, k, v, by_row(g), o, extra, terms, shift, first, pairs,
+            causal if is_causal else "no", block_b, swapped, held, after,
+        )
 
     def input_grad(grads, w, start=None, after=()):
         blocked = list(grads) + ([] if start is None else [start])
+        outs = [("kept", 2, width, F32), ("sent", width, BF)] if swapped else [(width, F32)]
         kernel = functools.partial(
-            input_grad_kernel, count=len(grads), start=0 if start is None else 1
+            input_grad_kernel, count=len(grads), start=0 if start is None else 1,
+            kept_blocks=kept_blocks,
         )
-        flops = 2 * tokens * width * w.shape[1]
-        if not swapped:
-            return token_call(kernel, block, blocked, (w,), [(width, F32)], place, flops=flops)[0], None
-        half = tokens // block // 2
-        (sent,) = token_call(
-            kernel, block, blocked, (w,), [("sent", width, BF)], place, flops=flops,
-            span=(half, half), after=after,
+        out = token_call(
+            kernel, block, blocked, (w,), outs, place, flops=2 * tokens * width * w.shape[1],
+            after=after,
         )
-        (kept,) = token_call(
-            kernel, block, blocked, (w,), [("kept", 2, width, F32)], place, flops=flops,
-            span=(0, half), after=(sent,),
-        )
-        return kept, sent
+        return out[0], out[-1]
 
     def give(out, got):
         if not swapped:
@@ -927,7 +952,7 @@
     else:
         both = [keys_of(qkv[0][..., width:])]
         self_q, self_k, self_v = (qkv, 0), (both, 0), (both, width)
-    self_o, self_lse = attention(self_q, self_k, self_v, True)
+    self_o, self_x = attention(self_q, self_k, self_v, True)
     self_ob = flat(self_o)
     n1, i1, h1b, cq = token_call(
         after_self_kernel, block, (self_ob, x_in),
@@ -947,12 +972,12 @@
     else:
         both = [keys_of(ckv[0])]
         cross_k, cross_v = (both, 0), (both, width)
-    cross_o, cross_lse = attention(cross_q, cross_k, cross_v, False)
+    cross_o, cross_x = attention(cross_q, cross_k, cross_v, False)
     cross_ob = flat(cross_o)
     outs = [("kept", 2, width, BF), ("sent", width, BF)] if swapped else [(width, BF)]
     *h3, act, dbf, h2b, dpre, dr2, dbc, dco, mid_sums = token_call(
         functools.partial(
-            middle_kernel, chunk=width, kept_blocks=tok_count // block if swapped else None
+            middle_kernel, chunk=width, kept_blocks=kept_blocks
         ),
         block, (cross_ob, n1, upstream),
         (
@@ -970,84 +995,138 @@
     )
     got_out = send_back(h3[-1])
 
+    def step(*reductions):
+        for r in reductions:
+            r.take()
+        return sum((r.send() for r in reductions), ())
+
     ra = Reduction(tall_grad(act, dbf, place, core_wide), X_FIRST)
     sent_a = ra.send()
     rb = Reduction(
         weight_grads(
-            [(h2b, dpre, 0), (cross_ob, dbc, 4)], [mid_sums], place, wide, core_side, sent_a
+            [(h2b, dpre, 0, hidden, 0), (cross_ob, dbc, 0, width, parts)], [mid_sums], place, wide,
+            core_side, sent_a,
         ),
         Y_FIRST,
     )
     sent_b = rb.send()
-    ra.take()
-    sent_a = ra.send()
-
-    def step(*reductions):
-        for r in reductions:
-            r.take()
-        return sum((r.send() for r in reductions), ())
-
+    sent_a = step(ra)
+    layer_out = give(h3[0], got_out)
+    sent_b = step(rb)
+    pairs = width // LANES
     dcq, dck, dcv = attention_back(
-        cross_q, cross_k, cross_v, dco, cross_o, cross_lse, False, 2,
-        [lambda: sent_a + sent_b, lambda: step(rb)],
-    )
+        cross_q, cross_k, cross_v, dco, cross_o, cross_x, False, 0, pairs, (),
+        sent_a + sent_b + (layer_out,),
+    )
+    dcq, dck, dcv = flat(dcq), flat(key_grads(dck)), flat(key_grads(dcv))
     sent = step(ra, rb)
+    rc = Reduction(
+        weight_grads(
+            [(h1b, dcq, 0, width, 0), (x_enc, dck, 0, width, None), (x_enc, dcv, 0, width, 1)],
+            [], place, wide, core_side, sent,
+        ),
+        Y_FIRST,
+    )
+    sent_c = rc.send()
     dr1, dba, dso, low_sums = token_call(
         before_self_kernel, block, (dcq, dr2, n1, i1), (cross_q_w, norm1_gain, self_out_w),
         [(width, F32), (width, BF), (width, BF), ("whole", width, LANES, F32)], place,
         scratch=[pltpu.VMEM((LANES, width), F32)],
-        flops=4 * tokens * width * width, after=sent,
-    )
-    rc = Reduction(
-        weight_grads(
-            [(h1b, dcq, 0), (x_enc, dck, None), (x_enc, dcv, 1), (self_ob, dba, 2)],
-            [low_sums], place, wide, core_side,
-        ),
-        Y_FIRST,
-    )
-    sent_c = rc.send()
-    enc_kept, enc_sent = input_grad([dck, dcv], cross_kv_w)
+        flops=4 * tokens * width * width, after=sent_c,
+    )
+    sent = step(ra, rb, rc)
+    enc_kept, enc_sent = input_grad([dck, dcv], cross_kv_w, None, sent)
     got_enc = send_back(enc_sent)
-    out_first = (got_out,) if swapped else ()
-    dsq, dsk, dsv = attention_back(
-        self_q, self_k, self_v, dso, self_o, self_lse, True, 2,
-        [lambda: step(ra, rb) + sent_c + out_first, lambda: step(ra, rb, rc)],
+    sent = step(ra, rb)
+    cut = pairs // 2
+    first = attention_back(
+        self_q, self_k, self_v, dso, self_o, self_x, True, 0, cut, (), sent,
     )
     sent = step(ra, rb, rc)
-    rd = Reduction(
-        weight_grads(
-            [(x_in, dsq, 0), (x_in, dsk, None), (x_in, dsv, 1)], [], place, wide, core_wide, sent
-        ),
-        X_FIRST,
-    )
-    sent = rd.send()
+    if swapped:
+        dsq, dsk, dsv = (flat(x) for x in first)
+        rd = Reduction(
+            weight_grads(
+                [
+                    (self_ob, dba, 0, width, 2),
+                    (x_in, dsq, 0, cut * LANES, 0),
+                    (x_in, dsk, 0, cut * LANES, None),
+                    (x_in, dsv, 0, cut * LANES, 1),
+                ],
+                [low_sums], place, wide, core_wide, sent,
+            ),
+            X_FIRST,
+        )
+        sent = rd.send()
+    encoded_grad = give(enc_kept, got_enc)
+    second = attention_back(
+        self_q, self_k, self_v, dso, self_o, self_x, True, cut, pairs - cut, first,
+        sent + (encoded_grad,),
+    )
+    dsq, dsk, dsv = (flat(x) for x in second)
+    if swapped:
+        re = Reduction(
+            weight_grads(
+                [
+                    (x_in, dsq, cut * LANES, width - cut * LANES, 0),
+                    (x_in, dsk, cut * LANES, width - cut * LANES, None),
+                    (x_in, dsv, cut * LANES, width - cut * LANES, 1),
+                ],
+                [], place, wide, core_wide, sent,
+            ),
+            X_FIRST,
+        )
+    else:
+        dsk, dsv = (flat(key_grads(by_keys(x))) for x in (dsk, dsv))
+        rd = Reduction(
+            weight_grads([(self_ob, dba, 0, width, 2)], [low_sums], place, wide, core_wide), X_FIRST
+        )
+        re = Reduction(
+            weight_grads(
+                [(x_in, dsq, 0, width, 0), (x_in, dsk, 0, width, None), (x_in, dsv, 0, width, 1)],
+                [], place, wide, core_wide,
+            ),
+            X_FIRST,
+        )
+    sent = re.send()
+    sent += step(rd)
+    sent += step(re)
     in_kept, in_sent = input_grad([dsq, dsk, dsv], self_qkv_w, dr1, sent)
     got_in = send_back(in_sent)
-    while any(r.steps for r in (ra, rb, rc, rd)):
-        step(ra, rb, rc, rd)
-    layer_out = give(h3[0], got_out)
-    encoded_grad = give(enc_kept, got_enc)
+    everything = (ra, rb, rc, rd, re)
+    while any(r.steps for r in everything):
+        step(*everything)
     target_grad = give(in_kept, got_in)
-    grad_a, grad_b, grad_c, grad_d = (r.result() for r in (ra, rb, rc, rd))
+    grad_a, grad_b, grad_c, grad_d, grad_e = (r.result() for r in everything)
 
     def matrix(x, first, count):
         return x[:, first * width : (first + count) * width].astype(F32)
 
-    parts = hidden // width
     (
         ffn_in_b_grad, cross_out_b_grad, norm3_gain_grad, norm3_bias_grad, ffn_out_b_grad,
         norm2_gain_grad, norm2_bias_grad,
     ) = vectors_of(
         grad_b[:, -LANES:], [(0, parts), (parts, 1)] + [(MID_ROWS + i, 1) for i in range(5)]
     )
-    cross_q_b_grad, cross_v_b_grad, self_out_b_grad, norm1_gain_grad, norm1_bias_grad = vectors_of(
-        grad_c[:, -LANES:], [(0, 1), (1, 1), (2, 1), (LOW_ROWS, 1), (LOW_ROWS + 1, 1)]
-    )
-    self_q_b_grad, self_v_b_grad = vectors_of(grad_d[:, -LANES:], [(0, 1), (1, 1)])
+    cross_q_b_grad, cross_v_b_grad = vectors_of(grad_c[:, -LANES:], [(0, 1), (1, 1)])
+    if swapped:
+        one, two = cut * LANES, width - cut * LANES
+        pieces = []
+        for i in range(3):
+            pieces += [(0, width + i * one, one), (1, i * two, two)]
+    else:
+        pieces = [(1, 0, 3 * width)]
+    (
+        self_out_w_grad, self_qkv_w_grad, self_q_b_grad, self_v_b_grad, self_out_b_grad,
+        norm1_gain_grad, norm1_bias_grad,
+    ) = widen(
+        (grad_d, grad_e), ([(0, 0, width)], pieces),
+        [(0, 1), (1, 1), (2, 1), (LOW_ROWS, 1), (LOW_ROWS + 1, 1)],
+    )
     return (
         layer_out, target_grad, encoded_grad,
-        matrix(grad_d, 0, 3), self_q_b_grad, self_v_b_grad,
-        matrix(grad_c, 3, 1), self_out_b_grad, norm1_gain_grad, norm1_bias_grad,
+        self_qkv_w_grad, self_q_b_grad, self_v_b_grad,
+        self_out_w_grad, self_out_b_grad, norm1_gain_grad, norm1_bias_grad,
         matrix(grad_c, 0, 1), cross_q_b_grad,
         matrix(grad_c, 1, 2), cross_v_b_grad,
         matrix(grad_b, parts, 1), cross_out_b_grad, norm2_gain_grad, norm2_bias_grad,

time: 539 us -> 579 us (1.074)
  blocking collectives: 0 us -> 33.3 us
  local copies, waits for them, and re-layouts: 28 us -> 14.3 us
  between operations: 1.59 us -> 14.6 us
  waiting for transfers between devices: 134 us -> 122 us
  Pallas kernels: 274 us -> 285 us
    all_gather x0 -> x1, blocking collectives: none -> 33.3 us  [send(): lax.all_gather(sent, ('core', 'side', 'near'), axis=0, tiled=True)]
    dynamic_slice x4 -> x0, local copies, waits for them, and re-layouts: 12.1 us -> none  [pick(): return lax.dynamic_slice_in_dim(x, index * half, half, 0)]
    ppermute x39 -> x32, waiting for transfers between devices: 134 us -> 122 us  [partner(): return lax.ppermute(x, axis, [(i, i ^ bit) for i in range(count)])]
    pallas_call x3 -> x4, Pallas kernels: 28.5 us -> 39.3 us  [weight_grads(): pl.pallas_call(kernel, grid_spec=pltpu.PrefetchScalarGridSpec(num_scalar_...]
    convert_element_type x20 -> x25, other arithmetic: 34.3 us -> 44.8 us  [total(): return sum((t.astype(F32) for t in terms)).astype(BF)]
    pallas_call x4 -> x3, Pallas kernels: 77.9 us -> 68.5 us  [attend_back(): pl.pallas_call(functools.partial(backward_kernel, parts=len(q[0]), skippe...]
    select_n x12 -> x0, other arithmetic: 7.9 us -> none  [the longest x11 6.39 us: take(): jnp.where(first, x, got)]
    ppermute x39 -> x32, starting transfers between devices: 32.4 us -> 37.6 us  [partner(): return lax.ppermute(x, axis, [(i, i ^ bit) for i in range(count)])]
  transfers between devices with their start and end apart: 39 -> 36, of which waited for: 17 -> 13; matrix products, arithmetic and copies ran while one was open for 13% -> 12% of each run, Pallas kernels for 41% -> 37%
where the time goes in v4:
time: 579 us; the launch traced here: 569 us
  Pallas kernels  285 us (49%)
  waiting for transfers between devices  122 us (21%)
  other arithmetic  61.8 us (11%)
  starting transfers between devices  37.8 us (7%)
  blocking collectives  33.3 us (6%)
  between operations  14.6 us (3%)
  local copies, waits for them, and re-layouts  14.3 us (2%)
    ppermute x32, waiting for transfers between devices, partner(): return lax.ppermute(x, axis, [(i, i ^ bit) for i in range(count)])  122 us
    pallas_call x9, Pallas kernels, token_call(): pl.pallas_call(run, grid_spec=pltpu.PrefetchScalarGridSpec(num_scalar_pre...  105 us
    pallas_call x3, Pallas kernels, attend_back(): pl.pallas_call(functools.partial(backward_kernel, parts=len(q[0]), skippe...  68.5 us
    pallas_call x2, Pallas kernels, attend(): pl.pallas_call(functools.partial(forward_kernel, parts=len(q[0]), skipped...  46 us
    convert_element_type x25, other arithmetic, total(): return sum((t.astype(F32) for t in terms)).astype(BF)  44.8 us
    pallas_call x4, Pallas kernels, weight_grads(): pl.pallas_call(kernel, grid_spec=pltpu.PrefetchScalarGridSpec(num_scalar_...  39.3 us
    ppermute x32, starting transfers between devices, partner(): return lax.ppermute(x, axis, [(i, i ^ bit) for i in range(count)])  37.6 us
    all_gather x1, blocking collectives, send(): lax.all_gather(sent, ('core', 'side', 'near'), axis=0, tiled=True)  33.3 us
  transfers between devices with their start and end apart: 36, of which 13 were waited for; matrix products, arithmetic and copies ran while one was open for 12% of the time, Pallas kernels for 37%

profile of v4, /device:TPU:0, one launch (start us, length us, event | category | flops | bytes accessed | tf_op | source)
XLA Modules:
  0.0 569.1 jit_solution(8747360344942066613)
XLA Ops:
  8.1 3.0 collective-permute-start.1
  12.6 2.0 collective-permute-start.2
  16.6 4.9 shard_map.428
  21.5 6.0 %shard_map.424 = bf16[512,2304]{1,0:T(8,128)(2,1)} custom-call(s32[2]{0:T(128)} %pad_add_fusion.1._.scalar_ref, bf16[2,512,768]{2,1,0:T(8,128)(2,1)} %refs_0_.5, bf16[768,2304]{1,0:T(8,128)(2,1)} %refs_4_.7, f32[2304]{0:T(1024)} %pad_maximum_fusion.refs_2_), custom_call_target="tpu_custom_call" | custom-call | flops 3623878656 | bytes 7480320 | tf_op jit(solution)/shard_map/pallas_call | solution.py:508
  28.7 4.2 collective-permute-done.refs_0_.refs_2_.refs_3_.refs_1_
  33.7 6.0 %shard_map.425 = bf16[512,2304]{1,0:T(8,128)(2,1)} custom-call(s32[2]{0:T(128)} %pad_add_fusion.1._.scalar_ref, bf16[512,768]{1,0:T(8,128)(2,1)} %copy-done.12, bf16[768,2304]{1,0:T(8,128)(2,1)} %refs_4_.7, f32[2304]{0:T(1024)} %pad_maximum_fusion.refs_2_), custom_call_target="tpu_custom_call" | custom-call | flops 3623878656 | bytes 6693888 | tf_op jit(solution)/shard_map/pallas_call | solution.py:508
  39.8 22.2 %shard_map.426 = (bf16[1,1024,768]{2,1,0:T(8,128)(2,1)}, bf16[1,1024,768]{2,1,0:T(8,128)(2,1)}) custom-call(s32[1]{0:T(128)} %bitcast.2.refs_0_, bf16[1,512,2304]{2,1,0:T(8,128)(2,1)} %bitcast.45, bf16[1,512,2304]{2,1,0:T(8,128)(2,1)} %bitcast.54, bf16[1,512,2304]{2,1,0:T(8,128)(2,1)} %bitcast.46, bf16[1,512,2304]{2,1,0:T(8,128)(2,1)} %bitcast.55, ...), custom_call_target="tpu_custom_call" | custom-call | flops 20132659200 | bytes 6291456 | tf_op jit(solution)/shard_map/pallas_call | solution.py:221
  62.0 9.1 %shard_map.427 = (f32[1024,768]{1,0:T(8,128)}, f32[1024,128]{1,0:T(8,128)}, bf16[1024,768]{1,0:T(8,128)(2,1)}, bf16[1024,768]{1,0:T(8,128)(2,1)}) custom-call(s32[2]{0:T(128)} %pad_add_fusion.1._.scalar_ref, bf16[1024,768]{1,0:T(8,128)(2,1)} %bitcast.63, bf16[2,512,768]{2,1,0:T(8,128)(2,1)} %refs_0_.5, bf16[512,768]{1,0:T(8,128)(2,1)} %copy-done.12, ...), custom_call_target="tpu_custom_call" | custom-call | flops 2415919104 | bytes 13119488 | tf_op jit(solution)/shard_map/pallas_call | solution.py:508
  71.1 2.6 fusion.7
  73.7 5.0 shard_map.429
  78.7 23.8 %shard_map.430 = (bf16[1,1024,768]{2,1,0:T(8,128)(2,1)}, bf16[1,1024,768]{2,1,0:T(8,128)(2,1)}) custom-call(s32[1]{0:T(128)} %bitcast.2.refs_0_, bf16[1,512,768]{2,1,0:T(8,128)(2,1)} %get-tuple-element.147.refs_1_, bf16[1,512,768]{2,1,0:T(8,128)(2,1)} %get-tuple-element.146.refs_2_, bf16[1,512,1536]{2,1,0:T(8,128)(2,1)} %bitcast.65, ...), custom_call_target="tpu_custom_call" | custom-call | flops 20132659200 | bytes 6291456 | tf_op jit(solution)/shard_map/pallas_call | solution.py:221
  102.5 45.6 %shard_map.431 = (bf16[2,512,768]{2,1,0:T(8,128)(2,1)}, bf16[512,768]{1,0:T(8,128)(2,1)}, bf16[1024,3072]{1,0:T(8,128)(2,1)}, bf16[1024,768]{1,0:T(8,128)(2,1)},...) custom-call(s32[2]{0:T(128)} %pad_add_fusion.1._.scalar_ref, ...), custom_call_target="tpu_custom_call" | custom-call | flops 21743271936 | bytes 42504192 | tf_op jit(solution)/shard_map/pallas_call | solution.py:508
  148.2 10.6 %shard_map.433 = (bf16[1536,768]{1,0:T(8,128)(2,1)}, bf16[1536,768]{1,0:T(8,128)(2,1)}) custom-call(s32[2]{0:T(128)} %pad_add_fusion.1._.scalar_ref, bf16[1024,3072]{1,0:T(8,128)(2,1)} %get-tuple-element.94.left_ref, bf16[1024,768]{1,0:T(8,128)(2,1)} %get-tuple-element.95.right_ref), custom_call_target="tpu_custom_call" | custom-call | flops 4831838208 | bytes 12582912 | tf_op jit(solution)/shard_map/pallas_call | solution.py:707
  158.7 12.9 %shard_map.434 = (bf16[384,3968]{1,0:T(8,128)(2,1)}, bf16[384,3968]{1,0:T(8,128)(2,1)}) custom-call(s32[2]{0:T(128)} %pad_add_fusion.1._.scalar_ref, bf16[1024,768]{1,0:T(8,128)(2,1)} %get-tuple-element.98.refs_0_, bf16[1024,3072]{1,0:T(8,128)(2,1)} %get-tuple-element.99.refs_1_, bf16[1024,768]{1,0:T(8,128)(2,1)} %bitcast.74, ...), custom_call_target="tpu_custom_call" | custom-call | flops 6241124352 | bytes 17104896 | tf_op jit(solution)/shard_map/pallas_call | solution.py:647
  172.1 8.2 %collective-permute-done.5 = bf16[1536,768]{1,0:T(8,128)(2,1)S(1)} collective-permute-done((bf16[1536,768]{1,0:T(8,128)(2,1)}, bf16[1536,768]{1,0:T(8,128)(2,1)S(1)}, u32[]{:S(2)}, u32[]{:S(2)}) %collective-permute-start.5) | collective-permute-done | bytes 2359328 | tf_op jit(solution)/shard_map/ppermute | solution.py:771
  181.8 3.1 add_convert_fusion.1.refs_11_
  185.0 2.9 add_convert_fusion.refs_12_
  187.9 2.0 collective-permute-start.8
  189.8 23.6 %collective-permute-done.7 = bf16[768,768]{1,0:T(8,128)(2,1)} collective-permute-done((bf16[768,768]{1,0:T(8,128)(2,1)}, bf16[768,768]{1,0:T(8,128)(2,1)}, u32[]{:S(2)}, u32[]{:S(2)}) %collective-permute-start.7) | collective-permute-done | bytes 1179680 | tf_op jit(solution)/shard_map/ppermute | solution.py:771
  213.5 2.6 add_convert_fusion.5.refs_6_
  218.1 18.2 %collective-permute-done.9 = bf16[384,768]{1,0:T(8,128)(2,1)} collective-permute-done((bf16[384,768]{1,0:T(8,128)(2,1)}, bf16[384,768]{1,0:T(8,128)(2,1)}, u32[]{:S(2)}, u32[]{:S(2)}) %collective-permute-start.9) | collective-permute-done | bytes 589856 | tf_op jit(solution)/shard_map/ppermute | solution.py:771
  236.4 2.2 add_convert_fusion.12.refs_3_
  238.6 1.8 collective-permute-start.10
  240.4 2.6 shard_map.432.refs_13_
  243.0 4.2 collective-permute-done.10
  249.5 2.6 collective-permute-start.13
  252.0 2.8 add_convert_fusion.4.refs_7_
  256.3 7.9 %collective-permute-done.13 = bf16[192,768]{1,0:T(8,128)(2,1)S(1)} collective-permute-done((bf16[192,768]{1,0:T(8,128)(2,1)S(1)}, bf16[192,768]{1,0:T(8,128)(2,1)S(1)}, u32[]{:S(2)}, u32[]{:S(2)}) %collective-permute-start.13) | collective-permute-done | bytes 294944 | tf_op jit(solution)/shard_map/ppermute | solution.py:771
  264.1 2.3 add_convert_fusion.11.refs_8_
  266.5 38.0 %shard_map.435 = (bf16[1,1024,768]{2,1,0:T(8,128)(2,1)}, bf16[1,1024,768]{2,1,0:T(8,128)(2,1)}, bf16[1,1024,768]{2,1,0:T(8,128)(2,1)}) custom-call(s32[1]{0:T(128)} %bitcast.2.refs_0_, bf16[1,512,768]{2,1,0:T(8,128)(2,1)} %get-tuple-element.147.refs_1_, bf16[1,512,768]{2,1,0:T(8,128)(2,1)} %get-tuple-element.146.refs_2_, bf16[1,512,1536]{2,1,0:T(8,128)(2,1)} %bitcast.67, ...), custom_call_target="tpu_custom_call" | custom-call | flops 32715571200 | bytes 12582912 | tf_op jit(solution)/shard_map/pallas_call | solution.py:250
  304.5 9.4 %shard_map.436 = (bf16[384,2432]{1,0:T(8,128)(2,1)}, bf16[384,2432]{1,0:T(8,128)(2,1)}) custom-call(s32[2]{0:T(128)} %pad_add_fusion.1._.scalar_ref, bf16[1024,768]{1,0:T(8,128)(2,1)} %get-tuple-element.87.refs_3_.refs_0_, bf16[1024,768]{1,0:T(8,128)(2,1)} %bitcast.39, bf16[2,512,768]{2,1,0:T(8,128)(2,1)} %refs_2_.5, ...), custom_call_target="tpu_custom_call" | custom-call | flops 3825205248 | bytes 12386304 | tf_op jit(solution)/shard_map/pallas_call | solution.py:647
  314.0 2.4 add_convert_fusion.10.refs_4_
  316.8 11.1 %collective-permute-done.12 = bf16[48,3968]{1,0:T(8,128)(2,1)S(1)} collective-permute-done((bf16[48,3968]{1,0:T(8,128)(2,1)}, bf16[48,3968]{1,0:T(8,128)(2,1)S(1)}, u32[]{:S(2)}, u32[]{:S(2)}) %collective-permute-start.12) | collective-permute-done | bytes 380960 | tf_op jit(solution)/shard_map/ppermute | solution.py:771
  329.5 2.1 collective-permute-start.14
  331.6 11.1 %shard_map.437 = (f32[1024,768]{1,0:T(8,128)}, bf16[1024,768]{1,0:T(8,128)(2,1)}, bf16[1024,768]{1,0:T(8,128)(2,1)}, f32[768,128]{1,0:T(8,128)}) custom-call(s32[2]{0:T(128)} %pad_add_fusion.1._.scalar_ref, bf16[1024,768]{1,0:T(8,128)(2,1)} %bitcast.40, f32[1024,768]{1,0:T(8,128)} %get-tuple-element.105.refs_1_, ...), custom_call_target="tpu_custom_call" | custom-call | flops 2415919104 | bytes 17435648 | tf_op jit(solution)/shard_map/pallas_call | solution.py:508
  342.7 2.3 add_convert_fusion.2.refs_5_
  346.6 2.5 collective-permute-done.14
  349.1 2.4 add_convert_fusion.9.refs_9_
  351.6 7.7 %shard_map.440 = (f32[2,512,768]{2,1,0:T(8,128)}, bf16[512,768]{1,0:T(8,128)(2,1)}) custom-call(s32[2]{0:T(128)} %pad_add_fusion.1._.scalar_ref, bf16[1024,768]{1,0:T(8,128)(2,1)} %bitcast.77, bf16[1024,768]{1,0:T(8,128)(2,1)} %bitcast.79, bf16[768,1536]{1,0:T(8,128)(2,1)} %refs_2_.7, bf16[192,768]{1,0:T(8,128)(2,1)} %add_convert_fusion.12.refs_3_, ...), custom_call_target="tpu_custom_call" | custom-call | flops 2415919104 | bytes 9437184 | tf_op jit(solution)/shard_map/pallas_call | solution.py:508
  360.6 13.2 %collective-permute-done.16 = bf16[192,2432]{1,0:T(8,128)(2,1)} collective-permute-done((bf16[192,2432]{1,0:T(8,128)(2,1)}, bf16[192,2432]{1,0:T(8,128)(2,1)}, u32[]{:S(2)}, u32[]{:S(2)}) %collective-permute-start.16) | collective-permute-done | bytes 933920 | tf_op jit(solution)/shard_map/ppermute | solution.py:771
  373.8 2.3 add_convert_fusion.7.refs_10_
  377.4 15.1 %shard_map.438 = (bf16[1,1024,768]{2,1,0:T(8,128)(2,1)}, bf16[1,1024,768]{2,1,0:T(8,128)(2,1)}, bf16[1,1024,768]{2,1,0:T(8,128)(2,1)}) custom-call(s32[1]{0:T(128)} %bitcast.2.refs_0_, bf16[1,512,2304]{2,1,0:T(8,128)(2,1)} %bitcast.48, bf16[1,512,2304]{2,1,0:T(8,128)(2,1)} %bitcast.57, bf16[1,512,2304]{2,1,0:T(8,128)(2,1)} %bitcast.49, ...), custom_call_target="tpu_custom_call" | custom-call | flops 16357785600 | bytes 6291456 | tf_op jit(solution)/shard_map/pallas_call | solution.py:250
  393.4 2.9 shard_map.441.refs_15_
  396.3 10.0 %shard_map.439 = (bf16[384,2048]{1,0:T(8,128)(2,1)}, bf16[384,2048]{1,0:T(8,128)(2,1)}) custom-call(s32[2]{0:T(128)} %pad_add_fusion.1._.scalar_ref, bf16[1024,768]{1,0:T(8,128)(2,1)} %bitcast.64, bf16[1024,768]{1,0:T(8,128)(2,1)} %get-tuple-element.115.refs_1_, bf16[2,512,768]{2,1,0:T(8,128)(2,1)} %refs_0_.5, bf16[512,768]{1,0:T(8,128)(2,1)} %copy-done.12, ...), custom_call_target="tpu_custom_call" | custom-call | flops 3221225472 | bytes 13369344 | tf_op jit(solution)/shard_map/pallas_call | solution.py:647
  407.7 1.9 collective-permute-start.30
  409.6 15.3 %shard_map.442 = (bf16[1,1024,768]{2,1,0:T(8,128)(2,1)}, bf16[1,1024,768]{2,1,0:T(8,128)(2,1)}, bf16[1,1024,768]{2,1,0:T(8,128)(2,1)}) custom-call(s32[1]{0:T(128)} %bitcast.2.refs_0_, bf16[1,512,2304]{2,1,0:T(8,128)(2,1)} %bitcast.51, bf16[1,512,2304]{2,1,0:T(8,128)(2,1)} %bitcast.60, ...), custom_call_target="tpu_custom_call", output_to_operand_aliasing={{0}: (11, {}), {1}: (12, {}), {2}: (13, {})} | custom-call | flops 16357785600 | bytes 6291456 | tf_op jit(solution)/shard_map/pallas_call | solution.py:250
  424.9 7.0 %shard_map.443 = (bf16[384,1280]{1,0:T(8,128)(2,1)}, bf16[384,1280]{1,0:T(8,128)(2,1)}) custom-call(s32[2]{0:T(128)} %pad_add_fusion.1._.scalar_ref, bf16[2,512,768]{2,1,0:T(8,128)(2,1)} %refs_0_.5, bf16[512,768]{1,0:T(8,128)(2,1)} %copy-done.12, bf16[1024,768]{1,0:T(8,128)(2,1)} %bitcast.30, bf16[1024,768]{1,0:T(8,128)(2,1)} %bitcast.33, ...), custom_call_target="tpu_custom_call" | custom-call | flops 2013265920 | bytes 9043968 | tf_op jit(solution)/shard_map/pallas_call | solution.py:647
  435.1 11.7 %collective-permute-done.31 = bf16[48,2432]{1,0:T(8,128)(2,1)S(1)} collective-permute-done((bf16[48,2432]{1,0:T(8,128)(2,1)S(1)}, bf16[48,2432]{1,0:T(8,128)(2,1)S(1)}, u32[]{:S(2)}, u32[]{:S(2)}) %collective-permute-start.31) | collective-permute-done | bytes 233504 | tf_op jit(solution)/shard_map/ppermute | solution.py:771
  446.9 2.0 add_convert_fusion.14
  451.2 4.4 convert_element_type.452
  456.9 2.5 collective-permute-start.22
  459.4 5.6 collective-permute-done.25
  466.3 2.2 collective-permute-start.26
  468.4 9.9 %shard_map.444 = (f32[2,512,768]{2,1,0:T(8,128)}, bf16[512,768]{1,0:T(8,128)(2,1)}) custom-call(s32[2]{0:T(128)} %pad_add_fusion.1._.scalar_ref, bf16[1024,768]{1,0:T(8,128)(2,1)} %bitcast.31, bf16[1024,768]{1,0:T(8,128)(2,1)} %bitcast.34, bf16[1024,768]{1,0:T(8,128)(2,1)} %bitcast.37, f32[1024,768]{1,0:T(8,128)} %get-tuple-element.124.refs_3_, ...), custom_call_target="tpu_custom_call" | custom-call | flops 3623878656 | bytes 15335424 | tf_op jit(solution)/shard_map/pallas_call | solution.py:508
  483.4 3.9 collective-permute-done.23
  488.4 2.5 collective-permute-start.24
  493.6 7.5 %collective-permute-done.24 = bf16[48,2048]{1,0:T(8,128)(2,1)S(1)} collective-permute-done((bf16[48,2048]{1,0:T(8,128)(2,1)S(1)}, bf16[48,2048]{1,0:T(8,128)(2,1)S(1)}, u32[]{:S(2)}, u32[]{:S(2)}) %collective-permute-start.24) | collective-permute-done | bytes 196640 | tf_op jit(solution)/shard_map/ppermute | solution.py:771
  501.1 1.8 add_convert_fusion.16
  504.2 33.3 %all_gather.16.refs_1_ = bf16[384,1280]{1,0:T(8,128)(2,1)} all-gather(bf16[48,1280]{1,0:T(8,128)(2,1)S(1)} %add_convert_fusion.18), channel_id=1, replica_groups=mesh['wide'=2,'far'=2,'near'=2,'side'=2,'core'=2] {'core','side','near'}, dimensions={0}, use_global_device_ids=true | all-gather | bytes 1105920 | tf_op jit(solution)/shard_map/all_gather | solution.py:799
  538.4 2.9 shard_map.445
  544.4 2.2 slice_convert_fusion.2
  546.5 4.4 slice_convert_fusion
  554.2 2.2 slice_convert_fusion.3
  558.0 4.1 shard_map.446
  (127 shorter events, 49.7 us)
Async XLA Ops:
  7.2 444.0 %all-gather.11.cloned.1.call-start = ((), (), s32[]{:S(2)}) async-start(), calls=%async_computation.3 | async-start | bytes 2654208 | tf_op jit(solution)/shard_map/all_gather | solution.py:799
  7.2 5.3 copy-start.16
  8.1 6.4 %copy-start.15 = (bf16[2,512,768]{2,1,0:T(8,128)(2,1)S(1)}, bf16[2,512,768]{2,1,0:T(8,128)(2,1)}, u32[]{:S(2)}) copy-start(bf16[2,512,768]{2,1,0:T(8,128)(2,1)} %refs_2_.4) | copy-start | bytes 4718596
  8.1 19.5 %collective-permute-start.1 = (s32[512]{0:T(512)S(1)}, s32[512]{0:T(512)S(1)}, u32[]{:S(2)}, u32[]{:S(2)}) collective-permute-start(s32[512]{0:T(512)S(1)} %bitcast.42), channel_id=1, source_target_pairs={{0,16},{16,0},{1,17},{17,1},{2,18},{18,2},{3,19},{19,3},{4,20},{20... | collective-permute-start | bytes 6152 | tf_op jit(solution)/shard_map/ppermute | solution.py:771
  12.3 3.1 copy-start.19
  12.3 3.7 copy-start.20
  12.3 3.7 copy-start.21
  12.3 20.5 %collective-permute-start = (bf16[512,768]{1,0:T(8,128)(2,1)S(1)}, bf16[512,768]{1,0:T(8,128)(2,1)S(1)}, u32[]{:S(2)}, u32[]{:S(2)}) collective-permute-start(bf16[512,768]{1,0:T(8,128)(2,1)S(1)} %dynamic-slice_bitcast_fusion.2), channel_id=1, source_target_pairs={{0,16},{16,0},{1,17},{17,1},{2,18},{18,2},{3,19},{19,3},{4,20},{20... | collective-permute-start | bytes 2359304 | tf_op jit(solution)/shard_map/ppermute | solution.py:771
  12.6 61.1 %collective-permute-start.2 = (bf16[512,768]{1,0:T(8,128)(2,1)S(1)}, bf16[512,768]{1,0:T(8,128)(2,1)}, u32[]{:S(2)}, u32[]{:S(2)}) collective-permute-start(bf16[512,768]{1,0:T(8,128)(2,1)S(1)} %dynamic-slice_bitcast_fusion.1), channel_id=1, source_target_pairs={{0,16},{16,0},{1,17},{17,1},{2,18},{18,2},{3,19},{19,3},{4,20},{20... | collective-permute-start | bytes 2359304 | tf_op jit(solution)/shard_map/ppermute | solution.py:771
  14.6 87.9 %collective-permute-start.3 = (bf16[512,768]{1,0:T(8,128)(2,1)S(1)}, bf16[512,768]{1,0:T(8,128)(2,1)}, u32[]{:S(2)}, u32[]{:S(2)}) collective-permute-start(bf16[512,768]{1,0:T(8,128)(2,1)S(1)} %dynamic-slice_bitcast_fusion), channel_id=1, source_target_pairs={{0,16},{16,0},{1,17},{17,1},{2,18},{18,2},{3,19},{19,3},{4,20},{20... | collective-permute-start | bytes 2359304 | tf_op jit(solution)/shard_map/ppermute | solution.py:771
  32.9 0.9 copy-start.12
  171.6 13.4 %collective-permute-start.6 = (bf16[384,3968]{1,0:T(8,128)(2,1)}, bf16[384,3968]{1,0:T(8,128)(2,1)}, u32[]{:S(2)}, u32[]{:S(2)}) collective-permute-start(bf16[384,3968]{1,0:T(8,128)(2,1)} %get-tuple-element.103), channel_id=1, source_target_pairs={{0,1},{1,0},{2,3},{3,2},{4,5},{5,4},{6,7},{7,6},{8,9},{9,8},{10,11... | collective-permute-start | bytes 9142280 | tf_op jit(solution)/shard_map/ppermute | solution.py:771
  171.6 8.8 %collective-permute-start.5 = (bf16[1536,768]{1,0:T(8,128)(2,1)}, bf16[1536,768]{1,0:T(8,128)(2,1)S(1)}, u32[]{:S(2)}, u32[]{:S(2)}) collective-permute-start(bf16[1536,768]{1,0:T(8,128)(2,1)} %get-tuple-element.97.refs_5_), channel_id=1, source_target_pairs={{0,1},{1,0},{2,3},{3,2},{4,5},{5,4},{6,7},{7,6},{8,9},{9,8},{10,11... | collective-permute-start | bytes 7077896 | tf_op jit(solution)/shard_map/ppermute | solution.py:771
  180.4 1.5 copy-start.2
  181.8 3.2 copy-start
  184.9 28.5 %collective-permute-start.7 = (bf16[768,768]{1,0:T(8,128)(2,1)}, bf16[768,768]{1,0:T(8,128)(2,1)}, u32[]{:S(2)}, u32[]{:S(2)}) collective-permute-start(bf16[768,768]{1,0:T(8,128)(2,1)} %add_convert_fusion.1.refs_11_), channel_id=1, source_target_pairs={{0,16},{16,0},{1,17},{17,1},{2,18},{18,2},{3,19},{19,3},{4,20},{20... | collective-permute-start | bytes 3538952 | tf_op jit(solution)/shard_map/ppermute | solution.py:771
  187.9 64.2 %collective-permute-start.8 = (bf16[192,3968]{1,0:T(8,128)(2,1)}, bf16[192,3968]{1,0:T(8,128)(2,1)}, u32[]{:S(2)}, u32[]{:S(2)}) collective-permute-start(bf16[192,3968]{1,0:T(8,128)(2,1)} %add_convert_fusion.refs_12_), channel_id=1, source_target_pairs={{0,2},{2,0},{1,3},{3,1},{4,6},{6,4},{5,7},{7,5},{8,10},{10,8},{9,1... | collective-permute-start | bytes 4571144 | tf_op jit(solution)/shard_map/ppermute | solution.py:771
  216.1 20.3 %collective-permute-start.9 = (bf16[384,768]{1,0:T(8,128)(2,1)}, bf16[384,768]{1,0:T(8,128)(2,1)}, u32[]{:S(2)}, u32[]{:S(2)}) collective-permute-start(bf16[384,768]{1,0:T(8,128)(2,1)} %add_convert_fusion.5.refs_6_), channel_id=1, source_target_pairs={{0,2},{2,0},{1,3},{3,1},{4,6},{6,4},{5,7},{7,5},{8,10},{10,8},{9,1... | collective-permute-start | bytes 1769480 | tf_op jit(solution)/shard_map/ppermute | solution.py:771
  217.6 22.8 %collective-permute-start.4 = (bf16[512,768]{1,0:T(8,128)(2,1)}, bf16[512,768]{1,0:T(8,128)(2,1)}, u32[]{:S(2)}, u32[]{:S(2)}) collective-permute-start(bf16[512,768]{1,0:T(8,128)(2,1)} %get-tuple-element.90), channel_id=1, source_target_pairs={{0,16},{16,0},{1,17},{17,1},{2,18},{18,2},{3,19},{19,3},{4,20},{20... | collective-permute-start | bytes 2359304 | tf_op jit(solution)/shard_map/ppermute | solution.py:771
  238.6 8.6 %collective-permute-start.10 = (bf16[192,768]{1,0:T(8,128)(2,1)}, bf16[192,768]{1,0:T(8,128)(2,1)S(1)}, u32[]{:S(2)}, u32[]{:S(2)}) collective-permute-start(bf16[192,768]{1,0:T(8,128)(2,1)} %add_convert_fusion.12.refs_3_), channel_id=1, source_target_pairs={{0,4},{4,0},{1,5},{5,1},{2,6},{6,2},{3,7},{7,3},{8,12},{12,8},{9,1... | collective-permute-start | bytes 884744 | tf_op jit(solution)/shard_map/ppermute | solution.py:771
  248.7 0.7 copy-start.18
  249.5 14.7 %collective-permute-start.13 = (bf16[192,768]{1,0:T(8,128)(2,1)S(1)}, bf16[192,768]{1,0:T(8,128)(2,1)S(1)}, u32[]{:S(2)}, u32[]{:S(2)}) collective-permute-start(bf16[192,768]{1,0:T(8,128)(2,1)S(1)} %fusion.5.refs_11_), channel_id=1, source_target_pairs={{0,8},{8,0},{1,9},{9,1},{2,10},{10,2},{3,11},{11,3},{4,12},{12,4},... | collective-permute-start | bytes 884744 | tf_op jit(solution)/shard_map/ppermute | solution.py:771
  254.8 59.2 %collective-permute-start.11 = (bf16[96,3968]{1,0:T(8,128)(2,1)}, bf16[96,3968]{1,0:T(8,128)(2,1)}, u32[]{:S(2)}, u32[]{:S(2)}) collective-permute-start(bf16[96,3968]{1,0:T(8,128)(2,1)} %add_convert_fusion.4.refs_7_), channel_id=1, source_target_pairs={{0,16},{16,0},{1,17},{17,1},{2,18},{18,2},{3,19},{19,3},{4,20},{20... | collective-permute-start | bytes 2285576 | tf_op jit(solution)/shard_map/ppermute | solution.py:771
  266.4 274.8 %all-gather.9.cloned.1.call-start = ((), (), s32[]{:S(2)}) async-start(), calls=%async_computation.2 | async-start | bytes 3428352 | tf_op jit(solution)/shard_map/all_gather | solution.py:799
  314.0 28.7 %collective-permute-start.15 = (bf16[384,2432]{1,0:T(8,128)(2,1)}, bf16[384,2432]{1,0:T(8,128)(2,1)}, u32[]{:S(2)}, u32[]{:S(2)}) collective-permute-start(bf16[384,2432]{1,0:T(8,128)(2,1)} %get-tuple-element.109.refs_7_), channel_id=1, source_target_pairs={{0,1},{1,0},{2,3},{3,2},{4,5},{5,4},{6,7},{7,6},{8,9},{9,8},{10,11... | collective-permute-start | bytes 5603336 | tf_op jit(solution)/shard_map/ppermute | solution.py:771
  316.4 11.5 %collective-permute-start.12 = (bf16[48,3968]{1,0:T(8,128)(2,1)}, bf16[48,3968]{1,0:T(8,128)(2,1)S(1)}, u32[]{:S(2)}, u32[]{:S(2)}) collective-permute-start(bf16[48,3968]{1,0:T(8,128)(2,1)} %add_convert_fusion.10.refs_4_), channel_id=1, source_target_pairs={{0,4},{4,0},{1,5},{5,1},{2,6},{6,2},{3,7},{7,3},{8,12},{12,8},{9,1... | collective-permute-start | bytes 1142792 | tf_op jit(solution)/shard_map/ppermute | solution.py:771
  329.5 13.2 %copy-start.17 = (bf16[48,3968]{1,0:T(8,128)(2,1)}, bf16[48,3968]{1,0:T(8,128)(2,1)S(1)}, u32[]{:S(2)}) copy-start(bf16[48,3968]{1,0:T(8,128)(2,1)S(1)} %fusion.6.refs_12_) | copy-start | bytes 1142788
  329.5 19.6 %collective-permute-start.14 = (bf16[48,3968]{1,0:T(8,128)(2,1)S(1)}, bf16[48,3968]{1,0:T(8,128)(2,1)S(1)}, u32[]{:S(2)}, u32[]{:S(2)}) collective-permute-start(bf16[48,3968]{1,0:T(8,128)(2,1)S(1)} %fusion.6.refs_12_), channel_id=1, source_target_pairs={{0,8},{8,0},{1,9},{9,1},{2,10},{10,2},{3,11},{11,3},{4,12},{12,4},... | collective-permute-start | bytes 1142792 | tf_op jit(solution)/shard_map/ppermute | solution.py:771
  331.6 11.1 %copy-start.3 = (bf16[384,2432]{1,0:T(8,128)(2,1)S(1)}, bf16[384,2432]{1,0:T(8,128)(2,1)}, u32[]{:S(2)}) copy-start(bf16[384,2432]{1,0:T(8,128)(2,1)} %get-tuple-element.117) | copy-start | bytes 5603332
  345.1 28.8 %collective-permute-start.16 = (bf16[192,2432]{1,0:T(8,128)(2,1)}, bf16[192,2432]{1,0:T(8,128)(2,1)}, u32[]{:S(2)}, u32[]{:S(2)}) collective-permute-start(bf16[192,2432]{1,0:T(8,128)(2,1)} %add_convert_fusion.2.refs_5_), channel_id=1, source_target_pairs={{0,2},{2,0},{1,3},{3,1},{4,6},{6,4},{5,7},{7,5},{8,10},{10,8},{9,1... | collective-permute-start | bytes 2801672 | tf_op jit(solution)/shard_map/ppermute | solution.py:771
  351.6 22.3 %copy-start.4 = (bf16[384,2432]{1,0:T(8,128)(2,1)S(1)}, bf16[384,2432]{1,0:T(8,128)(2,1)}, u32[]{:S(2)}) copy-start(bf16[384,2432]{1,0:T(8,128)(2,1)} %get-tuple-element.117) | copy-start | bytes 5603332
  351.6 199.4 %all-gather.7.cloned.1.call-start = ((), (), s32[]{:S(2)}) async-start(), calls=%async_computation.1 | async-start | bytes 2101248 | tf_op jit(solution)/shard_map/all_gather | solution.py:799
  359.4 33.2 %collective-permute-start.17 = (bf16[512,768]{1,0:T(8,128)(2,1)}, bf16[512,768]{1,0:T(8,128)(2,1)S(1)}, u32[]{:S(2)}, u32[]{:S(2)}) collective-permute-start(bf16[512,768]{1,0:T(8,128)(2,1)} %get-tuple-element.119), channel_id=1, source_target_pairs={{0,16},{16,0},{1,17},{17,1},{2,18},{18,2},{3,19},{19,3},{4,20},{20... | collective-permute-start | bytes 2359304 | tf_op jit(solution)/shard_map/ppermute | solution.py:771
  376.1 30.2 %collective-permute-start.29 = (bf16[96,2432]{1,0:T(8,128)(2,1)}, bf16[96,2432]{1,0:T(8,128)(2,1)S(1)}, u32[]{:S(2)}, u32[]{:S(2)}) collective-permute-start(bf16[96,2432]{1,0:T(8,128)(2,1)} %add_convert_fusion.7.refs_10_), channel_id=1, source_target_pairs={{0,16},{16,0},{1,17},{17,1},{2,18},{18,2},{3,19},{19,3},{4,20},{20... | collective-permute-start | bytes 1400840 | tf_op jit(solution)/shard_map/ppermute | solution.py:771
  392.5 0.9 copy-start.14
  406.3 27.1 %collective-permute-start.18 = (bf16[384,2048]{1,0:T(8,128)(2,1)}, bf16[384,2048]{1,0:T(8,128)(2,1)S(1)}, u32[]{:S(2)}, u32[]{:S(2)}) collective-permute-start(bf16[384,2048]{1,0:T(8,128)(2,1)} %get-tuple-element.118.refs_14_.refs_5_), channel_id=1, source_target_pairs={{0,1},{1,0},{2,3},{3,2},{4,5},{5,4},{6,7},{7,6},{8,9},{9,8},{10,11... | collective-permute-start | bytes 4718600 | tf_op jit(solution)/shard_map/ppermute | solution.py:771
  407.7 24.4 %collective-permute-start.30 = (bf16[48,2432]{1,0:T(8,128)(2,1)S(1)}, bf16[48,2432]{1,0:T(8,128)(2,1)S(1)}, u32[]{:S(2)}, u32[]{:S(2)}) collective-permute-start(bf16[48,2432]{1,0:T(8,128)(2,1)S(1)} %add_convert_fusion.15), channel_id=1, source_target_pairs={{0,4},{4,0},{1,5},{5,1},{2,6},{6,2},{3,7},{7,3},{8,12},{12,8},{9,1... | collective-permute-start | bytes 700424 | tf_op jit(solution)/shard_map/ppermute | solution.py:771
  424.9 8.6 %copy-start.5 = (bf16[384,2048]{1,0:T(8,128)(2,1)S(1)}, bf16[384,2048]{1,0:T(8,128)(2,1)}, u32[]{:S(2)}) copy-start(bf16[384,2048]{1,0:T(8,128)(2,1)} %get-tuple-element.126) | copy-start | bytes 4718596
  431.9 17.1 %collective-permute-start.19 = (bf16[384,1280]{1,0:T(8,128)(2,1)}, bf16[384,1280]{1,0:T(8,128)(2,1)}, u32[]{:S(2)}, u32[]{:S(2)}) collective-permute-start(bf16[384,1280]{1,0:T(8,128)(2,1)} %get-tuple-element.125.refs_5_), channel_id=1, source_target_pairs={{0,1},{1,0},{2,3},{3,2},{4,5},{5,4},{6,7},{7,6},{8,9},{9,8},{10,11... | collective-permute-start | bytes 2949128 | tf_op jit(solution)/shard_map/ppermute | solution.py:771
  433.4 13.5 %collective-permute-start.31 = (bf16[48,2432]{1,0:T(8,128)(2,1)S(1)}, bf16[48,2432]{1,0:T(8,128)(2,1)S(1)}, u32[]{:S(2)}, u32[]{:S(2)}) collective-permute-start(bf16[48,2432]{1,0:T(8,128)(2,1)S(1)} %fusion.4), channel_id=1, source_target_pairs={{0,8},{8,0},{1,9},{9,1},{2,10},{10,2},{3,11},{11,3},{4,12},{12,4},... | collective-permute-start | bytes 700424 | tf_op jit(solution)/shard_map/ppermute | solution.py:771
  433.5 1.1 copy-start.7
  434.6 15.7 %copy-start.1 = (bf16[192,2048]{1,0:T(8,128)(2,1)}, bf16[192,2048]{1,0:T(8,128)(2,1)S(1)}, u32[]{:S(2)}) copy-start(bf16[192,2048]{1,0:T(8,128)(2,1)S(1)} %add_convert_fusion.3.refs_6_) | copy-start | bytes 2359300
  434.6 20.9 %collective-permute-start.21 = (bf16[192,2048]{1,0:T(8,128)(2,1)S(1)}, bf16[192,2048]{1,0:T(8,128)(2,1)}, u32[]{:S(2)}, u32[]{:S(2)}) collective-permute-start(bf16[192,2048]{1,0:T(8,128)(2,1)S(1)} %add_convert_fusion.3.refs_6_), channel_id=1, source_target_pairs={{0,16},{16,0},{1,17},{17,1},{2,18},{18,2},{3,19},{19,3},{4,20},{20... | collective-permute-start | bytes 2359304 | tf_op jit(solution)/shard_map/ppermute | solution.py:771
  448.9 109.1 %all-gather.5.cloned.1.call-start = ((), (), s32[]{:S(2)}) async-start(), calls=%async_computation | async-start | bytes 1769472 | tf_op jit(solution)/shard_map/all_gather | solution.py:799
  450.3 5.3 copy-start.9
  450.3 14.7 %collective-permute-start.25 = (bf16[192,1280]{1,0:T(8,128)(2,1)S(1)}, bf16[192,1280]{1,0:T(8,128)(2,1)}, u32[]{:S(2)}, u32[]{:S(2)}) collective-permute-start(bf16[192,1280]{1,0:T(8,128)(2,1)S(1)} %add_convert_fusion.6.refs_7_), channel_id=1, source_target_pairs={{0,16},{16,0},{1,17},{17,1},{2,18},{18,2},{3,19},{19,3},{4,20},{20... | collective-permute-start | bytes 1474568 | tf_op jit(solution)/shard_map/ppermute | solution.py:771
  451.2 4.4 copy-start.6
  451.2 4.4 copy-start.8
  455.6 9.5 %copy-start.11 = (bf16[384,1280]{1,0:T(8,128)(2,1)S(1)}, bf16[384,1280]{1,0:T(8,128)(2,1)}, u32[]{:S(2)}) copy-start(bf16[384,1280]{1,0:T(8,128)(2,1)} %get-tuple-element.127) | copy-start | bytes 2949124
  456.9 22.1 %collective-permute-start.22 = (bf16[96,2048]{1,0:T(8,128)(2,1)S(1)}, bf16[96,2048]{1,0:T(8,128)(2,1)S(1)}, u32[]{:S(2)}, u32[]{:S(2)}) collective-permute-start(bf16[96,2048]{1,0:T(8,128)(2,1)S(1)} %add_convert_fusion.8), channel_id=1, source_target_pairs={{0,2},{2,0},{1,3},{3,1},{4,6},{6,4},{5,7},{7,5},{8,10},{10,8},{9,1... | collective-permute-start | bytes 1179656 | tf_op jit(solution)/shard_map/ppermute | solution.py:771
  466.3 14.6 %collective-permute-start.26 = (bf16[96,1280]{1,0:T(8,128)(2,1)S(1)}, bf16[96,1280]{1,0:T(8,128)(2,1)S(1)}, u32[]{:S(2)}, u32[]{:S(2)}) collective-permute-start(bf16[96,1280]{1,0:T(8,128)(2,1)S(1)} %add_convert_fusion.13), channel_id=1, source_target_pairs={{0,2},{2,0},{1,3},{3,1},{4,6},{6,4},{5,7},{7,5},{8,10},{10,8},{9,1... | collective-permute-start | bytes 737288 | tf_op jit(solution)/shard_map/ppermute | solution.py:771
  478.3 59.2 %collective-permute-start.20 = (bf16[512,768]{1,0:T(8,128)(2,1)}, bf16[512,768]{1,0:T(8,128)(2,1)S(1)}, u32[]{:S(2)}, u32[]{:S(2)}) collective-permute-start(bf16[512,768]{1,0:T(8,128)(2,1)} %get-tuple-element.128), channel_id=1, source_target_pairs={{0,16},{16,0},{1,17},{17,1},{2,18},{18,2},{3,19},{19,3},{4,20},{20... | collective-permute-start | bytes 2359304 | tf_op jit(solution)/shard_map/ppermute | solution.py:771
  480.2 7.1 %collective-permute-start.23 = (bf16[48,2048]{1,0:T(8,128)(2,1)S(1)}, bf16[48,2048]{1,0:T(8,128)(2,1)S(1)}, u32[]{:S(2)}, u32[]{:S(2)}) collective-permute-start(bf16[48,2048]{1,0:T(8,128)(2,1)S(1)} %add_convert_fusion.17), channel_id=1, source_target_pairs={{0,4},{4,0},{1,5},{5,1},{2,6},{6,2},{3,7},{7,3},{8,12},{12,8},{9,1... | collective-permute-start | bytes 589832 | tf_op jit(solution)/shard_map/ppermute | solution.py:771
  481.9 9.0 %collective-permute-start.27 = (bf16[48,1280]{1,0:T(8,128)(2,1)S(1)}, bf16[48,1280]{1,0:T(8,128)(2,1)S(1)}, u32[]{:S(2)}, u32[]{:S(2)}) collective-permute-start(bf16[48,1280]{1,0:T(8,128)(2,1)S(1)} %add_convert_fusion.19), channel_id=1, source_target_pairs={{0,4},{4,0},{1,5},{5,1},{2,6},{6,2},{3,7},{7,3},{8,12},{12,8},{9,1... | collective-permute-start | bytes 368648 | tf_op jit(solution)/shard_map/ppermute | solution.py:771
  488.4 12.6 %collective-permute-start.24 = (bf16[48,2048]{1,0:T(8,128)(2,1)S(1)}, bf16[48,2048]{1,0:T(8,128)(2,1)S(1)}, u32[]{:S(2)}, u32[]{:S(2)}) collective-permute-start(bf16[48,2048]{1,0:T(8,128)(2,1)S(1)} %fusion.3), channel_id=1, source_target_pairs={{0,8},{8,0},{1,9},{9,1},{2,10},{10,2},{3,11},{11,3},{4,12},{12,4},... | collective-permute-start | bytes 589832 | tf_op jit(solution)/shard_map/ppermute | solution.py:771
  492.1 10.8 %collective-permute-start.28 = (bf16[48,1280]{1,0:T(8,128)(2,1)S(1)}, bf16[48,1280]{1,0:T(8,128)(2,1)S(1)}, u32[]{:S(2)}, u32[]{:S(2)}) collective-permute-start(bf16[48,1280]{1,0:T(8,128)(2,1)S(1)} %fusion.2), channel_id=1, source_target_pairs={{0,8},{8,0},{1,9},{9,1},{2,10},{10,2},{3,11},{11,3},{4,12},{12,4},... | collective-permute-start | bytes 368648 | tf_op jit(solution)/shard_map/ppermute | solution.py:771
  537.5 0.9 copy-start.13
  550.9 5.4 copy-start.10
Sparse Core Ops, SparseCore 0:
  266.6 23.1 all-gather.10
  351.7 29.5 all-gather.8
  449.0 23.9 all-gather.6
  503.1 21.7 all-gather.4
